TPU v7x, 128 devices: a whole 4x4x4 slice. The times are simulated.
128 devices in a mesh: row: 16 (over z, x), col: 8 (over y, core).
Axes of the slice: x: 4, y: 4, z: 4, core: 2. Of those that a mesh axis runs over, the one named last changes fastest.
Arguments:
- block_pairs: int32 [128, 3, 2], P(('row', 'col')), may hold values from 0 to 127, as said below
- live_counts: int32 [128], P(('row', 'col')), may hold values from 1 to 3, as said below
- pair_blocks: bfloat16 [384, 1024, 1024], P(('row', 'col')), may hold values from -8 to 8, as said below
- start_basis: bfloat16 [128, 32, 1024], P(('row', 'col')), may hold values from -48 to 48
Outputs:
- first_basis: float32 [128, 32, 1024], P(('row', 'col'))
- embedding: float32 [128, 32, 1024], P(('row', 'col'))
Inputs may be any that keep to these rules, and one draw needn't show every extreme that they name: `block_pairs`: slot s of device d = (row index) * 8 + (col index) holds (i, j) with i <= j, i // 8 equal to the row index and j % 8 equal to the col index; live slots of one device are distinct pairs, and no pair stands on two devices; slots beyond the live count repeat a live pair. `live_counts`: some device has 3 live slots. `pair_blocks`: the block of a slot with i = j is symmetric.
All inputs are finite; a program needn't handle non-finite values.
Results may differ from a plain program's by a relative error of at most 0.0021.
Values may be sent and summed in bfloat16 or wider, within the bound.
No kernel may reach another device: no remote copies, remote signals or barrier semaphores. Data moves between devices by JAX's collectives and lax.ppermute only.
A program may use at most 64 MiB of HBM per device.

v0:
```python
import jax
import jax.numpy as jnp
from jax import lax
from jax.sharding import PartitionSpec as P


def lower_inverse(gram, width):
    factor = jnp.linalg.cholesky(gram)
    identity = jnp.eye(width, dtype=jnp.float32)
    return jax.scipy.linalg.solve_triangular(factor, identity, lower=True)


def local_gram(panel):
    return lax.dot_general(
        panel, panel, (((1,), (1,)), ((), ())), preferred_element_type=jnp.float32
    )


def local_gram_exact(panel):
    return jnp.dot(panel, panel.T, precision=lax.Precision.HIGHEST)


def on_device(block_pairs, live_counts, pair_blocks, start_basis):
    row_count = lax.axis_size("row")
    col_count = lax.axis_size("col")
    row_index = lax.axis_index("row")
    col_index = lax.axis_index("col")
    width = start_basis.shape[1]
    length = start_basis.shape[2]

    def product(panel):
        every = lax.all_gather(panel, ("row", "col"), axis=0, tiled=True)
        layout = every.reshape(row_count, col_count, width, length)
        band = lax.dynamic_index_in_dim(layout, row_index, 0, keepdims=False)
        column_set = lax.dynamic_index_in_dim(layout, col_index, 1, keepdims=False)

        def advance(slot, totals):
            band_total, class_total = totals
            first = block_pairs[0, slot, 0]
            second = block_pairs[0, slot, 1]
            band_slot = first - row_index * col_count
            class_slot = second // col_count
            matrix = lax.dynamic_index_in_dim(pair_blocks, slot, 0, keepdims=False)
            left = lax.dynamic_index_in_dim(column_set, class_slot, 0, keepdims=False)
            right = lax.dynamic_index_in_dim(band, band_slot, 0, keepdims=False)
            direct = lax.dot_general(
                left, matrix, (((1,), (1,)), ((), ())), preferred_element_type=jnp.float32
            )
            mirror = lax.dot_general(
                right, matrix, (((1,), (0,)), ((), ())), preferred_element_type=jnp.float32
            )
            mirror = jnp.where(first != second, mirror, 0.0)
            current = lax.dynamic_index_in_dim(band_total, band_slot, 0, keepdims=False)
            band_total = lax.dynamic_update_index_in_dim(band_total, current + direct, band_slot, 0)
            current = lax.dynamic_index_in_dim(class_total, class_slot, 0, keepdims=False)
            class_total = lax.dynamic_update_index_in_dim(
                class_total, current + mirror, class_slot, 0
            )
            return (band_total, class_total)

        start = (
            jnp.zeros((col_count, width, length), jnp.float32),
            jnp.zeros((row_count, width, length), jnp.float32),
        )
        band_total, class_total = lax.fori_loop(0, live_counts[0], advance, start)
        owned = lax.psum_scatter(band_total, "col", scatter_dimension=0, tiled=True)
        owned = owned + lax.psum_scatter(class_total, "row", scatter_dimension=0, tiled=True)
        return owned[0]

    users_total = row_count * col_count * length
    root_users = jnp.sqrt(jnp.float32(users_total))
    first_product = product(start_basis)
    panels = first_product.astype(jnp.bfloat16)
    gram_one = lax.psum(local_gram(panels), ("row", "col"))
    inverse_one = lower_inverse(gram_one, width)
    second_product = product(panels[None])
    scaled = jnp.dot(inverse_one, second_product, precision=lax.Precision.HIGHEST)
    gram_two = lax.psum(local_gram_exact(scaled), ("row", "col"))
    first_basis = jnp.dot(inverse_one, first_product, precision=lax.Precision.HIGHEST) * root_users
    inverse_two = lower_inverse(gram_two, width)
    result = jnp.dot(inverse_two, scaled, precision=lax.Precision.HIGHEST)
    return (first_basis[None], (result * root_users)[None])


def solution(mesh):
    in_specs = (
        P(("row", "col"), None, None),
        P(("row", "col")),
        P(("row", "col"), None, None),
        P(("row", "col"), None, None),
    )
    out_specs = (P(("row", "col"), None, None), P(("row", "col"), None, None))
    return jax.shard_map(
        on_device, mesh=mesh, in_specs=in_specs, out_specs=out_specs, check_vma=False
    )
```

profile of v0, /device:TPU:0, one launch (start us, length us, event | category | flops | bytes accessed | tf_op | source)
XLA Modules:
  0.0 525.0 jit_solution(8938701781563603468)
XLA Ops:
  7.2 0.7 all-gather.3.cloned.1.call-update
  7.9 75.7 %all-gather.3.cloned.1.call-done = bf16[128,32,1024]{2,1,0:T(8,128)(2,1)} async-done(((bf16[1,32,1024]{2,1,0:T(8,128)(2,1)}), bf16[128,32,1024]{2,1,0:T(8,128)(2,1)}) %all-gather.3.cloned.1.call-update) | async-done | bytes 8388624 | tf_op jit(solution)/shard_map/all_gather | solution.py:32
  83.6 1.9 dynamic-slice_bitcast_fusion.3
  85.5 2.4 dynamic-slice_bitcast_fusion.1
  88.5 31.4 %while.28 = (s32[]{:T(128)}, f32[8,32,1024]{2,1,0:T(8,128)S(1)}, f32[16,32,1024]{2,1,0:T(8,128)S(1)}, s32[]{:T(128)}, s32[1,3,2]{1,2,0:T(2,128)S(1)}, /*index=5*...) while((s32[]{:T(128)}, f32[8,32,1024]{2,1,0:T(8,128)S(1)}, ...), condition=%wide.region_1.2_spmd, body=%wide.region_0.1_spmd.sunk | while | flops 134316064 | bytes 5374427 | solution.py:65
  89.2 0.7 constant_dynamic-slice_fusion.12
  94.3 2.1 fusion.109
  96.4 2.4 fusion.108
  99.4 0.7 constant_dynamic-slice_fusion.12
  104.5 2.1 fusion.109
  106.6 2.4 fusion.108
  109.7 0.7 constant_dynamic-slice_fusion.12
  114.8 2.1 fusion.109
  116.9 2.4 fusion.108
  119.9 1.0 copy-done.3
  121.0 0.6 copy-done.1
  121.7 28.8 %reduce-scatter.9.cloned.1.call-done = f32[1,32,1024]{2,1,0:T(8,128)} async-done(((f32[8,32,1024]{2,1,0:T(8,128)}), f32[1,32,1024]{2,1,0:T(8,128)}) %reduce-scatter.9.cloned.1.call-update) | async-done | bytes 131088 | tf_op jit(solution)/shard_map/reduce_scatter | solution.py:66
  150.5 76.7 %reduce-scatter.13.cloned.1.call-done = f32[1,32,1024]{2,1,0:T(8,128)} async-done(((f32[16,32,1024]{2,1,0:T(8,128)}), f32[1,32,1024]{2,1,0:T(8,128)}) %reduce-scatter.13.cloned.1.call-update) | async-done | bytes 131088
  227.2 1.6 add_convert_fusion
  228.8 71.5 %all-gather.5.cloned.1.call-done = bf16[128,32,1024]{2,1,0:T(8,128)(2,1)} async-done(((bf16[1,32,1024]{2,1,0:T(8,128)(2,1)}), bf16[128,32,1024]{2,1,0:T(8,128)(2,1)}) %all-gather.5.cloned.1.call-update) | async-done | bytes 8388624 | tf_op jit(solution)/shard_map/all_gather | solution.py:32
  300.3 1.9 dynamic-slice_bitcast_fusion.2
  302.2 2.4 dynamic-slice_bitcast_fusion
  305.0 31.4 %while.29 = (s32[]{:T(128)}, f32[8,32,1024]{2,1,0:T(8,128)S(1)}, f32[16,32,1024]{2,1,0:T(8,128)S(1)}, s32[]{:T(128)}, s32[1,3,2]{1,2,0:T(2,128)S(1)}, /*index=5*...) while((s32[]{:T(128)}, f32[8,32,1024]{2,1,0:T(8,128)S(1)}, ...), condition=%wide.region_8.11_spmd, body=%wide.region_7.10_spmd.sunk | while | flops 134316064 | bytes 5374427 | solution.py:65
  305.6 0.7 constant_dynamic-slice_fusion.14
  310.7 2.1 fusion.115
  312.8 2.4 fusion.114
  315.9 0.7 constant_dynamic-slice_fusion.14
  321.0 2.1 fusion.115
  323.1 2.4 fusion.114
  326.1 0.7 constant_dynamic-slice_fusion.14
  331.2 2.1 fusion.115
  333.3 2.4 fusion.114
  336.4 1.0 copy-done.2
  337.4 0.6 copy-done
  338.1 63.2 %psum.14 = f32[32,32]{0,1:T(8,128)S(1)} all-reduce(f32[32,32]{0,1:T(8,128)S(1)} %fusion.72), channel_id=1, replica_groups=mesh['row'=16,'col'=8] {'row','col'}, use_global_device_ids=true, to_apply=%region_4.5 | all-reduce | flops 1024 | bytes 8192 | tf_op jit(solution)/shard_map/psum | solution.py:74
  401.5 2.9 cholesky.44
  404.4 0.6 compare_reduce_fusion.1
  405.1 0.7 fusion.79
  405.7 2.4 custom-call.6
  408.4 0.9 fusion.67
  409.3 34.8 %reduce-scatter.15.cloned.1.call-done = f32[1,32,1024]{2,1,0:T(8,128)} async-done(((f32[16,32,1024]{2,1,0:T(8,128)}), f32[1,32,1024]{2,1,0:T(8,128)}) %reduce-scatter.15.cloned.1.call-update) | async-done | bytes 131088
  444.1 1.2 fusion.68
  445.6 64.6 %psum.15 = f32[32,32]{0,1:T(8,128)S(1)} all-reduce(f32[32,32]{0,1:T(8,128)S(1)} %fusion.85), channel_id=1, replica_groups=mesh['row'=16,'col'=8] {'row','col'}, use_global_device_ids=true, to_apply=%region_11.14 | all-reduce | flops 1024 | bytes 8192 | tf_op jit(solution)/shard_map/psum | solution.py:78
  510.3 2.9 cholesky.55
  513.3 0.6 compare_reduce_fusion
  513.9 0.7 fusion.80
  514.6 2.4 custom-call.7
  517.2 0.9 fusion.66
  (44 shorter events, 2.7 us)
Async XLA Ops:
  7.2 76.5 %all-gather.3.cloned.1.call-start = ((), (), s32[]{:S(2)}) async-start(), calls=%async_computation.4 | async-start | bytes 8454144 | tf_op jit(solution)/shard_map/all_gather | solution.py:32
  7.9 142.6 %reduce-scatter.9.cloned.1.call-start = ((), (), s32[]{:S(2)}) async-start(), calls=%async_computation.5 | async-start | bytes 1179648 | tf_op jit(solution)/shard_map/reduce_scatter | solution.py:66
  87.9 0.7 copy-start.7
  119.9 1.0 copy-start.3
  119.9 1.6 copy-start.1
  120.9 106.2 %reduce-scatter.13.cloned.1.call-start = ((), (), s32[]{:S(2)}) async-start(), calls=%async_computation.8 | async-start | bytes 2228224
  121.7 178.7 %all-gather.5.cloned.1.call-start = ((), (), s32[]{:S(2)}) async-start(), calls=%async_computation.6 | async-start | bytes 8454144 | tf_op jit(solution)/shard_map/all_gather | solution.py:32
  228.8 180.5 %reduce-scatter.11.cloned.1.call-start = ((), (), s32[]{:S(2)}) async-start(), calls=%async_computation.7 | async-start | bytes 1179648 | tf_op jit(solution)/shard_map/reduce_scatter | solution.py:66
  336.3 1.0 copy-start.2
  336.3 1.6 copy-start
  336.4 1.7 copy-start.4
  336.4 72.0 %copy-start.5 = (f32[1,32,1024]{2,1,0:T(8,128)S(1)}, f32[1,32,1024]{2,1,0:T(8,128)}, u32[]{:S(2)}) copy-start(f32[1,32,1024]{2,1,0:T(8,128)} %reduce-scatter.9.cloned.1.call-done) | copy-start | bytes 393220
  336.4 72.0 %copy-start.6 = (f32[1,32,1024]{2,1,0:T(8,128)S(1)}, f32[1,32,1024]{2,1,0:T(8,128)}, u32[]{:S(2)}) copy-start(f32[1,32,1024]{2,1,0:T(8,128)} %reduce-scatter.13.cloned.1.call-done) | copy-start | bytes 393220
  337.4 106.7 %reduce-scatter.15.cloned.1.call-start = ((), (), s32[]{:S(2)}) async-start(), calls=%async_computation.9 | async-start | bytes 2228224
Sparse Core Ops, SparseCore 0:
  11.0 72.5 all-gather.2
  121.1 29.3 reduce-scatter.8
  153.8 73.3 reduce-scatter.12
  231.0 69.2 all-gather.4
  337.5 29.5 reduce-scatter.10
  370.5 73.5 reduce-scatter.14
where the time goes:
time: 527 us; the launch traced here: 525 us
  waiting for transfers between devices  288 us (55%)
  blocking collectives  128 us (24%)
  loops' own time  31.9 us (6%)
  matrix products  30.7 us (6%)
  local copies, waits for them, and re-layouts  16.8 us (3%)
  other arithmetic  15 us (3%)
  between operations  14.3 us (3%)
    all_gather x2, waiting for transfers between devices, product(): every = lax.all_gather(panel, ('row', 'col'), axis=0, tiled=True)  147 us
    unnamed x8, waiting for transfers between devices  112 us
    psum x1, blocking collectives, on_device(): gram_two = lax.psum(local_gram_exact(scaled), ('row', 'col'))  64.6 us
    psum x1, blocking collectives, on_device(): gram_one = lax.psum(local_gram(panels), ('row', 'col'))  63.2 us
    another operation x2, loops' own time, product(): band_total, class_total = lax.fori_loop(0, live_counts[0], advance, start)  31.9 us
    reduce_scatter x2, waiting for transfers between devices, product(): owned = lax.psum_scatter(band_total, 'col', scatter_dimension=0, tiled=True)  28.8 us
    dot_general x6, matrix products, advance(): lax.dot_general(left, matrix, (((1,), (1,)), ((), ())), preferred_element...  14.2 us
    dot_general x6, matrix products, advance(): lax.dot_general(right, matrix, (((1,), (0,)), ((), ())), preferred_elemen...  12.6 us
  transfers between devices with their start and end apart: 6, of which 5 were waited for; matrix products, arithmetic and copies ran while one was open for 2% of the time, Pallas kernels for 0%

commit v1 on v0

v1 whole, which is shorter than its diff:
```python
import functools

import jax
import jax.numpy as jnp
from jax import lax
from jax.experimental import pallas as pl
from jax.experimental.pallas import tpu as pltpu
from jax.sharding import PartitionSpec as P

BOTH = ("row", "col")
HIGHEST = lax.Precision.HIGHEST
VMEM = pl.BlockSpec(memory_space=pltpu.VMEM)
SMEM = pl.BlockSpec(memory_space=pltpu.SMEM)
ANY = pl.BlockSpec(memory_space=pl.ANY)
PARAMS = pltpu.CompilerParams(vmem_limit_bytes=48 * 1024 * 1024)


def permute(value, target):
    pairs = []
    for device in range(128):
        z, x, y, c = device // 32, device // 8 % 4, device // 2 % 4, device % 2
        tz, tx, ty, tc = target(z, x, y, c)
        pairs.append((device, ((tz % 4) * 4 + tx % 4) * 8 + (ty % 4) * 2 + tc % 2))
    return lax.ppermute(value, BOTH, pairs)


def send_inner(value, s):
    return permute(value, lambda z, x, y, c: (z + s, x, y, c) if c == 0 else (z, x + s, y, c))


def send_outer(value, s):
    return permute(value, lambda z, x, y, c: (z, x + s, y, c) if c == 0 else (z + s, x, y, c))


def send_y(value, s):
    return permute(value, lambda z, x, y, c: (z, x, y + s, c))


def send_z(value, s):
    return permute(value, lambda z, x, y, c: (z + s, x, y, c))


def send_x(value, s):
    return permute(value, lambda z, x, y, c: (z, x + s, y, c))


def send_core(value):
    return permute(value, lambda z, x, y, c: (z, x, y, c + 1))


def struct(shape, dtype):
    return jax.ShapeDtypeStruct(shape, dtype)


def product_kernel(pairs, live, blocks, g0, g1, g2, g3, h0, h1, *rest):
    gathered, pair_gathered = (g0, g1, g2, g3), (h0, h1)
    outs = rest[:6]
    matrices, lefts, rights, result, total, sems = rest[6:]
    count = live[0]
    row = pairs[0, 0, 0] // 8
    col = pairs[0, 0, 1] % 8
    z, x, y, c = row // 4, row % 4, col // 2, col % 2

    def shift(target):
        tz, tx = target // 4, target % 4
        dz, dx = (tz - z) & 3, (tx - x) & 3
        return jnp.where(c == 0, dx, dz), jnp.where(c == 0, dz, dx)

    def matrix_copy(slot):
        return pltpu.make_async_copy(blocks.at[slot], matrices.at[slot], sems.at[0, slot])

    def left_copy(slot, outer, inner):
        source = gathered[outer].at[inner, :, pl.ds(0, 1024)]
        return pltpu.make_async_copy(source, lefts.at[slot], sems.at[1, slot])

    def right_copy(slot, core, dy):
        source = pair_gathered[core].at[dy, :, pl.ds(0, 1024)]
        return pltpu.make_async_copy(source, rights.at[slot], sems.at[2, slot])

    for slot in range(3):
        @pl.when(slot < count)
        def _():
            matrix_copy(slot).start()

    for slot in range(3):
        @pl.when(slot < count)
        def _():
            first, second = pairs[0, slot, 0], pairs[0, slot, 1]
            outer, inner = shift(second // 8)
            outer, inner = (4 - outer) & 3, (4 - inner) & 3
            for t in range(4):
                @pl.when(outer == t)
                def _():
                    left_copy(slot, t, inner).start()
            dy = (y - first % 8 // 2) & 3
            dc = (first % 8 % 2) ^ c
            for t in range(2):
                @pl.when(dc == t)
                def _():
                    right_copy(slot, t, dy).start()

    total[...] = jnp.zeros_like(total)

    def advance(slot, carry):
        first, second = pairs[0, slot, 0], pairs[0, slot, 1]
        left_copy(slot, 0, 0).wait()
        right_copy(slot, 0, 0).wait()
        matrix_copy(slot).wait()
        outer, inner = shift(second // 8)
        dy = (first % 8 // 2 - y) & 3
        dc = (first % 8 % 2) ^ c
        band = 16 + dc * 4 + dy
        total[band] += lax.dot_general(
            lefts[slot], matrices[slot], (((1,), (1,)), ((), ())), preferred_element_type=jnp.float32
        )

        @pl.when(first != second)
        def _():
            part = outer * 4 + inner
            total[part] += lax.dot_general(
                rights[slot], matrices[slot], (((1,), (0,)), ((), ())), preferred_element_type=jnp.float32
            )

        return carry

    lax.fori_loop(0, count, advance, 0)
    for k, out in enumerate(outs):
        out[...] = total[4 * k : 4 * k + 4].astype(out.dtype)


def product(pairs, live, blocks, gathered, pair_gathered, sent):
    shape = (4, 32, 1024)
    f32 = jnp.float32
    return pl.pallas_call(
        product_kernel,
        out_shape=[struct(shape, f32)] + [struct(shape, sent)] * 3 + [struct(shape, f32), struct(shape, sent)],
        in_specs=[SMEM, SMEM] + [ANY] * 7,
        out_specs=[VMEM] * 6,
        scratch_shapes=[
            pltpu.VMEM((3, 1024, 1024), jnp.bfloat16),
            pltpu.VMEM((3, 32, 1024), jnp.bfloat16),
            pltpu.VMEM((3, 32, 1024), jnp.bfloat16),
            pltpu.VMEM((8, 128), f32),
            pltpu.VMEM((24, 32, 1024), f32),
            pltpu.SemaphoreType.DMA((3, 3)),
        ],
        compiler_params=PARAMS,
        cost_estimate=pl.CostEstimate(flops=800_000_000, bytes_accessed=10_000_000, transcendentals=0),
        name="product",
    )(pairs, live, blocks, *gathered, *pair_gathered)


def sum_kernel(own, *rest):
    received, outs = rest[: len(rest) - 4], rest[len(rest) - 4 :]
    for k, out in enumerate(outs):
        value = own[k]
        for array in received:
            value = value + array[k].astype(jnp.float32)
        out[...] = value.astype(out.dtype)


def add_received(own, received, sent):
    shape = (32, 1024)
    return pl.pallas_call(
        sum_kernel,
        out_shape=[struct(shape, jnp.float32)] + [struct(shape, sent)] * 3,
        in_specs=[VMEM] * (1 + len(received)),
        out_specs=[VMEM] * 4,
        compiler_params=PARAMS,
        name="add_received",
    )(own, *received)


def first_kernel(*refs):
    parts, (first, panel, gram) = refs[:8], refs[8:]
    value = parts[0][...] + parts[1][...]
    for part in parts[2:]:
        value = value + part[...].astype(jnp.float32)
    first[...] = value
    rounded = value.astype(jnp.bfloat16)
    panel[...] = rounded
    gram[...] = lax.dot_general(
        rounded, rounded, (((1,), (1,)), ((), ())), preferred_element_type=jnp.float32
    )


def finish_first(parts):
    return pl.pallas_call(
        first_kernel,
        out_shape=[
            struct((32, 1024), jnp.float32),
            struct((32, 1024), jnp.bfloat16),
            struct((32, 32), jnp.float32),
        ],
        in_specs=[VMEM] * 8,
        out_specs=[VMEM] * 3,
        compiler_params=PARAMS,
        name="finish_first",
    )(*parts)


def second_kernel(*refs):
    parts, inverse, (scaled, gram) = refs[:8], refs[8], refs[9:]
    value = parts[0][...] + parts[1][...]
    for part in parts[2:]:
        value = value + part[...].astype(jnp.float32)
    value = jnp.dot(inverse[...], value, precision=HIGHEST, preferred_element_type=jnp.float32)
    scaled[...] = value
    gram[...] = lax.dot_general(
        value, value, (((1,), (1,)), ((), ())), precision=HIGHEST, preferred_element_type=jnp.float32
    )


def finish_second(parts, inverse):
    return pl.pallas_call(
        second_kernel,
        out_shape=[struct((32, 1024), jnp.float32), struct((32, 32), jnp.float32)],
        in_specs=[VMEM] * 9,
        out_specs=[VMEM] * 2,
        compiler_params=PARAMS,
        name="finish_second",
    )(*parts, inverse)


def lower_inverse(gram):
    rows = lax.broadcasted_iota(jnp.int32, (32, 128), 0)
    lanes = lax.broadcasted_iota(jnp.int32, (32, 128), 1)
    wide = jnp.concatenate([gram, jnp.zeros((32, 96), jnp.float32)], axis=1)
    wide = jnp.where(lanes == rows + 32, 1.0, wide)
    for k in range(31):
        pivot = wide[k : k + 1, k : k + 1]
        factor = jnp.where(rows > k, wide[:, k : k + 1], 0.0)
        wide = wide - factor * (wide[k : k + 1, :] / pivot)
    diagonal = jnp.sum(jnp.where(lanes == rows, wide, 0.0), axis=1, keepdims=True)
    wide = wide / jnp.sqrt(diagonal)
    return wide[:, 32:64]


def factor_kernel(gram, panel, root, *outs):
    inverse = lower_inverse(gram[...])
    outs[0][...] = (
        jnp.dot(inverse, panel[...], precision=HIGHEST, preferred_element_type=jnp.float32) * root
    )
    if len(outs) > 1:
        outs[1][...] = inverse


def apply_factor(gram, panel, root, keep):
    return pl.pallas_call(
        lambda a, b, *outs: factor_kernel(a, b, root, *outs),
        out_shape=[struct((32, 1024), jnp.float32)] + [struct((32, 32), jnp.float32)] * keep,
        in_specs=[VMEM] * 2,
        out_specs=[VMEM] * (1 + keep),
        compiler_params=PARAMS,
        name="apply_factor",
    )(gram, panel)


SHIFTS = (1, 3, 2)


def spread(send, value):
    got = {s: send(value, s) for s in SHIFTS}
    return [value] + [got[s] for s in (1, 2, 3)]


def gather(panel):
    inner = jnp.stack(spread(send_inner, panel))
    along_y = jnp.stack(spread(send_y, panel))
    return spread(send_outer, inner), [along_y, send_core(along_y)]


def scatter(parts, sent):
    row_parts, pair_parts = parts[:4], parts[4:]
    got = {s: send_outer(row_parts[s], s) for s in SHIFTS}
    other = send_core(pair_parts[1])
    column = add_received(pair_parts[0], [other], sent)
    got_y = [send_y(column[s], s) for s in SHIFTS]
    row = add_received(row_parts[0], [got[s] for s in SHIFTS], sent)
    got_row = [send_inner(row[s], s) for s in SHIFTS]
    return [row[0], column[0]] + got_y + got_row


def total_gram(gram):
    gram = gram + send_core(gram)
    for send in (send_y, send_z, send_x):
        got = [send(gram, s) for s in SHIFTS]
        gram = gram + got[0] + got[1] + got[2]
    return gram


def on_device(block_pairs, live_counts, pair_blocks, start_basis):
    users = 128 * start_basis.shape[2]
    root = float(users) ** 0.5
    gathered, pair_gathered = gather(start_basis[0])
    parts = product(block_pairs, live_counts, pair_blocks, gathered, pair_gathered, jnp.float32)
    first, panel, gram = finish_first(scatter(parts, jnp.float32))
    gathered, pair_gathered = gather(panel)
    parts = product(block_pairs, live_counts, pair_blocks, gathered, pair_gathered, jnp.bfloat16)
    first_basis, inverse = apply_factor(total_gram(gram), first, root, 1)
    scaled, gram = finish_second(scatter(parts, jnp.bfloat16), inverse)
    (embedding,) = apply_factor(total_gram(gram), scaled, root, 0)
    return (first_basis[None], embedding[None])


def solution(mesh):
    spec = P(BOTH, None, None)
    return jax.shard_map(
        on_device, mesh=mesh, in_specs=(spec, P(BOTH), spec, spec), out_specs=(spec, spec), check_vma=False
    )
```

time: 527 us -> 167 us (0.32)
  waiting for transfers between devices: 288 us -> 69.6 us
  blocking collectives: 128 us -> 0 us
  starting transfers between devices: 0.24 us -> 73.2 us
  loops' own time: 31.9 us -> 0 us
  matrix products: 30.7 us -> 0 us
  Pallas kernels: 0 us -> 20.2 us
  local copies, waits for them, and re-layouts: 16.8 us -> 0.77 us
  other arithmetic: 15 us -> 1 us
  between operations: 14.3 us -> 1.45 us
    all_gather x2 -> x0, waiting for transfers between devices: 147 us -> none  [product(): every = lax.all_gather(panel, ('row', 'col'), axis=0, tiled=True)]
    psum x2 -> x0, blocking collectives: 128 us -> none  [the longest x1 64.6 us: on_device(): gram_two = lax.psum(local_gram_exact(scaled), ('row', 'col'))]
    unnamed x8 -> x0, waiting for transfers between devices: 112 us -> none
    ppermute x0 -> x60, starting transfers between devices: none -> 73.2 us  [permute(): return lax.ppermute(value, BOTH, pairs)]
    ppermute x0 -> x60, waiting for transfers between devices: none -> 69.6 us  [permute(): return lax.ppermute(value, BOTH, pairs)]
    another operation x2 -> x0, loops' own time: 31.9 us -> none  [product(): band_total, class_total = lax.fori_loop(0, live_counts[0], advance, start)]
    dot_general x17 -> x0, matrix products: 30.3 us -> none  [the longest x6 14.2 us: advance(): lax.dot_general(left, matrix, (((1,), (1,)), ((), ())), preferred_element...]
    reduce_scatter x2 -> x0, waiting for transfers between devices: 28.8 us -> none  [product(): owned = lax.psum_scatter(band_total, 'col', scatter_dimension=0, tiled=True)]
  transfers between devices with their start and end apart: 6 -> 60, of which waited for: 5 -> 32; matrix products, arithmetic and copies ran while one was open for 2% -> 0% of each run, Pallas kernels for 0% -> 2%
where the time goes in v1:
time: 167 us; the launch traced here: 166 us
  starting transfers between devices  73.2 us (44%)
  waiting for transfers between devices  69.6 us (42%)
  Pallas kernels  20.2 us (12%)
    ppermute x60, starting transfers between devices, permute(): return lax.ppermute(value, BOTH, pairs)  73.2 us
    ppermute x60, waiting for transfers between devices, permute(): return lax.ppermute(value, BOTH, pairs)  69.6 us
    pallas_call x2, Pallas kernels, product(): pl.pallas_call(product_kernel, out_shape=[struct(shape, f32)] + [struct(s...  12 us
    pallas_call x2, Pallas kernels, apply_factor(): pl.pallas_call(lambda a, b, *outs: factor_kernel(a, b, root, *outs), out_...  7.15 us
  transfers between devices with their start and end apart: 60, of which 32 were waited for; matrix products, arithmetic and copies ran while one was open for 0% of the time, Pallas kernels for 2%

profile of v1, /device:TPU:0, one launch (start us, length us, event | category | flops | bytes accessed | tf_op | source)
XLA Modules:
  0.0 166.2 jit_solution(12621058603233817136)
XLA Ops:
  0.6 3.2 %collective-permute-start.8 = (bf16[32,1024]{1,0:T(8,128)(2,1)}, bf16[32,1024]{1,0:T(8,128)(2,1)S(1)}, u32[]{:S(2)}, u32[]{:S(2)}) collective-permute-start(bf16[32,1024]{1,0:T(8,128)(2,1)} %bitcast.18), channel_id=1, source_target_pairs={{0,6},{1,7},{2,0},{3,1},{4,2},{5,3},{6,4},{7,5},{8,14},{9,15},{10,... | collective-permute-start | bytes 196616 | tf_op jit(solution)/shard_map/ppermute | solution.py:24
  5.4 4.0 %collective-permute-start.2 = (bf16[32,1024]{1,0:T(8,128)(2,1)}, bf16[32,1024]{1,0:T(8,128)(2,1)S(1)}, u32[]{:S(2)}, u32[]{:S(2)}) collective-permute-start(bf16[32,1024]{1,0:T(8,128)(2,1)} %bitcast.21), channel_id=1, source_target_pairs={{0,96},{1,25},{2,98},{3,27},{4,100},{5,29},{6,102},{7,31},{8,104},... | collective-permute-start | bytes 196616 | tf_op jit(solution)/shard_map/ppermute | solution.py:24
  11.7 3.9 %collective-permute-done.1 = bf16[32,1024]{1,0:T(8,128)(2,1)S(1)} collective-permute-done((bf16[32,1024]{1,0:T(8,128)(2,1)}, bf16[32,1024]{1,0:T(8,128)(2,1)S(1)}, u32[]{:S(2)}, u32[]{:S(2)}) %collective-permute-start.1) | collective-permute-done | bytes 65568 | tf_op jit(solution)/shard_map/ppermute | solution.py:24
  16.8 2.8 %collective-permute-start.5 = (bf16[4,32,1024]{2,1,0:T(8,128)(2,1)S(1)}, bf16[4,32,1024]{2,1,0:T(8,128)(2,1)S(1)}, u32[]{:S(2)}, u32[]{:S(2)}) collective-permute-start(bf16[4,32,1024]{2,1,0:T(8,128)(2,1)S(1)} %get-tuple-element.75.g0), channel_id=1, source_target_pairs={{0,24},{1,97},{2,26},{3,99},{4,28},{5,101},{6,30},{7,103},{8,0},{9... | collective-permute-start | bytes 786440 | tf_op jit(solution)/shard_map/ppermute | solution.py:24
  22.8 3.6 %collective-permute-done.5.g3 = bf16[4,32,1024]{2,1,0:T(8,128)(2,1)S(1)} collective-permute-done((bf16[4,32,1024]{2,1,0:T(8,128)(2,1)S(1)}, bf16[4,32,1024]{2,1,0:T(8,128)(2,1)S(1)}, u32[]{:S(2)}, u32[]{:S(2)}) %collective-permute-start.5) | collective-permute-done | bytes 262176 | tf_op jit(solution)/shard_map/ppermute | solution.py:24
  27.6 2.7 %collective-permute-done.3.g1 = bf16[4,32,1024]{2,1,0:T(8,128)(2,1)S(1)} collective-permute-done((bf16[4,32,1024]{2,1,0:T(8,128)(2,1)S(1)}, bf16[4,32,1024]{2,1,0:T(8,128)(2,1)S(1)}, u32[]{:S(2)}, u32[]{:S(2)}) %collective-permute-start.3) | collective-permute-done | bytes 262176 | tf_op jit(solution)/shard_map/ppermute | solution.py:24
  30.3 6.0 %product.2 = (f32[4,32,1024]{2,1,0:T(8,128)S(1)}, f32[4,32,1024]{2,1,0:T(8,128)S(1)}, f32[4,32,1024]{2,1,0:T(8,128)S(1)}, f32[4,32,1024]{2,1,0:T(8,128)S(1)}, f3...) custom-call(s32[1,3,2]{2,1,0:T(4,128)S(1)} %copy.6.pairs, s32[1]{0:T(128)S(6)} %copy.8.live, ...), custom_call_target="tpu_custom_call" | custom-call | flops 800000000 | bytes 10000000 | tf_op jit(solution)/shard_map/product/pallas_call | solution.py:134
  36.4 3.2 %collective-permute-start.11 = (f32[4,32,1024]{2,1,0:T(8,128)S(1)}, f32[4,32,1024]{2,1,0:T(8,128)S(1)}, u32[]{:S(2)}, u32[]{:S(2)}) collective-permute-start(f32[4,32,1024]{2,1,0:T(8,128)S(1)} %get-tuple-element.39), channel_id=1, source_target_pairs={{0,24},{1,97},{2,26},{3,99},{4,28},{5,101},{6,30},{7,103},{8,0},{9... | collective-permute-start | bytes 1572872 | tf_op jit(solution)/shard_map/ppermute | solution.py:24
  39.7 12.8 %collective-permute-done.10.rest_0_ = f32[4,32,1024]{2,1,0:T(8,128)S(1)} collective-permute-done((f32[4,32,1024]{2,1,0:T(8,128)S(1)}, f32[4,32,1024]{2,1,0:T(8,128)S(1)}, u32[]{:S(2)}, u32[]{:S(2)}) %collective-permute-start.10) | collective-permute-done | bytes 524320 | tf_op jit(solution)/shard_map/ppermute | solution.py:24
  52.6 3.2 %collective-permute-start.18 = (f32[32,1024]{1,0:T(8,128)S(1)}, f32[32,1024]{1,0:T(8,128)S(1)}, u32[]{:S(2)}, u32[]{:S(2)}) collective-permute-start(f32[32,1024]{1,0:T(8,128)S(1)} %get-tuple-element.49), channel_id=1, source_target_pairs={{0,96},{1,25},{2,98},{3,27},{4,100},{5,29},{6,102},{7,31},{8,104},... | collective-permute-start | bytes 393224 | tf_op jit(solution)/shard_map/ppermute | solution.py:24
  55.8 2.0 %collective-permute-start.19 = (f32[32,1024]{1,0:T(8,128)S(1)}, f32[32,1024]{1,0:T(8,128)S(1)}, u32[]{:S(2)}, u32[]{:S(2)}) collective-permute-start(f32[32,1024]{1,0:T(8,128)S(1)} %get-tuple-element.50), channel_id=1, source_target_pairs={{0,64},{1,17},{2,66},{3,19},{4,68},{5,21},{6,70},{7,23},{8,72},{9,... | collective-permute-start | bytes 393224 | tf_op jit(solution)/shard_map/ppermute | solution.py:24
  57.9 2.7 %collective-permute-start.14 = (f32[32,1024]{1,0:T(8,128)S(1)}, f32[32,1024]{1,0:T(8,128)S(1)}, u32[]{:S(2)}, u32[]{:S(2)}) collective-permute-start(f32[32,1024]{1,0:T(8,128)S(1)} %get-tuple-element.45), channel_id=1, source_target_pairs={{0,2},{1,3},{2,4},{3,5},{4,6},{5,7},{6,0},{7,1},{8,10},{9,11},{10,... | collective-permute-start | bytes 393224 | tf_op jit(solution)/shard_map/ppermute | solution.py:24
  61.2 1.6 collective-permute-start.16
  62.7 1.4 collective-permute-done.14.refs_2_
  64.1 2.8 %collective-permute-done.15.refs_3_ = f32[32,1024]{1,0:T(8,128)S(1)} collective-permute-done((f32[32,1024]{1,0:T(8,128)S(1)}, f32[32,1024]{1,0:T(8,128)S(1)}, u32[]{:S(2)}, u32[]{:S(2)}) %collective-permute-start.15) | collective-permute-done | bytes 131104 | tf_op jit(solution)/shard_map/ppermute | solution.py:24
  66.9 1.9 %collective-permute-done.16.refs_4_ = f32[32,1024]{1,0:T(8,128)S(1)} collective-permute-done((f32[32,1024]{1,0:T(8,128)S(1)}, f32[32,1024]{1,0:T(8,128)S(1)}, u32[]{:S(2)}, u32[]{:S(2)}) %collective-permute-start.16) | collective-permute-done | bytes 131104 | tf_op jit(solution)/shard_map/ppermute | solution.py:24
  69.0 2.2 %collective-permute-start.38 = (bf16[32,1024]{1,0:T(8,128)(2,1)S(1)}, bf16[32,1024]{1,0:T(8,128)(2,1)S(1)}, u32[]{:S(2)}, u32[]{:S(2)}) collective-permute-start(bf16[32,1024]{1,0:T(8,128)(2,1)S(1)} %get-tuple-element.54), channel_id=1, source_target_pairs={{0,6},{1,7},{2,0},{3,1},{4,2},{5,3},{6,4},{7,5},{8,14},{9,15},{10,... | collective-permute-start | bytes 196616 | tf_op jit(solution)/shard_map/ppermute | solution.py:24
  72.2 1.6 collective-permute-start.31
  74.7 2.3 %collective-permute-done.37 = bf16[32,1024]{1,0:T(8,128)(2,1)S(1)} collective-permute-done((bf16[32,1024]{1,0:T(8,128)(2,1)S(1)}, bf16[32,1024]{1,0:T(8,128)(2,1)S(1)}, u32[]{:S(2)}, u32[]{:S(2)}) %collective-permute-start.37) | collective-permute-done | bytes 65568 | tf_op jit(solution)/shard_map/ppermute | solution.py:24
  77.9 1.3 collective-permute-done.30
  79.4 3.4 %collective-permute-start.35 = (bf16[4,32,1024]{2,1,0:T(8,128)(2,1)S(1)}, bf16[4,32,1024]{2,1,0:T(8,128)(2,1)S(1)}, u32[]{:S(2)}, u32[]{:S(2)}) collective-permute-start(bf16[4,32,1024]{2,1,0:T(8,128)(2,1)S(1)} %get-tuple-element.73.g0), channel_id=1, source_target_pairs={{0,24},{1,97},{2,26},{3,99},{4,28},{5,101},{6,30},{7,103},{8,0},{9... | collective-permute-start | bytes 786440 | tf_op jit(solution)/shard_map/ppermute | solution.py:24
  83.7 5.7 %collective-permute-done.35.g3 = bf16[4,32,1024]{2,1,0:T(8,128)(2,1)S(1)} collective-permute-done((bf16[4,32,1024]{2,1,0:T(8,128)(2,1)S(1)}, bf16[4,32,1024]{2,1,0:T(8,128)(2,1)S(1)}, u32[]{:S(2)}, u32[]{:S(2)}) %collective-permute-start.35) | collective-permute-done | bytes 262176 | tf_op jit(solution)/shard_map/ppermute | solution.py:24
  90.7 2.4 %collective-permute-done.33.g1 = bf16[4,32,1024]{2,1,0:T(8,128)(2,1)S(1)} collective-permute-done((bf16[4,32,1024]{2,1,0:T(8,128)(2,1)S(1)}, bf16[4,32,1024]{2,1,0:T(8,128)(2,1)S(1)}, u32[]{:S(2)}, u32[]{:S(2)}) %collective-permute-start.33) | collective-permute-done | bytes 262176 | tf_op jit(solution)/shard_map/ppermute | solution.py:24
  93.1 6.0 %product.3 = (f32[4,32,1024]{2,1,0:T(8,128)S(1)}, bf16[4,32,1024]{2,1,0:T(8,128)(2,1)S(1)}, bf16[4,32,1024]{2,1,0:T(8,128)(2,1)S(1)}, bf16[4,32,1024]{2,1,0:T(8,...) custom-call(s32[1,3,2]{2,1,0:T(4,128)S(1)} %copy.6.pairs, s32[1]{0:T(128)S(6)} %copy.8.live, ...), custom_call_target="tpu_custom_call" | custom-call | flops 800000000 | bytes 10000000 | tf_op jit(solution)/shard_map/product/pallas_call | solution.py:134
  99.2 3.2 %collective-permute-start.41 = (bf16[4,32,1024]{2,1,0:T(8,128)(2,1)S(1)}, bf16[4,32,1024]{2,1,0:T(8,128)(2,1)S(1)}, u32[]{:S(2)}, u32[]{:S(2)}) collective-permute-start(bf16[4,32,1024]{2,1,0:T(8,128)(2,1)S(1)} %get-tuple-element.57), channel_id=1, source_target_pairs={{0,24},{1,97},{2,26},{3,99},{4,28},{5,101},{6,30},{7,103},{8,0},{9... | collective-permute-start | bytes 786440 | tf_op jit(solution)/shard_map/ppermute | solution.py:24
  103.6 2.0 %collective-permute-start.23 = (f32[32,32]{1,0:T(8,128)S(1)}, f32[32,32]{1,0:T(8,128)S(1)}, u32[]{:S(2)}, u32[]{:S(2)}) collective-permute-start(f32[32,32]{1,0:T(8,128)S(1)} %add.60), channel_id=1, source_target_pairs={{0,4},{1,5},{2,6},{3,7},{4,0},{5,1},{6,2},{7,3},{8,12},{9,13},{10,... | collective-permute-start | bytes 12296 | tf_op jit(solution)/shard_map/ppermute | solution.py:24
  105.6 1.8 %collective-permute-start.22 = (f32[32,32]{1,0:T(8,128)S(1)}, f32[32,32]{1,0:T(8,128)S(1)}, u32[]{:S(2)}, u32[]{:S(2)}) collective-permute-start(f32[32,32]{1,0:T(8,128)S(1)} %add.60), channel_id=1, source_target_pairs={{0,6},{1,7},{2,0},{3,1},{4,2},{5,3},{6,4},{7,5},{8,14},{9,15},{10,... | collective-permute-start | bytes 12296 | tf_op jit(solution)/shard_map/ppermute | solution.py:24
  107.5 1.4 collective-permute-done.23
  108.8 1.3 collective-permute-start.21
  110.2 3.6 %collective-permute-done.21 = f32[32,32]{1,0:T(8,128)S(1)} collective-permute-done((f32[32,32]{1,0:T(8,128)S(1)}, f32[32,32]{1,0:T(8,128)S(1)}, u32[]{:S(2)}, u32[]{:S(2)}) %collective-permute-start.21) | collective-permute-done | bytes 4128 | tf_op jit(solution)/shard_map/ppermute | solution.py:24
  113.8 1.3 collective-permute-start.26
  119.0 1.9 %collective-permute-done.24 = f32[32,32]{1,0:T(8,128)S(1)} collective-permute-done((f32[32,32]{1,0:T(8,128)S(1)}, f32[32,32]{1,0:T(8,128)S(1)}, u32[]{:S(2)}, u32[]{:S(2)}) %collective-permute-start.24) | collective-permute-done | bytes 4128 | tf_op jit(solution)/shard_map/ppermute | solution.py:24
  120.9 3.3 %collective-permute-start.29 = (f32[32,32]{1,0:T(8,128)S(1)}, f32[32,32]{1,0:T(8,128)S(1)}, u32[]{:S(2)}, u32[]{:S(2)}) collective-permute-start(f32[32,32]{1,0:T(8,128)S(1)} %add_add_fusion.4), channel_id=1, source_target_pairs={{0,16},{1,17},{2,18},{3,19},{4,20},{5,21},{6,22},{7,23},{8,24},{9,... | collective-permute-start | bytes 12296 | tf_op jit(solution)/shard_map/ppermute | solution.py:24
  127.3 1.4 collective-permute-start.49
  130.0 1.9 %collective-permute-start.45 = (bf16[32,1024]{1,0:T(8,128)(2,1)S(1)}, bf16[32,1024]{1,0:T(8,128)(2,1)S(1)}, u32[]{:S(2)}, u32[]{:S(2)}) collective-permute-start(bf16[32,1024]{1,0:T(8,128)(2,1)S(1)} %get-tuple-element.64), channel_id=1, source_target_pairs={{0,6},{1,7},{2,0},{3,1},{4,2},{5,3},{6,4},{7,5},{8,14},{9,15},{10,... | collective-permute-start | bytes 196616 | tf_op jit(solution)/shard_map/ppermute | solution.py:24
  132.9 3.6 %apply_factor.2 = (f32[32,1024]{1,0:T(8,128)}, f32[32,32]{1,0:T(8,128)S(1)}) custom-call(f32[32,32]{1,0:T(8,128)S(1)} %add_add_fusion.3.a, f32[32,1024]{1,0:T(8,128)S(1)} %get-tuple-element.52.b), custom_call_target="tpu_custom_call" | custom-call | tf_op jit(solution)/shard_map/apply_factor/pallas_call | solution.py:249
  139.4 1.4 collective-permute-start.53
  140.8 1.4 collective-permute-start.52
  142.8 1.8 %collective-permute-done.53 = f32[32,32]{1,0:T(8,128)S(1)} collective-permute-done((f32[32,32]{1,0:T(8,128)S(1)}, f32[32,32]{1,0:T(8,128)S(1)}, u32[]{:S(2)}, u32[]{:S(2)}) %collective-permute-start.53) | collective-permute-done | bytes 4128 | tf_op jit(solution)/shard_map/ppermute | solution.py:24
  144.7 2.5 %collective-permute-done.51 = f32[32,32]{1,0:T(8,128)S(1)} collective-permute-done((f32[32,32]{1,0:T(8,128)S(1)}, f32[32,32]{1,0:T(8,128)S(1)}, u32[]{:S(2)}, u32[]{:S(2)}) %collective-permute-start.51) | collective-permute-done | bytes 4128 | tf_op jit(solution)/shard_map/ppermute | solution.py:24
  147.1 1.3 collective-permute-start.56
  148.4 1.3 collective-permute-start.55
  150.5 1.9 %collective-permute-done.56 = f32[32,32]{1,0:T(8,128)S(1)} collective-permute-done((f32[32,32]{1,0:T(8,128)S(1)}, f32[32,32]{1,0:T(8,128)S(1)}, u32[]{:S(2)}, u32[]{:S(2)}) %collective-permute-start.56) | collective-permute-done | bytes 4128 | tf_op jit(solution)/shard_map/ppermute | solution.py:24
  152.4 2.3 %collective-permute-done.54 = f32[32,32]{1,0:T(8,128)S(1)} collective-permute-done((f32[32,32]{1,0:T(8,128)S(1)}, f32[32,32]{1,0:T(8,128)S(1)}, u32[]{:S(2)}, u32[]{:S(2)}) %collective-permute-start.54) | collective-permute-done | bytes 4128 | tf_op jit(solution)/shard_map/ppermute | solution.py:24
  154.7 1.8 %collective-permute-start.59 = (f32[32,32]{1,0:T(8,128)S(1)}, f32[32,32]{1,0:T(8,128)S(1)}, u32[]{:S(2)}, u32[]{:S(2)}) collective-permute-start(f32[32,32]{1,0:T(8,128)S(1)} %add_add_fusion.1), channel_id=1, source_target_pairs={{0,16},{1,17},{2,18},{3,19},{4,20},{5,21},{6,22},{7,23},{8,24},{9,... | collective-permute-start | bytes 12296 | tf_op jit(solution)/shard_map/ppermute | solution.py:24
  158.5 1.4 collective-permute-done.59
  160.2 2.3 %collective-permute-done.57 = f32[32,32]{1,0:T(8,128)S(1)} collective-permute-done((f32[32,32]{1,0:T(8,128)S(1)}, f32[32,32]{1,0:T(8,128)S(1)}, u32[]{:S(2)}, u32[]{:S(2)}) %collective-permute-start.57) | collective-permute-done | bytes 4128 | tf_op jit(solution)/shard_map/ppermute | solution.py:24
  162.6 3.6 %apply_factor.3 = f32[32,1024]{1,0:T(8,128)} custom-call(f32[32,32]{1,0:T(8,128)S(1)} %add_add_fusion.a, f32[32,1024]{1,0:T(8,128)S(1)} %get-tuple-element.71.b), custom_call_target="tpu_custom_call" | custom-call | tf_op jit(solution)/shard_map/apply_factor/pallas_call | solution.py:249
  (93 shorter events, 32.2 us)
Async XLA Ops:
  0.6 8.8 %collective-permute-start.8 = (bf16[32,1024]{1,0:T(8,128)(2,1)}, bf16[32,1024]{1,0:T(8,128)(2,1)S(1)}, u32[]{:S(2)}, u32[]{:S(2)}) collective-permute-start(bf16[32,1024]{1,0:T(8,128)(2,1)} %bitcast.18), channel_id=1, source_target_pairs={{0,6},{1,7},{2,0},{3,1},{4,2},{5,3},{6,4},{7,5},{8,14},{9,15},{10,... | collective-permute-start | bytes 196616 | tf_op jit(solution)/shard_map/ppermute | solution.py:24
  3.8 6.9 %collective-permute-start.7 = (bf16[32,1024]{1,0:T(8,128)(2,1)}, bf16[32,1024]{1,0:T(8,128)(2,1)S(1)}, u32[]{:S(2)}, u32[]{:S(2)}) collective-permute-start(bf16[32,1024]{1,0:T(8,128)(2,1)} %bitcast.19), channel_id=1, source_target_pairs={{0,4},{1,5},{2,6},{3,7},{4,0},{5,1},{6,2},{7,3},{8,12},{9,13},{10,... | collective-permute-start | bytes 196616 | tf_op jit(solution)/shard_map/ppermute | solution.py:24
  4.4 6.3 %collective-permute-start.6 = (bf16[32,1024]{1,0:T(8,128)(2,1)}, bf16[32,1024]{1,0:T(8,128)(2,1)S(1)}, u32[]{:S(2)}, u32[]{:S(2)}) collective-permute-start(bf16[32,1024]{1,0:T(8,128)(2,1)} %bitcast.20), channel_id=1, source_target_pairs={{0,2},{1,3},{2,4},{3,5},{4,6},{5,7},{6,0},{7,1},{8,10},{9,11},{10,... | collective-permute-start | bytes 196616 | tf_op jit(solution)/shard_map/ppermute | solution.py:24
  5.4 6.3 %collective-permute-start.2 = (bf16[32,1024]{1,0:T(8,128)(2,1)}, bf16[32,1024]{1,0:T(8,128)(2,1)S(1)}, u32[]{:S(2)}, u32[]{:S(2)}) collective-permute-start(bf16[32,1024]{1,0:T(8,128)(2,1)} %bitcast.21), channel_id=1, source_target_pairs={{0,96},{1,25},{2,98},{3,27},{4,100},{5,29},{6,102},{7,31},{8,104},... | collective-permute-start | bytes 196616 | tf_op jit(solution)/shard_map/ppermute | solution.py:24
  9.4 6.1 %collective-permute-start.1 = (bf16[32,1024]{1,0:T(8,128)(2,1)}, bf16[32,1024]{1,0:T(8,128)(2,1)S(1)}, u32[]{:S(2)}, u32[]{:S(2)}) collective-permute-start(bf16[32,1024]{1,0:T(8,128)(2,1)} %bitcast.22), channel_id=1, source_target_pairs={{0,64},{1,17},{2,66},{3,19},{4,68},{5,21},{6,70},{7,23},{8,72},{9,... | collective-permute-start | bytes 196616 | tf_op jit(solution)/shard_map/ppermute | solution.py:24
  9.4 6.4 %collective-permute-start = (bf16[32,1024]{1,0:T(8,128)(2,1)}, bf16[32,1024]{1,0:T(8,128)(2,1)S(1)}, u32[]{:S(2)}, u32[]{:S(2)}) collective-permute-start(bf16[32,1024]{1,0:T(8,128)(2,1)} %bitcast.23), channel_id=1, source_target_pairs={{0,32},{1,9},{2,34},{3,11},{4,36},{5,13},{6,38},{7,15},{8,40},{9,1... | collective-permute-start | bytes 196616 | tf_op jit(solution)/shard_map/ppermute | solution.py:24
  16.7 6.0 %collective-permute-start.9 = (bf16[4,32,1024]{2,1,0:T(8,128)(2,1)S(1)}, bf16[4,32,1024]{2,1,0:T(8,128)(2,1)S(1)}, u32[]{:S(2)}, u32[]{:S(2)}) collective-permute-start(bf16[4,32,1024]{2,1,0:T(8,128)(2,1)S(1)} %get-tuple-element.74.h0), channel_id=1, source_target_pairs={{0,1},{1,0},{2,3},{3,2},{4,5},{5,4},{6,7},{7,6},{8,9},{9,8},{10,11... | collective-permute-start | bytes 786440 | tf_op jit(solution)/shard_map/ppermute | solution.py:24
  16.8 9.6 %collective-permute-start.5 = (bf16[4,32,1024]{2,1,0:T(8,128)(2,1)S(1)}, bf16[4,32,1024]{2,1,0:T(8,128)(2,1)S(1)}, u32[]{:S(2)}, u32[]{:S(2)}) collective-permute-start(bf16[4,32,1024]{2,1,0:T(8,128)(2,1)S(1)} %get-tuple-element.75.g0), channel_id=1, source_target_pairs={{0,24},{1,97},{2,26},{3,99},{4,28},{5,101},{6,30},{7,103},{8,0},{9... | collective-permute-start | bytes 786440 | tf_op jit(solution)/shard_map/ppermute | solution.py:24
  19.7 8.0 %collective-permute-start.4 = (bf16[4,32,1024]{2,1,0:T(8,128)(2,1)S(1)}, bf16[4,32,1024]{2,1,0:T(8,128)(2,1)S(1)}, u32[]{:S(2)}, u32[]{:S(2)}) collective-permute-start(bf16[4,32,1024]{2,1,0:T(8,128)(2,1)S(1)} %get-tuple-element.75.g0), channel_id=1, source_target_pairs={{0,16},{1,65},{2,18},{3,67},{4,20},{5,69},{6,22},{7,71},{8,24},{9,... | collective-permute-start | bytes 786440 | tf_op jit(solution)/shard_map/ppermute | solution.py:24
  20.5 9.9 %collective-permute-start.3 = (bf16[4,32,1024]{2,1,0:T(8,128)(2,1)S(1)}, bf16[4,32,1024]{2,1,0:T(8,128)(2,1)S(1)}, u32[]{:S(2)}, u32[]{:S(2)}) collective-permute-start(bf16[4,32,1024]{2,1,0:T(8,128)(2,1)S(1)} %get-tuple-element.75.g0), channel_id=1, source_target_pairs={{0,8},{1,33},{2,10},{3,35},{4,12},{5,37},{6,14},{7,39},{8,16},{9,4... | collective-permute-start | bytes 786440 | tf_op jit(solution)/shard_map/ppermute | solution.py:24
  36.3 16.1 %collective-permute-start.10 = (f32[4,32,1024]{2,1,0:T(8,128)S(1)}, f32[4,32,1024]{2,1,0:T(8,128)S(1)}, u32[]{:S(2)}, u32[]{:S(2)}) collective-permute-start(f32[4,32,1024]{2,1,0:T(8,128)S(1)} %get-tuple-element.38), channel_id=1, source_target_pairs={{0,8},{1,33},{2,10},{3,35},{4,12},{5,37},{6,14},{7,39},{8,16},{9,4... | collective-permute-start | bytes 1572872 | tf_op jit(solution)/shard_map/ppermute | solution.py:24
  36.4 16.0 %collective-permute-start.11 = (f32[4,32,1024]{2,1,0:T(8,128)S(1)}, f32[4,32,1024]{2,1,0:T(8,128)S(1)}, u32[]{:S(2)}, u32[]{:S(2)}) collective-permute-start(f32[4,32,1024]{2,1,0:T(8,128)S(1)} %get-tuple-element.39), channel_id=1, source_target_pairs={{0,24},{1,97},{2,26},{3,99},{4,28},{5,101},{6,30},{7,103},{8,0},{9... | collective-permute-start | bytes 1572872 | tf_op jit(solution)/shard_map/ppermute | solution.py:24
  39.7 12.8 %collective-permute-start.12 = (f32[4,32,1024]{2,1,0:T(8,128)S(1)}, f32[4,32,1024]{2,1,0:T(8,128)S(1)}, u32[]{:S(2)}, u32[]{:S(2)}) collective-permute-start(f32[4,32,1024]{2,1,0:T(8,128)S(1)} %get-tuple-element.40), channel_id=1, source_target_pairs={{0,16},{1,65},{2,18},{3,67},{4,20},{5,69},{6,22},{7,71},{8,24},{9,... | collective-permute-start | bytes 1572872 | tf_op jit(solution)/shard_map/ppermute | solution.py:24
  39.7 18.1 %collective-permute-start.13 = (f32[4,32,1024]{2,1,0:T(8,128)S(1)}, f32[4,32,1024]{2,1,0:T(8,128)S(1)}, u32[]{:S(2)}, u32[]{:S(2)}) collective-permute-start(f32[4,32,1024]{2,1,0:T(8,128)S(1)} %get-tuple-element.43), channel_id=1, source_target_pairs={{0,1},{1,0},{2,3},{3,2},{4,5},{5,4},{6,7},{7,6},{8,9},{9,8},{10,11... | collective-permute-start | bytes 1572872 | tf_op jit(solution)/shard_map/ppermute | solution.py:24
  52.5 8.6 %collective-permute-start.17 = (f32[32,1024]{1,0:T(8,128)S(1)}, f32[32,1024]{1,0:T(8,128)S(1)}, u32[]{:S(2)}, u32[]{:S(2)}) collective-permute-start(f32[32,1024]{1,0:T(8,128)S(1)} %get-tuple-element.48), channel_id=1, source_target_pairs={{0,32},{1,9},{2,34},{3,11},{4,36},{5,13},{6,38},{7,15},{8,40},{9,1... | collective-permute-start | bytes 393224 | tf_op jit(solution)/shard_map/ppermute | solution.py:24
  52.6 10.1 %collective-permute-start.18 = (f32[32,1024]{1,0:T(8,128)S(1)}, f32[32,1024]{1,0:T(8,128)S(1)}, u32[]{:S(2)}, u32[]{:S(2)}) collective-permute-start(f32[32,1024]{1,0:T(8,128)S(1)} %get-tuple-element.49), channel_id=1, source_target_pairs={{0,96},{1,25},{2,98},{3,27},{4,100},{5,29},{6,102},{7,31},{8,104},... | collective-permute-start | bytes 393224 | tf_op jit(solution)/shard_map/ppermute | solution.py:24
  55.8 6.9 %collective-permute-start.19 = (f32[32,1024]{1,0:T(8,128)S(1)}, f32[32,1024]{1,0:T(8,128)S(1)}, u32[]{:S(2)}, u32[]{:S(2)}) collective-permute-start(f32[32,1024]{1,0:T(8,128)S(1)} %get-tuple-element.50), channel_id=1, source_target_pairs={{0,64},{1,17},{2,66},{3,19},{4,68},{5,21},{6,70},{7,23},{8,72},{9,... | collective-permute-start | bytes 393224 | tf_op jit(solution)/shard_map/ppermute | solution.py:24
  57.9 6.2 %collective-permute-start.14 = (f32[32,1024]{1,0:T(8,128)S(1)}, f32[32,1024]{1,0:T(8,128)S(1)}, u32[]{:S(2)}, u32[]{:S(2)}) collective-permute-start(f32[32,1024]{1,0:T(8,128)S(1)} %get-tuple-element.45), channel_id=1, source_target_pairs={{0,2},{1,3},{2,4},{3,5},{4,6},{5,7},{6,0},{7,1},{8,10},{9,11},{10,... | collective-permute-start | bytes 393224 | tf_op jit(solution)/shard_map/ppermute | solution.py:24
  60.6 6.3 %collective-permute-start.15 = (f32[32,1024]{1,0:T(8,128)S(1)}, f32[32,1024]{1,0:T(8,128)S(1)}, u32[]{:S(2)}, u32[]{:S(2)}) collective-permute-start(f32[32,1024]{1,0:T(8,128)S(1)} %get-tuple-element.46), channel_id=1, source_target_pairs={{0,6},{1,7},{2,0},{3,1},{4,2},{5,3},{6,4},{7,5},{8,14},{9,15},{10,... | collective-permute-start | bytes 393224 | tf_op jit(solution)/shard_map/ppermute | solution.py:24
  61.2 7.7 %collective-permute-start.16 = (f32[32,1024]{1,0:T(8,128)S(1)}, f32[32,1024]{1,0:T(8,128)S(1)}, u32[]{:S(2)}, u32[]{:S(2)}) collective-permute-start(f32[32,1024]{1,0:T(8,128)S(1)} %get-tuple-element.47), channel_id=1, source_target_pairs={{0,4},{1,5},{2,6},{3,7},{4,0},{5,1},{6,2},{7,3},{8,12},{9,13},{10,... | collective-permute-start | bytes 393224 | tf_op jit(solution)/shard_map/ppermute | solution.py:24
  71.2 5.8 %collective-permute-start.37 = (bf16[32,1024]{1,0:T(8,128)(2,1)S(1)}, bf16[32,1024]{1,0:T(8,128)(2,1)S(1)}, u32[]{:S(2)}, u32[]{:S(2)}) collective-permute-start(bf16[32,1024]{1,0:T(8,128)(2,1)S(1)} %get-tuple-element.54), channel_id=1, source_target_pairs={{0,4},{1,5},{2,6},{3,7},{4,0},{5,1},{6,2},{7,3},{8,12},{9,13},{10,... | collective-permute-start | bytes 196616 | tf_op jit(solution)/shard_map/ppermute | solution.py:24
  71.7 5.9 %collective-permute-start.36 = (bf16[32,1024]{1,0:T(8,128)(2,1)S(1)}, bf16[32,1024]{1,0:T(8,128)(2,1)S(1)}, u32[]{:S(2)}, u32[]{:S(2)}) collective-permute-start(bf16[32,1024]{1,0:T(8,128)(2,1)S(1)} %get-tuple-element.54), channel_id=1, source_target_pairs={{0,2},{1,3},{2,4},{3,5},{4,6},{5,7},{6,0},{7,1},{8,10},{9,11},{10,... | collective-permute-start | bytes 196616 | tf_op jit(solution)/shard_map/ppermute | solution.py:24
  72.2 5.5 %collective-permute-start.32 = (bf16[32,1024]{1,0:T(8,128)(2,1)S(1)}, bf16[32,1024]{1,0:T(8,128)(2,1)S(1)}, u32[]{:S(2)}, u32[]{:S(2)}) collective-permute-start(bf16[32,1024]{1,0:T(8,128)(2,1)S(1)} %get-tuple-element.54), channel_id=1, source_target_pairs={{0,96},{1,25},{2,98},{3,27},{4,100},{5,29},{6,102},{7,31},{8,104},... | collective-permute-start | bytes 196616 | tf_op jit(solution)/shard_map/ppermute | solution.py:24
  72.2 5.8 %collective-permute-start.31 = (bf16[32,1024]{1,0:T(8,128)(2,1)S(1)}, bf16[32,1024]{1,0:T(8,128)(2,1)S(1)}, u32[]{:S(2)}, u32[]{:S(2)}) collective-permute-start(bf16[32,1024]{1,0:T(8,128)(2,1)S(1)} %get-tuple-element.54), channel_id=1, source_target_pairs={{0,64},{1,17},{2,66},{3,19},{4,68},{5,21},{6,70},{7,23},{8,72},{9,... | collective-permute-start | bytes 196616 | tf_op jit(solution)/shard_map/ppermute | solution.py:24
  73.7 5.5 %collective-permute-start.30 = (bf16[32,1024]{1,0:T(8,128)(2,1)S(1)}, bf16[32,1024]{1,0:T(8,128)(2,1)S(1)}, u32[]{:S(2)}, u32[]{:S(2)}) collective-permute-start(bf16[32,1024]{1,0:T(8,128)(2,1)S(1)} %get-tuple-element.54), channel_id=1, source_target_pairs={{0,32},{1,9},{2,34},{3,11},{4,36},{5,13},{6,38},{7,15},{8,40},{9,1... | collective-permute-start | bytes 196616 | tf_op jit(solution)/shard_map/ppermute | solution.py:24
  79.4 10.1 %collective-permute-start.35 = (bf16[4,32,1024]{2,1,0:T(8,128)(2,1)S(1)}, bf16[4,32,1024]{2,1,0:T(8,128)(2,1)S(1)}, u32[]{:S(2)}, u32[]{:S(2)}) collective-permute-start(bf16[4,32,1024]{2,1,0:T(8,128)(2,1)S(1)} %get-tuple-element.73.g0), channel_id=1, source_target_pairs={{0,24},{1,97},{2,26},{3,99},{4,28},{5,101},{6,30},{7,103},{8,0},{9... | collective-permute-start | bytes 786440 | tf_op jit(solution)/shard_map/ppermute | solution.py:24
  82.7 8.0 %collective-permute-start.34 = (bf16[4,32,1024]{2,1,0:T(8,128)(2,1)S(1)}, bf16[4,32,1024]{2,1,0:T(8,128)(2,1)S(1)}, u32[]{:S(2)}, u32[]{:S(2)}) collective-permute-start(bf16[4,32,1024]{2,1,0:T(8,128)(2,1)S(1)} %get-tuple-element.73.g0), channel_id=1, source_target_pairs={{0,16},{1,65},{2,18},{3,67},{4,20},{5,69},{6,22},{7,71},{8,24},{9,... | collective-permute-start | bytes 786440 | tf_op jit(solution)/shard_map/ppermute | solution.py:24
  82.7 10.4 %collective-permute-start.33 = (bf16[4,32,1024]{2,1,0:T(8,128)(2,1)S(1)}, bf16[4,32,1024]{2,1,0:T(8,128)(2,1)S(1)}, u32[]{:S(2)}, u32[]{:S(2)}) collective-permute-start(bf16[4,32,1024]{2,1,0:T(8,128)(2,1)S(1)} %get-tuple-element.73.g0), channel_id=1, source_target_pairs={{0,8},{1,33},{2,10},{3,35},{4,12},{5,37},{6,14},{7,39},{8,16},{9,4... | collective-permute-start | bytes 786440 | tf_op jit(solution)/shard_map/ppermute | solution.py:24
  99.1 16.0 %collective-permute-start.40 = (bf16[4,32,1024]{2,1,0:T(8,128)(2,1)S(1)}, bf16[4,32,1024]{2,1,0:T(8,128)(2,1)S(1)}, u32[]{:S(2)}, u32[]{:S(2)}) collective-permute-start(bf16[4,32,1024]{2,1,0:T(8,128)(2,1)S(1)} %get-tuple-element.56), channel_id=1, source_target_pairs={{0,8},{1,33},{2,10},{3,35},{4,12},{5,37},{6,14},{7,39},{8,16},{9,4... | collective-permute-start | bytes 786440 | tf_op jit(solution)/shard_map/ppermute | solution.py:24
  99.2 16.8 %collective-permute-start.41 = (bf16[4,32,1024]{2,1,0:T(8,128)(2,1)S(1)}, bf16[4,32,1024]{2,1,0:T(8,128)(2,1)S(1)}, u32[]{:S(2)}, u32[]{:S(2)}) collective-permute-start(bf16[4,32,1024]{2,1,0:T(8,128)(2,1)S(1)} %get-tuple-element.57), channel_id=1, source_target_pairs={{0,24},{1,97},{2,26},{3,99},{4,28},{5,101},{6,30},{7,103},{8,0},{9... | collective-permute-start | bytes 786440 | tf_op jit(solution)/shard_map/ppermute | solution.py:24
  102.4 14.8 %collective-permute-start.42 = (bf16[4,32,1024]{2,1,0:T(8,128)(2,1)S(1)}, bf16[4,32,1024]{2,1,0:T(8,128)(2,1)S(1)}, u32[]{:S(2)}, u32[]{:S(2)}) collective-permute-start(bf16[4,32,1024]{2,1,0:T(8,128)(2,1)S(1)} %get-tuple-element.58), channel_id=1, source_target_pairs={{0,16},{1,65},{2,18},{3,67},{4,20},{5,69},{6,22},{7,71},{8,24},{9,... | collective-permute-start | bytes 786440 | tf_op jit(solution)/shard_map/ppermute | solution.py:24
  103.6 5.2 %collective-permute-start.23 = (f32[32,32]{1,0:T(8,128)S(1)}, f32[32,32]{1,0:T(8,128)S(1)}, u32[]{:S(2)}, u32[]{:S(2)}) collective-permute-start(f32[32,32]{1,0:T(8,128)S(1)} %add.60), channel_id=1, source_target_pairs={{0,4},{1,5},{2,6},{3,7},{4,0},{5,1},{6,2},{7,3},{8,12},{9,13},{10,... | collective-permute-start | bytes 12296 | tf_op jit(solution)/shard_map/ppermute | solution.py:24
  108.8 4.9 %collective-permute-start.21 = (f32[32,32]{1,0:T(8,128)S(1)}, f32[32,32]{1,0:T(8,128)S(1)}, u32[]{:S(2)}, u32[]{:S(2)}) collective-permute-start(f32[32,32]{1,0:T(8,128)S(1)} %add.60), channel_id=1, source_target_pairs={{0,2},{1,3},{2,4},{3,5},{4,6},{5,7},{6,0},{7,1},{8,10},{9,11},{10,... | collective-permute-start | bytes 12296 | tf_op jit(solution)/shard_map/ppermute | solution.py:24
  110.1 16.1 %collective-permute-start.43 = (bf16[4,32,1024]{2,1,0:T(8,128)(2,1)S(1)}, bf16[4,32,1024]{2,1,0:T(8,128)(2,1)S(1)}, u32[]{:S(2)}, u32[]{:S(2)}) collective-permute-start(bf16[4,32,1024]{2,1,0:T(8,128)(2,1)S(1)} %get-tuple-element.61), channel_id=1, source_target_pairs={{0,1},{1,0},{2,3},{3,2},{4,5},{5,4},{6,7},{7,6},{8,9},{9,8},{10,11... | collective-permute-start | bytes 786440 | tf_op jit(solution)/shard_map/ppermute | solution.py:24
  113.8 5.2 %collective-permute-start.26 = (f32[32,32]{1,0:T(8,128)S(1)}, f32[32,32]{1,0:T(8,128)S(1)}, u32[]{:S(2)}, u32[]{:S(2)}) collective-permute-start(f32[32,32]{1,0:T(8,128)S(1)} %add_add_fusion.5), channel_id=1, source_target_pairs={{0,64},{1,65},{2,66},{3,67},{4,68},{5,69},{6,70},{7,71},{8,72},{9,... | collective-permute-start | bytes 12296 | tf_op jit(solution)/shard_map/ppermute | solution.py:24
  116.0 5.0 %collective-permute-start.24 = (f32[32,32]{1,0:T(8,128)S(1)}, f32[32,32]{1,0:T(8,128)S(1)}, u32[]{:S(2)}, u32[]{:S(2)}) collective-permute-start(f32[32,32]{1,0:T(8,128)S(1)} %add_add_fusion.5), channel_id=1, source_target_pairs={{0,32},{1,33},{2,34},{3,35},{4,36},{5,37},{6,38},{7,39},{8,40},{9,... | collective-permute-start | bytes 12296 | tf_op jit(solution)/shard_map/ppermute | solution.py:24
  117.3 14.6 %collective-permute-start.47 = (bf16[32,1024]{1,0:T(8,128)(2,1)S(1)}, bf16[32,1024]{1,0:T(8,128)(2,1)S(1)}, u32[]{:S(2)}, u32[]{:S(2)}) collective-permute-start(bf16[32,1024]{1,0:T(8,128)(2,1)S(1)} %get-tuple-element.66), channel_id=1, source_target_pairs={{0,32},{1,9},{2,34},{3,11},{4,36},{5,13},{6,38},{7,15},{8,40},{9,1... | collective-permute-start | bytes 196616 | tf_op jit(solution)/shard_map/ppermute | solution.py:24
  120.9 6.3 %collective-permute-start.29 = (f32[32,32]{1,0:T(8,128)S(1)}, f32[32,32]{1,0:T(8,128)S(1)}, u32[]{:S(2)}, u32[]{:S(2)}) collective-permute-start(f32[32,32]{1,0:T(8,128)S(1)} %add_add_fusion.4), channel_id=1, source_target_pairs={{0,16},{1,17},{2,18},{3,19},{4,20},{5,21},{6,22},{7,23},{8,24},{9,... | collective-permute-start | bytes 12296 | tf_op jit(solution)/shard_map/ppermute | solution.py:24
  125.0 4.9 %collective-permute-start.27 = (f32[32,32]{1,0:T(8,128)S(1)}, f32[32,32]{1,0:T(8,128)S(1)}, u32[]{:S(2)}, u32[]{:S(2)}) collective-permute-start(f32[32,32]{1,0:T(8,128)S(1)} %add_add_fusion.4), channel_id=1, source_target_pairs={{0,8},{1,9},{2,10},{3,11},{4,12},{5,13},{6,14},{7,15},{8,16},{9,17... | collective-permute-start | bytes 12296 | tf_op jit(solution)/shard_map/ppermute | solution.py:24
  126.3 10.2 %collective-permute-start.48 = (bf16[32,1024]{1,0:T(8,128)(2,1)S(1)}, bf16[32,1024]{1,0:T(8,128)(2,1)S(1)}, u32[]{:S(2)}, u32[]{:S(2)}) collective-permute-start(bf16[32,1024]{1,0:T(8,128)(2,1)S(1)} %get-tuple-element.67), channel_id=1, source_target_pairs={{0,96},{1,25},{2,98},{3,27},{4,100},{5,29},{6,102},{7,31},{8,104},... | collective-permute-start | bytes 196616 | tf_op jit(solution)/shard_map/ppermute | solution.py:24
  127.3 9.2 %collective-permute-start.49 = (bf16[32,1024]{1,0:T(8,128)(2,1)S(1)}, bf16[32,1024]{1,0:T(8,128)(2,1)S(1)}, u32[]{:S(2)}, u32[]{:S(2)}) collective-permute-start(bf16[32,1024]{1,0:T(8,128)(2,1)S(1)} %get-tuple-element.68), channel_id=1, source_target_pairs={{0,64},{1,17},{2,66},{3,19},{4,68},{5,21},{6,70},{7,23},{8,72},{9,... | collective-permute-start | bytes 196616 | tf_op jit(solution)/shard_map/ppermute | solution.py:24
  128.7 7.8 %collective-permute-start.44 = (bf16[32,1024]{1,0:T(8,128)(2,1)S(1)}, bf16[32,1024]{1,0:T(8,128)(2,1)S(1)}, u32[]{:S(2)}, u32[]{:S(2)}) collective-permute-start(bf16[32,1024]{1,0:T(8,128)(2,1)S(1)} %get-tuple-element.63), channel_id=1, source_target_pairs={{0,2},{1,3},{2,4},{3,5},{4,6},{5,7},{6,0},{7,1},{8,10},{9,11},{10,... | collective-permute-start | bytes 196616 | tf_op jit(solution)/shard_map/ppermute | solution.py:24
  130.0 6.5 %collective-permute-start.45 = (bf16[32,1024]{1,0:T(8,128)(2,1)S(1)}, bf16[32,1024]{1,0:T(8,128)(2,1)S(1)}, u32[]{:S(2)}, u32[]{:S(2)}) collective-permute-start(bf16[32,1024]{1,0:T(8,128)(2,1)S(1)} %get-tuple-element.64), channel_id=1, source_target_pairs={{0,6},{1,7},{2,0},{3,1},{4,2},{5,3},{6,4},{7,5},{8,14},{9,15},{10,... | collective-permute-start | bytes 196616 | tf_op jit(solution)/shard_map/ppermute | solution.py:24
  131.9 5.8 %collective-permute-start.46 = (bf16[32,1024]{1,0:T(8,128)(2,1)S(1)}, bf16[32,1024]{1,0:T(8,128)(2,1)S(1)}, u32[]{:S(2)}, u32[]{:S(2)}) collective-permute-start(bf16[32,1024]{1,0:T(8,128)(2,1)S(1)} %get-tuple-element.65), channel_id=1, source_target_pairs={{0,4},{1,5},{2,6},{3,7},{4,0},{5,1},{6,2},{7,3},{8,12},{9,13},{10,... | collective-permute-start | bytes 196616 | tf_op jit(solution)/shard_map/ppermute | solution.py:24
  139.4 5.2 %collective-permute-start.53 = (f32[32,32]{1,0:T(8,128)S(1)}, f32[32,32]{1,0:T(8,128)S(1)}, u32[]{:S(2)}, u32[]{:S(2)}) collective-permute-start(f32[32,32]{1,0:T(8,128)S(1)} %add.70), channel_id=1, source_target_pairs={{0,4},{1,5},{2,6},{3,7},{4,0},{5,1},{6,2},{7,3},{8,12},{9,13},{10,... | collective-permute-start | bytes 12296 | tf_op jit(solution)/shard_map/ppermute | solution.py:24
  142.2 4.9 %collective-permute-start.51 = (f32[32,32]{1,0:T(8,128)S(1)}, f32[32,32]{1,0:T(8,128)S(1)}, u32[]{:S(2)}, u32[]{:S(2)}) collective-permute-start(f32[32,32]{1,0:T(8,128)S(1)} %add.70), channel_id=1, source_target_pairs={{0,2},{1,3},{2,4},{3,5},{4,6},{5,7},{6,0},{7,1},{8,10},{9,11},{10,... | collective-permute-start | bytes 12296 | tf_op jit(solution)/shard_map/ppermute | solution.py:24
  147.1 5.2 %collective-permute-start.56 = (f32[32,32]{1,0:T(8,128)S(1)}, f32[32,32]{1,0:T(8,128)S(1)}, u32[]{:S(2)}, u32[]{:S(2)}) collective-permute-start(f32[32,32]{1,0:T(8,128)S(1)} %add_add_fusion.2), channel_id=1, source_target_pairs={{0,64},{1,65},{2,66},{3,67},{4,68},{5,69},{6,70},{7,71},{8,72},{9,... | collective-permute-start | bytes 12296 | tf_op jit(solution)/shard_map/ppermute | solution.py:24
  154.7 5.2 %collective-permute-start.59 = (f32[32,32]{1,0:T(8,128)S(1)}, f32[32,32]{1,0:T(8,128)S(1)}, u32[]{:S(2)}, u32[]{:S(2)}) collective-permute-start(f32[32,32]{1,0:T(8,128)S(1)} %add_add_fusion.1), channel_id=1, source_target_pairs={{0,16},{1,17},{2,18},{3,19},{4,20},{5,21},{6,22},{7,23},{8,24},{9,... | collective-permute-start | bytes 12296 | tf_op jit(solution)/shard_map/ppermute | solution.py:24
  (12 other events, 45.8 us)

commit v2 on v1

v2 whole, which is shorter than its diff:
```python
import functools

import jax
import jax.numpy as jnp
from jax import lax
from jax.experimental import pallas as pl
from jax.experimental.pallas import tpu as pltpu
from jax.sharding import PartitionSpec as P

BOTH = ("row", "col")
HIGHEST = lax.Precision.HIGHEST
VMEM = pl.BlockSpec(memory_space=pltpu.VMEM)
SMEM = pl.BlockSpec(memory_space=pltpu.SMEM)
PARAMS = pltpu.CompilerParams(vmem_limit_bytes=24 * 1024 * 1024)


def permute(value, target):
    pairs = []
    for device in range(128):
        z, x, y, c = device // 32, device // 8 % 4, device // 2 % 4, device % 2
        tz, tx, ty, tc = target(z, x, y, c)
        pairs.append((device, ((tz % 4) * 4 + tx % 4) * 8 + (ty % 4) * 2 + tc % 2))
    return lax.ppermute(value, BOTH, pairs)


def send_inner(value, s):
    return permute(value, lambda z, x, y, c: (z + s, x, y, c) if c == 0 else (z, x + s, y, c))


def send_outer(value, s):
    return permute(value, lambda z, x, y, c: (z, x + s, y, c) if c == 0 else (z + s, x, y, c))


def send_y(value, s):
    return permute(value, lambda z, x, y, c: (z, x, y ^ s, c))


def send_core(value):
    return permute(value, lambda z, x, y, c: (z, x, y, c + 1))


def struct(shape, dtype):
    return jax.ShapeDtypeStruct(shape, dtype)


def fold(gram):
    return jnp.concatenate([gram[8 * k : 8 * k + 8] for k in range(4)], axis=1)


def unfold(tile):
    return jnp.concatenate([tile[:, 32 * k : 32 * k + 32] for k in range(4)], axis=0)


def split(tile):
    terms = []
    for _ in range(3):
        term = tile.astype(jnp.bfloat16).astype(jnp.float32)
        terms.append(term)
        tile = tile - term
    return jnp.concatenate(terms + [jnp.zeros_like(tile)], axis=0).astype(jnp.bfloat16)


def merge(terms):
    terms = terms.astype(jnp.float32)
    return terms[0:8] + terms[8:16] + terms[16:24]


def product_kernel(with_gram, pairs, live, blocks, g0, g1, g2, g3, h0, h1, *rest):
    gathered, pair_gathered = (g0, g1, g2, g3), (h0, h1)
    outs = rest[:6]
    lefts, rights, results = rest[-3:]
    count = live[0]
    row = pairs[0, 0, 0] // 8
    col = pairs[0, 0, 1] % 8
    z, x, y, c = row // 4, row % 4, col // 2, col % 2

    def row_shift(target):
        dz, dx = (target // 4 - z) & 3, (target % 4 - x) & 3
        return jnp.where(c == 0, dx, dz), jnp.where(c == 0, dz, dx)

    for out in outs:
        out[...] = jnp.zeros_like(out)
    if with_gram:
        gram = merge(g0[0, :, 1024:1152])
        for array in gathered[1:]:
            gram = gram + merge(array[0, :, 1024:1152])
        rest[6][...] = gram
        outs[5][0, :, 1024:1152] = split(gram)

    def advance(slot, carry):
        first, second = pairs[0, slot, 0], pairs[0, slot, 1]
        outer, inner = row_shift(second // 8)
        dy = (first % 8 // 2) ^ y
        dy = dy ^ (dy >> 1)
        dc = (first % 8 % 2) ^ c
        for t in range(4):
            @pl.when((-outer & 3) == t)
            def _():
                lefts[...] = gathered[t][-inner & 3, :, 0:1024]
        for t in range(2):
            @pl.when(dc == t)
            def _():
                rights[...] = pair_gathered[t][dy]
        matrix = blocks[slot]
        direct = lax.dot_general(
            lefts[...], matrix, (((1,), (1,)), ((), ())), preferred_element_type=jnp.float32
        )
        mirror = lax.dot_general(
            rights[...], matrix, (((1,), (0,)), ((), ())), preferred_element_type=jnp.float32
        )
        results[slot, 0] = direct
        results[slot, 1] = jnp.where(first != second, mirror, 0.0)

        def earlier(before, carry):
            @pl.when(pairs[0, before, 0] == first)
            def _():
                lefts_sum = results[3, 0] + results[before, 0]
                results[3, 0] = lefts_sum

            @pl.when(pairs[0, before, 1] == second)
            def _():
                results[3, 1] = results[3, 1] + results[before, 1]

            return carry

        results[3] = results[slot]
        lax.fori_loop(0, slot, earlier, 0)
        for t in range(4):
            @pl.when(outer == t)
            def _():
                outs[t][inner] = results[3, 1].astype(outs[t].dtype)
        for t in range(2):
            @pl.when(dc == t)
            def _():
                outs[4 + t][dy, :, 0:1024] = results[3, 0].astype(outs[4 + t].dtype)
        return carry

    lax.fori_loop(0, count, advance, 0)


def product(pairs, live, blocks, gathered, pair_gathered, sent, with_gram):
    shape = (4, 32, 1024)
    f32 = jnp.float32
    outs = [struct(shape, f32)] + [struct(shape, sent)] * 3 + [struct(shape, f32)]
    outs += [struct((4, 32, 1152) if with_gram else shape, sent)]
    outs += [struct((8, 128), f32)] * with_gram
    return pl.pallas_call(
        functools.partial(product_kernel, with_gram),
        out_shape=outs,
        in_specs=[SMEM, SMEM] + [VMEM] * 7,
        out_specs=[VMEM] * len(outs),
        scratch_shapes=[
            pltpu.VMEM((32, 1024), jnp.bfloat16),
            pltpu.VMEM((32, 1024), jnp.bfloat16),
            pltpu.VMEM((4, 2, 32, 1024), f32),
        ],
        compiler_params=PARAMS,
        cost_estimate=pl.CostEstimate(flops=800_000_000, bytes_accessed=10_000_000, transcendentals=0),
        name="product",
    )(pairs, live, blocks, *gathered, *pair_gathered)


def join_kernel(with_gram, *refs):
    parts, pair, joined, joined_pair = refs[:4], refs[4:6], refs[6], refs[7]
    for k, part in enumerate(parts):
        joined[k] = part[...]
    if with_gram:
        gram = merge(parts[0][:, 1024:1152])
        for part in parts[1:]:
            gram = gram + merge(part[:, 1024:1152])
        joined[0, :, 1024:1152] = split(gram)
    for k, part in enumerate(pair):
        joined_pair[k] = part[...]


def join(parts, pair, with_gram):
    shapes = [(4,) + parts[0].shape, (2,) + pair[0].shape]
    return pl.pallas_call(
        functools.partial(join_kernel, with_gram),
        out_shape=[struct(shape, jnp.bfloat16) for shape in shapes],
        in_specs=[VMEM] * 6,
        out_specs=[VMEM] * 2,
        compiler_params=PARAMS,
        name="join",
    )(*parts, *pair)


def halve_kernel(with_gram, own, received, *rest):
    outs = rest[with_gram:]
    keep, send = outs[:2]
    half = keep.shape[0]
    for k in range(2 * half):
        value = own[k] + received[k, :, 0:1024].astype(jnp.float32)
        if k < half:
            keep[k] = value
        else:
            send[k - half, :, 0:1024] = value.astype(send.dtype)
    if with_gram:
        gram = rest[0][...] + merge(received[0, :, 1024:1152])
        outs[2][...] = gram
        for k in range(half):
            send[k, :, 1024:1152] = split(gram)


def halve(own, received, gram):
    f32 = jnp.float32
    half = own.shape[0] // 2
    outs = [struct((half, 32, 1024), f32), struct((half,) + received.shape[1:], received.dtype)]
    outs += [struct((8, 128), f32)] * len(gram)
    return pl.pallas_call(
        functools.partial(halve_kernel, len(gram)),
        out_shape=outs,
        in_specs=[VMEM] * (2 + len(gram)),
        out_specs=[VMEM] * len(outs),
        compiler_params=PARAMS,
        name="halve",
    )(own, received, *gram)


def row_kernel(own, *refs):
    received, outs = refs[:3], refs[3:]
    for k in range(4):
        value = own[k]
        for array in received:
            value = value + array[k].astype(jnp.float32)
        outs[k][...] = value.astype(outs[k].dtype)


def add_outer(own, received, sent):
    return pl.pallas_call(
        row_kernel,
        out_shape=[struct((32, 1024), jnp.float32)] + [struct((32, 1024), sent)] * 3,
        in_specs=[VMEM] * 4,
        out_specs=[VMEM] * 4,
        compiler_params=PARAMS,
        name="add_outer",
    )(own, *received)


def add_parts(parts):
    value = parts[0][...] + parts[1][0]
    for part in parts[2:5]:
        value = value + part[...].astype(jnp.float32)
    return value + parts[5][0, :, 0:1024].astype(jnp.float32)


def first_kernel(*refs):
    parts, (first, panel, own) = refs[:6], refs[6:]
    value = add_parts(parts)
    first[...] = value
    rounded = value.astype(jnp.bfloat16)
    panel[:, 0:1024] = rounded
    own[...] = rounded
    panel[:, 1024:1152] = split(
        fold(
            lax.dot_general(
                rounded, rounded, (((1,), (1,)), ((), ())), preferred_element_type=jnp.float32
            )
        )
    )


def finish_first(parts):
    return pl.pallas_call(
        first_kernel,
        out_shape=[
            struct((32, 1024), jnp.float32),
            struct((32, 1152), jnp.bfloat16),
            struct((32, 1024), jnp.bfloat16),
        ],
        in_specs=[VMEM] * 6,
        out_specs=[VMEM] * 3,
        compiler_params=PARAMS,
        name="finish_first",
    )(*parts)


def second_kernel(*refs):
    parts, inverse, (scaled, gram) = refs[:6], refs[6], refs[7:]
    value = add_parts(parts)
    value = jnp.dot(inverse[...], value, precision=HIGHEST, preferred_element_type=jnp.float32)
    scaled[...] = value
    tile = fold(
        lax.dot_general(
            value, value, (((1,), (1,)), ((), ())), precision=HIGHEST, preferred_element_type=jnp.float32
        )
    )
    for k in range(8):
        gram[k] = tile


def finish_second(parts, inverse):
    return pl.pallas_call(
        second_kernel,
        out_shape=[struct((32, 1024), jnp.float32), struct((8, 8, 128), jnp.float32)],
        in_specs=[VMEM] * 7,
        out_specs=[VMEM] * 2,
        compiler_params=PARAMS,
        name="finish_second",
    )(*parts, inverse)


def total_kernel(tiles, out):
    total = tiles[0]
    for k in range(1, 8):
        total = total + tiles[k]
    for k in range(16):
        out[k] = total


def total_gram(tiles):
    tiles = lax.all_to_all(tiles, "col", 0, 0, tiled=True)
    tiles = pl.pallas_call(
        total_kernel,
        out_shape=struct((16, 8, 128), jnp.float32),
        in_specs=[VMEM],
        out_specs=VMEM,
        compiler_params=PARAMS,
        name="total_gram",
    )(tiles)
    return lax.all_to_all(tiles, "row", 0, 0, tiled=True)


def lower_inverse(gram):
    rows = lax.broadcasted_iota(jnp.int32, (32, 128), 0)
    lanes = lax.broadcasted_iota(jnp.int32, (32, 128), 1)
    wide = jnp.concatenate([gram, jnp.zeros((32, 96), jnp.float32)], axis=1)
    wide = jnp.where(lanes == rows + 32, 1.0, wide)
    for k in range(31):
        pivot = wide[k : k + 1, k : k + 1]
        factor = jnp.where(rows > k, wide[:, k : k + 1], 0.0)
        wide = wide - factor * (wide[k : k + 1, :] / pivot)
    diagonal = jnp.sum(jnp.where(lanes == rows, wide, 0.0), axis=1, keepdims=True)
    wide = wide / jnp.sqrt(diagonal)
    return wide[:, 32:64]


def factor_kernel(root, gram, panel, *outs):
    tile = gram[0]
    for k in range(1, 16):
        tile = tile + gram[k]
    inverse = lower_inverse(unfold(tile))
    outs[0][...] = (
        jnp.dot(inverse, panel[...], precision=HIGHEST, preferred_element_type=jnp.float32) * root
    )


def factor_first_kernel(root, gram, received, panel, basis, inverse):
    inverse[...] = lower_inverse(unfold(gram[...] + merge(received[0, :, 1024:1152])))
    basis[...] = (
        jnp.dot(inverse[...], panel[...], precision=HIGHEST, preferred_element_type=jnp.float32) * root
    )


def factor_first(gram, received, first, root):
    return pl.pallas_call(
        functools.partial(factor_first_kernel, root),
        out_shape=[struct((32, 1024), jnp.float32), struct((32, 32), jnp.float32)],
        in_specs=[VMEM] * 3,
        out_specs=[VMEM] * 2,
        compiler_params=PARAMS,
        cost_estimate=pl.CostEstimate(flops=1_000_000, bytes_accessed=10_000_000, transcendentals=0),
        name="factor_first",
    )(gram, received, first)


def factor_second(gram, scaled, root):
    return pl.pallas_call(
        functools.partial(factor_kernel, root),
        out_shape=struct((32, 1024), jnp.float32),
        in_specs=[VMEM] * 2,
        out_specs=VMEM,
        compiler_params=PARAMS,
        name="factor_second",
    )(gram, scaled)


SHIFTS = (1, 3, 2)


def spread(send, value):
    got = {s: send(value, s) for s in SHIFTS}
    return [value] + [got[s] for s in (1, 2, 3)]


def gather(panel, own, with_gram):
    inner, pair = join(spread(send_inner, panel), [own, send_y(own, 1)], with_gram)
    outer = spread(send_outer, inner)
    along_y = jnp.concatenate([pair, send_y(pair, 3)])
    return outer, [along_y, send_core(along_y)]


def scatter(parts, sent):
    got = [send_outer(parts[s], s) for s in SHIFTS]
    column, send, *gram = halve(parts[4], send_core(parts[5]), parts[6:])
    column, send, *gram = halve(column, send_y(send, 3), gram)
    along_y = send_y(send, 1)
    row = add_outer(parts[0], got, sent)
    return [row[0], column] + [send_inner(row[s], s) for s in SHIFTS] + [along_y], gram


def hold_kernel(source, target, sem):
    copy = pltpu.make_async_copy(source, target, sem)
    copy.start()
    copy.wait()


def hold(blocks):
    return pl.pallas_call(
        hold_kernel,
        out_shape=struct(blocks.shape, blocks.dtype),
        in_specs=[pl.BlockSpec(memory_space=pl.ANY)],
        out_specs=VMEM,
        scratch_shapes=[pltpu.SemaphoreType.DMA(())],
        compiler_params=PARAMS,
        cost_estimate=pl.CostEstimate(flops=0, bytes_accessed=6_000_000, transcendentals=0),
        name="hold",
    )(blocks)


def on_device(block_pairs, live_counts, pair_blocks, start_basis):
    users = 128 * start_basis.shape[2]
    root = float(users) ** 0.5
    pair_blocks = hold(pair_blocks)
    gathered, pair_gathered = gather(start_basis[0], start_basis[0], False)
    parts = product(block_pairs, live_counts, pair_blocks, gathered, pair_gathered, jnp.float32, False)
    first, panel, own = finish_first(scatter(parts, jnp.float32)[0])
    gathered, pair_gathered = gather(panel, own, True)
    parts = product(block_pairs, live_counts, pair_blocks, gathered, pair_gathered, jnp.bfloat16, True)
    parts, (gram,) = scatter(parts, jnp.bfloat16)
    first_basis, inverse = factor_first(gram, parts[5], first, root)
    scaled, tiles = finish_second(parts, inverse)
    embedding = factor_second(total_gram(tiles), scaled, root)
    return (first_basis[None], embedding[None])


def solution(mesh):
    spec = P(BOTH, None, None)
    return jax.shard_map(
        on_device, mesh=mesh, in_specs=(spec, P(BOTH), spec, spec), out_specs=(spec, spec), check_vma=False
    )
```

time: 167 us -> 134 us (0.80)
  starting transfers between devices: 73.2 us -> 40.1 us
  waiting for transfers between devices: 69.6 us -> 48.1 us
  blocking collectives: 0 us -> 21 us
  local copies, waits for them, and re-layouts: 0.77 us -> 4.43 us
  Pallas kernels: 20.2 us -> 17.9 us
    ppermute x60 -> x36, starting transfers between devices: 73.2 us -> 40.1 us  [permute(): return lax.ppermute(value, BOTH, pairs)]
    ppermute x60 -> x36, waiting for transfers between devices: 69.6 us -> 48.1 us  [permute(): return lax.ppermute(value, BOTH, pairs)]
    all_to_all x0 -> x2, blocking collectives: none -> 21 us  [the longest x1 12.1 us: total_gram(): return lax.all_to_all(tiles, 'row', 0, 0, tiled=True)]
    unnamed x1 -> x7, local copies, waits for them, and re-layouts: 0.77 us -> 4.41 us
    pallas_call x8 -> x14, Pallas kernels: 19.5 us -> 17.1 us  [the longest x2 8.93 us: product(): pl.pallas_call(functools.partial(product_kernel, with_gram), out_shape=ou...]
  transfers between devices with their start and end apart: 60 -> 36, of which waited for: 32 -> 17; matrix products, arithmetic and copies ran while one was open for 0% -> 1% of each run, Pallas kernels for 2% -> 3%
where the time goes in v2:
time: 134 us; the launch traced here: 133 us
  waiting for transfers between devices  48.1 us (36%)
  starting transfers between devices  40.1 us (30%)
  blocking collectives  21 us (16%)
  Pallas kernels  17.9 us (13%)
  local copies, waits for them, and re-layouts  4.43 us (3%)
  between operations  1.5 us (1%)
    ppermute x36, waiting for transfers between devices, permute(): return lax.ppermute(value, BOTH, pairs)  48.1 us
    ppermute x36, starting transfers between devices, permute(): return lax.ppermute(value, BOTH, pairs)  40.1 us
    all_to_all x1, blocking collectives, total_gram(): return lax.all_to_all(tiles, 'row', 0, 0, tiled=True)  12.1 us
    pallas_call x2, Pallas kernels, product(): pl.pallas_call(functools.partial(product_kernel, with_gram), out_shape=ou...  8.93 us
    all_to_all x1, blocking collectives, total_gram(): tiles = lax.all_to_all(tiles, 'col', 0, 0, tiled=True)  8.88 us
    unnamed x7, local copies, waits for them, and re-layouts  4.41 us
    pallas_call x1, Pallas kernels, factor_second(): pl.pallas_call(functools.partial(factor_kernel, root), out_shape=struct((...  3.61 us
    pallas_call x1, Pallas kernels, factor_first(): pl.pallas_call(functools.partial(factor_first_kernel, root), out_shape=[s...  3.61 us
  transfers between devices with their start and end apart: 36, of which 17 were waited for; matrix products, arithmetic and copies ran while one was open for 1% of the time, Pallas kernels for 3%

profile of v2, /device:TPU:0, one launch (start us, length us, event | category | flops | bytes accessed | tf_op | source)
XLA Modules:
  0.0 133.1 jit_solution(265488101095453496)
XLA Ops:
  0.6 1.7 %collective-permute-start.3 = (bf16[32,1024]{1,0:T(8,128)(2,1)}, bf16[32,1024]{1,0:T(8,128)(2,1)S(1)}, u32[]{:S(2)}, u32[]{:S(2)}) collective-permute-start(bf16[32,1024]{1,0:T(8,128)(2,1)} %bitcast.3), channel_id=1, source_target_pairs={{0,2},{1,3},{2,0},{3,1},{4,6},{5,7},{6,4},{7,5},{8,10},{9,11},{10,... | collective-permute-start | bytes 196616 | tf_op jit(solution)/shard_map/ppermute | solution.py:23
  2.4 4.0 %collective-permute-start.2 = (bf16[32,1024]{1,0:T(8,128)(2,1)}, bf16[32,1024]{1,0:T(8,128)(2,1)S(1)}, u32[]{:S(2)}, u32[]{:S(2)}) collective-permute-start(bf16[32,1024]{1,0:T(8,128)(2,1)} %bitcast.4), channel_id=1, source_target_pairs={{0,96},{1,25},{2,98},{3,27},{4,100},{5,29},{6,102},{7,31},{8,104},... | collective-permute-start | bytes 196616 | tf_op jit(solution)/shard_map/ppermute | solution.py:23
  6.4 1.3 collective-permute-start
  7.7 1.0 collective-permute-done.2.refs_3_
  8.6 3.9 %collective-permute-done.1.refs_2_ = bf16[32,1024]{1,0:T(8,128)(2,1)S(1)} collective-permute-done((bf16[32,1024]{1,0:T(8,128)(2,1)}, bf16[32,1024]{1,0:T(8,128)(2,1)S(1)}, u32[]{:S(2)}, u32[]{:S(2)}) %collective-permute-start.1) | collective-permute-done | bytes 65568 | tf_op jit(solution)/shard_map/ppermute | solution.py:23
  12.5 0.3 collective-permute-done.refs_1_
  12.8 0.8 copy-done.1
  13.7 2.3 %collective-permute-start.7 = (bf16[2,32,1024]{2,1,0:T(8,128)(2,1)S(1)}, bf16[2,32,1024]{2,1,0:T(8,128)(2,1)S(1)}, u32[]{:S(2)}, u32[]{:S(2)}) collective-permute-start(bf16[2,32,1024]{2,1,0:T(8,128)(2,1)S(1)} %get-tuple-element.45), channel_id=1, source_target_pairs={{0,6},{1,7},{2,4},{3,5},{4,2},{5,3},{6,0},{7,1},{8,14},{9,15},{10,... | collective-permute-start | bytes 393224 | tf_op jit(solution)/shard_map/ppermute | solution.py:23
  15.9 2.8 %collective-permute-start.6 = (bf16[4,32,1024]{2,1,0:T(8,128)(2,1)S(1)}, bf16[4,32,1024]{2,1,0:T(8,128)(2,1)S(1)}, u32[]{:S(2)}, u32[]{:S(2)}) collective-permute-start(bf16[4,32,1024]{2,1,0:T(8,128)(2,1)S(1)} %get-tuple-element.44.g0), channel_id=1, source_target_pairs={{0,24},{1,97},{2,26},{3,99},{4,28},{5,101},{6,30},{7,103},{8,0},{9... | collective-permute-start | bytes 786440 | tf_op jit(solution)/shard_map/ppermute | solution.py:23
  18.7 0.8 collective-permute-start.5
  19.5 0.9 collective-permute-start.4
  21.2 0.8 copy.7.pairs
  21.9 2.8 %copy-done = bf16[3,1024,1024]{2,1,0:T(8,128)(2,1)S(1)} copy-done((bf16[3,1024,1024]{2,1,0:T(8,128)(2,1)S(1)}, bf16[3,1024,1024]{2,1,0:T(8,128)(2,1)}, u32[]{:S(2)}) %copy-start) | copy-done | bytes 6291480
  24.7 0.4 hold.1.blocks
  25.4 1.2 collective-permute-done.5.g2
  26.7 2.7 %collective-permute-done.4.g1 = bf16[4,32,1024]{2,1,0:T(8,128)(2,1)S(1)} collective-permute-done((bf16[4,32,1024]{2,1,0:T(8,128)(2,1)S(1)}, bf16[4,32,1024]{2,1,0:T(8,128)(2,1)S(1)}, u32[]{:S(2)}, u32[]{:S(2)}) %collective-permute-start.4) | collective-permute-done | bytes 262176 | tf_op jit(solution)/shard_map/ppermute | solution.py:23
  29.4 4.5 %product.2 = (f32[4,32,1024]{2,1,0:T(8,128)S(1)}, f32[4,32,1024]{2,1,0:T(8,128)S(1)}, f32[4,32,1024]{2,1,0:T(8,128)S(1)}, f32[4,32,1024]{2,1,0:T(8,128)S(1)}, f3...) custom-call(s32[1,3,2]{2,1,0:T(4,128)S(1)} %copy.7.pairs, s32[1]{0:T(128)S(6)} %copy.10.live, ...), custom_call_target="tpu_custom_call" | custom-call | flops 800000000 | bytes 10000000 | tf_op jit(solution)/shard_map/product/pallas_call | solution.py:147
  34.1 3.2 %collective-permute-start.10 = (f32[4,32,1024]{2,1,0:T(8,128)S(1)}, f32[4,32,1024]{2,1,0:T(8,128)S(1)}, u32[]{:S(2)}, u32[]{:S(2)}) collective-permute-start(f32[4,32,1024]{2,1,0:T(8,128)S(1)} %get-tuple-element.48), channel_id=1, source_target_pairs={{0,24},{1,97},{2,26},{3,99},{4,28},{5,101},{6,30},{7,103},{8,0},{9... | collective-permute-start | bytes 1572872 | tf_op jit(solution)/shard_map/ppermute | solution.py:23
  37.4 0.7 collective-permute-start.13
  38.1 12.0 %collective-permute-done.9.refs_0_ = f32[4,32,1024]{2,1,0:T(8,128)S(1)} collective-permute-done((f32[4,32,1024]{2,1,0:T(8,128)S(1)}, f32[4,32,1024]{2,1,0:T(8,128)S(1)}, u32[]{:S(2)}, u32[]{:S(2)}) %collective-permute-start.9) | collective-permute-done | bytes 524320 | tf_op jit(solution)/shard_map/ppermute | solution.py:23
  50.3 3.2 %collective-permute-start.15 = (f32[32,1024]{1,0:T(8,128)S(1)}, f32[32,1024]{1,0:T(8,128)S(1)}, u32[]{:S(2)}, u32[]{:S(2)}) collective-permute-start(f32[32,1024]{1,0:T(8,128)S(1)} %get-tuple-element.57), channel_id=1, source_target_pairs={{0,96},{1,25},{2,98},{3,27},{4,100},{5,29},{6,102},{7,31},{8,104},... | collective-permute-start | bytes 393224 | tf_op jit(solution)/shard_map/ppermute | solution.py:23
  53.5 0.4 collective-permute-start.16
  54.0 2.4 %collective-permute-done.14.refs_2_ = f32[32,1024]{1,0:T(8,128)S(1)} collective-permute-done((f32[32,1024]{1,0:T(8,128)S(1)}, f32[32,1024]{1,0:T(8,128)S(1)}, u32[]{:S(2)}, u32[]{:S(2)}) %collective-permute-start.14) | collective-permute-done | bytes 131104 | tf_op jit(solution)/shard_map/ppermute | solution.py:23
  56.5 1.0 collective-permute-done.15.refs_3_
  57.4 2.5 %collective-permute-done.16.refs_4_ = f32[32,1024]{1,0:T(8,128)S(1)} collective-permute-done((f32[32,1024]{1,0:T(8,128)S(1)}, f32[32,1024]{1,0:T(8,128)S(1)}, u32[]{:S(2)}, u32[]{:S(2)}) %collective-permute-start.16) | collective-permute-done | bytes 131104 | tf_op jit(solution)/shard_map/ppermute | solution.py:23
  60.2 1.1 collective-permute-start.20
  61.4 1.1 collective-permute-start.19
  62.5 1.3 collective-permute-start.18
  63.8 4.3 %collective-permute-done.21.refs_5_ = bf16[32,1024]{1,0:T(8,128)(2,1)S(1)} collective-permute-done((bf16[32,1024]{1,0:T(8,128)(2,1)S(1)}, bf16[32,1024]{1,0:T(8,128)(2,1)S(1)}, u32[]{:S(2)}, u32[]{:S(2)}) %collective-permute-start.21) | collective-permute-done | bytes 65568 | tf_op jit(solution)/shard_map/ppermute | solution.py:23
  68.2 3.3 %collective-permute-start.24 = (bf16[4,32,1152]{2,1,0:T(8,128)(2,1)S(1)}, bf16[4,32,1152]{2,1,0:T(8,128)(2,1)S(1)}, u32[]{:S(2)}, u32[]{:S(2)}) collective-permute-start(bf16[4,32,1152]{2,1,0:T(8,128)(2,1)S(1)} %get-tuple-element.62.g0), channel_id=1, source_target_pairs={{0,24},{1,97},{2,26},{3,99},{4,28},{5,101},{6,30},{7,103},{8,0},{9... | collective-permute-start | bytes 884744 | tf_op jit(solution)/shard_map/ppermute | solution.py:23
  71.5 0.9 collective-permute-start.22
  72.5 1.9 %collective-permute-done.25 = bf16[2,32,1024]{2,1,0:T(8,128)(2,1)S(1)} collective-permute-done((bf16[2,32,1024]{2,1,0:T(8,128)(2,1)S(1)}, bf16[2,32,1024]{2,1,0:T(8,128)(2,1)S(1)}, u32[]{:S(2)}, u32[]{:S(2)}) %collective-permute-start.25) | collective-permute-done | bytes 131104 | tf_op jit(solution)/shard_map/ppermute | solution.py:23
  74.5 4.4 %collective-permute-done.24.g3 = bf16[4,32,1152]{2,1,0:T(8,128)(2,1)S(1)} collective-permute-done((bf16[4,32,1152]{2,1,0:T(8,128)(2,1)S(1)}, bf16[4,32,1152]{2,1,0:T(8,128)(2,1)S(1)}, u32[]{:S(2)}, u32[]{:S(2)}) %collective-permute-start.24) | collective-permute-done | bytes 294944 | tf_op jit(solution)/shard_map/ppermute | solution.py:23
  78.9 0.9 collective-permute-done.23.g2
  79.9 2.8 %collective-permute-done.22.g1 = bf16[4,32,1152]{2,1,0:T(8,128)(2,1)S(1)} collective-permute-done((bf16[4,32,1152]{2,1,0:T(8,128)(2,1)S(1)}, bf16[4,32,1152]{2,1,0:T(8,128)(2,1)S(1)}, u32[]{:S(2)}, u32[]{:S(2)}) %collective-permute-start.22) | collective-permute-done | bytes 294944 | tf_op jit(solution)/shard_map/ppermute | solution.py:23
  82.6 4.4 %product.3 = (f32[4,32,1024]{2,1,0:T(8,128)S(1)}, bf16[4,32,1024]{2,1,0:T(8,128)(2,1)S(1)}, bf16[4,32,1024]{2,1,0:T(8,128)(2,1)S(1)}, bf16[4,32,1024]{2,1,0:T(8,...) custom-call(s32[1,3,2]{2,1,0:T(4,128)S(1)} %copy.7.pairs, ...), custom_call_target="tpu_custom_call" | custom-call | flops 800000000 | bytes 10000000 | tf_op jit(solution)/shard_map/product/pallas_call | solution.py:147
  87.4 3.2 %collective-permute-start.31 = (bf16[4,32,1024]{2,1,0:T(8,128)(2,1)S(1)}, bf16[4,32,1024]{2,1,0:T(8,128)(2,1)S(1)}, u32[]{:S(2)}, u32[]{:S(2)}) collective-permute-start(bf16[4,32,1024]{2,1,0:T(8,128)(2,1)S(1)} %get-tuple-element.76), channel_id=1, source_target_pairs={{0,24},{1,97},{2,26},{3,99},{4,28},{5,101},{6,30},{7,103},{8,0},{9... | collective-permute-start | bytes 786440 | tf_op jit(solution)/shard_map/ppermute | solution.py:23
  90.7 2.3 %collective-permute-start.28 = (bf16[2,32,1152]{2,1,0:T(8,128)(2,1)S(1)}, bf16[2,32,1152]{2,1,0:T(8,128)(2,1)S(1)}, u32[]{:S(2)}, u32[]{:S(2)}) collective-permute-start(bf16[2,32,1152]{2,1,0:T(8,128)(2,1)S(1)} %get-tuple-element.68), channel_id=1, source_target_pairs={{0,6},{1,7},{2,4},{3,5},{4,2},{5,3},{6,0},{7,1},{8,14},{9,15},{10,... | collective-permute-start | bytes 442376 | tf_op jit(solution)/shard_map/ppermute | solution.py:23
  93.0 5.5 %collective-permute-done.28.received = bf16[2,32,1152]{2,1,0:T(8,128)(2,1)S(1)} collective-permute-done((bf16[2,32,1152]{2,1,0:T(8,128)(2,1)S(1)}, bf16[2,32,1152]{2,1,0:T(8,128)(2,1)S(1)}, u32[]{:S(2)}, u32[]{:S(2)}) %collective-permute-start.28) | collective-permute-done | bytes 147488 | tf_op jit(solution)/shard_map/ppermute | solution.py:23
  98.9 0.9 collective-permute-start.33
  99.8 2.4 %collective-permute-start.34 = (bf16[32,1024]{1,0:T(8,128)(2,1)S(1)}, bf16[32,1024]{1,0:T(8,128)(2,1)S(1)}, u32[]{:S(2)}, u32[]{:S(2)}) collective-permute-start(bf16[32,1024]{1,0:T(8,128)(2,1)S(1)} %get-tuple-element.81), channel_id=1, source_target_pairs={{0,96},{1,25},{2,98},{3,27},{4,100},{5,29},{6,102},{7,31},{8,104},... | collective-permute-start | bytes 196616 | tf_op jit(solution)/shard_map/ppermute | solution.py:23
  102.2 1.2 collective-permute-start.35
  103.3 3.6 %factor_first.1 = (f32[32,1024]{1,0:T(8,128)}, f32[32,32]{1,0:T(8,128)S(1)}) custom-call(f32[8,128]{1,0:T(8,128)S(1)} %get-tuple-element.70.gram, bf16[1,32,1152]{2,1,0:T(8,128)(2,1)S(1)} %collective-permute-done.29.received.refs_5_, f32[32,1024]{1,0:T(8,128)S(1)} %get-tuple-element.72.panel), custom_call_target="tpu_custom_call" | custom-call | flops 1000000 | bytes 10000000 | tf_op jit(solution)/shard_map/factor_first/pallas_call | solution.py:356
  107.0 1.0 collective-permute-done.35.refs_4_
  107.9 0.6 finish_second.1
  108.5 8.9 %all_to_all.10.tiles = f32[8,8,128]{2,1,0:T(8,128)S(1)} all-to-all(f32[8,8,128]{2,1,0:T(8,128)S(1)} %get-tuple-element.84), channel_id=1, replica_groups=mesh['row'=16,'col'=8] {'col'}, dimensions={0} | all-to-all | bytes 65536 | tf_op jit(solution)/shard_map/all_to_all | solution.py:312
  117.4 12.1 %all_to_all.11.gram = f32[16,8,128]{2,1,0:T(8,128)S(1)} all-to-all(f32[16,8,128]{2,1,0:T(8,128)S(1)} %total_gram.1), channel_id=1, replica_groups=mesh['row'=16,'col'=8] {'row'}, dimensions={0} | all-to-all | bytes 131072 | tf_op jit(solution)/shard_map/all_to_all | solution.py:321
  129.5 3.6 %factor_second.1 = f32[32,1024]{1,0:T(8,128)} custom-call(f32[16,8,128]{2,1,0:T(8,128)S(1)} %all_to_all.11.gram, f32[32,1024]{1,0:T(8,128)S(1)} %get-tuple-element.85.panel), custom_call_target="tpu_custom_call" | custom-call | tf_op jit(solution)/shard_map/factor_second/pallas_call | solution.py:368
  (51 shorter events, 2.2 us)
Async XLA Ops:
  0.6 7.0 %collective-permute-start.3 = (bf16[32,1024]{1,0:T(8,128)(2,1)}, bf16[32,1024]{1,0:T(8,128)(2,1)S(1)}, u32[]{:S(2)}, u32[]{:S(2)}) collective-permute-start(bf16[32,1024]{1,0:T(8,128)(2,1)} %bitcast.3), channel_id=1, source_target_pairs={{0,2},{1,3},{2,0},{3,1},{4,6},{5,7},{6,4},{7,5},{8,10},{9,11},{10,... | collective-permute-start | bytes 196616 | tf_op jit(solution)/shard_map/ppermute | solution.py:23
  2.4 6.3 %collective-permute-start.2 = (bf16[32,1024]{1,0:T(8,128)(2,1)}, bf16[32,1024]{1,0:T(8,128)(2,1)S(1)}, u32[]{:S(2)}, u32[]{:S(2)}) collective-permute-start(bf16[32,1024]{1,0:T(8,128)(2,1)} %bitcast.4), channel_id=1, source_target_pairs={{0,96},{1,25},{2,98},{3,27},{4,100},{5,29},{6,102},{7,31},{8,104},... | collective-permute-start | bytes 196616 | tf_op jit(solution)/shard_map/ppermute | solution.py:23
  6.4 6.1 %collective-permute-start.1 = (bf16[32,1024]{1,0:T(8,128)(2,1)}, bf16[32,1024]{1,0:T(8,128)(2,1)S(1)}, u32[]{:S(2)}, u32[]{:S(2)}) collective-permute-start(bf16[32,1024]{1,0:T(8,128)(2,1)} %bitcast.5), channel_id=1, source_target_pairs={{0,64},{1,17},{2,66},{3,19},{4,68},{5,21},{6,70},{7,23},{8,72},{9,... | collective-permute-start | bytes 196616 | tf_op jit(solution)/shard_map/ppermute | solution.py:23
  6.4 6.4 %collective-permute-start = (bf16[32,1024]{1,0:T(8,128)(2,1)}, bf16[32,1024]{1,0:T(8,128)(2,1)S(1)}, u32[]{:S(2)}, u32[]{:S(2)}) collective-permute-start(bf16[32,1024]{1,0:T(8,128)(2,1)} %bitcast.6), channel_id=1, source_target_pairs={{0,32},{1,9},{2,34},{3,11},{4,36},{5,13},{6,38},{7,15},{8,40},{9,1... | collective-permute-start | bytes 196616 | tf_op jit(solution)/shard_map/ppermute | solution.py:23
  12.8 0.8 copy-start.1
  13.7 6.7 %collective-permute-start.7 = (bf16[2,32,1024]{2,1,0:T(8,128)(2,1)S(1)}, bf16[2,32,1024]{2,1,0:T(8,128)(2,1)S(1)}, u32[]{:S(2)}, u32[]{:S(2)}) collective-permute-start(bf16[2,32,1024]{2,1,0:T(8,128)(2,1)S(1)} %get-tuple-element.45), channel_id=1, source_target_pairs={{0,6},{1,7},{2,4},{3,5},{4,2},{5,3},{6,0},{7,1},{8,14},{9,15},{10,... | collective-permute-start | bytes 393224 | tf_op jit(solution)/shard_map/ppermute | solution.py:23
  15.9 9.5 %collective-permute-start.6 = (bf16[4,32,1024]{2,1,0:T(8,128)(2,1)S(1)}, bf16[4,32,1024]{2,1,0:T(8,128)(2,1)S(1)}, u32[]{:S(2)}, u32[]{:S(2)}) collective-permute-start(bf16[4,32,1024]{2,1,0:T(8,128)(2,1)S(1)} %get-tuple-element.44.g0), channel_id=1, source_target_pairs={{0,24},{1,97},{2,26},{3,99},{4,28},{5,101},{6,30},{7,103},{8,0},{9... | collective-permute-start | bytes 786440 | tf_op jit(solution)/shard_map/ppermute | solution.py:23
  18.7 8.0 %collective-permute-start.5 = (bf16[4,32,1024]{2,1,0:T(8,128)(2,1)S(1)}, bf16[4,32,1024]{2,1,0:T(8,128)(2,1)S(1)}, u32[]{:S(2)}, u32[]{:S(2)}) collective-permute-start(bf16[4,32,1024]{2,1,0:T(8,128)(2,1)S(1)} %get-tuple-element.44.g0), channel_id=1, source_target_pairs={{0,16},{1,65},{2,18},{3,67},{4,20},{5,69},{6,22},{7,71},{8,24},{9,... | collective-permute-start | bytes 786440 | tf_op jit(solution)/shard_map/ppermute | solution.py:23
  19.5 9.9 %collective-permute-start.4 = (bf16[4,32,1024]{2,1,0:T(8,128)(2,1)S(1)}, bf16[4,32,1024]{2,1,0:T(8,128)(2,1)S(1)}, u32[]{:S(2)}, u32[]{:S(2)}) collective-permute-start(bf16[4,32,1024]{2,1,0:T(8,128)(2,1)S(1)} %get-tuple-element.44.g0), channel_id=1, source_target_pairs={{0,8},{1,33},{2,10},{3,35},{4,12},{5,37},{6,14},{7,39},{8,16},{9,4... | collective-permute-start | bytes 786440 | tf_op jit(solution)/shard_map/ppermute | solution.py:23
  20.4 9.0 %collective-permute-start.8 = (bf16[4,32,1024]{2,1,0:T(8,128)(2,1)S(1)}, bf16[4,32,1024]{2,1,0:T(8,128)(2,1)S(1)}, u32[]{:S(2)}, u32[]{:S(2)}) collective-permute-start(bf16[4,32,1024]{2,1,0:T(8,128)(2,1)S(1)} %constant_dynamic-update-slice_fusion.h0), channel_id=1, source_target_pairs={{0,1},{1,0},{2,3},{3,2},{4,5},{5,4},{6,7},{7,6},{8,9},{9,8},{10,11... | collective-permute-start | bytes 786440 | tf_op jit(solution)/shard_map/ppermute | solution.py:23
  21.9 2.8 %copy-start = (bf16[3,1024,1024]{2,1,0:T(8,128)(2,1)S(1)}, bf16[3,1024,1024]{2,1,0:T(8,128)(2,1)}, u32[]{:S(2)}) copy-start(bf16[3,1024,1024]{2,1,0:T(8,128)(2,1)} %source.1) | copy-start | bytes 18874372
  33.9 3.4 %collective-permute-start.12 = (f32[4,32,1024]{2,1,0:T(8,128)S(1)}, f32[4,32,1024]{2,1,0:T(8,128)S(1)}, u32[]{:S(2)}, u32[]{:S(2)}) collective-permute-start(f32[4,32,1024]{2,1,0:T(8,128)S(1)} %get-tuple-element.52), channel_id=1, source_target_pairs={{0,1},{1,0},{2,3},{3,2},{4,5},{5,4},{6,7},{7,6},{8,9},{9,8},{10,11... | collective-permute-start | bytes 1572872 | tf_op jit(solution)/shard_map/ppermute | solution.py:23
  34.0 16.1 %collective-permute-start.9 = (f32[4,32,1024]{2,1,0:T(8,128)S(1)}, f32[4,32,1024]{2,1,0:T(8,128)S(1)}, u32[]{:S(2)}, u32[]{:S(2)}) collective-permute-start(f32[4,32,1024]{2,1,0:T(8,128)S(1)} %get-tuple-element.47), channel_id=1, source_target_pairs={{0,8},{1,33},{2,10},{3,35},{4,12},{5,37},{6,14},{7,39},{8,16},{9,4... | collective-permute-start | bytes 1572872 | tf_op jit(solution)/shard_map/ppermute | solution.py:23
  34.1 16.0 %collective-permute-start.10 = (f32[4,32,1024]{2,1,0:T(8,128)S(1)}, f32[4,32,1024]{2,1,0:T(8,128)S(1)}, u32[]{:S(2)}, u32[]{:S(2)}) collective-permute-start(f32[4,32,1024]{2,1,0:T(8,128)S(1)} %get-tuple-element.48), channel_id=1, source_target_pairs={{0,24},{1,97},{2,26},{3,99},{4,28},{5,101},{6,30},{7,103},{8,0},{9... | collective-permute-start | bytes 1572872 | tf_op jit(solution)/shard_map/ppermute | solution.py:23
  37.3 12.8 %collective-permute-start.11 = (f32[4,32,1024]{2,1,0:T(8,128)S(1)}, f32[4,32,1024]{2,1,0:T(8,128)S(1)}, u32[]{:S(2)}, u32[]{:S(2)}) collective-permute-start(f32[4,32,1024]{2,1,0:T(8,128)S(1)} %get-tuple-element.49), channel_id=1, source_target_pairs={{0,16},{1,65},{2,18},{3,67},{4,20},{5,69},{6,22},{7,71},{8,24},{9,... | collective-permute-start | bytes 1572872 | tf_op jit(solution)/shard_map/ppermute | solution.py:23
  37.4 16.5 %collective-permute-start.13 = (f32[2,32,1024]{2,1,0:T(8,128)S(1)}, f32[2,32,1024]{2,1,0:T(8,128)S(1)}, u32[]{:S(2)}, u32[]{:S(2)}) collective-permute-start(f32[2,32,1024]{2,1,0:T(8,128)S(1)} %get-tuple-element.54), channel_id=1, source_target_pairs={{0,6},{1,7},{2,4},{3,5},{4,2},{5,3},{6,0},{7,1},{8,14},{9,15},{10,... | collective-permute-start | bytes 786440 | tf_op jit(solution)/shard_map/ppermute | solution.py:23
  50.2 6.2 %collective-permute-start.14 = (f32[32,1024]{1,0:T(8,128)S(1)}, f32[32,1024]{1,0:T(8,128)S(1)}, u32[]{:S(2)}, u32[]{:S(2)}) collective-permute-start(f32[32,1024]{1,0:T(8,128)S(1)} %get-tuple-element.56), channel_id=1, source_target_pairs={{0,32},{1,9},{2,34},{3,11},{4,36},{5,13},{6,38},{7,15},{8,40},{9,1... | collective-permute-start | bytes 393224 | tf_op jit(solution)/shard_map/ppermute | solution.py:23
  50.3 7.1 %collective-permute-start.15 = (f32[32,1024]{1,0:T(8,128)S(1)}, f32[32,1024]{1,0:T(8,128)S(1)}, u32[]{:S(2)}, u32[]{:S(2)}) collective-permute-start(f32[32,1024]{1,0:T(8,128)S(1)} %get-tuple-element.57), channel_id=1, source_target_pairs={{0,96},{1,25},{2,98},{3,27},{4,100},{5,29},{6,102},{7,31},{8,104},... | collective-permute-start | bytes 393224 | tf_op jit(solution)/shard_map/ppermute | solution.py:23
  53.5 6.5 %collective-permute-start.16 = (f32[32,1024]{1,0:T(8,128)S(1)}, f32[32,1024]{1,0:T(8,128)S(1)}, u32[]{:S(2)}, u32[]{:S(2)}) collective-permute-start(f32[32,1024]{1,0:T(8,128)S(1)} %get-tuple-element.58), channel_id=1, source_target_pairs={{0,64},{1,17},{2,66},{3,19},{4,68},{5,21},{6,70},{7,23},{8,72},{9,... | collective-permute-start | bytes 393224 | tf_op jit(solution)/shard_map/ppermute | solution.py:23
  53.9 6.1 %collective-permute-start.17 = (f32[1,32,1024]{2,1,0:T(8,128)S(1)}, f32[1,32,1024]{2,1,0:T(8,128)S(1)}, u32[]{:S(2)}, u32[]{:S(2)}) collective-permute-start(f32[1,32,1024]{2,1,0:T(8,128)S(1)} %get-tuple-element.59), channel_id=1, source_target_pairs={{0,2},{1,3},{2,0},{3,1},{4,6},{5,7},{6,4},{7,5},{8,10},{9,11},{10,... | collective-permute-start | bytes 393224 | tf_op jit(solution)/shard_map/ppermute | solution.py:23
  60.2 7.8 %collective-permute-start.20 = (bf16[32,1152]{1,0:T(8,128)(2,1)S(1)}, bf16[32,1152]{1,0:T(8,128)(2,1)S(1)}, u32[]{:S(2)}, u32[]{:S(2)}) collective-permute-start(bf16[32,1152]{1,0:T(8,128)(2,1)S(1)} %get-tuple-element.60.refs_0_), channel_id=1, source_target_pairs={{0,96},{1,25},{2,98},{3,27},{4,100},{5,29},{6,102},{7,31},{8,104},... | collective-permute-start | bytes 221192 | tf_op jit(solution)/shard_map/ppermute | solution.py:23
  61.4 6.7 %collective-permute-start.19 = (bf16[32,1152]{1,0:T(8,128)(2,1)S(1)}, bf16[32,1152]{1,0:T(8,128)(2,1)S(1)}, u32[]{:S(2)}, u32[]{:S(2)}) collective-permute-start(bf16[32,1152]{1,0:T(8,128)(2,1)S(1)} %get-tuple-element.60.refs_0_), channel_id=1, source_target_pairs={{0,64},{1,17},{2,66},{3,19},{4,68},{5,21},{6,70},{7,23},{8,72},{9,... | collective-permute-start | bytes 221192 | tf_op jit(solution)/shard_map/ppermute | solution.py:23
  62.5 5.6 %collective-permute-start.18 = (bf16[32,1152]{1,0:T(8,128)(2,1)S(1)}, bf16[32,1152]{1,0:T(8,128)(2,1)S(1)}, u32[]{:S(2)}, u32[]{:S(2)}) collective-permute-start(bf16[32,1152]{1,0:T(8,128)(2,1)S(1)} %get-tuple-element.60.refs_0_), channel_id=1, source_target_pairs={{0,32},{1,9},{2,34},{3,11},{4,36},{5,13},{6,38},{7,15},{8,40},{9,1... | collective-permute-start | bytes 221192 | tf_op jit(solution)/shard_map/ppermute | solution.py:23
  63.8 4.3 %collective-permute-start.21 = (bf16[32,1024]{1,0:T(8,128)(2,1)S(1)}, bf16[32,1024]{1,0:T(8,128)(2,1)S(1)}, u32[]{:S(2)}, u32[]{:S(2)}) collective-permute-start(bf16[32,1024]{1,0:T(8,128)(2,1)S(1)} %get-tuple-element.61.refs_4_), channel_id=1, source_target_pairs={{0,2},{1,3},{2,0},{3,1},{4,6},{5,7},{6,4},{7,5},{8,10},{9,11},{10,... | collective-permute-start | bytes 196616 | tf_op jit(solution)/shard_map/ppermute | solution.py:23
  68.1 6.3 %collective-permute-start.25 = (bf16[2,32,1024]{2,1,0:T(8,128)(2,1)S(1)}, bf16[2,32,1024]{2,1,0:T(8,128)(2,1)S(1)}, u32[]{:S(2)}, u32[]{:S(2)}) collective-permute-start(bf16[2,32,1024]{2,1,0:T(8,128)(2,1)S(1)} %get-tuple-element.63), channel_id=1, source_target_pairs={{0,6},{1,7},{2,4},{3,5},{4,2},{5,3},{6,0},{7,1},{8,14},{9,15},{10,... | collective-permute-start | bytes 393224 | tf_op jit(solution)/shard_map/ppermute | solution.py:23
  68.2 10.7 %collective-permute-start.24 = (bf16[4,32,1152]{2,1,0:T(8,128)(2,1)S(1)}, bf16[4,32,1152]{2,1,0:T(8,128)(2,1)S(1)}, u32[]{:S(2)}, u32[]{:S(2)}) collective-permute-start(bf16[4,32,1152]{2,1,0:T(8,128)(2,1)S(1)} %get-tuple-element.62.g0), channel_id=1, source_target_pairs={{0,24},{1,97},{2,26},{3,99},{4,28},{5,101},{6,30},{7,103},{8,0},{9... | collective-permute-start | bytes 884744 | tf_op jit(solution)/shard_map/ppermute | solution.py:23
  71.5 8.3 %collective-permute-start.23 = (bf16[4,32,1152]{2,1,0:T(8,128)(2,1)S(1)}, bf16[4,32,1152]{2,1,0:T(8,128)(2,1)S(1)}, u32[]{:S(2)}, u32[]{:S(2)}) collective-permute-start(bf16[4,32,1152]{2,1,0:T(8,128)(2,1)S(1)} %get-tuple-element.62.g0), channel_id=1, source_target_pairs={{0,16},{1,65},{2,18},{3,67},{4,20},{5,69},{6,22},{7,71},{8,24},{9,... | collective-permute-start | bytes 884744 | tf_op jit(solution)/shard_map/ppermute | solution.py:23
  71.5 11.1 %collective-permute-start.22 = (bf16[4,32,1152]{2,1,0:T(8,128)(2,1)S(1)}, bf16[4,32,1152]{2,1,0:T(8,128)(2,1)S(1)}, u32[]{:S(2)}, u32[]{:S(2)}) collective-permute-start(bf16[4,32,1152]{2,1,0:T(8,128)(2,1)S(1)} %get-tuple-element.62.g0), channel_id=1, source_target_pairs={{0,8},{1,33},{2,10},{3,35},{4,12},{5,37},{6,14},{7,39},{8,16},{9,4... | collective-permute-start | bytes 884744 | tf_op jit(solution)/shard_map/ppermute | solution.py:23
  74.4 8.2 %collective-permute-start.26 = (bf16[4,32,1024]{2,1,0:T(8,128)(2,1)S(1)}, bf16[4,32,1024]{2,1,0:T(8,128)(2,1)S(1)}, u32[]{:S(2)}, u32[]{:S(2)}) collective-permute-start(bf16[4,32,1024]{2,1,0:T(8,128)(2,1)S(1)} %constant_dynamic-update-slice_fusion.2.h0), channel_id=1, source_target_pairs={{0,1},{1,0},{2,3},{3,2},{4,5},{5,4},{6,7},{7,6},{8,9},{9,8},{10,11... | collective-permute-start | bytes 786440 | tf_op jit(solution)/shard_map/ppermute | solution.py:23
  87.1 3.6 %collective-permute-start.27 = (bf16[4,32,1152]{2,1,0:T(8,128)(2,1)S(1)}, bf16[4,32,1152]{2,1,0:T(8,128)(2,1)S(1)}, u32[]{:S(2)}, u32[]{:S(2)}) collective-permute-start(bf16[4,32,1152]{2,1,0:T(8,128)(2,1)S(1)} %get-tuple-element.65), channel_id=1, source_target_pairs={{0,1},{1,0},{2,3},{3,2},{4,5},{5,4},{6,7},{7,6},{8,9},{9,8},{10,11... | collective-permute-start | bytes 884744 | tf_op jit(solution)/shard_map/ppermute | solution.py:23
  87.2 11.5 %collective-permute-start.30 = (bf16[4,32,1024]{2,1,0:T(8,128)(2,1)S(1)}, bf16[4,32,1024]{2,1,0:T(8,128)(2,1)S(1)}, u32[]{:S(2)}, u32[]{:S(2)}) collective-permute-start(bf16[4,32,1024]{2,1,0:T(8,128)(2,1)S(1)} %get-tuple-element.75), channel_id=1, source_target_pairs={{0,8},{1,33},{2,10},{3,35},{4,12},{5,37},{6,14},{7,39},{8,16},{9,4... | collective-permute-start | bytes 786440 | tf_op jit(solution)/shard_map/ppermute | solution.py:23
  87.4 11.3 %collective-permute-start.31 = (bf16[4,32,1024]{2,1,0:T(8,128)(2,1)S(1)}, bf16[4,32,1024]{2,1,0:T(8,128)(2,1)S(1)}, u32[]{:S(2)}, u32[]{:S(2)}) collective-permute-start(bf16[4,32,1024]{2,1,0:T(8,128)(2,1)S(1)} %get-tuple-element.76), channel_id=1, source_target_pairs={{0,24},{1,97},{2,26},{3,99},{4,28},{5,101},{6,30},{7,103},{8,0},{9... | collective-permute-start | bytes 786440 | tf_op jit(solution)/shard_map/ppermute | solution.py:23
  90.6 8.1 %collective-permute-start.32 = (bf16[4,32,1024]{2,1,0:T(8,128)(2,1)S(1)}, bf16[4,32,1024]{2,1,0:T(8,128)(2,1)S(1)}, u32[]{:S(2)}, u32[]{:S(2)}) collective-permute-start(bf16[4,32,1024]{2,1,0:T(8,128)(2,1)S(1)} %get-tuple-element.77), channel_id=1, source_target_pairs={{0,16},{1,65},{2,18},{3,67},{4,20},{5,69},{6,22},{7,71},{8,24},{9,... | collective-permute-start | bytes 786440 | tf_op jit(solution)/shard_map/ppermute | solution.py:23
  90.7 7.8 %collective-permute-start.28 = (bf16[2,32,1152]{2,1,0:T(8,128)(2,1)S(1)}, bf16[2,32,1152]{2,1,0:T(8,128)(2,1)S(1)}, u32[]{:S(2)}, u32[]{:S(2)}) collective-permute-start(bf16[2,32,1152]{2,1,0:T(8,128)(2,1)S(1)} %get-tuple-element.68), channel_id=1, source_target_pairs={{0,6},{1,7},{2,4},{3,5},{4,2},{5,3},{6,0},{7,1},{8,14},{9,15},{10,... | collective-permute-start | bytes 442376 | tf_op jit(solution)/shard_map/ppermute | solution.py:23
  98.6 4.8 %collective-permute-start.29 = (bf16[1,32,1152]{2,1,0:T(8,128)(2,1)S(1)}, bf16[1,32,1152]{2,1,0:T(8,128)(2,1)S(1)}, u32[]{:S(2)}, u32[]{:S(2)}) collective-permute-start(bf16[1,32,1152]{2,1,0:T(8,128)(2,1)S(1)} %get-tuple-element.71), channel_id=1, source_target_pairs={{0,2},{1,3},{2,0},{3,1},{4,6},{5,7},{6,4},{7,5},{8,10},{9,11},{10,... | collective-permute-start | bytes 221192 | tf_op jit(solution)/shard_map/ppermute | solution.py:23
  98.9 8.1 %collective-permute-start.33 = (bf16[32,1024]{1,0:T(8,128)(2,1)S(1)}, bf16[32,1024]{1,0:T(8,128)(2,1)S(1)}, u32[]{:S(2)}, u32[]{:S(2)}) collective-permute-start(bf16[32,1024]{1,0:T(8,128)(2,1)S(1)} %get-tuple-element.80), channel_id=1, source_target_pairs={{0,32},{1,9},{2,34},{3,11},{4,36},{5,13},{6,38},{7,15},{8,40},{9,1... | collective-permute-start | bytes 196616 | tf_op jit(solution)/shard_map/ppermute | solution.py:23
  99.8 7.2 %collective-permute-start.34 = (bf16[32,1024]{1,0:T(8,128)(2,1)S(1)}, bf16[32,1024]{1,0:T(8,128)(2,1)S(1)}, u32[]{:S(2)}, u32[]{:S(2)}) collective-permute-start(bf16[32,1024]{1,0:T(8,128)(2,1)S(1)} %get-tuple-element.81), channel_id=1, source_target_pairs={{0,96},{1,25},{2,98},{3,27},{4,100},{5,29},{6,102},{7,31},{8,104},... | collective-permute-start | bytes 196616 | tf_op jit(solution)/shard_map/ppermute | solution.py:23
  102.2 5.8 %collective-permute-start.35 = (bf16[32,1024]{1,0:T(8,128)(2,1)S(1)}, bf16[32,1024]{1,0:T(8,128)(2,1)S(1)}, u32[]{:S(2)}, u32[]{:S(2)}) collective-permute-start(bf16[32,1024]{1,0:T(8,128)(2,1)S(1)} %get-tuple-element.82), channel_id=1, source_target_pairs={{0,64},{1,17},{2,66},{3,19},{4,68},{5,21},{6,70},{7,23},{8,72},{9,... | collective-permute-start | bytes 196616 | tf_op jit(solution)/shard_map/ppermute | solution.py:23

commit v3 on v2

--- a/solution.py
+++ b/solution.py
@@ -5,9 +5,10 @@
 from jax import lax
 from jax.experimental import pallas as pl
 from jax.experimental.pallas import tpu as pltpu
+from jax.sharding import Mesh
 from jax.sharding import PartitionSpec as P
 
-BOTH = ("row", "col")
+AXES = ("z", "x", "y", "core")
 HIGHEST = lax.Precision.HIGHEST
 VMEM = pl.BlockSpec(memory_space=pltpu.VMEM)
 SMEM = pl.BlockSpec(memory_space=pltpu.SMEM)
@@ -20,7 +21,7 @@
         z, x, y, c = device // 32, device // 8 % 4, device // 2 % 4, device % 2
         tz, tx, ty, tc = target(z, x, y, c)
         pairs.append((device, ((tz % 4) * 4 + tx % 4) * 8 + (ty % 4) * 2 + tc % 2))
-    return lax.ppermute(value, BOTH, pairs)
+    return lax.ppermute(value, AXES, pairs)
 
 
 def send_inner(value, s):
@@ -58,6 +59,24 @@
         terms.append(term)
         tile = tile - term
     return jnp.concatenate(terms + [jnp.zeros_like(tile)], axis=0).astype(jnp.bfloat16)
+
+
+def encode(value):
+    top = jnp.max(jnp.abs(value), axis=1, keepdims=True)
+    power = jnp.floor(jnp.log2(jnp.maximum(top, 1e-30))) - 13.0
+    return jnp.concatenate([value * jnp.exp2(-power), jnp.broadcast_to(power, (32, 128))], axis=1)
+
+
+def decode(value):
+    if value.dtype == jnp.bfloat16:
+        return value[:, 0:1024].astype(jnp.float32)
+    return value[:, 0:1024] * jnp.exp2(value[:, 1024:1025])
+
+
+def carry(send, value, *args):
+    if value.dtype == jnp.bfloat16:
+        return send(value, *args)
+    return send(value.astype(jnp.float16), *args).astype(jnp.float32)
 
 
 def merge(terms):
@@ -128,21 +147,28 @@
         for t in range(4):
             @pl.when(outer == t)
             def _():
-                outs[t][inner] = results[3, 1].astype(outs[t].dtype)
+                if t and not with_gram:
+                    outs[t][inner] = encode(results[3, 1])
+                else:
+                    outs[t][inner] = results[3, 1].astype(outs[t].dtype)
         for t in range(2):
             @pl.when(dc == t)
             def _():
-                outs[4 + t][dy, :, 0:1024] = results[3, 0].astype(outs[4 + t].dtype)
+                if t and not with_gram:
+                    outs[5][dy] = encode(results[3, 0])
+                else:
+                    outs[4 + t][dy, :, 0:1024] = results[3, 0].astype(outs[4 + t].dtype)
         return carry
 
     lax.fori_loop(0, count, advance, 0)
 
 
-def product(pairs, live, blocks, gathered, pair_gathered, sent, with_gram):
+def product(pairs, live, blocks, gathered, pair_gathered, with_gram):
     shape = (4, 32, 1024)
     f32 = jnp.float32
-    outs = [struct(shape, f32)] + [struct(shape, sent)] * 3 + [struct(shape, f32)]
-    outs += [struct((4, 32, 1152) if with_gram else shape, sent)]
+    sent = jnp.bfloat16 if with_gram else f32
+    outs = [struct(shape, f32)] + [struct(shape if with_gram else (4, 32, 1152), sent)] * 3
+    outs += [struct(shape, f32), struct((4, 32, 1152), sent)]
     outs += [struct((8, 128), f32)] * with_gram
     return pl.pallas_call(
         functools.partial(product_kernel, with_gram),
@@ -190,9 +216,11 @@
     keep, send = outs[:2]
     half = keep.shape[0]
     for k in range(2 * half):
-        value = own[k] + received[k, :, 0:1024].astype(jnp.float32)
+        value = own[k] + decode(received[k])
         if k < half:
             keep[k] = value
+        elif not with_gram:
+            send[k - half] = encode(value)
         else:
             send[k - half, :, 0:1024] = value.astype(send.dtype)
     if with_gram:
@@ -222,14 +250,17 @@
     for k in range(4):
         value = own[k]
         for array in received:
-            value = value + array[k].astype(jnp.float32)
+            value = value + decode(array[k])
+        if outs[k].shape[1] > 1024:
+            value = encode(value)
         outs[k][...] = value.astype(outs[k].dtype)
 
 
-def add_outer(own, received, sent):
+def add_outer(own, received):
+    sent = struct(received[0].shape[1:], received[0].dtype)
     return pl.pallas_call(
         row_kernel,
-        out_shape=[struct((32, 1024), jnp.float32)] + [struct((32, 1024), sent)] * 3,
+        out_shape=[struct((32, 1024), jnp.float32)] + [sent] * 3,
         in_specs=[VMEM] * 4,
         out_specs=[VMEM] * 4,
         compiler_params=PARAMS,
@@ -240,8 +271,8 @@
 def add_parts(parts):
     value = parts[0][...] + parts[1][0]
     for part in parts[2:5]:
-        value = value + part[...].astype(jnp.float32)
-    return value + parts[5][0, :, 0:1024].astype(jnp.float32)
+        value = value + decode(part[...])
+    return value + decode(parts[5][0])
 
 
 def first_kernel(*refs):
@@ -285,14 +316,13 @@
             value, value, (((1,), (1,)), ((), ())), precision=HIGHEST, preferred_element_type=jnp.float32
         )
     )
-    for k in range(8):
-        gram[k] = tile
+    gram[...] = tile
 
 
 def finish_second(parts, inverse):
     return pl.pallas_call(
         second_kernel,
-        out_shape=[struct((32, 1024), jnp.float32), struct((8, 8, 128), jnp.float32)],
+        out_shape=[struct((32, 1024), jnp.float32), struct((8, 128), jnp.float32)],
         in_specs=[VMEM] * 7,
         out_specs=[VMEM] * 2,
         compiler_params=PARAMS,
@@ -300,25 +330,22 @@
     )(*parts, inverse)
 
 
-def total_kernel(tiles, out):
-    total = tiles[0]
-    for k in range(1, 8):
-        total = total + tiles[k]
-    for k in range(16):
+def total_kernel(own, other, out):
+    total = own[...] + other[...]
+    for k in range(64):
         out[k] = total
 
 
-def total_gram(tiles):
-    tiles = lax.all_to_all(tiles, "col", 0, 0, tiled=True)
+def total_gram(tile):
     tiles = pl.pallas_call(
         total_kernel,
-        out_shape=struct((16, 8, 128), jnp.float32),
-        in_specs=[VMEM],
+        out_shape=struct((64, 8, 128), jnp.float32),
+        in_specs=[VMEM] * 2,
         out_specs=VMEM,
         compiler_params=PARAMS,
         name="total_gram",
-    )(tiles)
-    return lax.all_to_all(tiles, "row", 0, 0, tiled=True)
+    )(tile, send_core(tile))
+    return lax.all_to_all(tiles, ("z", "x", "y"), 0, 0, tiled=True)
 
 
 def lower_inverse(gram):
@@ -326,10 +353,38 @@
     lanes = lax.broadcasted_iota(jnp.int32, (32, 128), 1)
     wide = jnp.concatenate([gram, jnp.zeros((32, 96), jnp.float32)], axis=1)
     wide = jnp.where(lanes == rows + 32, 1.0, wide)
-    for k in range(31):
-        pivot = wide[k : k + 1, k : k + 1]
-        factor = jnp.where(rows > k, wide[:, k : k + 1], 0.0)
-        wide = wide - factor * (wide[k : k + 1, :] / pivot)
+    parts = [wide[8 * k : 8 * k + 8] for k in range(4)]
+    inside = rows[0:8]
+    for step in range(4):
+        columns = [
+            [jnp.broadcast_to(part[:, k : k + 1], (8, 128)) for k in range(8 * step, 8 * step + 8)]
+            for part in parts
+        ]
+        pivot = parts[step]
+        schur = {(i, j): columns[step][j][i : i + 1] for i in range(8) for j in range(i + 1)}
+        lines = [pivot[i : i + 1] for i in range(8)]
+        factors, inverses = {}, []
+        for j in range(8):
+            inverses.append(1.0 / schur[j, j])
+            for i in range(j + 1, 8):
+                factors[i, j] = schur[i, j] * inverses[j]
+            for i in range(j + 1, 8):
+                for t in range(j + 1, i + 1):
+                    schur[i, t] = schur[i, t] - factors[i, j] * schur[t, j]
+                lines[i] = lines[i] - factors[i, j] * lines[j]
+        for i in range(1, 8):
+            pivot = jnp.where(inside == i, lines[i], pivot)
+        parts[step] = pivot
+        solved = [None] * 8
+        for j in reversed(range(8)):
+            value = lines[j] * inverses[j]
+            for i in range(j + 1, 8):
+                value = value - factors[i, j] * solved[i]
+            solved[j] = value
+        for later in range(step + 1, 4):
+            for j in range(8):
+                parts[later] = parts[later] - columns[later][j] * solved[j]
+    wide = jnp.concatenate(parts, axis=0)
     diagonal = jnp.sum(jnp.where(lanes == rows, wide, 0.0), axis=1, keepdims=True)
     wide = wide / jnp.sqrt(diagonal)
     return wide[:, 32:64]
@@ -337,7 +392,7 @@
 
 def factor_kernel(root, gram, panel, *outs):
     tile = gram[0]
-    for k in range(1, 16):
+    for k in range(1, 64):
         tile = tile + gram[k]
     inverse = lower_inverse(unfold(tile))
     outs[0][...] = (
@@ -390,13 +445,13 @@
     return outer, [along_y, send_core(along_y)]
 
 
-def scatter(parts, sent):
-    got = [send_outer(parts[s], s) for s in SHIFTS]
-    column, send, *gram = halve(parts[4], send_core(parts[5]), parts[6:])
-    column, send, *gram = halve(column, send_y(send, 3), gram)
-    along_y = send_y(send, 1)
-    row = add_outer(parts[0], got, sent)
-    return [row[0], column] + [send_inner(row[s], s) for s in SHIFTS] + [along_y], gram
+def scatter(parts):
+    got = [carry(send_outer, parts[s], s) for s in SHIFTS]
+    column, send, *gram = halve(parts[4], carry(send_core, parts[5]), parts[6:])
+    column, send, *gram = halve(column, carry(send_y, send, 3), gram)
+    along_y = carry(send_y, send, 1)
+    row = add_outer(parts[0], got)
+    return [row[0], column] + [carry(send_inner, row[s], s) for s in SHIFTS] + [along_y], gram
 
 
 def hold_kernel(source, target, sem):
@@ -423,11 +478,11 @@
     root = float(users) ** 0.5
     pair_blocks = hold(pair_blocks)
     gathered, pair_gathered = gather(start_basis[0], start_basis[0], False)
-    parts = product(block_pairs, live_counts, pair_blocks, gathered, pair_gathered, jnp.float32, False)
-    first, panel, own = finish_first(scatter(parts, jnp.float32)[0])
+    parts = product(block_pairs, live_counts, pair_blocks, gathered, pair_gathered, False)
+    first, panel, own = finish_first(scatter(parts)[0])
     gathered, pair_gathered = gather(panel, own, True)
-    parts = product(block_pairs, live_counts, pair_blocks, gathered, pair_gathered, jnp.bfloat16, True)
-    parts, (gram,) = scatter(parts, jnp.bfloat16)
+    parts = product(block_pairs, live_counts, pair_blocks, gathered, pair_gathered, True)
+    parts, (gram,) = scatter(parts)
     first_basis, inverse = factor_first(gram, parts[5], first, root)
     scaled, tiles = finish_second(parts, inverse)
     embedding = factor_second(total_gram(tiles), scaled, root)
@@ -435,7 +490,8 @@
 
 
 def solution(mesh):
-    spec = P(BOTH, None, None)
+    mesh = Mesh(mesh.devices.reshape(4, 4, 4, 2), AXES)
+    spec = P(AXES, None, None)
     return jax.shard_map(
-        on_device, mesh=mesh, in_specs=(spec, P(BOTH), spec, spec), out_specs=(spec, spec), check_vma=False
+        on_device, mesh=mesh, in_specs=(spec, P(AXES), spec, spec), out_specs=(spec, spec), check_vma=False
     )

time: 134 us -> 123 us (0.918)
  blocking collectives: 21 us -> 17 us
  starting transfers between devices: 40.1 us -> 36.1 us
  Pallas kernels: 17.9 us -> 15.7 us
    ppermute x36 -> x37, starting transfers between devices: 40.1 us -> 36.1 us  [permute(): return lax.ppermute(value, AXES, pairs)]
    all_to_all x2 -> x1, blocking collectives: 21 us -> 17 us  [total_gram(): return lax.all_to_all(tiles, ('z', 'x', 'y'), 0, 0, tiled=True)]
    pallas_call x1, Pallas kernels: 3.61 us -> 1.91 us  [factor_first(): pl.pallas_call(functools.partial(factor_first_kernel, root), out_shape=[s...]
    pallas_call x1, Pallas kernels: 3.61 us -> 1.97 us  [factor_second(): pl.pallas_call(functools.partial(factor_kernel, root), out_shape=struct((...]
    ppermute x36 -> x37, waiting for transfers between devices: 48.1 us -> 46.9 us  [permute(): return lax.ppermute(value, AXES, pairs)]
  transfers between devices with their start and end apart: 36 -> 37, of which waited for: 17 -> 23; matrix products, arithmetic and copies ran while one was open for 1% -> 1% of each run, Pallas kernels for 3% -> 3%
where the time goes in v3:
time: 123 us; the launch traced here: 122 us
  waiting for transfers between devices  46.9 us (38%)
  starting transfers between devices  36.1 us (29%)
  blocking collectives  17 us (14%)
  Pallas kernels  15.7 us (13%)
  local copies, waits for them, and re-layouts  4.43 us (4%)
  between operations  1.62 us (1%)
    ppermute x37, waiting for transfers between devices, permute(): return lax.ppermute(value, AXES, pairs)  46.9 us
    ppermute x37, starting transfers between devices, permute(): return lax.ppermute(value, AXES, pairs)  36.1 us
    all_to_all x1, blocking collectives, total_gram(): return lax.all_to_all(tiles, ('z', 'x', 'y'), 0, 0, tiled=True)  17 us
    pallas_call x2, Pallas kernels, product(): pl.pallas_call(functools.partial(product_kernel, with_gram), out_shape=ou...  9.48 us
    unnamed x7, local copies, waits for them, and re-layouts  4.41 us
  transfers between devices with their start and end apart: 37, of which 23 were waited for; matrix products, arithmetic and copies ran while one was open for 1% of the time, Pallas kernels for 3%

profile of v3, /device:TPU:0, one launch (start us, length us, event | category | flops | bytes accessed | tf_op | source)
XLA Modules:
  0.0 122.1 jit_solution(7146528574348128324)
XLA Ops:
  0.6 1.7 %collective-permute-start.3 = (bf16[32,1024]{1,0:T(8,128)(2,1)}, bf16[32,1024]{1,0:T(8,128)(2,1)S(1)}, u32[]{:S(2)}, u32[]{:S(2)}) collective-permute-start(bf16[32,1024]{1,0:T(8,128)(2,1)} %bitcast.3), channel_id=1, source_target_pairs={{0,2},{1,3},{2,0},{3,1},{4,6},{5,7},{6,4},{7,5},{8,10},{9,11},{10,... | collective-permute-start | bytes 196616 | tf_op jit(solution)/shard_map/ppermute | solution.py:24
  2.4 4.0 %collective-permute-start.2 = (bf16[32,1024]{1,0:T(8,128)(2,1)}, bf16[32,1024]{1,0:T(8,128)(2,1)S(1)}, u32[]{:S(2)}, u32[]{:S(2)}) collective-permute-start(bf16[32,1024]{1,0:T(8,128)(2,1)} %bitcast.4), channel_id=1, source_target_pairs={{0,96},{1,25},{2,98},{3,27},{4,100},{5,29},{6,102},{7,31},{8,104},... | collective-permute-start | bytes 196616 | tf_op jit(solution)/shard_map/ppermute | solution.py:24
  6.4 1.3 %collective-permute-start = (bf16[32,1024]{1,0:T(8,128)(2,1)}, bf16[32,1024]{1,0:T(8,128)(2,1)S(1)}, u32[]{:S(2)}, u32[]{:S(2)}) collective-permute-start(bf16[32,1024]{1,0:T(8,128)(2,1)} %bitcast.6), channel_id=1, source_target_pairs={{0,32},{1,9},{2,34},{3,11},{4,36},{5,13},{6,38},{7,15},{8,40},{9,1... | collective-permute-start | bytes 196616 | tf_op jit(solution)/shard_map/ppermute | solution.py:24
  7.7 1.0 collective-permute-done.2.refs_3_
  8.6 3.9 %collective-permute-done.1.refs_2_ = bf16[32,1024]{1,0:T(8,128)(2,1)S(1)} collective-permute-done((bf16[32,1024]{1,0:T(8,128)(2,1)}, bf16[32,1024]{1,0:T(8,128)(2,1)S(1)}, u32[]{:S(2)}, u32[]{:S(2)}) %collective-permute-start.1) | collective-permute-done | bytes 65568 | tf_op jit(solution)/shard_map/ppermute | solution.py:24
  12.8 0.8 copy-done.1
  13.7 2.3 %collective-permute-start.7 = (bf16[2,32,1024]{2,1,0:T(8,128)(2,1)S(1)}, bf16[2,32,1024]{2,1,0:T(8,128)(2,1)S(1)}, u32[]{:S(2)}, u32[]{:S(2)}) collective-permute-start(bf16[2,32,1024]{2,1,0:T(8,128)(2,1)S(1)} %get-tuple-element.45), channel_id=1, source_target_pairs={{0,6},{1,7},{2,4},{3,5},{4,2},{5,3},{6,0},{7,1},{8,14},{9,15},{10,... | collective-permute-start | bytes 393224 | tf_op jit(solution)/shard_map/ppermute | solution.py:24
  15.9 2.8 %collective-permute-start.6 = (bf16[4,32,1024]{2,1,0:T(8,128)(2,1)S(1)}, bf16[4,32,1024]{2,1,0:T(8,128)(2,1)S(1)}, u32[]{:S(2)}, u32[]{:S(2)}) collective-permute-start(bf16[4,32,1024]{2,1,0:T(8,128)(2,1)S(1)} %get-tuple-element.44.g0), channel_id=1, source_target_pairs={{0,24},{1,97},{2,26},{3,99},{4,28},{5,101},{6,30},{7,103},{8,0},{9... | collective-permute-start | bytes 786440 | tf_op jit(solution)/shard_map/ppermute | solution.py:24
  18.7 0.8 collective-permute-start.5
  19.5 0.9 collective-permute-start.4
  21.2 0.8 copy.7.pairs
  21.9 2.8 %copy-done = bf16[3,1024,1024]{2,1,0:T(8,128)(2,1)S(1)} copy-done((bf16[3,1024,1024]{2,1,0:T(8,128)(2,1)S(1)}, bf16[3,1024,1024]{2,1,0:T(8,128)(2,1)}, u32[]{:S(2)}) %copy-start) | copy-done | bytes 6291480
  25.4 1.2 %collective-permute-done.5.g2 = bf16[4,32,1024]{2,1,0:T(8,128)(2,1)S(1)} collective-permute-done((bf16[4,32,1024]{2,1,0:T(8,128)(2,1)S(1)}, bf16[4,32,1024]{2,1,0:T(8,128)(2,1)S(1)}, u32[]{:S(2)}, u32[]{:S(2)}) %collective-permute-start.5) | collective-permute-done | bytes 262176 | tf_op jit(solution)/shard_map/ppermute | solution.py:24
  26.7 2.7 %collective-permute-done.4.g1 = bf16[4,32,1024]{2,1,0:T(8,128)(2,1)S(1)} collective-permute-done((bf16[4,32,1024]{2,1,0:T(8,128)(2,1)S(1)}, bf16[4,32,1024]{2,1,0:T(8,128)(2,1)S(1)}, u32[]{:S(2)}, u32[]{:S(2)}) %collective-permute-start.4) | collective-permute-done | bytes 262176 | tf_op jit(solution)/shard_map/ppermute | solution.py:24
  29.4 4.9 %product.2 = (f32[4,32,1024]{2,1,0:T(8,128)S(1)}, f32[4,32,1152]{2,1,0:T(8,128)S(1)}, f32[4,32,1152]{2,1,0:T(8,128)S(1)}, f32[4,32,1152]{2,1,0:T(8,128)S(1)}, f3...) custom-call(s32[1,3,2]{2,1,0:T(4,128)S(1)} %copy.7.pairs, s32[1]{0:T(128)S(6)} %copy.10.live, ...), custom_call_target="tpu_custom_call" | custom-call | flops 800000000 | bytes 10000000 | tf_op jit(solution)/shard_map/product/pallas_call | solution.py:173
  34.6 0.6 collective-permute-start.10
  35.2 1.6 %collective-permute-start.9 = (f16[4,32,1152]{2,1,0:T(8,128)(2,1)S(1)}, f16[4,32,1152]{2,1,0:T(8,128)(2,1)S(1)}, u32[]{:S(2)}, u32[]{:S(2)}) collective-permute-start(f16[4,32,1152]{2,1,0:T(8,128)(2,1)S(1)} %convert_element_type.54), channel_id=1, source_target_pairs={{0,8},{1,33},{2,10},{3,35},{4,12},{5,37},{6,14},{7,39},{8,16},{9,4... | collective-permute-start | bytes 884744 | tf_op jit(solution)/shard_map/ppermute | solution.py:24
  37.1 0.5 collective-permute-start.13
  37.5 5.3 %collective-permute-done.11 = f16[4,32,1152]{2,1,0:T(8,128)(2,1)S(1)} collective-permute-done((f16[4,32,1152]{2,1,0:T(8,128)(2,1)S(1)}, f16[4,32,1152]{2,1,0:T(8,128)(2,1)S(1)}, u32[]{:S(2)}, u32[]{:S(2)}) %collective-permute-start.11) | collective-permute-done | bytes 294944 | tf_op jit(solution)/shard_map/ppermute | solution.py:24
  43.0 3.0 %collective-permute-done.9 = f16[4,32,1152]{2,1,0:T(8,128)(2,1)S(1)} collective-permute-done((f16[4,32,1152]{2,1,0:T(8,128)(2,1)S(1)}, f16[4,32,1152]{2,1,0:T(8,128)(2,1)S(1)}, u32[]{:S(2)}, u32[]{:S(2)}) %collective-permute-start.9) | collective-permute-done | bytes 294944 | tf_op jit(solution)/shard_map/ppermute | solution.py:24
  46.7 1.9 %collective-permute-start.15 = (f16[32,1152]{1,0:T(8,128)(2,1)S(1)}, f16[32,1152]{1,0:T(8,128)(2,1)S(1)}, u32[]{:S(2)}, u32[]{:S(2)}) collective-permute-start(f16[32,1152]{1,0:T(8,128)(2,1)S(1)} %convert_element_type.66), channel_id=1, source_target_pairs={{0,96},{1,25},{2,98},{3,27},{4,100},{5,29},{6,102},{7,31},{8,104},... | collective-permute-start | bytes 221192 | tf_op jit(solution)/shard_map/ppermute | solution.py:24
  49.0 2.1 %collective-permute-start.17 = (f16[1,32,1152]{2,1,0:T(8,128)(2,1)S(1)}, f16[1,32,1152]{2,1,0:T(8,128)(2,1)S(1)}, u32[]{:S(2)}, u32[]{:S(2)}) collective-permute-start(f16[1,32,1152]{2,1,0:T(8,128)(2,1)S(1)} %convert_element_type.70), channel_id=1, source_target_pairs={{0,2},{1,3},{2,0},{3,1},{4,6},{5,7},{6,4},{7,5},{8,10},{9,11},{10,... | collective-permute-start | bytes 221192 | tf_op jit(solution)/shard_map/ppermute | solution.py:24
  51.1 1.2 collective-permute-done.16
  52.3 1.8 %collective-permute-done.14 = f16[32,1152]{1,0:T(8,128)(2,1)S(1)} collective-permute-done((f16[32,1152]{1,0:T(8,128)(2,1)S(1)}, f16[32,1152]{1,0:T(8,128)(2,1)S(1)}, u32[]{:S(2)}, u32[]{:S(2)}) %collective-permute-start.14) | collective-permute-done | bytes 73760 | tf_op jit(solution)/shard_map/ppermute | solution.py:24
  54.5 2.3 %collective-permute-start.20 = (bf16[32,1152]{1,0:T(8,128)(2,1)S(1)}, bf16[32,1152]{1,0:T(8,128)(2,1)S(1)}, u32[]{:S(2)}, u32[]{:S(2)}) collective-permute-start(bf16[32,1152]{1,0:T(8,128)(2,1)S(1)} %get-tuple-element.60.refs_0_), channel_id=1, source_target_pairs={{0,96},{1,25},{2,98},{3,27},{4,100},{5,29},{6,102},{7,31},{8,104},... | collective-permute-start | bytes 221192 | tf_op jit(solution)/shard_map/ppermute | solution.py:24
  57.1 1.3 %collective-permute-start.18 = (bf16[32,1152]{1,0:T(8,128)(2,1)S(1)}, bf16[32,1152]{1,0:T(8,128)(2,1)S(1)}, u32[]{:S(2)}, u32[]{:S(2)}) collective-permute-start(bf16[32,1152]{1,0:T(8,128)(2,1)S(1)} %get-tuple-element.60.refs_0_), channel_id=1, source_target_pairs={{0,32},{1,9},{2,34},{3,11},{4,36},{5,13},{6,38},{7,15},{8,40},{9,1... | collective-permute-start | bytes 221192 | tf_op jit(solution)/shard_map/ppermute | solution.py:24
  58.4 0.7 collective-permute-start.21
  59.1 3.6 %collective-permute-done.21.refs_5_ = bf16[32,1024]{1,0:T(8,128)(2,1)S(1)} collective-permute-done((bf16[32,1024]{1,0:T(8,128)(2,1)S(1)}, bf16[32,1024]{1,0:T(8,128)(2,1)S(1)}, u32[]{:S(2)}, u32[]{:S(2)}) %collective-permute-start.21) | collective-permute-done | bytes 65568 | tf_op jit(solution)/shard_map/ppermute | solution.py:24
  62.8 0.7 collective-permute-done.18.refs_1_
  63.6 1.6 %collective-permute-start.24 = (bf16[4,32,1152]{2,1,0:T(8,128)(2,1)S(1)}, bf16[4,32,1152]{2,1,0:T(8,128)(2,1)S(1)}, u32[]{:S(2)}, u32[]{:S(2)}) collective-permute-start(bf16[4,32,1152]{2,1,0:T(8,128)(2,1)S(1)} %get-tuple-element.62.g0), channel_id=1, source_target_pairs={{0,24},{1,97},{2,26},{3,99},{4,28},{5,101},{6,30},{7,103},{8,0},{9... | collective-permute-start | bytes 884744 | tf_op jit(solution)/shard_map/ppermute | solution.py:24
  65.2 0.8 collective-permute-start.22
  66.0 3.7 %collective-permute-done.25 = bf16[2,32,1024]{2,1,0:T(8,128)(2,1)S(1)} collective-permute-done((bf16[2,32,1024]{2,1,0:T(8,128)(2,1)S(1)}, bf16[2,32,1024]{2,1,0:T(8,128)(2,1)S(1)}, u32[]{:S(2)}, u32[]{:S(2)}) %collective-permute-start.25) | collective-permute-done | bytes 131104 | tf_op jit(solution)/shard_map/ppermute | solution.py:24
  69.9 0.5 collective-permute-done.24.g3
  70.4 3.1 %collective-permute-done.23.g2 = bf16[4,32,1152]{2,1,0:T(8,128)(2,1)S(1)} collective-permute-done((bf16[4,32,1152]{2,1,0:T(8,128)(2,1)S(1)}, bf16[4,32,1152]{2,1,0:T(8,128)(2,1)S(1)}, u32[]{:S(2)}, u32[]{:S(2)}) %collective-permute-start.23) | collective-permute-done | bytes 294944 | tf_op jit(solution)/shard_map/ppermute | solution.py:24
  73.5 2.8 %collective-permute-done.22.g1 = bf16[4,32,1152]{2,1,0:T(8,128)(2,1)S(1)} collective-permute-done((bf16[4,32,1152]{2,1,0:T(8,128)(2,1)S(1)}, bf16[4,32,1152]{2,1,0:T(8,128)(2,1)S(1)}, u32[]{:S(2)}, u32[]{:S(2)}) %collective-permute-start.22) | collective-permute-done | bytes 294944 | tf_op jit(solution)/shard_map/ppermute | solution.py:24
  76.3 4.6 %product.3 = (f32[4,32,1024]{2,1,0:T(8,128)S(1)}, bf16[4,32,1024]{2,1,0:T(8,128)(2,1)S(1)}, bf16[4,32,1024]{2,1,0:T(8,128)(2,1)S(1)}, bf16[4,32,1024]{2,1,0:T(8,...) custom-call(s32[1,3,2]{2,1,0:T(4,128)S(1)} %copy.7.pairs, ...), custom_call_target="tpu_custom_call" | custom-call | flops 800000000 | bytes 10000000 | tf_op jit(solution)/shard_map/product/pallas_call | solution.py:173
  81.1 3.2 %collective-permute-start.31 = (bf16[4,32,1024]{2,1,0:T(8,128)(2,1)S(1)}, bf16[4,32,1024]{2,1,0:T(8,128)(2,1)S(1)}, u32[]{:S(2)}, u32[]{:S(2)}) collective-permute-start(bf16[4,32,1024]{2,1,0:T(8,128)(2,1)S(1)} %get-tuple-element.76), channel_id=1, source_target_pairs={{0,24},{1,97},{2,26},{3,99},{4,28},{5,101},{6,30},{7,103},{8,0},{9... | collective-permute-start | bytes 786440 | tf_op jit(solution)/shard_map/ppermute | solution.py:24
  84.4 0.8 collective-permute-start.28
  85.2 6.2 %collective-permute-done.28.received = bf16[2,32,1152]{2,1,0:T(8,128)(2,1)S(1)} collective-permute-done((bf16[2,32,1152]{2,1,0:T(8,128)(2,1)S(1)}, bf16[2,32,1152]{2,1,0:T(8,128)(2,1)S(1)}, u32[]{:S(2)}, u32[]{:S(2)}) %collective-permute-start.28) | collective-permute-done | bytes 147488 | tf_op jit(solution)/shard_map/ppermute | solution.py:24
  91.5 0.7 collective-permute-done.32.refs_2_
  92.3 1.3 %collective-permute-start.33 = (bf16[32,1024]{1,0:T(8,128)(2,1)S(1)}, bf16[32,1024]{1,0:T(8,128)(2,1)S(1)}, u32[]{:S(2)}, u32[]{:S(2)}) collective-permute-start(bf16[32,1024]{1,0:T(8,128)(2,1)S(1)} %get-tuple-element.80), channel_id=1, source_target_pairs={{0,32},{1,9},{2,34},{3,11},{4,36},{5,13},{6,38},{7,15},{8,40},{9,1... | collective-permute-start | bytes 196616 | tf_op jit(solution)/shard_map/ppermute | solution.py:24
  93.6 2.0 %collective-permute-start.34 = (bf16[32,1024]{1,0:T(8,128)(2,1)S(1)}, bf16[32,1024]{1,0:T(8,128)(2,1)S(1)}, u32[]{:S(2)}, u32[]{:S(2)}) collective-permute-start(bf16[32,1024]{1,0:T(8,128)(2,1)S(1)} %get-tuple-element.81), channel_id=1, source_target_pairs={{0,96},{1,25},{2,98},{3,27},{4,100},{5,29},{6,102},{7,31},{8,104},... | collective-permute-start | bytes 196616 | tf_op jit(solution)/shard_map/ppermute | solution.py:24
  95.8 1.9 %factor_first.1 = (f32[32,1024]{1,0:T(8,128)}, f32[32,32]{1,0:T(8,128)S(1)}) custom-call(f32[8,128]{1,0:T(8,128)S(1)} %get-tuple-element.70.gram, bf16[1,32,1152]{2,1,0:T(8,128)(2,1)S(1)} %collective-permute-done.29.received.refs_5_, f32[32,1024]{1,0:T(8,128)S(1)} %get-tuple-element.72.panel), custom_call_target="tpu_custom_call" | custom-call | flops 1000000 | bytes 10000000 | tf_op jit(solution)/shard_map/factor_first/pallas_call | solution.py:411
  98.2 3.3 %collective-permute-done.35.refs_4_ = bf16[32,1024]{1,0:T(8,128)(2,1)S(1)} collective-permute-done((bf16[32,1024]{1,0:T(8,128)(2,1)S(1)}, bf16[32,1024]{1,0:T(8,128)(2,1)S(1)}, u32[]{:S(2)}, u32[]{:S(2)}) %collective-permute-start.35) | collective-permute-done | bytes 65568 | tf_op jit(solution)/shard_map/ppermute | solution.py:24
  101.4 0.6 finish_second.1
  102.0 1.2 collective-permute-done.36.other
  103.2 17.0 %all_to_all.5.gram = f32[64,8,128]{2,1,0:T(8,128)S(1)} all-to-all(f32[64,8,128]{2,1,0:T(8,128)S(1)} %total_gram.1), channel_id=1, replica_groups=mesh['z'=4,'x'=4,'y'=4,'core'=2] {'z','x','y'}, dimensions={0} | all-to-all | bytes 524288 | tf_op jit(solution)/shard_map/all_to_all | solution.py:348
  120.2 2.0 %factor_second.1 = f32[32,1024]{1,0:T(8,128)} custom-call(f32[64,8,128]{2,1,0:T(8,128)S(1)} %all_to_all.5.gram, f32[32,1024]{1,0:T(8,128)S(1)} %get-tuple-element.85.panel), custom_call_target="tpu_custom_call" | custom-call | tf_op jit(solution)/shard_map/factor_second/pallas_call | solution.py:423
  (70 shorter events, 5.0 us)
Async XLA Ops:
  0.6 7.0 %collective-permute-start.3 = (bf16[32,1024]{1,0:T(8,128)(2,1)}, bf16[32,1024]{1,0:T(8,128)(2,1)S(1)}, u32[]{:S(2)}, u32[]{:S(2)}) collective-permute-start(bf16[32,1024]{1,0:T(8,128)(2,1)} %bitcast.3), channel_id=1, source_target_pairs={{0,2},{1,3},{2,0},{3,1},{4,6},{5,7},{6,4},{7,5},{8,10},{9,11},{10,... | collective-permute-start | bytes 196616 | tf_op jit(solution)/shard_map/ppermute | solution.py:24
  2.4 6.3 %collective-permute-start.2 = (bf16[32,1024]{1,0:T(8,128)(2,1)}, bf16[32,1024]{1,0:T(8,128)(2,1)S(1)}, u32[]{:S(2)}, u32[]{:S(2)}) collective-permute-start(bf16[32,1024]{1,0:T(8,128)(2,1)} %bitcast.4), channel_id=1, source_target_pairs={{0,96},{1,25},{2,98},{3,27},{4,100},{5,29},{6,102},{7,31},{8,104},... | collective-permute-start | bytes 196616 | tf_op jit(solution)/shard_map/ppermute | solution.py:24
  6.4 6.1 %collective-permute-start.1 = (bf16[32,1024]{1,0:T(8,128)(2,1)}, bf16[32,1024]{1,0:T(8,128)(2,1)S(1)}, u32[]{:S(2)}, u32[]{:S(2)}) collective-permute-start(bf16[32,1024]{1,0:T(8,128)(2,1)} %bitcast.5), channel_id=1, source_target_pairs={{0,64},{1,17},{2,66},{3,19},{4,68},{5,21},{6,70},{7,23},{8,72},{9,... | collective-permute-start | bytes 196616 | tf_op jit(solution)/shard_map/ppermute | solution.py:24
  6.4 6.4 %collective-permute-start = (bf16[32,1024]{1,0:T(8,128)(2,1)}, bf16[32,1024]{1,0:T(8,128)(2,1)S(1)}, u32[]{:S(2)}, u32[]{:S(2)}) collective-permute-start(bf16[32,1024]{1,0:T(8,128)(2,1)} %bitcast.6), channel_id=1, source_target_pairs={{0,32},{1,9},{2,34},{3,11},{4,36},{5,13},{6,38},{7,15},{8,40},{9,1... | collective-permute-start | bytes 196616 | tf_op jit(solution)/shard_map/ppermute | solution.py:24
  12.8 0.8 copy-start.1
  13.7 6.7 %collective-permute-start.7 = (bf16[2,32,1024]{2,1,0:T(8,128)(2,1)S(1)}, bf16[2,32,1024]{2,1,0:T(8,128)(2,1)S(1)}, u32[]{:S(2)}, u32[]{:S(2)}) collective-permute-start(bf16[2,32,1024]{2,1,0:T(8,128)(2,1)S(1)} %get-tuple-element.45), channel_id=1, source_target_pairs={{0,6},{1,7},{2,4},{3,5},{4,2},{5,3},{6,0},{7,1},{8,14},{9,15},{10,... | collective-permute-start | bytes 393224 | tf_op jit(solution)/shard_map/ppermute | solution.py:24
  15.9 9.5 %collective-permute-start.6 = (bf16[4,32,1024]{2,1,0:T(8,128)(2,1)S(1)}, bf16[4,32,1024]{2,1,0:T(8,128)(2,1)S(1)}, u32[]{:S(2)}, u32[]{:S(2)}) collective-permute-start(bf16[4,32,1024]{2,1,0:T(8,128)(2,1)S(1)} %get-tuple-element.44.g0), channel_id=1, source_target_pairs={{0,24},{1,97},{2,26},{3,99},{4,28},{5,101},{6,30},{7,103},{8,0},{9... | collective-permute-start | bytes 786440 | tf_op jit(solution)/shard_map/ppermute | solution.py:24
  18.7 8.0 %collective-permute-start.5 = (bf16[4,32,1024]{2,1,0:T(8,128)(2,1)S(1)}, bf16[4,32,1024]{2,1,0:T(8,128)(2,1)S(1)}, u32[]{:S(2)}, u32[]{:S(2)}) collective-permute-start(bf16[4,32,1024]{2,1,0:T(8,128)(2,1)S(1)} %get-tuple-element.44.g0), channel_id=1, source_target_pairs={{0,16},{1,65},{2,18},{3,67},{4,20},{5,69},{6,22},{7,71},{8,24},{9,... | collective-permute-start | bytes 786440 | tf_op jit(solution)/shard_map/ppermute | solution.py:24
  19.5 9.9 %collective-permute-start.4 = (bf16[4,32,1024]{2,1,0:T(8,128)(2,1)S(1)}, bf16[4,32,1024]{2,1,0:T(8,128)(2,1)S(1)}, u32[]{:S(2)}, u32[]{:S(2)}) collective-permute-start(bf16[4,32,1024]{2,1,0:T(8,128)(2,1)S(1)} %get-tuple-element.44.g0), channel_id=1, source_target_pairs={{0,8},{1,33},{2,10},{3,35},{4,12},{5,37},{6,14},{7,39},{8,16},{9,4... | collective-permute-start | bytes 786440 | tf_op jit(solution)/shard_map/ppermute | solution.py:24
  20.4 9.0 %collective-permute-start.8 = (bf16[4,32,1024]{2,1,0:T(8,128)(2,1)S(1)}, bf16[4,32,1024]{2,1,0:T(8,128)(2,1)S(1)}, u32[]{:S(2)}, u32[]{:S(2)}) collective-permute-start(bf16[4,32,1024]{2,1,0:T(8,128)(2,1)S(1)} %constant_dynamic-update-slice_fusion.h0), channel_id=1, source_target_pairs={{0,1},{1,0},{2,3},{3,2},{4,5},{5,4},{6,7},{7,6},{8,9},{9,8},{10,11... | collective-permute-start | bytes 786440 | tf_op jit(solution)/shard_map/ppermute | solution.py:24
  21.9 2.8 %copy-start = (bf16[3,1024,1024]{2,1,0:T(8,128)(2,1)S(1)}, bf16[3,1024,1024]{2,1,0:T(8,128)(2,1)}, u32[]{:S(2)}) copy-start(bf16[3,1024,1024]{2,1,0:T(8,128)(2,1)} %source.1) | copy-start | bytes 18874372
  34.3 2.5 %collective-permute-start.12 = (f16[4,32,1152]{2,1,0:T(8,128)(2,1)S(1)}, f16[4,32,1152]{2,1,0:T(8,128)(2,1)S(1)}, u32[]{:S(2)}, u32[]{:S(2)}) collective-permute-start(f16[4,32,1152]{2,1,0:T(8,128)(2,1)S(1)} %convert_element_type.60), channel_id=1, source_target_pairs={{0,1},{1,0},{2,3},{3,2},{4,5},{5,4},{6,7},{7,6},{8,9},{9,8},{10,11... | collective-permute-start | bytes 884744 | tf_op jit(solution)/shard_map/ppermute | solution.py:24
  34.5 8.4 %collective-permute-start.11 = (f16[4,32,1152]{2,1,0:T(8,128)(2,1)S(1)}, f16[4,32,1152]{2,1,0:T(8,128)(2,1)S(1)}, u32[]{:S(2)}, u32[]{:S(2)}) collective-permute-start(f16[4,32,1152]{2,1,0:T(8,128)(2,1)S(1)} %convert_element_type.58), channel_id=1, source_target_pairs={{0,16},{1,65},{2,18},{3,67},{4,20},{5,69},{6,22},{7,71},{8,24},{9,... | collective-permute-start | bytes 884744 | tf_op jit(solution)/shard_map/ppermute | solution.py:24
  34.6 8.4 %collective-permute-start.10 = (f16[4,32,1152]{2,1,0:T(8,128)(2,1)S(1)}, f16[4,32,1152]{2,1,0:T(8,128)(2,1)S(1)}, u32[]{:S(2)}, u32[]{:S(2)}) collective-permute-start(f16[4,32,1152]{2,1,0:T(8,128)(2,1)S(1)} %convert_element_type.56), channel_id=1, source_target_pairs={{0,24},{1,97},{2,26},{3,99},{4,28},{5,101},{6,30},{7,103},{8,0},{9... | collective-permute-start | bytes 884744 | tf_op jit(solution)/shard_map/ppermute | solution.py:24
  35.2 10.7 %collective-permute-start.9 = (f16[4,32,1152]{2,1,0:T(8,128)(2,1)S(1)}, f16[4,32,1152]{2,1,0:T(8,128)(2,1)S(1)}, u32[]{:S(2)}, u32[]{:S(2)}) collective-permute-start(f16[4,32,1152]{2,1,0:T(8,128)(2,1)S(1)} %convert_element_type.54), channel_id=1, source_target_pairs={{0,8},{1,33},{2,10},{3,35},{4,12},{5,37},{6,14},{7,39},{8,16},{9,4... | collective-permute-start | bytes 884744 | tf_op jit(solution)/shard_map/ppermute | solution.py:24
  37.1 11.7 %collective-permute-start.13 = (f16[2,32,1152]{2,1,0:T(8,128)(2,1)S(1)}, f16[2,32,1152]{2,1,0:T(8,128)(2,1)S(1)}, u32[]{:S(2)}, u32[]{:S(2)}) collective-permute-start(f16[2,32,1152]{2,1,0:T(8,128)(2,1)S(1)} %convert_element_type.62), channel_id=1, source_target_pairs={{0,6},{1,7},{2,4},{3,5},{4,2},{5,3},{6,0},{7,1},{8,14},{9,15},{10,... | collective-permute-start | bytes 442376 | tf_op jit(solution)/shard_map/ppermute | solution.py:24
  46.4 5.9 %collective-permute-start.16 = (f16[32,1152]{1,0:T(8,128)(2,1)S(1)}, f16[32,1152]{1,0:T(8,128)(2,1)S(1)}, u32[]{:S(2)}, u32[]{:S(2)}) collective-permute-start(f16[32,1152]{1,0:T(8,128)(2,1)S(1)} %convert_element_type.68), channel_id=1, source_target_pairs={{0,64},{1,17},{2,66},{3,19},{4,68},{5,21},{6,70},{7,23},{8,72},{9,... | collective-permute-start | bytes 221192 | tf_op jit(solution)/shard_map/ppermute | solution.py:24
  46.7 5.6 %collective-permute-start.15 = (f16[32,1152]{1,0:T(8,128)(2,1)S(1)}, f16[32,1152]{1,0:T(8,128)(2,1)S(1)}, u32[]{:S(2)}, u32[]{:S(2)}) collective-permute-start(f16[32,1152]{1,0:T(8,128)(2,1)S(1)} %convert_element_type.66), channel_id=1, source_target_pairs={{0,96},{1,25},{2,98},{3,27},{4,100},{5,29},{6,102},{7,31},{8,104},... | collective-permute-start | bytes 221192 | tf_op jit(solution)/shard_map/ppermute | solution.py:24
  48.6 5.6 %collective-permute-start.14 = (f16[32,1152]{1,0:T(8,128)(2,1)S(1)}, f16[32,1152]{1,0:T(8,128)(2,1)S(1)}, u32[]{:S(2)}, u32[]{:S(2)}) collective-permute-start(f16[32,1152]{1,0:T(8,128)(2,1)S(1)} %convert_element_type.64), channel_id=1, source_target_pairs={{0,32},{1,9},{2,34},{3,11},{4,36},{5,13},{6,38},{7,15},{8,40},{9,1... | collective-permute-start | bytes 221192 | tf_op jit(solution)/shard_map/ppermute | solution.py:24
  49.0 5.2 %collective-permute-start.17 = (f16[1,32,1152]{2,1,0:T(8,128)(2,1)S(1)}, f16[1,32,1152]{2,1,0:T(8,128)(2,1)S(1)}, u32[]{:S(2)}, u32[]{:S(2)}) collective-permute-start(f16[1,32,1152]{2,1,0:T(8,128)(2,1)S(1)} %convert_element_type.70), channel_id=1, source_target_pairs={{0,2},{1,3},{2,0},{3,1},{4,6},{5,7},{6,4},{7,5},{8,10},{9,11},{10,... | collective-permute-start | bytes 221192 | tf_op jit(solution)/shard_map/ppermute | solution.py:24
  54.5 8.2 %collective-permute-start.20 = (bf16[32,1152]{1,0:T(8,128)(2,1)S(1)}, bf16[32,1152]{1,0:T(8,128)(2,1)S(1)}, u32[]{:S(2)}, u32[]{:S(2)}) collective-permute-start(bf16[32,1152]{1,0:T(8,128)(2,1)S(1)} %get-tuple-element.60.refs_0_), channel_id=1, source_target_pairs={{0,96},{1,25},{2,98},{3,27},{4,100},{5,29},{6,102},{7,31},{8,104},... | collective-permute-start | bytes 221192 | tf_op jit(solution)/shard_map/ppermute | solution.py:24
  56.8 5.9 %collective-permute-start.19 = (bf16[32,1152]{1,0:T(8,128)(2,1)S(1)}, bf16[32,1152]{1,0:T(8,128)(2,1)S(1)}, u32[]{:S(2)}, u32[]{:S(2)}) collective-permute-start(bf16[32,1152]{1,0:T(8,128)(2,1)S(1)} %get-tuple-element.60.refs_0_), channel_id=1, source_target_pairs={{0,64},{1,17},{2,66},{3,19},{4,68},{5,21},{6,70},{7,23},{8,72},{9,... | collective-permute-start | bytes 221192 | tf_op jit(solution)/shard_map/ppermute | solution.py:24
  57.1 6.3 %collective-permute-start.18 = (bf16[32,1152]{1,0:T(8,128)(2,1)S(1)}, bf16[32,1152]{1,0:T(8,128)(2,1)S(1)}, u32[]{:S(2)}, u32[]{:S(2)}) collective-permute-start(bf16[32,1152]{1,0:T(8,128)(2,1)S(1)} %get-tuple-element.60.refs_0_), channel_id=1, source_target_pairs={{0,32},{1,9},{2,34},{3,11},{4,36},{5,13},{6,38},{7,15},{8,40},{9,1... | collective-permute-start | bytes 221192 | tf_op jit(solution)/shard_map/ppermute | solution.py:24
  58.4 4.3 %collective-permute-start.21 = (bf16[32,1024]{1,0:T(8,128)(2,1)S(1)}, bf16[32,1024]{1,0:T(8,128)(2,1)S(1)}, u32[]{:S(2)}, u32[]{:S(2)}) collective-permute-start(bf16[32,1024]{1,0:T(8,128)(2,1)S(1)} %get-tuple-element.61.refs_4_), channel_id=1, source_target_pairs={{0,2},{1,3},{2,0},{3,1},{4,6},{5,7},{6,4},{7,5},{8,10},{9,11},{10,... | collective-permute-start | bytes 196616 | tf_op jit(solution)/shard_map/ppermute | solution.py:24
  63.5 6.3 %collective-permute-start.25 = (bf16[2,32,1024]{2,1,0:T(8,128)(2,1)S(1)}, bf16[2,32,1024]{2,1,0:T(8,128)(2,1)S(1)}, u32[]{:S(2)}, u32[]{:S(2)}) collective-permute-start(bf16[2,32,1024]{2,1,0:T(8,128)(2,1)S(1)} %get-tuple-element.63), channel_id=1, source_target_pairs={{0,6},{1,7},{2,4},{3,5},{4,2},{5,3},{6,0},{7,1},{8,14},{9,15},{10,... | collective-permute-start | bytes 393224 | tf_op jit(solution)/shard_map/ppermute | solution.py:24
  63.6 6.8 %collective-permute-start.24 = (bf16[4,32,1152]{2,1,0:T(8,128)(2,1)S(1)}, bf16[4,32,1152]{2,1,0:T(8,128)(2,1)S(1)}, u32[]{:S(2)}, u32[]{:S(2)}) collective-permute-start(bf16[4,32,1152]{2,1,0:T(8,128)(2,1)S(1)} %get-tuple-element.62.g0), channel_id=1, source_target_pairs={{0,24},{1,97},{2,26},{3,99},{4,28},{5,101},{6,30},{7,103},{8,0},{9... | collective-permute-start | bytes 884744 | tf_op jit(solution)/shard_map/ppermute | solution.py:24
  65.2 8.3 %collective-permute-start.23 = (bf16[4,32,1152]{2,1,0:T(8,128)(2,1)S(1)}, bf16[4,32,1152]{2,1,0:T(8,128)(2,1)S(1)}, u32[]{:S(2)}, u32[]{:S(2)}) collective-permute-start(bf16[4,32,1152]{2,1,0:T(8,128)(2,1)S(1)} %get-tuple-element.62.g0), channel_id=1, source_target_pairs={{0,16},{1,65},{2,18},{3,67},{4,20},{5,69},{6,22},{7,71},{8,24},{9,... | collective-permute-start | bytes 884744 | tf_op jit(solution)/shard_map/ppermute | solution.py:24
  65.2 11.1 %collective-permute-start.22 = (bf16[4,32,1152]{2,1,0:T(8,128)(2,1)S(1)}, bf16[4,32,1152]{2,1,0:T(8,128)(2,1)S(1)}, u32[]{:S(2)}, u32[]{:S(2)}) collective-permute-start(bf16[4,32,1152]{2,1,0:T(8,128)(2,1)S(1)} %get-tuple-element.62.g0), channel_id=1, source_target_pairs={{0,8},{1,33},{2,10},{3,35},{4,12},{5,37},{6,14},{7,39},{8,16},{9,4... | collective-permute-start | bytes 884744 | tf_op jit(solution)/shard_map/ppermute | solution.py:24
  69.8 6.5 %collective-permute-start.26 = (bf16[4,32,1024]{2,1,0:T(8,128)(2,1)S(1)}, bf16[4,32,1024]{2,1,0:T(8,128)(2,1)S(1)}, u32[]{:S(2)}, u32[]{:S(2)}) collective-permute-start(bf16[4,32,1024]{2,1,0:T(8,128)(2,1)S(1)} %constant_dynamic-update-slice_fusion.2.h0), channel_id=1, source_target_pairs={{0,1},{1,0},{2,3},{3,2},{4,5},{5,4},{6,7},{7,6},{8,9},{9,8},{10,11... | collective-permute-start | bytes 786440 | tf_op jit(solution)/shard_map/ppermute | solution.py:24
  80.9 3.4 %collective-permute-start.27 = (bf16[4,32,1152]{2,1,0:T(8,128)(2,1)S(1)}, bf16[4,32,1152]{2,1,0:T(8,128)(2,1)S(1)}, u32[]{:S(2)}, u32[]{:S(2)}) collective-permute-start(bf16[4,32,1152]{2,1,0:T(8,128)(2,1)S(1)} %get-tuple-element.65), channel_id=1, source_target_pairs={{0,1},{1,0},{2,3},{3,2},{4,5},{5,4},{6,7},{7,6},{8,9},{9,8},{10,11... | collective-permute-start | bytes 884744 | tf_op jit(solution)/shard_map/ppermute | solution.py:24
  81.0 10.5 %collective-permute-start.30 = (bf16[4,32,1024]{2,1,0:T(8,128)(2,1)S(1)}, bf16[4,32,1024]{2,1,0:T(8,128)(2,1)S(1)}, u32[]{:S(2)}, u32[]{:S(2)}) collective-permute-start(bf16[4,32,1024]{2,1,0:T(8,128)(2,1)S(1)} %get-tuple-element.75), channel_id=1, source_target_pairs={{0,8},{1,33},{2,10},{3,35},{4,12},{5,37},{6,14},{7,39},{8,16},{9,4... | collective-permute-start | bytes 786440 | tf_op jit(solution)/shard_map/ppermute | solution.py:24
  81.1 10.4 %collective-permute-start.31 = (bf16[4,32,1024]{2,1,0:T(8,128)(2,1)S(1)}, bf16[4,32,1024]{2,1,0:T(8,128)(2,1)S(1)}, u32[]{:S(2)}, u32[]{:S(2)}) collective-permute-start(bf16[4,32,1024]{2,1,0:T(8,128)(2,1)S(1)} %get-tuple-element.76), channel_id=1, source_target_pairs={{0,24},{1,97},{2,26},{3,99},{4,28},{5,101},{6,30},{7,103},{8,0},{9... | collective-permute-start | bytes 786440 | tf_op jit(solution)/shard_map/ppermute | solution.py:24
  84.3 7.9 %collective-permute-start.32 = (bf16[4,32,1024]{2,1,0:T(8,128)(2,1)S(1)}, bf16[4,32,1024]{2,1,0:T(8,128)(2,1)S(1)}, u32[]{:S(2)}, u32[]{:S(2)}) collective-permute-start(bf16[4,32,1024]{2,1,0:T(8,128)(2,1)S(1)} %get-tuple-element.77), channel_id=1, source_target_pairs={{0,16},{1,65},{2,18},{3,67},{4,20},{5,69},{6,22},{7,71},{8,24},{9,... | collective-permute-start | bytes 786440 | tf_op jit(solution)/shard_map/ppermute | solution.py:24
  84.4 7.0 %collective-permute-start.28 = (bf16[2,32,1152]{2,1,0:T(8,128)(2,1)S(1)}, bf16[2,32,1152]{2,1,0:T(8,128)(2,1)S(1)}, u32[]{:S(2)}, u32[]{:S(2)}) collective-permute-start(bf16[2,32,1152]{2,1,0:T(8,128)(2,1)S(1)} %get-tuple-element.68), channel_id=1, source_target_pairs={{0,6},{1,7},{2,4},{3,5},{4,2},{5,3},{6,0},{7,1},{8,14},{9,15},{10,... | collective-permute-start | bytes 442376 | tf_op jit(solution)/shard_map/ppermute | solution.py:24
  91.4 4.4 %collective-permute-start.29 = (bf16[1,32,1152]{2,1,0:T(8,128)(2,1)S(1)}, bf16[1,32,1152]{2,1,0:T(8,128)(2,1)S(1)}, u32[]{:S(2)}, u32[]{:S(2)}) collective-permute-start(bf16[1,32,1152]{2,1,0:T(8,128)(2,1)S(1)} %get-tuple-element.71), channel_id=1, source_target_pairs={{0,2},{1,3},{2,0},{3,1},{4,6},{5,7},{6,4},{7,5},{8,10},{9,11},{10,... | collective-permute-start | bytes 221192 | tf_op jit(solution)/shard_map/ppermute | solution.py:24
  92.3 5.5 %collective-permute-start.33 = (bf16[32,1024]{1,0:T(8,128)(2,1)S(1)}, bf16[32,1024]{1,0:T(8,128)(2,1)S(1)}, u32[]{:S(2)}, u32[]{:S(2)}) collective-permute-start(bf16[32,1024]{1,0:T(8,128)(2,1)S(1)} %get-tuple-element.80), channel_id=1, source_target_pairs={{0,32},{1,9},{2,34},{3,11},{4,36},{5,13},{6,38},{7,15},{8,40},{9,1... | collective-permute-start | bytes 196616 | tf_op jit(solution)/shard_map/ppermute | solution.py:24
  93.6 4.5 %collective-permute-start.34 = (bf16[32,1024]{1,0:T(8,128)(2,1)S(1)}, bf16[32,1024]{1,0:T(8,128)(2,1)S(1)}, u32[]{:S(2)}, u32[]{:S(2)}) collective-permute-start(bf16[32,1024]{1,0:T(8,128)(2,1)S(1)} %get-tuple-element.81), channel_id=1, source_target_pairs={{0,96},{1,25},{2,98},{3,27},{4,100},{5,29},{6,102},{7,31},{8,104},... | collective-permute-start | bytes 196616 | tf_op jit(solution)/shard_map/ppermute | solution.py:24
  95.6 5.8 %collective-permute-start.35 = (bf16[32,1024]{1,0:T(8,128)(2,1)S(1)}, bf16[32,1024]{1,0:T(8,128)(2,1)S(1)}, u32[]{:S(2)}, u32[]{:S(2)}) collective-permute-start(bf16[32,1024]{1,0:T(8,128)(2,1)S(1)} %get-tuple-element.82), channel_id=1, source_target_pairs={{0,64},{1,17},{2,66},{3,19},{4,68},{5,21},{6,70},{7,23},{8,72},{9,... | collective-permute-start | bytes 196616 | tf_op jit(solution)/shard_map/ppermute | solution.py:24
  102.0 1.2 collective-permute-start.36

commit v4 on v3

--- a/solution.py
+++ b/solution.py
@@ -33,7 +33,7 @@
 
 
 def send_y(value, s):
-    return permute(value, lambda z, x, y, c: (z, x, y ^ s, c))
+    return permute(value, lambda z, x, y, c: (z, x, y ^ s if c == 0 else y ^ (4 - s), c))
 
 
 def send_core(value):
@@ -73,6 +73,26 @@
     return value[:, 0:1024] * jnp.exp2(value[:, 1024:1025])
 
 
+def put(ref, k, value):
+    for i in range(2):
+        for j in range(8):
+            ref[16 * k + 8 * i + j] = value[16 * i : 16 * i + 16, 128 * j : 128 * j + 128]
+
+
+def take(ref, k):
+    rows = [jnp.concatenate([ref[16 * k + 8 * i + j] for j in range(8)], axis=1) for i in range(2)]
+    return jnp.concatenate(rows, axis=0)
+
+
+def take_extra(ref, k):
+    return jnp.concatenate([ref[16 * k], ref[16 * k + 1]], axis=0)
+
+
+def put_extra(ref, k, value):
+    ref[16 * k] = value[0:16]
+    ref[16 * k + 1] = value[16:32]
+
+
 def carry(send, value, *args):
     if value.dtype == jnp.bfloat16:
         return send(value, *args)
@@ -84,123 +104,185 @@
     return terms[0:8] + terms[8:16] + terms[16:24]
 
 
-def product_kernel(with_gram, pairs, live, blocks, g0, g1, g2, g3, h0, h1, *rest):
-    gathered, pair_gathered = (g0, g1, g2, g3), (h0, h1)
-    outs = rest[:6]
-    lefts, rights, results = rest[-3:]
-    count = live[0]
-    row = pairs[0, 0, 0] // 8
-    col = pairs[0, 0, 1] % 8
-    z, x, y, c = row // 4, row % 4, col // 2, col % 2
-
-    def row_shift(target):
-        dz, dx = (target // 4 - z) & 3, (target % 4 - x) & 3
-        return jnp.where(c == 0, dx, dz), jnp.where(c == 0, dz, dx)
-
+def places(pairs, slot):
+    first, second = pairs[0, slot, 0], pairs[0, slot, 1]
+    row, col = first // 8, second % 8
+    dz, dx = (second // 8 // 4 - row // 4) & 3, (second // 8 % 4 - row % 4) & 3
+    c = col % 2
+    outer, inner = jnp.where(c == 0, dx, dz), jnp.where(c == 0, dz, dx)
+    dy = (first % 8 // 2) ^ (col // 2)
+    dy = dy ^ (dy >> 1)
+    dy = jnp.where(first % 2 == 0, dy, (dy & 1) * 2 + (dy >> 1))
+    return outer, inner, (first % 2) ^ c, dy
+
+
+def load_right(pairs, slot, pair_gathered, rights):
+    outer, inner, dc, dy = places(pairs, slot)
+    for t in range(2):
+        @pl.when(dc == t)
+        def _():
+            rights[...] = pair_gathered[t][dy]
+
+
+def load_left(pairs, slot, gathered, lefts):
+    outer, inner, dc, dy = places(pairs, slot)
+    for t in range(4):
+        @pl.when((-outer & 3) == t)
+        def _():
+            lefts[...] = take(gathered[t], -inner & 3)
+
+
+def multiply(panel, matrix):
+    return jnp.dot(panel[...], matrix, preferred_element_type=jnp.float32)
+
+
+def store_mirror(pairs, slot, value, outs, half):
+    outer, inner, dc, dy = places(pairs, slot)
+    value = jnp.where(pairs[0, slot, 0] != pairs[0, slot, 1], value, 0.0)
+    lanes = lax.broadcasted_iota(jnp.int32, (32, 128), 1)
+
+    @pl.when(outer == 0)
+    def _():
+        outs[0][inner] = outs[0][inner] + value
+
+    for t in range(1, 4):
+        @pl.when(outer == t)
+        def _():
+            place = jnp.where(lanes == 8 * slot + inner, 1.0, 0.0)
+            if half:
+                coded = encode(value)
+                put(outs[t], slot, coded[:, 0:1024])
+                place = place + jnp.where(lanes == 8 * slot + 4, coded[:, 1024:1152], 0.0)
+            else:
+                put(outs[t], slot, value.astype(jnp.bfloat16))
+            extra = take_extra(outs[t], 3).astype(jnp.float32) + place
+            put_extra(outs[t], 3, extra.astype(outs[t].dtype))
+
+
+def store_direct(pairs, slot, value, outs, results, half):
+    outer, inner, dc, dy = places(pairs, slot)
+    results[slot] = value
+    results[3] = value
+
+    def earlier(before, carry):
+        @pl.when(pairs[0, before, 0] == pairs[0, slot, 0])
+        def _():
+            results[3] = results[3] + results[before]
+
+        return carry
+
+    lax.fori_loop(0, slot, earlier, 0)
+    for t in range(2):
+        @pl.when(dc == t)
+        def _():
+            if t and half:
+                outs[1][dy] = encode(results[3])
+            else:
+                outs[t][dy, :, 0:1024] = results[3].astype(outs[t].dtype)
+
+
+def add_gram(gathered, out, sent):
+    gram = merge(take_extra(gathered[0], 4))
+    for array in gathered[1:]:
+        gram = gram + merge(take_extra(array, 4))
+    out[...] = gram
+    sent[0, :, 1024:1152] = split(gram)
+
+
+def clear(outs):
     for out in outs:
         out[...] = jnp.zeros_like(out)
-    if with_gram:
-        gram = merge(g0[0, :, 1024:1152])
-        for array in gathered[1:]:
-            gram = gram + merge(array[0, :, 1024:1152])
-        rest[6][...] = gram
-        outs[5][0, :, 1024:1152] = split(gram)
+
+
+def both_kernel(pairs, live, blocks, turned, g0, g1, g2, g3, h0, h1, *rest):
+    outs, (lefts, rights, results) = rest[:6], rest[6:]
+    clear(outs)
 
     def advance(slot, carry):
-        first, second = pairs[0, slot, 0], pairs[0, slot, 1]
-        outer, inner = row_shift(second // 8)
-        dy = (first % 8 // 2) ^ y
-        dy = dy ^ (dy >> 1)
-        dc = (first % 8 % 2) ^ c
-        for t in range(4):
-            @pl.when((-outer & 3) == t)
-            def _():
-                lefts[...] = gathered[t][-inner & 3, :, 0:1024]
-        for t in range(2):
-            @pl.when(dc == t)
-            def _():
-                rights[...] = pair_gathered[t][dy]
-        matrix = blocks[slot]
-        direct = lax.dot_general(
-            lefts[...], matrix, (((1,), (1,)), ((), ())), preferred_element_type=jnp.float32
-        )
-        mirror = lax.dot_general(
-            rights[...], matrix, (((1,), (0,)), ((), ())), preferred_element_type=jnp.float32
-        )
-        results[slot, 0] = direct
-        results[slot, 1] = jnp.where(first != second, mirror, 0.0)
-
-        def earlier(before, carry):
-            @pl.when(pairs[0, before, 0] == first)
-            def _():
-                lefts_sum = results[3, 0] + results[before, 0]
-                results[3, 0] = lefts_sum
-
-            @pl.when(pairs[0, before, 1] == second)
-            def _():
-                results[3, 1] = results[3, 1] + results[before, 1]
-
-            return carry
-
-        results[3] = results[slot]
-        lax.fori_loop(0, slot, earlier, 0)
-        for t in range(4):
-            @pl.when(outer == t)
-            def _():
-                if t and not with_gram:
-                    outs[t][inner] = encode(results[3, 1])
-                else:
-                    outs[t][inner] = results[3, 1].astype(outs[t].dtype)
-        for t in range(2):
-            @pl.when(dc == t)
-            def _():
-                if t and not with_gram:
-                    outs[5][dy] = encode(results[3, 0])
-                else:
-                    outs[4 + t][dy, :, 0:1024] = results[3, 0].astype(outs[4 + t].dtype)
+        load_left(pairs, slot, (g0, g1, g2, g3), lefts)
+        load_right(pairs, slot, (h0, h1), rights)
+        direct = multiply(lefts, turned[slot])
+        mirror = multiply(rights, blocks[slot])
+        store_direct(pairs, slot, direct, outs[4:], results, True)
+        store_mirror(pairs, slot, mirror, outs, True)
         return carry
 
-    lax.fori_loop(0, count, advance, 0)
-
-
-def product(pairs, live, blocks, gathered, pair_gathered, with_gram):
-    shape = (4, 32, 1024)
+    lax.fori_loop(0, live[0], advance, 0)
+
+
+def mirror_kernel(pairs, live, blocks, h0, h1, *rest):
+    outs, (rights,) = rest[:4], rest[4:]
+    clear(outs)
+
+    def advance(slot, carry):
+        load_right(pairs, slot, (h0, h1), rights)
+        store_mirror(pairs, slot, multiply(rights, blocks[slot]), outs, False)
+        return carry
+
+    lax.fori_loop(0, live[0], advance, 0)
+
+
+def direct_kernel(pairs, live, turned, g0, g1, g2, g3, after, *rest):
+    outs, (lefts, results) = rest[:3], rest[3:]
+    clear(outs[:2])
+    add_gram((g0, g1, g2, g3), outs[2], outs[1])
+
+    def advance(slot, carry):
+        load_left(pairs, slot, (g0, g1, g2, g3), lefts)
+        store_direct(pairs, slot, multiply(lefts, turned[slot]), outs, results, False)
+        return carry
+
+    lax.fori_loop(0, live[0], advance, 0)
+
+
+PANEL = pltpu.VMEM((32, 1024), jnp.bfloat16)
+RESULTS = pltpu.VMEM((4, 32, 1024), jnp.float32)
+
+
+def product_call(kernel, outs, scratch, name, pairs, live, *arrays):
+    return pl.pallas_call(
+        kernel,
+        out_shape=outs,
+        in_specs=[SMEM, SMEM] + [VMEM] * len(arrays),
+        out_specs=[VMEM] * len(outs),
+        scratch_shapes=scratch,
+        compiler_params=PARAMS,
+        name=name,
+    )(pairs, live, *arrays)
+
+
+def first_product(pairs, live, blocks, turned, gathered, pair_gathered):
     f32 = jnp.float32
-    sent = jnp.bfloat16 if with_gram else f32
-    outs = [struct(shape, f32)] + [struct(shape if with_gram else (4, 32, 1152), sent)] * 3
-    outs += [struct(shape, f32), struct((4, 32, 1152), sent)]
-    outs += [struct((8, 128), f32)] * with_gram
-    return pl.pallas_call(
-        functools.partial(product_kernel, with_gram),
-        out_shape=outs,
-        in_specs=[SMEM, SMEM] + [VMEM] * 7,
-        out_specs=[VMEM] * len(outs),
-        scratch_shapes=[
-            pltpu.VMEM((32, 1024), jnp.bfloat16),
-            pltpu.VMEM((32, 1024), jnp.bfloat16),
-            pltpu.VMEM((4, 2, 32, 1024), f32),
-        ],
-        compiler_params=PARAMS,
-        cost_estimate=pl.CostEstimate(flops=800_000_000, bytes_accessed=10_000_000, transcendentals=0),
-        name="product",
-    )(pairs, live, blocks, *gathered, *pair_gathered)
+    outs = [struct((4, 32, 1024), f32)] + [struct((50, 16, 128), f32)] * 3
+    outs += [struct((4, 32, 1024), f32), struct((4, 32, 1152), f32)]
+    arrays = (blocks, turned, *gathered, *pair_gathered)
+    return product_call(both_kernel, outs, [PANEL, PANEL, RESULTS], "product", pairs, live, *arrays)
+
+
+def second_product(pairs, live, blocks, turned, gathered, pair_gathered):
+    f32, bf16 = jnp.float32, jnp.bfloat16
+    outs = [struct((4, 32, 1024), f32)] + [struct((50, 16, 128), bf16)] * 3
+    rows = product_call(mirror_kernel, outs, [PANEL], "mirror", pairs, live, blocks, *pair_gathered)
+    outs = [struct((4, 32, 1024), f32), struct((4, 32, 1152), bf16), struct((8, 128), f32)]
+    arrays = (turned, *gathered, rows[0])
+    return rows + product_call(direct_kernel, outs, [PANEL, RESULTS], "direct", pairs, live, *arrays)
 
 
 def join_kernel(with_gram, *refs):
     parts, pair, joined, joined_pair = refs[:4], refs[4:6], refs[6], refs[7]
     for k, part in enumerate(parts):
-        joined[k] = part[...]
+        put(joined, k, part[:, 0:1024])
     if with_gram:
         gram = merge(parts[0][:, 1024:1152])
         for part in parts[1:]:
             gram = gram + merge(part[:, 1024:1152])
-        joined[0, :, 1024:1152] = split(gram)
+        put_extra(joined, 4, split(gram))
     for k, part in enumerate(pair):
         joined_pair[k] = part[...]
 
 
 def join(parts, pair, with_gram):
-    shapes = [(4,) + parts[0].shape, (2,) + pair[0].shape]
+    shapes = [(66 if with_gram else 64, 16, 128), (2,) + pair[0].shape]
     return pl.pallas_call(
         functools.partial(join_kernel, with_gram),
         out_shape=[struct(shape, jnp.bfloat16) for shape in shapes],
@@ -245,24 +327,40 @@
     )(own, received, *gram)
 
 
-def row_kernel(own, *refs):
-    received, outs = refs[:3], refs[3:]
-    for k in range(4):
-        value = own[k]
-        for array in received:
-            value = value + decode(array[k])
-        if outs[k].shape[1] > 1024:
-            value = encode(value)
-        outs[k][...] = value.astype(outs[k].dtype)
+def row_kernel(half, own, *refs):
+    received, outs, (weights, total) = refs[:3], refs[3:7], refs[7:]
+    entries = [(array, k) for array in received for k in range(3)]
+    extras = [take_extra(array, 3).astype(jnp.float32) for array in received]
+    for e, (array, k) in enumerate(entries):
+        extra = extras[e // 3]
+        scale = jnp.exp2(extra[:, 8 * k + 4 : 8 * k + 5]) if half else 1.0
+        for s in range(4):
+            weights[4 * e + s] = jnp.broadcast_to(extra[:, 8 * k + s : 8 * k + s + 1] * scale, (32, 128))
+    for i in range(2):
+        rows = slice(16 * i, 16 * i + 16)
+        for j in range(8):
+            columns = slice(128 * j, 128 * j + 128)
+            sums = [own[s, rows, columns] for s in range(4)]
+            for e, (array, k) in enumerate(entries):
+                value = array[16 * k + 8 * i + j].astype(jnp.float32)
+                for s in range(4):
+                    sums[s] = sums[s] + value * weights[4 * e + s, rows]
+            for s in range(4):
+                total[s, rows, columns] = sums[s]
+    outs[0][...] = total[0]
+    for s in range(1, 4):
+        outs[s][...] = encode(total[s]) if half else total[s].astype(outs[s].dtype)
 
 
 def add_outer(own, received):
-    sent = struct(received[0].shape[1:], received[0].dtype)
-    return pl.pallas_call(
-        row_kernel,
+    half = received[0].dtype == jnp.float32
+    sent = struct((32, 1152), jnp.float32) if half else struct((32, 1024), jnp.bfloat16)
+    return pl.pallas_call(
+        functools.partial(row_kernel, half),
         out_shape=[struct((32, 1024), jnp.float32)] + [sent] * 3,
         in_specs=[VMEM] * 4,
         out_specs=[VMEM] * 4,
+        scratch_shapes=[pltpu.VMEM((36, 32, 128), jnp.float32), pltpu.VMEM((4, 32, 1024), jnp.float32)],
         compiler_params=PARAMS,
         name="add_outer",
     )(own, *received)
@@ -446,42 +544,56 @@
 
 
 def scatter(parts):
-    got = [carry(send_outer, parts[s], s) for s in SHIFTS]
+    got = [carry(send_outer, parts[s], s) for s in (1, 2, 3)]
     column, send, *gram = halve(parts[4], carry(send_core, parts[5]), parts[6:])
     column, send, *gram = halve(column, carry(send_y, send, 3), gram)
     along_y = carry(send_y, send, 1)
     row = add_outer(parts[0], got)
-    return [row[0], column] + [carry(send_inner, row[s], s) for s in SHIFTS] + [along_y], gram
-
-
-def hold_kernel(source, target, sem):
-    copy = pltpu.make_async_copy(source, target, sem)
-    copy.start()
-    copy.wait()
+    return [row[0], column] + [carry(send_inner, row[s], s) for s in (1, 2, 3)] + [along_y], gram
+
+
+def hold_kernel(source, target, turned, sems):
+    copies = [pltpu.make_async_copy(source.at[k], target.at[k], sems.at[k]) for k in range(3)]
+    for copy in copies:
+        copy.start()
+    for k, copy in enumerate(copies):
+        copy.wait()
+        turned[k] = target[k].T
 
 
 def hold(blocks):
     return pl.pallas_call(
         hold_kernel,
-        out_shape=struct(blocks.shape, blocks.dtype),
+        out_shape=[struct(blocks.shape, blocks.dtype)] * 2,
         in_specs=[pl.BlockSpec(memory_space=pl.ANY)],
-        out_specs=VMEM,
-        scratch_shapes=[pltpu.SemaphoreType.DMA(())],
+        out_specs=[VMEM] * 2,
+        scratch_shapes=[pltpu.SemaphoreType.DMA((3,))],
         compiler_params=PARAMS,
         cost_estimate=pl.CostEstimate(flops=0, bytes_accessed=6_000_000, transcendentals=0),
         name="hold",
     )(blocks)
 
 
+def load(panel):
+    return pl.pallas_call(
+        lambda source, target: target.__setitem__(..., source[...]),
+        out_shape=struct(panel.shape, panel.dtype),
+        in_specs=[VMEM],
+        out_specs=VMEM,
+        compiler_params=PARAMS,
+        name="load",
+    )(panel)
+
+
 def on_device(block_pairs, live_counts, pair_blocks, start_basis):
     users = 128 * start_basis.shape[2]
     root = float(users) ** 0.5
-    pair_blocks = hold(pair_blocks)
+    pair_blocks, turned = hold(pair_blocks)
     gathered, pair_gathered = gather(start_basis[0], start_basis[0], False)
-    parts = product(block_pairs, live_counts, pair_blocks, gathered, pair_gathered, False)
+    parts = first_product(block_pairs, live_counts, pair_blocks, turned, gathered, pair_gathered)
     first, panel, own = finish_first(scatter(parts)[0])
     gathered, pair_gathered = gather(panel, own, True)
-    parts = product(block_pairs, live_counts, pair_blocks, gathered, pair_gathered, True)
+    parts = second_product(block_pairs, live_counts, pair_blocks, turned, gathered, pair_gathered)
     parts, (gram,) = scatter(parts)
     first_basis, inverse = factor_first(gram, parts[5], first, root)
     scaled, tiles = finish_second(parts, inverse)

time: 123 us -> 120 us (0.976)
  waiting for transfers between devices: 46.9 us -> 33.6 us
  starting transfers between devices: 36.1 us -> 41.3 us
  blocking collectives: 17 us -> 20.5 us
  Pallas kernels: 15.7 us -> 18 us
    ppermute x37, waiting for transfers between devices: 46.9 us -> 33.6 us  [permute(): return lax.ppermute(value, AXES, pairs)]
    ppermute x37, starting transfers between devices: 36.1 us -> 41.3 us  [permute(): return lax.ppermute(value, AXES, pairs)]
    all_to_all x1, blocking collectives: 17 us -> 20.5 us  [total_gram(): return lax.all_to_all(tiles, ('z', 'x', 'y'), 0, 0, tiled=True)]
    pallas_call x5 -> x6, Pallas kernels: 10.3 us -> 12.6 us  [the longest x3 8.76 us: product_call(): pl.pallas_call(kernel, out_shape=outs, in_specs=[SMEM, SMEM] + [VMEM] * l...]
  transfers between devices with their start and end apart: 37 -> 37, of which waited for: 23 -> 21; matrix products, arithmetic and copies ran while one was open for 1% -> 1% of each run, Pallas kernels for 3% -> 7%
where the time goes in v4:
time: 120 us
  starting transfers between devices  41.3 us (34%)
  waiting for transfers between devices  33.6 us (28%)
  blocking collectives  20.5 us (17%)
  Pallas kernels  18 us (15%)
  local copies, waits for them, and re-layouts  4.43 us (4%)
  between operations  1.63 us (1%)
    ppermute x37, starting transfers between devices, permute(): return lax.ppermute(value, AXES, pairs)  41.3 us
    ppermute x37, waiting for transfers between devices, permute(): return lax.ppermute(value, AXES, pairs)  33.6 us
    all_to_all x1, blocking collectives, total_gram(): return lax.all_to_all(tiles, ('z', 'x', 'y'), 0, 0, tiled=True)  20.5 us
    pallas_call x3, Pallas kernels, product_call(): pl.pallas_call(kernel, out_shape=outs, in_specs=[SMEM, SMEM] + [VMEM] * l...  8.76 us
    unnamed x7, local copies, waits for them, and re-layouts  4.41 us
  transfers between devices with their start and end apart: 37, of which 21 were waited for; matrix products, arithmetic and copies ran while one was open for 1% of the time, Pallas kernels for 7%

profile of v4, /device:TPU:0, one launch (start us, length us, event | category | flops | bytes accessed | tf_op | source)
XLA Modules:
  0.0 119.8 jit_solution(14337408192729958659)
XLA Ops:
  0.6 1.7 %collective-permute-start.3 = (bf16[32,1024]{1,0:T(8,128)(2,1)}, bf16[32,1024]{1,0:T(8,128)(2,1)S(1)}, u32[]{:S(2)}, u32[]{:S(2)}) collective-permute-start(bf16[32,1024]{1,0:T(8,128)(2,1)} %bitcast.3), channel_id=1, source_target_pairs={{0,2},{1,7},{2,0},{3,5},{4,6},{5,3},{6,4},{7,1},{8,10},{9,15},{10,... | collective-permute-start | bytes 196616 | tf_op jit(solution)/shard_map/ppermute | solution.py:24
  2.4 4.0 %collective-permute-start.2 = (bf16[32,1024]{1,0:T(8,128)(2,1)}, bf16[32,1024]{1,0:T(8,128)(2,1)S(1)}, u32[]{:S(2)}, u32[]{:S(2)}) collective-permute-start(bf16[32,1024]{1,0:T(8,128)(2,1)} %bitcast.4), channel_id=1, source_target_pairs={{0,96},{1,25},{2,98},{3,27},{4,100},{5,29},{6,102},{7,31},{8,104},... | collective-permute-start | bytes 196616 | tf_op jit(solution)/shard_map/ppermute | solution.py:24
  6.4 1.3 %collective-permute-start = (bf16[32,1024]{1,0:T(8,128)(2,1)}, bf16[32,1024]{1,0:T(8,128)(2,1)S(1)}, u32[]{:S(2)}, u32[]{:S(2)}) collective-permute-start(bf16[32,1024]{1,0:T(8,128)(2,1)} %bitcast.6), channel_id=1, source_target_pairs={{0,32},{1,9},{2,34},{3,11},{4,36},{5,13},{6,38},{7,15},{8,40},{9,1... | collective-permute-start | bytes 196616 | tf_op jit(solution)/shard_map/ppermute | solution.py:24
  7.7 1.0 collective-permute-done.2.refs_3_
  8.6 3.9 %collective-permute-done.1.refs_2_ = bf16[32,1024]{1,0:T(8,128)(2,1)S(1)} collective-permute-done((bf16[32,1024]{1,0:T(8,128)(2,1)}, bf16[32,1024]{1,0:T(8,128)(2,1)S(1)}, u32[]{:S(2)}, u32[]{:S(2)}) %collective-permute-start.1) | collective-permute-done | bytes 65568 | tf_op jit(solution)/shard_map/ppermute | solution.py:24
  12.8 0.8 copy-done.1
  13.7 2.3 %collective-permute-start.7 = (bf16[2,32,1024]{2,1,0:T(8,128)(2,1)S(1)}, bf16[2,32,1024]{2,1,0:T(8,128)(2,1)S(1)}, u32[]{:S(2)}, u32[]{:S(2)}) collective-permute-start(bf16[2,32,1024]{2,1,0:T(8,128)(2,1)S(1)} %get-tuple-element.49), channel_id=1, source_target_pairs={{0,6},{1,3},{2,4},{3,1},{4,2},{5,7},{6,0},{7,5},{8,14},{9,11},{10,... | collective-permute-start | bytes 393224 | tf_op jit(solution)/shard_map/ppermute | solution.py:24
  15.9 2.8 %collective-permute-start.6 = (bf16[64,16,128]{2,1,0:T(8,128)(2,1)S(1)}, bf16[64,16,128]{2,1,0:T(8,128)(2,1)S(1)}, u32[]{:S(2)}, u32[]{:S(2)}) collective-permute-start(bf16[64,16,128]{2,1,0:T(8,128)(2,1)S(1)} %get-tuple-element.48.g0), channel_id=1, source_target_pairs={{0,24},{1,97},{2,26},{3,99},{4,28},{5,101},{6,30},{7,103},{8,0},{9... | collective-permute-start | bytes 786440 | tf_op jit(solution)/shard_map/ppermute | solution.py:24
  18.7 0.8 collective-permute-start.5
  19.5 0.9 collective-permute-start.4
  21.2 0.8 copy.8.pairs
  21.9 2.8 %copy-done = bf16[3,1024,1024]{2,1,0:T(8,128)(2,1)S(1)} copy-done((bf16[3,1024,1024]{2,1,0:T(8,128)(2,1)S(1)}, bf16[3,1024,1024]{2,1,0:T(8,128)(2,1)}, u32[]{:S(2)}) %copy-start) | copy-done | bytes 6291480
  24.7 2.4 %hold.1 = (bf16[3,1024,1024]{2,1,0:T(8,128)(2,1)S(1)}, bf16[3,1024,1024]{2,1,0:T(8,128)(2,1)S(1)}) custom-call(bf16[3,1024,1024]{2,1,0:T(8,128)(2,1)S(1)} %copy-done), custom_call_target="tpu_custom_call" | custom-call | bytes 6000000 | tf_op jit(solution)/shard_map/hold/pallas_call | solution.py:565
  27.1 2.3 %collective-permute-done.4.g1 = bf16[64,16,128]{2,1,0:T(8,128)(2,1)S(1)} collective-permute-done((bf16[64,16,128]{2,1,0:T(8,128)(2,1)S(1)}, bf16[64,16,128]{2,1,0:T(8,128)(2,1)S(1)}, u32[]{:S(2)}, u32[]{:S(2)}) %collective-permute-start.4) | collective-permute-done | bytes 262176 | tf_op jit(solution)/shard_map/ppermute | solution.py:24
  29.4 4.2 %product.1 = (f32[4,32,1024]{2,1,0:T(8,128)S(1)}, f32[50,16,128]{2,1,0:T(8,128)S(1)}, f32[50,16,128]{2,1,0:T(8,128)S(1)}, f32[50,16,128]{2,1,0:T(8,128)S(1)}, f3...) custom-call(s32[1,3,2]{2,1,0:T(4,128)S(1)} %copy.8.pairs, s32[1]{0:T(128)S(6)} %copy.11.live, ...), custom_call_target="tpu_custom_call" | custom-call | tf_op jit(solution)/shard_map/product/pallas_call | solution.py:243
  34.5 1.5 %collective-permute-start.9 = (f16[50,16,128]{2,1,0:T(8,128)(2,1)S(1)}, f16[50,16,128]{2,1,0:T(8,128)(2,1)S(1)}, u32[]{:S(2)}, u32[]{:S(2)}) collective-permute-start(f16[50,16,128]{2,1,0:T(8,128)(2,1)S(1)} %convert_element_type.54), channel_id=1, source_target_pairs={{0,8},{1,33},{2,10},{3,35},{4,12},{5,37},{6,14},{7,39},{8,16},{9,4... | collective-permute-start | bytes 614408 | tf_op jit(solution)/shard_map/ppermute | solution.py:24
  36.3 2.5 %collective-permute-start.13 = (f16[2,32,1152]{2,1,0:T(8,128)(2,1)S(1)}, f16[2,32,1152]{2,1,0:T(8,128)(2,1)S(1)}, u32[]{:S(2)}, u32[]{:S(2)}) collective-permute-start(f16[2,32,1152]{2,1,0:T(8,128)(2,1)S(1)} %convert_element_type.62), channel_id=1, source_target_pairs={{0,6},{1,3},{2,4},{3,1},{4,2},{5,7},{6,0},{7,5},{8,14},{9,11},{10,... | collective-permute-start | bytes 442376 | tf_op jit(solution)/shard_map/ppermute | solution.py:24
  38.8 0.9 collective-permute-done.11
  39.7 2.2 %collective-permute-done.10 = f16[50,16,128]{2,1,0:T(8,128)(2,1)S(1)} collective-permute-done((f16[50,16,128]{2,1,0:T(8,128)(2,1)S(1)}, f16[50,16,128]{2,1,0:T(8,128)(2,1)S(1)}, u32[]{:S(2)}, u32[]{:S(2)}) %collective-permute-start.10) | collective-permute-done | bytes 204832 | tf_op jit(solution)/shard_map/ppermute | solution.py:24
  41.9 2.1 %collective-permute-done.9 = f16[50,16,128]{2,1,0:T(8,128)(2,1)S(1)} collective-permute-done((f16[50,16,128]{2,1,0:T(8,128)(2,1)S(1)}, f16[50,16,128]{2,1,0:T(8,128)(2,1)S(1)}, u32[]{:S(2)}, u32[]{:S(2)}) %collective-permute-start.9) | collective-permute-done | bytes 204832 | tf_op jit(solution)/shard_map/ppermute | solution.py:24
  44.0 1.0 add_outer.2
  45.1 1.7 %collective-permute-start.15 = (f16[32,1152]{1,0:T(8,128)(2,1)S(1)}, f16[32,1152]{1,0:T(8,128)(2,1)S(1)}, u32[]{:S(2)}, u32[]{:S(2)}) collective-permute-start(f16[32,1152]{1,0:T(8,128)(2,1)S(1)} %convert_element_type.66), channel_id=1, source_target_pairs={{0,64},{1,17},{2,66},{3,19},{4,68},{5,21},{6,70},{7,23},{8,72},{9,... | collective-permute-start | bytes 221192 | tf_op jit(solution)/shard_map/ppermute | solution.py:24
  46.8 1.3 %collective-permute-start.14 = (f16[32,1152]{1,0:T(8,128)(2,1)S(1)}, f16[32,1152]{1,0:T(8,128)(2,1)S(1)}, u32[]{:S(2)}, u32[]{:S(2)}) collective-permute-start(f16[32,1152]{1,0:T(8,128)(2,1)S(1)} %convert_element_type.64), channel_id=1, source_target_pairs={{0,32},{1,9},{2,34},{3,11},{4,36},{5,13},{6,38},{7,15},{8,40},{9,1... | collective-permute-start | bytes 221192 | tf_op jit(solution)/shard_map/ppermute | solution.py:24
  49.5 1.6 %collective-permute-done.15 = f16[32,1152]{1,0:T(8,128)(2,1)S(1)} collective-permute-done((f16[32,1152]{1,0:T(8,128)(2,1)S(1)}, f16[32,1152]{1,0:T(8,128)(2,1)S(1)}, u32[]{:S(2)}, u32[]{:S(2)}) %collective-permute-start.15) | collective-permute-done | bytes 73760 | tf_op jit(solution)/shard_map/ppermute | solution.py:24
  51.0 1.3 %collective-permute-done.14 = f16[32,1152]{1,0:T(8,128)(2,1)S(1)} collective-permute-done((f16[32,1152]{1,0:T(8,128)(2,1)S(1)}, f16[32,1152]{1,0:T(8,128)(2,1)S(1)}, u32[]{:S(2)}, u32[]{:S(2)}) %collective-permute-start.14) | collective-permute-done | bytes 73760 | tf_op jit(solution)/shard_map/ppermute | solution.py:24
  53.1 1.9 %collective-permute-start.20 = (bf16[32,1152]{1,0:T(8,128)(2,1)S(1)}, bf16[32,1152]{1,0:T(8,128)(2,1)S(1)}, u32[]{:S(2)}, u32[]{:S(2)}) collective-permute-start(bf16[32,1152]{1,0:T(8,128)(2,1)S(1)} %get-tuple-element.64.refs_0_), channel_id=1, source_target_pairs={{0,96},{1,25},{2,98},{3,27},{4,100},{5,29},{6,102},{7,31},{8,104},... | collective-permute-start | bytes 221192 | tf_op jit(solution)/shard_map/ppermute | solution.py:24
  55.1 1.3 %collective-permute-start.19 = (bf16[32,1152]{1,0:T(8,128)(2,1)S(1)}, bf16[32,1152]{1,0:T(8,128)(2,1)S(1)}, u32[]{:S(2)}, u32[]{:S(2)}) collective-permute-start(bf16[32,1152]{1,0:T(8,128)(2,1)S(1)} %get-tuple-element.64.refs_0_), channel_id=1, source_target_pairs={{0,64},{1,17},{2,66},{3,19},{4,68},{5,21},{6,70},{7,23},{8,72},{9,... | collective-permute-start | bytes 221192 | tf_op jit(solution)/shard_map/ppermute | solution.py:24
  56.4 1.3 %collective-permute-start.18 = (bf16[32,1152]{1,0:T(8,128)(2,1)S(1)}, bf16[32,1152]{1,0:T(8,128)(2,1)S(1)}, u32[]{:S(2)}, u32[]{:S(2)}) collective-permute-start(bf16[32,1152]{1,0:T(8,128)(2,1)S(1)} %get-tuple-element.64.refs_0_), channel_id=1, source_target_pairs={{0,32},{1,9},{2,34},{3,11},{4,36},{5,13},{6,38},{7,15},{8,40},{9,1... | collective-permute-start | bytes 221192 | tf_op jit(solution)/shard_map/ppermute | solution.py:24
  58.1 3.9 %collective-permute-done.21.refs_5_ = bf16[32,1024]{1,0:T(8,128)(2,1)S(1)} collective-permute-done((bf16[32,1024]{1,0:T(8,128)(2,1)S(1)}, bf16[32,1024]{1,0:T(8,128)(2,1)S(1)}, u32[]{:S(2)}, u32[]{:S(2)}) %collective-permute-start.21) | collective-permute-done | bytes 65568 | tf_op jit(solution)/shard_map/ppermute | solution.py:24
  62.0 1.9 %collective-permute-start.25 = (bf16[2,32,1024]{2,1,0:T(8,128)(2,1)S(1)}, bf16[2,32,1024]{2,1,0:T(8,128)(2,1)S(1)}, u32[]{:S(2)}, u32[]{:S(2)}) collective-permute-start(bf16[2,32,1024]{2,1,0:T(8,128)(2,1)S(1)} %get-tuple-element.67), channel_id=1, source_target_pairs={{0,6},{1,3},{2,4},{3,1},{4,2},{5,7},{6,0},{7,5},{8,14},{9,11},{10,... | collective-permute-start | bytes 393224 | tf_op jit(solution)/shard_map/ppermute | solution.py:24
  64.5 0.8 collective-permute-start.23
  65.3 0.9 collective-permute-start.22
  66.2 2.1 %collective-permute-done.25 = bf16[2,32,1024]{2,1,0:T(8,128)(2,1)S(1)} collective-permute-done((bf16[2,32,1024]{2,1,0:T(8,128)(2,1)S(1)}, bf16[2,32,1024]{2,1,0:T(8,128)(2,1)S(1)}, u32[]{:S(2)}, u32[]{:S(2)}) %collective-permute-start.25) | collective-permute-done | bytes 131104 | tf_op jit(solution)/shard_map/ppermute | solution.py:24
  68.4 1.5 %collective-permute-done.26.h1 = bf16[4,32,1024]{2,1,0:T(8,128)(2,1)S(1)} collective-permute-done((bf16[4,32,1024]{2,1,0:T(8,128)(2,1)S(1)}, bf16[4,32,1024]{2,1,0:T(8,128)(2,1)S(1)}, u32[]{:S(2)}, u32[]{:S(2)}) %collective-permute-start.26) | collective-permute-done | bytes 262176 | tf_op jit(solution)/shard_map/ppermute | solution.py:24
  69.9 2.2 %mirror.1 = (f32[4,32,1024]{2,1,0:T(8,128)S(1)}, bf16[50,16,128]{2,1,0:T(8,128)(2,1)S(1)}, bf16[50,16,128]{2,1,0:T(8,128)(2,1)S(1)}, bf16[50,16,128]{2,1,0:T(8,128)(2,1)S(1)}) custom-call(s32[1,3,2]{2,1,0:T(4,128)S(1)} %copy.8.pairs, s32[1]{0:T(128)S(6)} %copy.11.live, bf16[3,1024,1024]{2,1,0:T(8,128)(2,1)S(1)} %get-tuple-element.47.blocks, ...), custom_call_target="tpu_custom_call" | custom-call | tf_op jit(solution)/shard_map/mirror/pallas_call | solution.py:243
  72.6 2.8 %collective-permute-done.22.g1 = bf16[66,16,128]{2,1,0:T(8,128)(2,1)S(1)} collective-permute-done((bf16[66,16,128]{2,1,0:T(8,128)(2,1)S(1)}, bf16[66,16,128]{2,1,0:T(8,128)(2,1)S(1)}, u32[]{:S(2)}, u32[]{:S(2)}) %collective-permute-start.22) | collective-permute-done | bytes 270368 | tf_op jit(solution)/shard_map/ppermute | solution.py:24
  75.4 2.3 %direct.1 = (f32[4,32,1024]{2,1,0:T(8,128)S(1)}, bf16[4,32,1152]{2,1,0:T(8,128)(2,1)S(1)}, f32[8,128]{1,0:T(8,128)S(1)}) custom-call(s32[1,3,2]{2,1,0:T(4,128)S(1)} %copy.8.pairs, s32[1]{0:T(128)S(6)} %copy.11.live, bf16[3,1024,1024]{2,1,0:T(8,128)(2,1)S(1)} %get-tuple-element.46.turned, bf16[66,16,128]{2,1,0:T(8,128)(2,1)S(1)} %get-tuple-element.66.g0, ...), custom_call_target="tpu_custom_call" | custom-call | tf_op jit(solution)/shard_map/direct/pallas_call | solution.py:243
  77.9 0.9 collective-permute-start.31
  78.8 2.3 %collective-permute-start.32 = (bf16[50,16,128]{2,1,0:T(8,128)(2,1)S(1)}, bf16[50,16,128]{2,1,0:T(8,128)(2,1)S(1)}, u32[]{:S(2)}, u32[]{:S(2)}) collective-permute-start(bf16[50,16,128]{2,1,0:T(8,128)(2,1)S(1)} %get-tuple-element.81), channel_id=1, source_target_pairs={{0,24},{1,97},{2,26},{3,99},{4,28},{5,101},{6,30},{7,103},{8,0},{9... | collective-permute-start | bytes 614408 | tf_op jit(solution)/shard_map/ppermute | solution.py:24
  81.2 1.5 %collective-permute-start.28 = (bf16[2,32,1152]{2,1,0:T(8,128)(2,1)S(1)}, bf16[2,32,1152]{2,1,0:T(8,128)(2,1)S(1)}, u32[]{:S(2)}, u32[]{:S(2)}) collective-permute-start(bf16[2,32,1152]{2,1,0:T(8,128)(2,1)S(1)} %get-tuple-element.73), channel_id=1, source_target_pairs={{0,6},{1,3},{2,4},{3,1},{4,2},{5,7},{6,0},{7,5},{8,14},{9,11},{10,... | collective-permute-start | bytes 442376 | tf_op jit(solution)/shard_map/ppermute | solution.py:24
  82.7 4.9 %collective-permute-done.28.received = bf16[2,32,1152]{2,1,0:T(8,128)(2,1)S(1)} collective-permute-done((bf16[2,32,1152]{2,1,0:T(8,128)(2,1)S(1)}, bf16[2,32,1152]{2,1,0:T(8,128)(2,1)S(1)}, u32[]{:S(2)}, u32[]{:S(2)}) %collective-permute-start.28) | collective-permute-done | bytes 147488 | tf_op jit(solution)/shard_map/ppermute | solution.py:24
  88.5 1.2 %collective-permute-start.33 = (bf16[32,1024]{1,0:T(8,128)(2,1)S(1)}, bf16[32,1024]{1,0:T(8,128)(2,1)S(1)}, u32[]{:S(2)}, u32[]{:S(2)}) collective-permute-start(bf16[32,1024]{1,0:T(8,128)(2,1)S(1)} %get-tuple-element.84), channel_id=1, source_target_pairs={{0,32},{1,9},{2,34},{3,11},{4,36},{5,13},{6,38},{7,15},{8,40},{9,1... | collective-permute-start | bytes 196616 | tf_op jit(solution)/shard_map/ppermute | solution.py:24
  89.7 0.9 collective-permute-start.34
  90.6 2.5 %collective-permute-start.35 = (bf16[32,1024]{1,0:T(8,128)(2,1)S(1)}, bf16[32,1024]{1,0:T(8,128)(2,1)S(1)}, u32[]{:S(2)}, u32[]{:S(2)}) collective-permute-start(bf16[32,1024]{1,0:T(8,128)(2,1)S(1)} %get-tuple-element.86), channel_id=1, source_target_pairs={{0,96},{1,25},{2,98},{3,27},{4,100},{5,29},{6,102},{7,31},{8,104},... | collective-permute-start | bytes 196616 | tf_op jit(solution)/shard_map/ppermute | solution.py:24
  93.2 1.9 %factor_first.1 = (f32[32,1024]{1,0:T(8,128)}, f32[32,32]{1,0:T(8,128)S(1)}) custom-call(f32[8,128]{1,0:T(8,128)S(1)} %get-tuple-element.75.gram, bf16[1,32,1152]{2,1,0:T(8,128)(2,1)S(1)} %collective-permute-done.29.received.refs_5_, f32[32,1024]{1,0:T(8,128)S(1)} %get-tuple-element.77.panel), custom_call_target="tpu_custom_call" | custom-call | flops 1000000 | bytes 10000000 | tf_op jit(solution)/shard_map/factor_first/pallas_call | solution.py:509
  96.2 1.2 collective-permute-done.36.other
  97.3 20.5 %all_to_all.5.gram = f32[64,8,128]{2,1,0:T(8,128)S(1)} all-to-all(f32[64,8,128]{2,1,0:T(8,128)S(1)} %total_gram.1), channel_id=1, replica_groups=mesh['z'=4,'x'=4,'y'=4,'core'=2] {'z','x','y'}, dimensions={0} | all-to-all | bytes 524288 | tf_op jit(solution)/shard_map/all_to_all | solution.py:446
  117.8 2.0 %factor_second.1 = f32[32,1024]{1,0:T(8,128)} custom-call(f32[64,8,128]{2,1,0:T(8,128)S(1)} %all_to_all.5.gram, f32[32,1024]{1,0:T(8,128)S(1)} %get-tuple-element.89.panel), custom_call_target="tpu_custom_call" | custom-call | tf_op jit(solution)/shard_map/factor_second/pallas_call | solution.py:521
  (71 shorter events, 7.6 us)
Async XLA Ops:
  0.6 7.0 %collective-permute-start.3 = (bf16[32,1024]{1,0:T(8,128)(2,1)}, bf16[32,1024]{1,0:T(8,128)(2,1)S(1)}, u32[]{:S(2)}, u32[]{:S(2)}) collective-permute-start(bf16[32,1024]{1,0:T(8,128)(2,1)} %bitcast.3), channel_id=1, source_target_pairs={{0,2},{1,7},{2,0},{3,5},{4,6},{5,3},{6,4},{7,1},{8,10},{9,15},{10,... | collective-permute-start | bytes 196616 | tf_op jit(solution)/shard_map/ppermute | solution.py:24
  2.4 6.3 %collective-permute-start.2 = (bf16[32,1024]{1,0:T(8,128)(2,1)}, bf16[32,1024]{1,0:T(8,128)(2,1)S(1)}, u32[]{:S(2)}, u32[]{:S(2)}) collective-permute-start(bf16[32,1024]{1,0:T(8,128)(2,1)} %bitcast.4), channel_id=1, source_target_pairs={{0,96},{1,25},{2,98},{3,27},{4,100},{5,29},{6,102},{7,31},{8,104},... | collective-permute-start | bytes 196616 | tf_op jit(solution)/shard_map/ppermute | solution.py:24
  6.4 6.1 %collective-permute-start.1 = (bf16[32,1024]{1,0:T(8,128)(2,1)}, bf16[32,1024]{1,0:T(8,128)(2,1)S(1)}, u32[]{:S(2)}, u32[]{:S(2)}) collective-permute-start(bf16[32,1024]{1,0:T(8,128)(2,1)} %bitcast.5), channel_id=1, source_target_pairs={{0,64},{1,17},{2,66},{3,19},{4,68},{5,21},{6,70},{7,23},{8,72},{9,... | collective-permute-start | bytes 196616 | tf_op jit(solution)/shard_map/ppermute | solution.py:24
  6.4 6.4 %collective-permute-start = (bf16[32,1024]{1,0:T(8,128)(2,1)}, bf16[32,1024]{1,0:T(8,128)(2,1)S(1)}, u32[]{:S(2)}, u32[]{:S(2)}) collective-permute-start(bf16[32,1024]{1,0:T(8,128)(2,1)} %bitcast.6), channel_id=1, source_target_pairs={{0,32},{1,9},{2,34},{3,11},{4,36},{5,13},{6,38},{7,15},{8,40},{9,1... | collective-permute-start | bytes 196616 | tf_op jit(solution)/shard_map/ppermute | solution.py:24
  12.8 0.8 copy-start.1
  13.7 6.7 %collective-permute-start.7 = (bf16[2,32,1024]{2,1,0:T(8,128)(2,1)S(1)}, bf16[2,32,1024]{2,1,0:T(8,128)(2,1)S(1)}, u32[]{:S(2)}, u32[]{:S(2)}) collective-permute-start(bf16[2,32,1024]{2,1,0:T(8,128)(2,1)S(1)} %get-tuple-element.49), channel_id=1, source_target_pairs={{0,6},{1,3},{2,4},{3,1},{4,2},{5,7},{6,0},{7,5},{8,14},{9,11},{10,... | collective-permute-start | bytes 393224 | tf_op jit(solution)/shard_map/ppermute | solution.py:24
  15.9 11.2 %collective-permute-start.6 = (bf16[64,16,128]{2,1,0:T(8,128)(2,1)S(1)}, bf16[64,16,128]{2,1,0:T(8,128)(2,1)S(1)}, u32[]{:S(2)}, u32[]{:S(2)}) collective-permute-start(bf16[64,16,128]{2,1,0:T(8,128)(2,1)S(1)} %get-tuple-element.48.g0), channel_id=1, source_target_pairs={{0,24},{1,97},{2,26},{3,99},{4,28},{5,101},{6,30},{7,103},{8,0},{9... | collective-permute-start | bytes 786440 | tf_op jit(solution)/shard_map/ppermute | solution.py:24
  18.7 8.4 %collective-permute-start.5 = (bf16[64,16,128]{2,1,0:T(8,128)(2,1)S(1)}, bf16[64,16,128]{2,1,0:T(8,128)(2,1)S(1)}, u32[]{:S(2)}, u32[]{:S(2)}) collective-permute-start(bf16[64,16,128]{2,1,0:T(8,128)(2,1)S(1)} %get-tuple-element.48.g0), channel_id=1, source_target_pairs={{0,16},{1,65},{2,18},{3,67},{4,20},{5,69},{6,22},{7,71},{8,24},{9,... | collective-permute-start | bytes 786440 | tf_op jit(solution)/shard_map/ppermute | solution.py:24
  19.5 9.9 %collective-permute-start.4 = (bf16[64,16,128]{2,1,0:T(8,128)(2,1)S(1)}, bf16[64,16,128]{2,1,0:T(8,128)(2,1)S(1)}, u32[]{:S(2)}, u32[]{:S(2)}) collective-permute-start(bf16[64,16,128]{2,1,0:T(8,128)(2,1)S(1)} %get-tuple-element.48.g0), channel_id=1, source_target_pairs={{0,8},{1,33},{2,10},{3,35},{4,12},{5,37},{6,14},{7,39},{8,16},{9,4... | collective-permute-start | bytes 786440 | tf_op jit(solution)/shard_map/ppermute | solution.py:24
  20.4 9.0 %collective-permute-start.8 = (bf16[4,32,1024]{2,1,0:T(8,128)(2,1)S(1)}, bf16[4,32,1024]{2,1,0:T(8,128)(2,1)S(1)}, u32[]{:S(2)}, u32[]{:S(2)}) collective-permute-start(bf16[4,32,1024]{2,1,0:T(8,128)(2,1)S(1)} %constant_dynamic-update-slice_fusion.h0), channel_id=1, source_target_pairs={{0,1},{1,0},{2,3},{3,2},{4,5},{5,4},{6,7},{7,6},{8,9},{9,8},{10,11... | collective-permute-start | bytes 786440 | tf_op jit(solution)/shard_map/ppermute | solution.py:24
  21.9 2.8 %copy-start = (bf16[3,1024,1024]{2,1,0:T(8,128)(2,1)S(1)}, bf16[3,1024,1024]{2,1,0:T(8,128)(2,1)}, u32[]{:S(2)}) copy-start(bf16[3,1024,1024]{2,1,0:T(8,128)(2,1)} %source.1) | copy-start | bytes 18874372
  33.6 2.4 %collective-permute-start.12 = (f16[4,32,1152]{2,1,0:T(8,128)(2,1)S(1)}, f16[4,32,1152]{2,1,0:T(8,128)(2,1)S(1)}, u32[]{:S(2)}, u32[]{:S(2)}) collective-permute-start(f16[4,32,1152]{2,1,0:T(8,128)(2,1)S(1)} %convert_element_type.60), channel_id=1, source_target_pairs={{0,1},{1,0},{2,3},{3,2},{4,5},{5,4},{6,7},{7,6},{8,9},{9,8},{10,11... | collective-permute-start | bytes 884744 | tf_op jit(solution)/shard_map/ppermute | solution.py:24
  33.8 5.8 %collective-permute-start.11 = (f16[50,16,128]{2,1,0:T(8,128)(2,1)S(1)}, f16[50,16,128]{2,1,0:T(8,128)(2,1)S(1)}, u32[]{:S(2)}, u32[]{:S(2)}) collective-permute-start(f16[50,16,128]{2,1,0:T(8,128)(2,1)S(1)} %convert_element_type.58), channel_id=1, source_target_pairs={{0,24},{1,97},{2,26},{3,99},{4,28},{5,101},{6,30},{7,103},{8,0},{9... | collective-permute-start | bytes 614408 | tf_op jit(solution)/shard_map/ppermute | solution.py:24
  34.5 7.4 %collective-permute-start.10 = (f16[50,16,128]{2,1,0:T(8,128)(2,1)S(1)}, f16[50,16,128]{2,1,0:T(8,128)(2,1)S(1)}, u32[]{:S(2)}, u32[]{:S(2)}) collective-permute-start(f16[50,16,128]{2,1,0:T(8,128)(2,1)S(1)} %convert_element_type.56), channel_id=1, source_target_pairs={{0,16},{1,65},{2,18},{3,67},{4,20},{5,69},{6,22},{7,71},{8,24},{9,... | collective-permute-start | bytes 614408 | tf_op jit(solution)/shard_map/ppermute | solution.py:24
  34.5 9.4 %collective-permute-start.9 = (f16[50,16,128]{2,1,0:T(8,128)(2,1)S(1)}, f16[50,16,128]{2,1,0:T(8,128)(2,1)S(1)}, u32[]{:S(2)}, u32[]{:S(2)}) collective-permute-start(f16[50,16,128]{2,1,0:T(8,128)(2,1)S(1)} %convert_element_type.54), channel_id=1, source_target_pairs={{0,8},{1,33},{2,10},{3,35},{4,12},{5,37},{6,14},{7,39},{8,16},{9,4... | collective-permute-start | bytes 614408 | tf_op jit(solution)/shard_map/ppermute | solution.py:24
  36.3 11.8 %collective-permute-start.13 = (f16[2,32,1152]{2,1,0:T(8,128)(2,1)S(1)}, f16[2,32,1152]{2,1,0:T(8,128)(2,1)S(1)}, u32[]{:S(2)}, u32[]{:S(2)}) collective-permute-start(f16[2,32,1152]{2,1,0:T(8,128)(2,1)S(1)} %convert_element_type.62), channel_id=1, source_target_pairs={{0,6},{1,3},{2,4},{3,1},{4,2},{5,7},{6,0},{7,5},{8,14},{9,11},{10,... | collective-permute-start | bytes 442376 | tf_op jit(solution)/shard_map/ppermute | solution.py:24
  45.0 4.4 %collective-permute-start.16 = (f16[32,1152]{1,0:T(8,128)(2,1)S(1)}, f16[32,1152]{1,0:T(8,128)(2,1)S(1)}, u32[]{:S(2)}, u32[]{:S(2)}) collective-permute-start(f16[32,1152]{1,0:T(8,128)(2,1)S(1)} %convert_element_type.68), channel_id=1, source_target_pairs={{0,96},{1,25},{2,98},{3,27},{4,100},{5,29},{6,102},{7,31},{8,104},... | collective-permute-start | bytes 221192 | tf_op jit(solution)/shard_map/ppermute | solution.py:24
  45.1 5.9 %collective-permute-start.15 = (f16[32,1152]{1,0:T(8,128)(2,1)S(1)}, f16[32,1152]{1,0:T(8,128)(2,1)S(1)}, u32[]{:S(2)}, u32[]{:S(2)}) collective-permute-start(f16[32,1152]{1,0:T(8,128)(2,1)S(1)} %convert_element_type.66), channel_id=1, source_target_pairs={{0,64},{1,17},{2,66},{3,19},{4,68},{5,21},{6,70},{7,23},{8,72},{9,... | collective-permute-start | bytes 221192 | tf_op jit(solution)/shard_map/ppermute | solution.py:24
  46.8 5.6 %collective-permute-start.14 = (f16[32,1152]{1,0:T(8,128)(2,1)S(1)}, f16[32,1152]{1,0:T(8,128)(2,1)S(1)}, u32[]{:S(2)}, u32[]{:S(2)}) collective-permute-start(f16[32,1152]{1,0:T(8,128)(2,1)S(1)} %convert_element_type.64), channel_id=1, source_target_pairs={{0,32},{1,9},{2,34},{3,11},{4,36},{5,13},{6,38},{7,15},{8,40},{9,1... | collective-permute-start | bytes 221192 | tf_op jit(solution)/shard_map/ppermute | solution.py:24
  48.4 4.4 %collective-permute-start.17 = (f16[1,32,1152]{2,1,0:T(8,128)(2,1)S(1)}, f16[1,32,1152]{2,1,0:T(8,128)(2,1)S(1)}, u32[]{:S(2)}, u32[]{:S(2)}) collective-permute-start(f16[1,32,1152]{2,1,0:T(8,128)(2,1)S(1)} %convert_element_type.70), channel_id=1, source_target_pairs={{0,2},{1,7},{2,0},{3,5},{4,6},{5,3},{6,4},{7,1},{8,10},{9,15},{10,... | collective-permute-start | bytes 221192 | tf_op jit(solution)/shard_map/ppermute | solution.py:24
  53.1 8.8 %collective-permute-start.20 = (bf16[32,1152]{1,0:T(8,128)(2,1)S(1)}, bf16[32,1152]{1,0:T(8,128)(2,1)S(1)}, u32[]{:S(2)}, u32[]{:S(2)}) collective-permute-start(bf16[32,1152]{1,0:T(8,128)(2,1)S(1)} %get-tuple-element.64.refs_0_), channel_id=1, source_target_pairs={{0,96},{1,25},{2,98},{3,27},{4,100},{5,29},{6,102},{7,31},{8,104},... | collective-permute-start | bytes 221192 | tf_op jit(solution)/shard_map/ppermute | solution.py:24
  55.1 6.9 %collective-permute-start.19 = (bf16[32,1152]{1,0:T(8,128)(2,1)S(1)}, bf16[32,1152]{1,0:T(8,128)(2,1)S(1)}, u32[]{:S(2)}, u32[]{:S(2)}) collective-permute-start(bf16[32,1152]{1,0:T(8,128)(2,1)S(1)} %get-tuple-element.64.refs_0_), channel_id=1, source_target_pairs={{0,64},{1,17},{2,66},{3,19},{4,68},{5,21},{6,70},{7,23},{8,72},{9,... | collective-permute-start | bytes 221192 | tf_op jit(solution)/shard_map/ppermute | solution.py:24
  56.4 5.6 %collective-permute-start.18 = (bf16[32,1152]{1,0:T(8,128)(2,1)S(1)}, bf16[32,1152]{1,0:T(8,128)(2,1)S(1)}, u32[]{:S(2)}, u32[]{:S(2)}) collective-permute-start(bf16[32,1152]{1,0:T(8,128)(2,1)S(1)} %get-tuple-element.64.refs_0_), channel_id=1, source_target_pairs={{0,32},{1,9},{2,34},{3,11},{4,36},{5,13},{6,38},{7,15},{8,40},{9,1... | collective-permute-start | bytes 221192 | tf_op jit(solution)/shard_map/ppermute | solution.py:24
  57.7 4.3 %collective-permute-start.21 = (bf16[32,1024]{1,0:T(8,128)(2,1)S(1)}, bf16[32,1024]{1,0:T(8,128)(2,1)S(1)}, u32[]{:S(2)}, u32[]{:S(2)}) collective-permute-start(bf16[32,1024]{1,0:T(8,128)(2,1)S(1)} %get-tuple-element.65.refs_4_), channel_id=1, source_target_pairs={{0,2},{1,7},{2,0},{3,5},{4,6},{5,3},{6,4},{7,1},{8,10},{9,15},{10,... | collective-permute-start | bytes 196616 | tf_op jit(solution)/shard_map/ppermute | solution.py:24
  62.0 6.3 %collective-permute-start.25 = (bf16[2,32,1024]{2,1,0:T(8,128)(2,1)S(1)}, bf16[2,32,1024]{2,1,0:T(8,128)(2,1)S(1)}, u32[]{:S(2)}, u32[]{:S(2)}) collective-permute-start(bf16[2,32,1024]{2,1,0:T(8,128)(2,1)S(1)} %get-tuple-element.67), channel_id=1, source_target_pairs={{0,6},{1,3},{2,4},{3,1},{4,2},{5,7},{6,0},{7,5},{8,14},{9,11},{10,... | collective-permute-start | bytes 393224 | tf_op jit(solution)/shard_map/ppermute | solution.py:24
  63.9 8.2 %collective-permute-start.24 = (bf16[66,16,128]{2,1,0:T(8,128)(2,1)S(1)}, bf16[66,16,128]{2,1,0:T(8,128)(2,1)S(1)}, u32[]{:S(2)}, u32[]{:S(2)}) collective-permute-start(bf16[66,16,128]{2,1,0:T(8,128)(2,1)S(1)} %get-tuple-element.66.g0), channel_id=1, source_target_pairs={{0,24},{1,97},{2,26},{3,99},{4,28},{5,101},{6,30},{7,103},{8,0},{9... | collective-permute-start | bytes 811016 | tf_op jit(solution)/shard_map/ppermute | solution.py:24
  64.5 8.1 %collective-permute-start.23 = (bf16[66,16,128]{2,1,0:T(8,128)(2,1)S(1)}, bf16[66,16,128]{2,1,0:T(8,128)(2,1)S(1)}, u32[]{:S(2)}, u32[]{:S(2)}) collective-permute-start(bf16[66,16,128]{2,1,0:T(8,128)(2,1)S(1)} %get-tuple-element.66.g0), channel_id=1, source_target_pairs={{0,16},{1,65},{2,18},{3,67},{4,20},{5,69},{6,22},{7,71},{8,24},{9,... | collective-permute-start | bytes 811016 | tf_op jit(solution)/shard_map/ppermute | solution.py:24
  65.3 10.1 %collective-permute-start.22 = (bf16[66,16,128]{2,1,0:T(8,128)(2,1)S(1)}, bf16[66,16,128]{2,1,0:T(8,128)(2,1)S(1)}, u32[]{:S(2)}, u32[]{:S(2)}) collective-permute-start(bf16[66,16,128]{2,1,0:T(8,128)(2,1)S(1)} %get-tuple-element.66.g0), channel_id=1, source_target_pairs={{0,8},{1,33},{2,10},{3,35},{4,12},{5,37},{6,14},{7,39},{8,16},{9,4... | collective-permute-start | bytes 811016 | tf_op jit(solution)/shard_map/ppermute | solution.py:24
  68.3 1.6 %collective-permute-start.26 = (bf16[4,32,1024]{2,1,0:T(8,128)(2,1)S(1)}, bf16[4,32,1024]{2,1,0:T(8,128)(2,1)S(1)}, u32[]{:S(2)}, u32[]{:S(2)}) collective-permute-start(bf16[4,32,1024]{2,1,0:T(8,128)(2,1)S(1)} %constant_dynamic-update-slice_fusion.2.h0), channel_id=1, source_target_pairs={{0,1},{1,0},{2,3},{3,2},{4,5},{5,4},{6,7},{7,6},{8,9},{9,8},{10,11... | collective-permute-start | bytes 786440 | tf_op jit(solution)/shard_map/ppermute | solution.py:24
  77.7 3.4 %collective-permute-start.27 = (bf16[4,32,1152]{2,1,0:T(8,128)(2,1)S(1)}, bf16[4,32,1152]{2,1,0:T(8,128)(2,1)S(1)}, u32[]{:S(2)}, u32[]{:S(2)}) collective-permute-start(bf16[4,32,1152]{2,1,0:T(8,128)(2,1)S(1)} %get-tuple-element.70), channel_id=1, source_target_pairs={{0,1},{1,0},{2,3},{3,2},{4,5},{5,4},{6,7},{7,6},{8,9},{9,8},{10,11... | collective-permute-start | bytes 884744 | tf_op jit(solution)/shard_map/ppermute | solution.py:24
  77.8 10.0 %collective-permute-start.30 = (bf16[50,16,128]{2,1,0:T(8,128)(2,1)S(1)}, bf16[50,16,128]{2,1,0:T(8,128)(2,1)S(1)}, u32[]{:S(2)}, u32[]{:S(2)}) collective-permute-start(bf16[50,16,128]{2,1,0:T(8,128)(2,1)S(1)} %get-tuple-element.79), channel_id=1, source_target_pairs={{0,8},{1,33},{2,10},{3,35},{4,12},{5,37},{6,14},{7,39},{8,16},{9,4... | collective-permute-start | bytes 614408 | tf_op jit(solution)/shard_map/ppermute | solution.py:24
  77.9 9.9 %collective-permute-start.31 = (bf16[50,16,128]{2,1,0:T(8,128)(2,1)S(1)}, bf16[50,16,128]{2,1,0:T(8,128)(2,1)S(1)}, u32[]{:S(2)}, u32[]{:S(2)}) collective-permute-start(bf16[50,16,128]{2,1,0:T(8,128)(2,1)S(1)} %get-tuple-element.80), channel_id=1, source_target_pairs={{0,16},{1,65},{2,18},{3,67},{4,20},{5,69},{6,22},{7,71},{8,24},{9,... | collective-permute-start | bytes 614408 | tf_op jit(solution)/shard_map/ppermute | solution.py:24
  78.8 9.1 %collective-permute-start.32 = (bf16[50,16,128]{2,1,0:T(8,128)(2,1)S(1)}, bf16[50,16,128]{2,1,0:T(8,128)(2,1)S(1)}, u32[]{:S(2)}, u32[]{:S(2)}) collective-permute-start(bf16[50,16,128]{2,1,0:T(8,128)(2,1)S(1)} %get-tuple-element.81), channel_id=1, source_target_pairs={{0,24},{1,97},{2,26},{3,99},{4,28},{5,101},{6,30},{7,103},{8,0},{9... | collective-permute-start | bytes 614408 | tf_op jit(solution)/shard_map/ppermute | solution.py:24
  81.2 6.4 %collective-permute-start.28 = (bf16[2,32,1152]{2,1,0:T(8,128)(2,1)S(1)}, bf16[2,32,1152]{2,1,0:T(8,128)(2,1)S(1)}, u32[]{:S(2)}, u32[]{:S(2)}) collective-permute-start(bf16[2,32,1152]{2,1,0:T(8,128)(2,1)S(1)} %get-tuple-element.73), channel_id=1, source_target_pairs={{0,6},{1,3},{2,4},{3,1},{4,2},{5,7},{6,0},{7,5},{8,14},{9,11},{10,... | collective-permute-start | bytes 442376 | tf_op jit(solution)/shard_map/ppermute | solution.py:24
  87.7 5.5 %collective-permute-start.29 = (bf16[1,32,1152]{2,1,0:T(8,128)(2,1)S(1)}, bf16[1,32,1152]{2,1,0:T(8,128)(2,1)S(1)}, u32[]{:S(2)}, u32[]{:S(2)}) collective-permute-start(bf16[1,32,1152]{2,1,0:T(8,128)(2,1)S(1)} %get-tuple-element.76), channel_id=1, source_target_pairs={{0,2},{1,7},{2,0},{3,5},{4,6},{5,3},{6,4},{7,1},{8,10},{9,15},{10,... | collective-permute-start | bytes 221192 | tf_op jit(solution)/shard_map/ppermute | solution.py:24
  88.5 6.6 %collective-permute-start.33 = (bf16[32,1024]{1,0:T(8,128)(2,1)S(1)}, bf16[32,1024]{1,0:T(8,128)(2,1)S(1)}, u32[]{:S(2)}, u32[]{:S(2)}) collective-permute-start(bf16[32,1024]{1,0:T(8,128)(2,1)S(1)} %get-tuple-element.84), channel_id=1, source_target_pairs={{0,32},{1,9},{2,34},{3,11},{4,36},{5,13},{6,38},{7,15},{8,40},{9,1... | collective-permute-start | bytes 196616 | tf_op jit(solution)/shard_map/ppermute | solution.py:24
  89.7 5.8 %collective-permute-start.34 = (bf16[32,1024]{1,0:T(8,128)(2,1)S(1)}, bf16[32,1024]{1,0:T(8,128)(2,1)S(1)}, u32[]{:S(2)}, u32[]{:S(2)}) collective-permute-start(bf16[32,1024]{1,0:T(8,128)(2,1)S(1)} %get-tuple-element.85), channel_id=1, source_target_pairs={{0,64},{1,17},{2,66},{3,19},{4,68},{5,21},{6,70},{7,23},{8,72},{9,... | collective-permute-start | bytes 196616 | tf_op jit(solution)/shard_map/ppermute | solution.py:24
  90.6 4.9 %collective-permute-start.35 = (bf16[32,1024]{1,0:T(8,128)(2,1)S(1)}, bf16[32,1024]{1,0:T(8,128)(2,1)S(1)}, u32[]{:S(2)}, u32[]{:S(2)}) collective-permute-start(bf16[32,1024]{1,0:T(8,128)(2,1)S(1)} %get-tuple-element.86), channel_id=1, source_target_pairs={{0,96},{1,25},{2,98},{3,27},{4,100},{5,29},{6,102},{7,31},{8,104},... | collective-permute-start | bytes 196616 | tf_op jit(solution)/shard_map/ppermute | solution.py:24
  96.1 1.2 collective-permute-start.36

commit v5 on v4

--- a/solution.py
+++ b/solution.py
@@ -194,42 +194,27 @@
         out[...] = jnp.zeros_like(out)
 
 
-def both_kernel(pairs, live, blocks, turned, g0, g1, g2, g3, h0, h1, *rest):
-    outs, (lefts, rights, results) = rest[:6], rest[6:]
+def mirror_kernel(half, pairs, live, blocks, h0, h1, *rest):
+    outs, (rights,) = rest[:4], rest[4:]
     clear(outs)
+
+    def advance(slot, carry):
+        load_right(pairs, slot, (h0, h1), rights)
+        store_mirror(pairs, slot, multiply(rights, blocks[slot]), outs, half)
+        return carry
+
+    lax.fori_loop(0, live[0], advance, 0)
+
+
+def direct_kernel(half, pairs, live, turned, g0, g1, g2, g3, after, *rest):
+    outs, (lefts, results) = rest[:-2], rest[-2:]
+    clear(outs[:2])
+    if not half:
+        add_gram((g0, g1, g2, g3), outs[2], outs[1])
 
     def advance(slot, carry):
         load_left(pairs, slot, (g0, g1, g2, g3), lefts)
-        load_right(pairs, slot, (h0, h1), rights)
-        direct = multiply(lefts, turned[slot])
-        mirror = multiply(rights, blocks[slot])
-        store_direct(pairs, slot, direct, outs[4:], results, True)
-        store_mirror(pairs, slot, mirror, outs, True)
-        return carry
-
-    lax.fori_loop(0, live[0], advance, 0)
-
-
-def mirror_kernel(pairs, live, blocks, h0, h1, *rest):
-    outs, (rights,) = rest[:4], rest[4:]
-    clear(outs)
-
-    def advance(slot, carry):
-        load_right(pairs, slot, (h0, h1), rights)
-        store_mirror(pairs, slot, multiply(rights, blocks[slot]), outs, False)
-        return carry
-
-    lax.fori_loop(0, live[0], advance, 0)
-
-
-def direct_kernel(pairs, live, turned, g0, g1, g2, g3, after, *rest):
-    outs, (lefts, results) = rest[:3], rest[3:]
-    clear(outs[:2])
-    add_gram((g0, g1, g2, g3), outs[2], outs[1])
-
-    def advance(slot, carry):
-        load_left(pairs, slot, (g0, g1, g2, g3), lefts)
-        store_direct(pairs, slot, multiply(lefts, turned[slot]), outs, results, False)
+        store_direct(pairs, slot, multiply(lefts, turned[slot]), outs, results, half)
         return carry
 
     lax.fori_loop(0, live[0], advance, 0)
@@ -251,21 +236,17 @@
     )(pairs, live, *arrays)
 
 
-def first_product(pairs, live, blocks, turned, gathered, pair_gathered):
+def product(pairs, live, blocks, turned, gathered, pair_gathered, half):
     f32 = jnp.float32
-    outs = [struct((4, 32, 1024), f32)] + [struct((50, 16, 128), f32)] * 3
-    outs += [struct((4, 32, 1024), f32), struct((4, 32, 1152), f32)]
-    arrays = (blocks, turned, *gathered, *pair_gathered)
-    return product_call(both_kernel, outs, [PANEL, PANEL, RESULTS], "product", pairs, live, *arrays)
-
-
-def second_product(pairs, live, blocks, turned, gathered, pair_gathered):
-    f32, bf16 = jnp.float32, jnp.bfloat16
-    outs = [struct((4, 32, 1024), f32)] + [struct((50, 16, 128), bf16)] * 3
-    rows = product_call(mirror_kernel, outs, [PANEL], "mirror", pairs, live, blocks, *pair_gathered)
-    outs = [struct((4, 32, 1024), f32), struct((4, 32, 1152), bf16), struct((8, 128), f32)]
+    sent = f32 if half else jnp.bfloat16
+    outs = [struct((4, 32, 1024), f32)] + [struct((50, 16, 128), sent)] * 3
+    kernel = functools.partial(mirror_kernel, half)
+    rows = product_call(kernel, outs, [PANEL], "mirror", pairs, live, blocks, *pair_gathered)
+    outs = [struct((4, 32, 1024), f32), struct((4, 32, 1152), sent)]
+    outs += [] if half else [struct((8, 128), f32)]
+    kernel = functools.partial(direct_kernel, half)
     arrays = (turned, *gathered, rows[0])
-    return rows + product_call(direct_kernel, outs, [PANEL, RESULTS], "direct", pairs, live, *arrays)
+    return rows + product_call(kernel, outs, [PANEL, RESULTS], "direct", pairs, live, *arrays)
 
 
 def join_kernel(with_gram, *refs):
@@ -277,12 +258,14 @@
         for part in parts[1:]:
             gram = gram + merge(part[:, 1024:1152])
         put_extra(joined, 4, split(gram))
+    else:
+        put_extra(joined, 4, jnp.zeros((32, 128), jnp.bfloat16))
     for k, part in enumerate(pair):
         joined_pair[k] = part[...]
 
 
 def join(parts, pair, with_gram):
-    shapes = [(66 if with_gram else 64, 16, 128), (2,) + pair[0].shape]
+    shapes = [(66, 16, 128), (2,) + pair[0].shape]
     return pl.pallas_call(
         functools.partial(join_kernel, with_gram),
         out_shape=[struct(shape, jnp.bfloat16) for shape in shapes],
@@ -552,48 +535,32 @@
     return [row[0], column] + [carry(send_inner, row[s], s) for s in (1, 2, 3)] + [along_y], gram
 
 
-def hold_kernel(source, target, turned, sems):
-    copies = [pltpu.make_async_copy(source.at[k], target.at[k], sems.at[k]) for k in range(3)]
-    for copy in copies:
-        copy.start()
-    for k, copy in enumerate(copies):
-        copy.wait()
-        turned[k] = target[k].T
-
-
-def hold(blocks):
-    return pl.pallas_call(
-        hold_kernel,
-        out_shape=[struct(blocks.shape, blocks.dtype)] * 2,
-        in_specs=[pl.BlockSpec(memory_space=pl.ANY)],
-        out_specs=[VMEM] * 2,
-        scratch_shapes=[pltpu.SemaphoreType.DMA((3,))],
-        compiler_params=PARAMS,
-        cost_estimate=pl.CostEstimate(flops=0, bytes_accessed=6_000_000, transcendentals=0),
-        name="hold",
-    )(blocks)
-
-
-def load(panel):
-    return pl.pallas_call(
-        lambda source, target: target.__setitem__(..., source[...]),
-        out_shape=struct(panel.shape, panel.dtype),
+def turn_kernel(source, turned):
+    for k in range(3):
+        turned[k] = source[k].T
+
+
+def turn(blocks):
+    return pl.pallas_call(
+        turn_kernel,
+        out_shape=struct(blocks.shape, blocks.dtype),
         in_specs=[VMEM],
         out_specs=VMEM,
         compiler_params=PARAMS,
-        name="load",
-    )(panel)
+        cost_estimate=pl.CostEstimate(flops=0, bytes_accessed=6_000_000, transcendentals=0),
+        name="turn",
+    )(blocks)
 
 
 def on_device(block_pairs, live_counts, pair_blocks, start_basis):
     users = 128 * start_basis.shape[2]
     root = float(users) ** 0.5
-    pair_blocks, turned = hold(pair_blocks)
+    turned = turn(pair_blocks)
     gathered, pair_gathered = gather(start_basis[0], start_basis[0], False)
-    parts = first_product(block_pairs, live_counts, pair_blocks, turned, gathered, pair_gathered)
+    parts = product(block_pairs, live_counts, pair_blocks, turned, gathered, pair_gathered, True)
     first, panel, own = finish_first(scatter(parts)[0])
     gathered, pair_gathered = gather(panel, own, True)
-    parts = second_product(block_pairs, live_counts, pair_blocks, turned, gathered, pair_gathered)
+    parts = product(block_pairs, live_counts, pair_blocks, turned, gathered, pair_gathered, False)
     parts, (gram,) = scatter(parts)
     first_basis, inverse = factor_first(gram, parts[5], first, root)
     scaled, tiles = finish_second(parts, inverse)

time: 120 us -> 119 us (level)
  blocking collectives: 20.5 us -> 18.5 us
  starting transfers between devices: 41.3 us -> 42.7 us
    all_to_all x1, blocking collectives: 20.5 us -> 18.5 us  [total_gram(): return lax.all_to_all(tiles, ('z', 'x', 'y'), 0, 0, tiled=True)]
    ppermute x37, starting transfers between devices: 41.3 us -> 42.7 us  [permute(): return lax.ppermute(value, AXES, pairs)]
    pallas_call x3 -> x4, Pallas kernels: 8.76 us -> 9.64 us  [product_call(): pl.pallas_call(kernel, out_shape=outs, in_specs=[SMEM, SMEM] + [VMEM] * l...]
    unnamed x7 -> x11, local copies, waits for them, and re-layouts: 4.41 us -> 4.42 us
  transfers between devices with their start and end apart: 37 -> 37, of which waited for: 21 -> 21; matrix products, arithmetic and copies ran while one was open for 1% -> 1% of each run, Pallas kernels for 7% -> 9%
where the time goes in v5:
time: 119 us; the launch traced here: 118 us
  starting transfers between devices  42.7 us (36%)
  waiting for transfers between devices  32.6 us (27%)
  blocking collectives  18.5 us (16%)
  Pallas kernels  18.3 us (15%)
  local copies, waits for them, and re-layouts  4.44 us (4%)
  between operations  1.64 us (1%)
    ppermute x37, starting transfers between devices, permute(): return lax.ppermute(value, AXES, pairs)  42.7 us
    ppermute x37, waiting for transfers between devices, permute(): return lax.ppermute(value, AXES, pairs)  32.6 us
    all_to_all x1, blocking collectives, total_gram(): return lax.all_to_all(tiles, ('z', 'x', 'y'), 0, 0, tiled=True)  18.5 us
    pallas_call x4, Pallas kernels, product_call(): pl.pallas_call(kernel, out_shape=outs, in_specs=[SMEM, SMEM] + [VMEM] * l...  9.64 us
    unnamed x11, local copies, waits for them, and re-layouts  4.42 us
  transfers between devices with their start and end apart: 37, of which 21 were waited for; matrix products, arithmetic and copies ran while one was open for 1% of the time, Pallas kernels for 9%

profile of v5, /device:TPU:0, one launch (start us, length us, event | category | flops | bytes accessed | tf_op | source)
XLA Modules:
  0.0 118.5 jit_solution(2511993287227104086)
XLA Ops:
  0.6 1.7 %collective-permute-start.3 = (bf16[32,1024]{1,0:T(8,128)(2,1)}, bf16[32,1024]{1,0:T(8,128)(2,1)S(1)}, u32[]{:S(2)}, u32[]{:S(2)}) collective-permute-start(bf16[32,1024]{1,0:T(8,128)(2,1)} %bitcast.5), channel_id=1, source_target_pairs={{0,2},{1,7},{2,0},{3,5},{4,6},{5,3},{6,4},{7,1},{8,10},{9,15},{10,... | collective-permute-start | bytes 196616 | tf_op jit(solution)/shard_map/ppermute | solution.py:24
  2.4 4.0 %collective-permute-start.2 = (bf16[32,1024]{1,0:T(8,128)(2,1)}, bf16[32,1024]{1,0:T(8,128)(2,1)S(1)}, u32[]{:S(2)}, u32[]{:S(2)}) collective-permute-start(bf16[32,1024]{1,0:T(8,128)(2,1)} %bitcast.6), channel_id=1, source_target_pairs={{0,96},{1,25},{2,98},{3,27},{4,100},{5,29},{6,102},{7,31},{8,104},... | collective-permute-start | bytes 196616 | tf_op jit(solution)/shard_map/ppermute | solution.py:24
  6.4 1.3 %collective-permute-start = (bf16[32,1024]{1,0:T(8,128)(2,1)}, bf16[32,1024]{1,0:T(8,128)(2,1)S(1)}, u32[]{:S(2)}, u32[]{:S(2)}) collective-permute-start(bf16[32,1024]{1,0:T(8,128)(2,1)} %bitcast.8), channel_id=1, source_target_pairs={{0,32},{1,9},{2,34},{3,11},{4,36},{5,13},{6,38},{7,15},{8,40},{9,1... | collective-permute-start | bytes 196616 | tf_op jit(solution)/shard_map/ppermute | solution.py:24
  7.7 1.0 collective-permute-done.2.refs_3_
  8.6 3.9 %collective-permute-done.1.refs_2_ = bf16[32,1024]{1,0:T(8,128)(2,1)S(1)} collective-permute-done((bf16[32,1024]{1,0:T(8,128)(2,1)}, bf16[32,1024]{1,0:T(8,128)(2,1)S(1)}, u32[]{:S(2)}, u32[]{:S(2)}) %collective-permute-start.1) | collective-permute-done | bytes 65568 | tf_op jit(solution)/shard_map/ppermute | solution.py:24
  12.8 0.8 copy-done.1
  13.7 2.3 %collective-permute-start.4 = (bf16[2,32,1024]{2,1,0:T(8,128)(2,1)S(1)}, bf16[2,32,1024]{2,1,0:T(8,128)(2,1)S(1)}, u32[]{:S(2)}, u32[]{:S(2)}) collective-permute-start(bf16[2,32,1024]{2,1,0:T(8,128)(2,1)S(1)} %get-tuple-element.44), channel_id=1, source_target_pairs={{0,6},{1,3},{2,4},{3,1},{4,2},{5,7},{6,0},{7,5},{8,14},{9,11},{10,... | collective-permute-start | bytes 393224 | tf_op jit(solution)/shard_map/ppermute | solution.py:24
  15.9 2.8 %collective-permute-start.11 = (bf16[66,16,128]{2,1,0:T(8,128)(2,1)S(1)}, bf16[66,16,128]{2,1,0:T(8,128)(2,1)S(1)}, u32[]{:S(2)}, u32[]{:S(2)}) collective-permute-start(bf16[66,16,128]{2,1,0:T(8,128)(2,1)S(1)} %get-tuple-element.50.g0), channel_id=1, source_target_pairs={{0,24},{1,97},{2,26},{3,99},{4,28},{5,101},{6,30},{7,103},{8,0},{9... | collective-permute-start | bytes 811016 | tf_op jit(solution)/shard_map/ppermute | solution.py:24
  19.5 0.9 collective-permute-start.9
  21.9 2.8 %copy-done = bf16[3,1024,1024]{2,1,0:T(8,128)(2,1)S(1)} copy-done((bf16[3,1024,1024]{2,1,0:T(8,128)(2,1)S(1)}, bf16[3,1024,1024]{2,1,0:T(8,128)(2,1)}, u32[]{:S(2)}) %copy-start) | copy-done | bytes 6291480
  24.7 1.8 %turn.1.turned = bf16[3,1024,1024]{2,1,0:T(8,128)(2,1)S(1)} custom-call(bf16[3,1024,1024]{2,1,0:T(8,128)(2,1)S(1)} %copy-done), custom_call_target="tpu_custom_call" | custom-call | bytes 6000000 | tf_op jit(solution)/shard_map/turn/pallas_call | solution.py:544
  26.6 2.5 %mirror.2 = (f32[4,32,1024]{2,1,0:T(8,128)S(1)}, f32[50,16,128]{2,1,0:T(8,128)S(1)}, f32[50,16,128]{2,1,0:T(8,128)S(1)}, f32[50,16,128]{2,1,0:T(8,128)S(1)}) custom-call(s32[1,3,2]{2,1,0:T(4,128)S(1)} %copy.9.pairs, s32[1]{0:T(128)S(6)} %copy.12.live, bf16[3,1024,1024]{2,1,0:T(8,128)(2,1)S(1)} %copy-done, ...), custom_call_target="tpu_custom_call" | custom-call | tf_op jit(solution)/shard_map/mirror/pallas_call | solution.py:228
  29.6 2.5 %direct.2 = (f32[4,32,1024]{2,1,0:T(8,128)S(1)}, f32[4,32,1152]{2,1,0:T(8,128)S(1)}) custom-call(s32[1,3,2]{2,1,0:T(4,128)S(1)} %copy.9.pairs, s32[1]{0:T(128)S(6)} %copy.12.live, bf16[3,1024,1024]{2,1,0:T(8,128)(2,1)S(1)} %turn.1.turned, bf16[66,16,128]{2,1,0:T(8,128)(2,1)S(1)} %get-tuple-element.50.g0, bf16[66,16,128]{2,1,0:T(8,128)(2,1)S(1)} %collective-permute-done.9.g1, ...), custom_call_target="tpu_custom_call" | custom-call | tf_op jit(solution)/shard_map/direct/pallas_call | solution.py:228
  32.3 1.2 collective-permute-start.8
  33.5 2.0 %collective-permute-start.7 = (f16[50,16,128]{2,1,0:T(8,128)(2,1)S(1)}, f16[50,16,128]{2,1,0:T(8,128)(2,1)S(1)}, u32[]{:S(2)}, u32[]{:S(2)}) collective-permute-start(f16[50,16,128]{2,1,0:T(8,128)(2,1)S(1)} %convert_element_type.56), channel_id=1, source_target_pairs={{0,16},{1,65},{2,18},{3,67},{4,20},{5,69},{6,22},{7,71},{8,24},{9,... | collective-permute-start | bytes 614408 | tf_op jit(solution)/shard_map/ppermute | solution.py:24
  36.1 1.6 %collective-permute-start.13 = (f16[2,32,1152]{2,1,0:T(8,128)(2,1)S(1)}, f16[2,32,1152]{2,1,0:T(8,128)(2,1)S(1)}, u32[]{:S(2)}, u32[]{:S(2)}) collective-permute-start(f16[2,32,1152]{2,1,0:T(8,128)(2,1)S(1)} %convert_element_type.62), channel_id=1, source_target_pairs={{0,6},{1,3},{2,4},{3,1},{4,2},{5,7},{6,0},{7,5},{8,14},{9,11},{10,... | collective-permute-start | bytes 442376 | tf_op jit(solution)/shard_map/ppermute | solution.py:24
  38.2 2.6 %collective-permute-done.7 = f16[50,16,128]{2,1,0:T(8,128)(2,1)S(1)} collective-permute-done((f16[50,16,128]{2,1,0:T(8,128)(2,1)S(1)}, f16[50,16,128]{2,1,0:T(8,128)(2,1)S(1)}, u32[]{:S(2)}, u32[]{:S(2)}) %collective-permute-start.7) | collective-permute-done | bytes 204832 | tf_op jit(solution)/shard_map/ppermute | solution.py:24
  40.8 2.1 %collective-permute-done.6 = f16[50,16,128]{2,1,0:T(8,128)(2,1)S(1)} collective-permute-done((f16[50,16,128]{2,1,0:T(8,128)(2,1)S(1)}, f16[50,16,128]{2,1,0:T(8,128)(2,1)S(1)}, u32[]{:S(2)}, u32[]{:S(2)}) %collective-permute-start.6) | collective-permute-done | bytes 204832 | tf_op jit(solution)/shard_map/ppermute | solution.py:24
  43.0 1.0 add_outer.2
  44.0 1.0 collective-permute-start.16
  45.8 1.3 %collective-permute-start.14 = (f16[32,1152]{1,0:T(8,128)(2,1)S(1)}, f16[32,1152]{1,0:T(8,128)(2,1)S(1)}, u32[]{:S(2)}, u32[]{:S(2)}) collective-permute-start(f16[32,1152]{1,0:T(8,128)(2,1)S(1)} %convert_element_type.64), channel_id=1, source_target_pairs={{0,32},{1,9},{2,34},{3,11},{4,36},{5,13},{6,38},{7,15},{8,40},{9,1... | collective-permute-start | bytes 221192 | tf_op jit(solution)/shard_map/ppermute | solution.py:24
  47.4 1.0 collective-permute-start.17
  48.5 2.4 %collective-permute-done.15 = f16[32,1152]{1,0:T(8,128)(2,1)S(1)} collective-permute-done((f16[32,1152]{1,0:T(8,128)(2,1)S(1)}, f16[32,1152]{1,0:T(8,128)(2,1)S(1)}, u32[]{:S(2)}, u32[]{:S(2)}) %collective-permute-start.15) | collective-permute-done | bytes 73760 | tf_op jit(solution)/shard_map/ppermute | solution.py:24
  52.1 1.9 %collective-permute-start.20 = (bf16[32,1152]{1,0:T(8,128)(2,1)S(1)}, bf16[32,1152]{1,0:T(8,128)(2,1)S(1)}, u32[]{:S(2)}, u32[]{:S(2)}) collective-permute-start(bf16[32,1152]{1,0:T(8,128)(2,1)S(1)} %get-tuple-element.60.refs_0_), channel_id=1, source_target_pairs={{0,96},{1,25},{2,98},{3,27},{4,100},{5,29},{6,102},{7,31},{8,104},... | collective-permute-start | bytes 221192 | tf_op jit(solution)/shard_map/ppermute | solution.py:24
  54.1 1.5 %collective-permute-start.19 = (bf16[32,1152]{1,0:T(8,128)(2,1)S(1)}, bf16[32,1152]{1,0:T(8,128)(2,1)S(1)}, u32[]{:S(2)}, u32[]{:S(2)}) collective-permute-start(bf16[32,1152]{1,0:T(8,128)(2,1)S(1)} %get-tuple-element.60.refs_0_), channel_id=1, source_target_pairs={{0,64},{1,17},{2,66},{3,19},{4,68},{5,21},{6,70},{7,23},{8,72},{9,... | collective-permute-start | bytes 221192 | tf_op jit(solution)/shard_map/ppermute | solution.py:24
  55.6 1.1 collective-permute-start.18
  56.7 1.2 %collective-permute-start.21 = (bf16[32,1024]{1,0:T(8,128)(2,1)S(1)}, bf16[32,1024]{1,0:T(8,128)(2,1)S(1)}, u32[]{:S(2)}, u32[]{:S(2)}) collective-permute-start(bf16[32,1024]{1,0:T(8,128)(2,1)S(1)} %get-tuple-element.61.refs_4_), channel_id=1, source_target_pairs={{0,2},{1,7},{2,0},{3,5},{4,6},{5,3},{6,4},{7,1},{8,10},{9,15},{10,... | collective-permute-start | bytes 196616 | tf_op jit(solution)/shard_map/ppermute | solution.py:24
  57.9 3.1 %collective-permute-done.21.refs_5_ = bf16[32,1024]{1,0:T(8,128)(2,1)S(1)} collective-permute-done((bf16[32,1024]{1,0:T(8,128)(2,1)S(1)}, bf16[32,1024]{1,0:T(8,128)(2,1)S(1)}, u32[]{:S(2)}, u32[]{:S(2)}) %collective-permute-start.21) | collective-permute-done | bytes 65568 | tf_op jit(solution)/shard_map/ppermute | solution.py:24
  61.2 2.7 %collective-permute-start.25 = (bf16[2,32,1024]{2,1,0:T(8,128)(2,1)S(1)}, bf16[2,32,1024]{2,1,0:T(8,128)(2,1)S(1)}, u32[]{:S(2)}, u32[]{:S(2)}) collective-permute-start(bf16[2,32,1024]{2,1,0:T(8,128)(2,1)S(1)} %get-tuple-element.63), channel_id=1, source_target_pairs={{0,6},{1,3},{2,4},{3,1},{4,2},{5,7},{6,0},{7,5},{8,14},{9,11},{10,... | collective-permute-start | bytes 393224 | tf_op jit(solution)/shard_map/ppermute | solution.py:24
  64.4 1.0 collective-permute-start.23
  65.4 0.8 collective-permute-start.22
  66.3 1.2 %collective-permute-done.25 = bf16[2,32,1024]{2,1,0:T(8,128)(2,1)S(1)} collective-permute-done((bf16[2,32,1024]{2,1,0:T(8,128)(2,1)S(1)}, bf16[2,32,1024]{2,1,0:T(8,128)(2,1)S(1)}, u32[]{:S(2)}, u32[]{:S(2)}) %collective-permute-start.25) | collective-permute-done | bytes 131104 | tf_op jit(solution)/shard_map/ppermute | solution.py:24
  67.6 1.5 %collective-permute-done.26.h1 = bf16[4,32,1024]{2,1,0:T(8,128)(2,1)S(1)} collective-permute-done((bf16[4,32,1024]{2,1,0:T(8,128)(2,1)S(1)}, bf16[4,32,1024]{2,1,0:T(8,128)(2,1)S(1)}, u32[]{:S(2)}, u32[]{:S(2)}) %collective-permute-start.26) | collective-permute-done | bytes 262176 | tf_op jit(solution)/shard_map/ppermute | solution.py:24
  69.1 2.3 %mirror.3 = (f32[4,32,1024]{2,1,0:T(8,128)S(1)}, bf16[50,16,128]{2,1,0:T(8,128)(2,1)S(1)}, bf16[50,16,128]{2,1,0:T(8,128)(2,1)S(1)}, bf16[50,16,128]{2,1,0:T(8,128)(2,1)S(1)}) custom-call(s32[1,3,2]{2,1,0:T(4,128)S(1)} %copy.9.pairs, s32[1]{0:T(128)S(6)} %copy.12.live, bf16[3,1024,1024]{2,1,0:T(8,128)(2,1)S(1)} %bitcast.4, ...), custom_call_target="tpu_custom_call" | custom-call | tf_op jit(solution)/shard_map/mirror/pallas_call | solution.py:228
  71.4 1.1 collective-permute-done.23.g2
  72.5 2.8 %collective-permute-done.22.g1 = bf16[66,16,128]{2,1,0:T(8,128)(2,1)S(1)} collective-permute-done((bf16[66,16,128]{2,1,0:T(8,128)(2,1)S(1)}, bf16[66,16,128]{2,1,0:T(8,128)(2,1)S(1)}, u32[]{:S(2)}, u32[]{:S(2)}) %collective-permute-start.22) | collective-permute-done | bytes 270368 | tf_op jit(solution)/shard_map/ppermute | solution.py:24
  75.3 2.3 %direct.3 = (f32[4,32,1024]{2,1,0:T(8,128)S(1)}, bf16[4,32,1152]{2,1,0:T(8,128)(2,1)S(1)}, f32[8,128]{1,0:T(8,128)S(1)}) custom-call(s32[1,3,2]{2,1,0:T(4,128)S(1)} %copy.9.pairs, s32[1]{0:T(128)S(6)} %copy.12.live, bf16[3,1024,1024]{2,1,0:T(8,128)(2,1)S(1)} %turn.1.turned, bf16[66,16,128]{2,1,0:T(8,128)(2,1)S(1)} %get-tuple-element.62.g0, ...), custom_call_target="tpu_custom_call" | custom-call | tf_op jit(solution)/shard_map/direct/pallas_call | solution.py:228
  77.8 1.1 collective-permute-start.31
  78.8 2.5 %collective-permute-start.32 = (bf16[50,16,128]{2,1,0:T(8,128)(2,1)S(1)}, bf16[50,16,128]{2,1,0:T(8,128)(2,1)S(1)}, u32[]{:S(2)}, u32[]{:S(2)}) collective-permute-start(bf16[50,16,128]{2,1,0:T(8,128)(2,1)S(1)} %get-tuple-element.77), channel_id=1, source_target_pairs={{0,24},{1,97},{2,26},{3,99},{4,28},{5,101},{6,30},{7,103},{8,0},{9... | collective-permute-start | bytes 614408 | tf_op jit(solution)/shard_map/ppermute | solution.py:24
  81.5 0.8 collective-permute-start.28
  82.3 5.6 %collective-permute-done.28.received = bf16[2,32,1152]{2,1,0:T(8,128)(2,1)S(1)} collective-permute-done((bf16[2,32,1152]{2,1,0:T(8,128)(2,1)S(1)}, bf16[2,32,1152]{2,1,0:T(8,128)(2,1)S(1)}, u32[]{:S(2)}, u32[]{:S(2)}) %collective-permute-start.28) | collective-permute-done | bytes 147488 | tf_op jit(solution)/shard_map/ppermute | solution.py:24
  88.6 1.2 collective-permute-start.33
  89.7 2.3 %collective-permute-start.34 = (bf16[32,1024]{1,0:T(8,128)(2,1)S(1)}, bf16[32,1024]{1,0:T(8,128)(2,1)S(1)}, u32[]{:S(2)}, u32[]{:S(2)}) collective-permute-start(bf16[32,1024]{1,0:T(8,128)(2,1)S(1)} %get-tuple-element.81), channel_id=1, source_target_pairs={{0,64},{1,17},{2,66},{3,19},{4,68},{5,21},{6,70},{7,23},{8,72},{9,... | collective-permute-start | bytes 196616 | tf_op jit(solution)/shard_map/ppermute | solution.py:24
  92.5 1.9 %factor_first.1 = (f32[32,1024]{1,0:T(8,128)}, f32[32,32]{1,0:T(8,128)S(1)}) custom-call(f32[8,128]{1,0:T(8,128)S(1)} %get-tuple-element.71.gram, bf16[1,32,1152]{2,1,0:T(8,128)(2,1)S(1)} %collective-permute-done.29.received.refs_5_, f32[32,1024]{1,0:T(8,128)S(1)} %get-tuple-element.73.panel), custom_call_target="tpu_custom_call" | custom-call | flops 1000000 | bytes 10000000 | tf_op jit(solution)/shard_map/factor_first/pallas_call | solution.py:492
  94.4 1.1 collective-permute-done.34.refs_3_
  96.9 1.2 collective-permute-done.36.other
  98.1 18.5 %all_to_all.5.gram = f32[64,8,128]{2,1,0:T(8,128)S(1)} all-to-all(f32[64,8,128]{2,1,0:T(8,128)S(1)} %total_gram.1), channel_id=1, replica_groups=mesh['z'=4,'x'=4,'y'=4,'core'=2] {'z','x','y'}, dimensions={0} | all-to-all | bytes 524288 | tf_op jit(solution)/shard_map/all_to_all | solution.py:429
  116.5 2.0 %factor_second.1 = f32[32,1024]{1,0:T(8,128)} custom-call(f32[64,8,128]{2,1,0:T(8,128)S(1)} %all_to_all.5.gram, f32[32,1024]{1,0:T(8,128)S(1)} %get-tuple-element.85.panel), custom_call_target="tpu_custom_call" | custom-call | tf_op jit(solution)/shard_map/factor_second/pallas_call | solution.py:504
  (77 shorter events, 9.8 us)
Async XLA Ops:
  0.6 7.0 %collective-permute-start.3 = (bf16[32,1024]{1,0:T(8,128)(2,1)}, bf16[32,1024]{1,0:T(8,128)(2,1)S(1)}, u32[]{:S(2)}, u32[]{:S(2)}) collective-permute-start(bf16[32,1024]{1,0:T(8,128)(2,1)} %bitcast.5), channel_id=1, source_target_pairs={{0,2},{1,7},{2,0},{3,5},{4,6},{5,3},{6,4},{7,1},{8,10},{9,15},{10,... | collective-permute-start | bytes 196616 | tf_op jit(solution)/shard_map/ppermute | solution.py:24
  2.4 6.3 %collective-permute-start.2 = (bf16[32,1024]{1,0:T(8,128)(2,1)}, bf16[32,1024]{1,0:T(8,128)(2,1)S(1)}, u32[]{:S(2)}, u32[]{:S(2)}) collective-permute-start(bf16[32,1024]{1,0:T(8,128)(2,1)} %bitcast.6), channel_id=1, source_target_pairs={{0,96},{1,25},{2,98},{3,27},{4,100},{5,29},{6,102},{7,31},{8,104},... | collective-permute-start | bytes 196616 | tf_op jit(solution)/shard_map/ppermute | solution.py:24
  6.4 6.1 %collective-permute-start.1 = (bf16[32,1024]{1,0:T(8,128)(2,1)}, bf16[32,1024]{1,0:T(8,128)(2,1)S(1)}, u32[]{:S(2)}, u32[]{:S(2)}) collective-permute-start(bf16[32,1024]{1,0:T(8,128)(2,1)} %bitcast.7), channel_id=1, source_target_pairs={{0,64},{1,17},{2,66},{3,19},{4,68},{5,21},{6,70},{7,23},{8,72},{9,... | collective-permute-start | bytes 196616 | tf_op jit(solution)/shard_map/ppermute | solution.py:24
  6.4 6.4 %collective-permute-start = (bf16[32,1024]{1,0:T(8,128)(2,1)}, bf16[32,1024]{1,0:T(8,128)(2,1)S(1)}, u32[]{:S(2)}, u32[]{:S(2)}) collective-permute-start(bf16[32,1024]{1,0:T(8,128)(2,1)} %bitcast.8), channel_id=1, source_target_pairs={{0,32},{1,9},{2,34},{3,11},{4,36},{5,13},{6,38},{7,15},{8,40},{9,1... | collective-permute-start | bytes 196616 | tf_op jit(solution)/shard_map/ppermute | solution.py:24
  12.8 0.8 copy-start.1
  13.7 6.7 %collective-permute-start.4 = (bf16[2,32,1024]{2,1,0:T(8,128)(2,1)S(1)}, bf16[2,32,1024]{2,1,0:T(8,128)(2,1)S(1)}, u32[]{:S(2)}, u32[]{:S(2)}) collective-permute-start(bf16[2,32,1024]{2,1,0:T(8,128)(2,1)S(1)} %get-tuple-element.44), channel_id=1, source_target_pairs={{0,6},{1,3},{2,4},{3,1},{4,2},{5,7},{6,0},{7,5},{8,14},{9,11},{10,... | collective-permute-start | bytes 393224 | tf_op jit(solution)/shard_map/ppermute | solution.py:24
  15.9 13.2 %collective-permute-start.11 = (bf16[66,16,128]{2,1,0:T(8,128)(2,1)S(1)}, bf16[66,16,128]{2,1,0:T(8,128)(2,1)S(1)}, u32[]{:S(2)}, u32[]{:S(2)}) collective-permute-start(bf16[66,16,128]{2,1,0:T(8,128)(2,1)S(1)} %get-tuple-element.50.g0), channel_id=1, source_target_pairs={{0,24},{1,97},{2,26},{3,99},{4,28},{5,101},{6,30},{7,103},{8,0},{9... | collective-permute-start | bytes 811016 | tf_op jit(solution)/shard_map/ppermute | solution.py:24
  18.7 10.4 %collective-permute-start.10 = (bf16[66,16,128]{2,1,0:T(8,128)(2,1)S(1)}, bf16[66,16,128]{2,1,0:T(8,128)(2,1)S(1)}, u32[]{:S(2)}, u32[]{:S(2)}) collective-permute-start(bf16[66,16,128]{2,1,0:T(8,128)(2,1)S(1)} %get-tuple-element.50.g0), channel_id=1, source_target_pairs={{0,16},{1,65},{2,18},{3,67},{4,20},{5,69},{6,22},{7,71},{8,24},{9,... | collective-permute-start | bytes 811016 | tf_op jit(solution)/shard_map/ppermute | solution.py:24
  19.5 10.1 %collective-permute-start.9 = (bf16[66,16,128]{2,1,0:T(8,128)(2,1)S(1)}, bf16[66,16,128]{2,1,0:T(8,128)(2,1)S(1)}, u32[]{:S(2)}, u32[]{:S(2)}) collective-permute-start(bf16[66,16,128]{2,1,0:T(8,128)(2,1)S(1)} %get-tuple-element.50.g0), channel_id=1, source_target_pairs={{0,8},{1,33},{2,10},{3,35},{4,12},{5,37},{6,14},{7,39},{8,16},{9,4... | collective-permute-start | bytes 811016 | tf_op jit(solution)/shard_map/ppermute | solution.py:24
  20.4 6.1 %collective-permute-start.5 = (bf16[4,32,1024]{2,1,0:T(8,128)(2,1)S(1)}, bf16[4,32,1024]{2,1,0:T(8,128)(2,1)S(1)}, u32[]{:S(2)}, u32[]{:S(2)}) collective-permute-start(bf16[4,32,1024]{2,1,0:T(8,128)(2,1)S(1)} %constant_dynamic-update-slice_fusion.h0), channel_id=1, source_target_pairs={{0,1},{1,0},{2,3},{3,2},{4,5},{5,4},{6,7},{7,6},{8,9},{9,8},{10,11... | collective-permute-start | bytes 786440 | tf_op jit(solution)/shard_map/ppermute | solution.py:24
  21.9 2.8 %copy-start = (bf16[3,1024,1024]{2,1,0:T(8,128)(2,1)S(1)}, bf16[3,1024,1024]{2,1,0:T(8,128)(2,1)}, u32[]{:S(2)}) copy-start(bf16[3,1024,1024]{2,1,0:T(8,128)(2,1)} %blocks.3) | copy-start | bytes 18874372
  29.6 39.5 %slice-start = ((s8[6291456]{0:T(1024)(128)(4,1)}), s8[2097152]{0:T(1024)(128)(4,1)S(1)}, s32[]{:S(2)}) async-start(s8[6291456]{0:T(1024)(128)(4,1)} %bitcast.3), calls=%async_computation.1 | async-start | bytes 4194304
  32.1 3.7 %collective-permute-start.12 = (f16[4,32,1152]{2,1,0:T(8,128)(2,1)S(1)}, f16[4,32,1152]{2,1,0:T(8,128)(2,1)S(1)}, u32[]{:S(2)}, u32[]{:S(2)}) collective-permute-start(f16[4,32,1152]{2,1,0:T(8,128)(2,1)S(1)} %convert_element_type.60), channel_id=1, source_target_pairs={{0,1},{1,0},{2,3},{3,2},{4,5},{5,4},{6,7},{7,6},{8,9},{9,8},{10,11... | collective-permute-start | bytes 884744 | tf_op jit(solution)/shard_map/ppermute | solution.py:24
  32.3 5.8 %collective-permute-start.8 = (f16[50,16,128]{2,1,0:T(8,128)(2,1)S(1)}, f16[50,16,128]{2,1,0:T(8,128)(2,1)S(1)}, u32[]{:S(2)}, u32[]{:S(2)}) collective-permute-start(f16[50,16,128]{2,1,0:T(8,128)(2,1)S(1)} %convert_element_type.58), channel_id=1, source_target_pairs={{0,24},{1,97},{2,26},{3,99},{4,28},{5,101},{6,30},{7,103},{8,0},{9... | collective-permute-start | bytes 614408 | tf_op jit(solution)/shard_map/ppermute | solution.py:24
  33.5 7.3 %collective-permute-start.7 = (f16[50,16,128]{2,1,0:T(8,128)(2,1)S(1)}, f16[50,16,128]{2,1,0:T(8,128)(2,1)S(1)}, u32[]{:S(2)}, u32[]{:S(2)}) collective-permute-start(f16[50,16,128]{2,1,0:T(8,128)(2,1)S(1)} %convert_element_type.56), channel_id=1, source_target_pairs={{0,16},{1,65},{2,18},{3,67},{4,20},{5,69},{6,22},{7,71},{8,24},{9,... | collective-permute-start | bytes 614408 | tf_op jit(solution)/shard_map/ppermute | solution.py:24
  35.5 33.6 %slice-start.1 = ((s8[6291456]{0:T(1024)(128)(4,1)}), s8[4194304]{0:T(1024)(128)(4,1)S(1)}, s32[]{:S(2)}) async-start(s8[6291456]{0:T(1024)(128)(4,1)} %bitcast.3), calls=%async_computation.2 | async-start | bytes 8388608
  35.5 7.5 %collective-permute-start.6 = (f16[50,16,128]{2,1,0:T(8,128)(2,1)S(1)}, f16[50,16,128]{2,1,0:T(8,128)(2,1)S(1)}, u32[]{:S(2)}, u32[]{:S(2)}) collective-permute-start(f16[50,16,128]{2,1,0:T(8,128)(2,1)S(1)} %convert_element_type.54), channel_id=1, source_target_pairs={{0,8},{1,33},{2,10},{3,35},{4,12},{5,37},{6,14},{7,39},{8,16},{9,4... | collective-permute-start | bytes 614408 | tf_op jit(solution)/shard_map/ppermute | solution.py:24
  36.1 11.0 %collective-permute-start.13 = (f16[2,32,1152]{2,1,0:T(8,128)(2,1)S(1)}, f16[2,32,1152]{2,1,0:T(8,128)(2,1)S(1)}, u32[]{:S(2)}, u32[]{:S(2)}) collective-permute-start(f16[2,32,1152]{2,1,0:T(8,128)(2,1)S(1)} %convert_element_type.62), channel_id=1, source_target_pairs={{0,6},{1,3},{2,4},{3,1},{4,2},{5,7},{6,0},{7,5},{8,14},{9,11},{10,... | collective-permute-start | bytes 442376 | tf_op jit(solution)/shard_map/ppermute | solution.py:24
  44.0 4.4 %collective-permute-start.16 = (f16[32,1152]{1,0:T(8,128)(2,1)S(1)}, f16[32,1152]{1,0:T(8,128)(2,1)S(1)}, u32[]{:S(2)}, u32[]{:S(2)}) collective-permute-start(f16[32,1152]{1,0:T(8,128)(2,1)S(1)} %convert_element_type.68), channel_id=1, source_target_pairs={{0,96},{1,25},{2,98},{3,27},{4,100},{5,29},{6,102},{7,31},{8,104},... | collective-permute-start | bytes 221192 | tf_op jit(solution)/shard_map/ppermute | solution.py:24
  45.0 5.9 %collective-permute-start.15 = (f16[32,1152]{1,0:T(8,128)(2,1)S(1)}, f16[32,1152]{1,0:T(8,128)(2,1)S(1)}, u32[]{:S(2)}, u32[]{:S(2)}) collective-permute-start(f16[32,1152]{1,0:T(8,128)(2,1)S(1)} %convert_element_type.66), channel_id=1, source_target_pairs={{0,64},{1,17},{2,66},{3,19},{4,68},{5,21},{6,70},{7,23},{8,72},{9,... | collective-permute-start | bytes 221192 | tf_op jit(solution)/shard_map/ppermute | solution.py:24
  45.8 5.8 %collective-permute-start.14 = (f16[32,1152]{1,0:T(8,128)(2,1)S(1)}, f16[32,1152]{1,0:T(8,128)(2,1)S(1)}, u32[]{:S(2)}, u32[]{:S(2)}) collective-permute-start(f16[32,1152]{1,0:T(8,128)(2,1)S(1)} %convert_element_type.64), channel_id=1, source_target_pairs={{0,32},{1,9},{2,34},{3,11},{4,36},{5,13},{6,38},{7,15},{8,40},{9,1... | collective-permute-start | bytes 221192 | tf_op jit(solution)/shard_map/ppermute | solution.py:24
  47.4 4.4 %collective-permute-start.17 = (f16[1,32,1152]{2,1,0:T(8,128)(2,1)S(1)}, f16[1,32,1152]{2,1,0:T(8,128)(2,1)S(1)}, u32[]{:S(2)}, u32[]{:S(2)}) collective-permute-start(f16[1,32,1152]{2,1,0:T(8,128)(2,1)S(1)} %convert_element_type.70), channel_id=1, source_target_pairs={{0,2},{1,7},{2,0},{3,5},{4,6},{5,3},{6,4},{7,1},{8,10},{9,15},{10,... | collective-permute-start | bytes 221192 | tf_op jit(solution)/shard_map/ppermute | solution.py:24
  52.1 8.8 %collective-permute-start.20 = (bf16[32,1152]{1,0:T(8,128)(2,1)S(1)}, bf16[32,1152]{1,0:T(8,128)(2,1)S(1)}, u32[]{:S(2)}, u32[]{:S(2)}) collective-permute-start(bf16[32,1152]{1,0:T(8,128)(2,1)S(1)} %get-tuple-element.60.refs_0_), channel_id=1, source_target_pairs={{0,96},{1,25},{2,98},{3,27},{4,100},{5,29},{6,102},{7,31},{8,104},... | collective-permute-start | bytes 221192 | tf_op jit(solution)/shard_map/ppermute | solution.py:24
  54.1 6.9 %collective-permute-start.19 = (bf16[32,1152]{1,0:T(8,128)(2,1)S(1)}, bf16[32,1152]{1,0:T(8,128)(2,1)S(1)}, u32[]{:S(2)}, u32[]{:S(2)}) collective-permute-start(bf16[32,1152]{1,0:T(8,128)(2,1)S(1)} %get-tuple-element.60.refs_0_), channel_id=1, source_target_pairs={{0,64},{1,17},{2,66},{3,19},{4,68},{5,21},{6,70},{7,23},{8,72},{9,... | collective-permute-start | bytes 221192 | tf_op jit(solution)/shard_map/ppermute | solution.py:24
  55.6 5.6 %collective-permute-start.18 = (bf16[32,1152]{1,0:T(8,128)(2,1)S(1)}, bf16[32,1152]{1,0:T(8,128)(2,1)S(1)}, u32[]{:S(2)}, u32[]{:S(2)}) collective-permute-start(bf16[32,1152]{1,0:T(8,128)(2,1)S(1)} %get-tuple-element.60.refs_0_), channel_id=1, source_target_pairs={{0,32},{1,9},{2,34},{3,11},{4,36},{5,13},{6,38},{7,15},{8,40},{9,1... | collective-permute-start | bytes 221192 | tf_op jit(solution)/shard_map/ppermute | solution.py:24
  56.7 4.3 %collective-permute-start.21 = (bf16[32,1024]{1,0:T(8,128)(2,1)S(1)}, bf16[32,1024]{1,0:T(8,128)(2,1)S(1)}, u32[]{:S(2)}, u32[]{:S(2)}) collective-permute-start(bf16[32,1024]{1,0:T(8,128)(2,1)S(1)} %get-tuple-element.61.refs_4_), channel_id=1, source_target_pairs={{0,2},{1,7},{2,0},{3,5},{4,6},{5,3},{6,4},{7,1},{8,10},{9,15},{10,... | collective-permute-start | bytes 196616 | tf_op jit(solution)/shard_map/ppermute | solution.py:24
  61.2 6.3 %collective-permute-start.25 = (bf16[2,32,1024]{2,1,0:T(8,128)(2,1)S(1)}, bf16[2,32,1024]{2,1,0:T(8,128)(2,1)S(1)}, u32[]{:S(2)}, u32[]{:S(2)}) collective-permute-start(bf16[2,32,1024]{2,1,0:T(8,128)(2,1)S(1)} %get-tuple-element.63), channel_id=1, source_target_pairs={{0,6},{1,3},{2,4},{3,1},{4,2},{5,7},{6,0},{7,5},{8,14},{9,11},{10,... | collective-permute-start | bytes 393224 | tf_op jit(solution)/shard_map/ppermute | solution.py:24
  63.9 7.5 %collective-permute-start.24 = (bf16[66,16,128]{2,1,0:T(8,128)(2,1)S(1)}, bf16[66,16,128]{2,1,0:T(8,128)(2,1)S(1)}, u32[]{:S(2)}, u32[]{:S(2)}) collective-permute-start(bf16[66,16,128]{2,1,0:T(8,128)(2,1)S(1)} %get-tuple-element.62.g0), channel_id=1, source_target_pairs={{0,24},{1,97},{2,26},{3,99},{4,28},{5,101},{6,30},{7,103},{8,0},{9... | collective-permute-start | bytes 811016 | tf_op jit(solution)/shard_map/ppermute | solution.py:24
  64.4 8.1 %collective-permute-start.23 = (bf16[66,16,128]{2,1,0:T(8,128)(2,1)S(1)}, bf16[66,16,128]{2,1,0:T(8,128)(2,1)S(1)}, u32[]{:S(2)}, u32[]{:S(2)}) collective-permute-start(bf16[66,16,128]{2,1,0:T(8,128)(2,1)S(1)} %get-tuple-element.62.g0), channel_id=1, source_target_pairs={{0,16},{1,65},{2,18},{3,67},{4,20},{5,69},{6,22},{7,71},{8,24},{9,... | collective-permute-start | bytes 811016 | tf_op jit(solution)/shard_map/ppermute | solution.py:24
  65.4 9.9 %collective-permute-start.22 = (bf16[66,16,128]{2,1,0:T(8,128)(2,1)S(1)}, bf16[66,16,128]{2,1,0:T(8,128)(2,1)S(1)}, u32[]{:S(2)}, u32[]{:S(2)}) collective-permute-start(bf16[66,16,128]{2,1,0:T(8,128)(2,1)S(1)} %get-tuple-element.62.g0), channel_id=1, source_target_pairs={{0,8},{1,33},{2,10},{3,35},{4,12},{5,37},{6,14},{7,39},{8,16},{9,4... | collective-permute-start | bytes 811016 | tf_op jit(solution)/shard_map/ppermute | solution.py:24
  67.5 1.6 %collective-permute-start.26 = (bf16[4,32,1024]{2,1,0:T(8,128)(2,1)S(1)}, bf16[4,32,1024]{2,1,0:T(8,128)(2,1)S(1)}, u32[]{:S(2)}, u32[]{:S(2)}) collective-permute-start(bf16[4,32,1024]{2,1,0:T(8,128)(2,1)S(1)} %constant_dynamic-update-slice_fusion.2.h0), channel_id=1, source_target_pairs={{0,1},{1,0},{2,3},{3,2},{4,5},{5,4},{6,7},{7,6},{8,9},{9,8},{10,11... | collective-permute-start | bytes 786440 | tf_op jit(solution)/shard_map/ppermute | solution.py:24
  77.6 3.8 %collective-permute-start.27 = (bf16[4,32,1152]{2,1,0:T(8,128)(2,1)S(1)}, bf16[4,32,1152]{2,1,0:T(8,128)(2,1)S(1)}, u32[]{:S(2)}, u32[]{:S(2)}) collective-permute-start(bf16[4,32,1152]{2,1,0:T(8,128)(2,1)S(1)} %get-tuple-element.66), channel_id=1, source_target_pairs={{0,1},{1,0},{2,3},{3,2},{4,5},{5,4},{6,7},{7,6},{8,9},{9,8},{10,11... | collective-permute-start | bytes 884744 | tf_op jit(solution)/shard_map/ppermute | solution.py:24
  77.7 10.3 %collective-permute-start.30 = (bf16[50,16,128]{2,1,0:T(8,128)(2,1)S(1)}, bf16[50,16,128]{2,1,0:T(8,128)(2,1)S(1)}, u32[]{:S(2)}, u32[]{:S(2)}) collective-permute-start(bf16[50,16,128]{2,1,0:T(8,128)(2,1)S(1)} %get-tuple-element.75), channel_id=1, source_target_pairs={{0,8},{1,33},{2,10},{3,35},{4,12},{5,37},{6,14},{7,39},{8,16},{9,4... | collective-permute-start | bytes 614408 | tf_op jit(solution)/shard_map/ppermute | solution.py:24
  77.8 10.3 %collective-permute-start.31 = (bf16[50,16,128]{2,1,0:T(8,128)(2,1)S(1)}, bf16[50,16,128]{2,1,0:T(8,128)(2,1)S(1)}, u32[]{:S(2)}, u32[]{:S(2)}) collective-permute-start(bf16[50,16,128]{2,1,0:T(8,128)(2,1)S(1)} %get-tuple-element.76), channel_id=1, source_target_pairs={{0,16},{1,65},{2,18},{3,67},{4,20},{5,69},{6,22},{7,71},{8,24},{9,... | collective-permute-start | bytes 614408 | tf_op jit(solution)/shard_map/ppermute | solution.py:24
  78.8 9.2 %collective-permute-start.32 = (bf16[50,16,128]{2,1,0:T(8,128)(2,1)S(1)}, bf16[50,16,128]{2,1,0:T(8,128)(2,1)S(1)}, u32[]{:S(2)}, u32[]{:S(2)}) collective-permute-start(bf16[50,16,128]{2,1,0:T(8,128)(2,1)S(1)} %get-tuple-element.77), channel_id=1, source_target_pairs={{0,24},{1,97},{2,26},{3,99},{4,28},{5,101},{6,30},{7,103},{8,0},{9... | collective-permute-start | bytes 614408 | tf_op jit(solution)/shard_map/ppermute | solution.py:24
  81.5 6.4 %collective-permute-start.28 = (bf16[2,32,1152]{2,1,0:T(8,128)(2,1)S(1)}, bf16[2,32,1152]{2,1,0:T(8,128)(2,1)S(1)}, u32[]{:S(2)}, u32[]{:S(2)}) collective-permute-start(bf16[2,32,1152]{2,1,0:T(8,128)(2,1)S(1)} %get-tuple-element.69), channel_id=1, source_target_pairs={{0,6},{1,3},{2,4},{3,1},{4,2},{5,7},{6,0},{7,5},{8,14},{9,11},{10,... | collective-permute-start | bytes 442376 | tf_op jit(solution)/shard_map/ppermute | solution.py:24
  87.9 4.6 %collective-permute-start.29 = (bf16[1,32,1152]{2,1,0:T(8,128)(2,1)S(1)}, bf16[1,32,1152]{2,1,0:T(8,128)(2,1)S(1)}, u32[]{:S(2)}, u32[]{:S(2)}) collective-permute-start(bf16[1,32,1152]{2,1,0:T(8,128)(2,1)S(1)} %get-tuple-element.72), channel_id=1, source_target_pairs={{0,2},{1,7},{2,0},{3,5},{4,6},{5,3},{6,4},{7,1},{8,10},{9,15},{10,... | collective-permute-start | bytes 221192 | tf_op jit(solution)/shard_map/ppermute | solution.py:24
  88.6 5.8 %collective-permute-start.33 = (bf16[32,1024]{1,0:T(8,128)(2,1)S(1)}, bf16[32,1024]{1,0:T(8,128)(2,1)S(1)}, u32[]{:S(2)}, u32[]{:S(2)}) collective-permute-start(bf16[32,1024]{1,0:T(8,128)(2,1)S(1)} %get-tuple-element.80), channel_id=1, source_target_pairs={{0,32},{1,9},{2,34},{3,11},{4,36},{5,13},{6,38},{7,15},{8,40},{9,1... | collective-permute-start | bytes 196616 | tf_op jit(solution)/shard_map/ppermute | solution.py:24
  89.7 5.8 %collective-permute-start.34 = (bf16[32,1024]{1,0:T(8,128)(2,1)S(1)}, bf16[32,1024]{1,0:T(8,128)(2,1)S(1)}, u32[]{:S(2)}, u32[]{:S(2)}) collective-permute-start(bf16[32,1024]{1,0:T(8,128)(2,1)S(1)} %get-tuple-element.81), channel_id=1, source_target_pairs={{0,64},{1,17},{2,66},{3,19},{4,68},{5,21},{6,70},{7,23},{8,72},{9,... | collective-permute-start | bytes 196616 | tf_op jit(solution)/shard_map/ppermute | solution.py:24
  92.0 4.3 %collective-permute-start.35 = (bf16[32,1024]{1,0:T(8,128)(2,1)S(1)}, bf16[32,1024]{1,0:T(8,128)(2,1)S(1)}, u32[]{:S(2)}, u32[]{:S(2)}) collective-permute-start(bf16[32,1024]{1,0:T(8,128)(2,1)S(1)} %get-tuple-element.82), channel_id=1, source_target_pairs={{0,96},{1,25},{2,98},{3,27},{4,100},{5,29},{6,102},{7,31},{8,104},... | collective-permute-start | bytes 196616 | tf_op jit(solution)/shard_map/ppermute | solution.py:24
  96.9 1.2 %collective-permute-start.36 = (f32[8,128]{1,0:T(8,128)S(1)}, f32[8,128]{1,0:T(8,128)S(1)}, u32[]{:S(2)}, u32[]{:S(2)}) collective-permute-start(f32[8,128]{1,0:T(8,128)S(1)} %get-tuple-element.84.own), channel_id=1, source_target_pairs={{0,1},{1,0},{2,3},{3,2},{4,5},{5,4},{6,7},{7,6},{8,9},{9,8},{10,11... | collective-permute-start | bytes 12296 | tf_op jit(solution)/shard_map/ppermute | solution.py:24

commit v6 on v5

--- a/solution.py
+++ b/solution.py
@@ -314,9 +314,10 @@
     received, outs, (weights, total) = refs[:3], refs[3:7], refs[7:]
     entries = [(array, k) for array in received for k in range(3)]
     extras = [take_extra(array, 3).astype(jnp.float32) for array in received]
+    powers = [jnp.exp2(extra) for extra in extras]
     for e, (array, k) in enumerate(entries):
         extra = extras[e // 3]
-        scale = jnp.exp2(extra[:, 8 * k + 4 : 8 * k + 5]) if half else 1.0
+        scale = powers[e // 3][:, 8 * k + 4 : 8 * k + 5] if half else 1.0
         for s in range(4):
             weights[4 * e + s] = jnp.broadcast_to(extra[:, 8 * k + s : 8 * k + s + 1] * scale, (32, 128))
     for i in range(2):
@@ -411,21 +412,21 @@
     )(*parts, inverse)
 
 
-def total_kernel(own, other, out):
+def total_kernel(own, other, after, out):
     total = own[...] + other[...]
     for k in range(64):
         out[k] = total
 
 
-def total_gram(tile):
+def total_gram(tile, after):
     tiles = pl.pallas_call(
         total_kernel,
         out_shape=struct((64, 8, 128), jnp.float32),
-        in_specs=[VMEM] * 2,
+        in_specs=[VMEM] * 2 + [pl.BlockSpec(memory_space=pl.ANY)],
         out_specs=VMEM,
         compiler_params=PARAMS,
         name="total_gram",
-    )(tile, send_core(tile))
+    )(tile, send_core(tile), after)
     return lax.all_to_all(tiles, ("z", "x", "y"), 0, 0, tiled=True)
 
 
@@ -481,23 +482,37 @@
     )
 
 
-def factor_first_kernel(root, gram, received, panel, basis, inverse):
+def invert_kernel(gram, received, inverse):
     inverse[...] = lower_inverse(unfold(gram[...] + merge(received[0, :, 1024:1152])))
+
+
+def invert_first(gram, received):
+    return pl.pallas_call(
+        invert_kernel,
+        out_shape=struct((32, 32), jnp.float32),
+        in_specs=[VMEM] * 2,
+        out_specs=VMEM,
+        compiler_params=PARAMS,
+        name="invert_first",
+    )(gram, received)
+
+
+def basis_kernel(root, inverse, first, after, basis, done):
     basis[...] = (
-        jnp.dot(inverse[...], panel[...], precision=HIGHEST, preferred_element_type=jnp.float32) * root
+        jnp.dot(inverse[...], first[...], precision=HIGHEST, preferred_element_type=jnp.float32) * root
     )
-
-
-def factor_first(gram, received, first, root):
-    return pl.pallas_call(
-        functools.partial(factor_first_kernel, root),
-        out_shape=[struct((32, 1024), jnp.float32), struct((32, 32), jnp.float32)],
-        in_specs=[VMEM] * 3,
+    done[...] = jnp.zeros_like(done)
+
+
+def apply_first(inverse, first, after, root):
+    return pl.pallas_call(
+        functools.partial(basis_kernel, root),
+        out_shape=[struct((32, 1024), jnp.float32), struct((8, 128), jnp.float32)],
+        in_specs=[VMEM] * 2 + [pl.BlockSpec(memory_space=pl.ANY)],
         out_specs=[VMEM] * 2,
         compiler_params=PARAMS,
-        cost_estimate=pl.CostEstimate(flops=1_000_000, bytes_accessed=10_000_000, transcendentals=0),
-        name="factor_first",
-    )(gram, received, first)
+        name="apply_first",
+    )(inverse, first, after)
 
 
 def factor_second(gram, scaled, root):
@@ -562,9 +577,10 @@
     gathered, pair_gathered = gather(panel, own, True)
     parts = product(block_pairs, live_counts, pair_blocks, turned, gathered, pair_gathered, False)
     parts, (gram,) = scatter(parts)
-    first_basis, inverse = factor_first(gram, parts[5], first, root)
-    scaled, tiles = finish_second(parts, inverse)
-    embedding = factor_second(total_gram(tiles), scaled, root)
+    inverse = invert_first(gram, parts[5])
+    scaled, tile = finish_second(parts, inverse)
+    first_basis, done = apply_first(inverse, first, tile, root)
+    embedding = factor_second(total_gram(tile, done), scaled, root)
     return (first_basis[None], embedding[None])
 
 

time: 119 us -> 120 us (level)
  transfers between devices with their start and end apart: 37 -> 37, of which waited for: 21 -> 20; matrix products, arithmetic and copies ran while one was open for 1% -> 1% of each run, Pallas kernels for 9% -> 9%
where the time goes in v6:
time: 120 us; the launch traced here: 119 us
  starting transfers between devices  43.2 us (36%)
  waiting for transfers between devices  32.2 us (27%)
  blocking collectives  19.1 us (16%)
  Pallas kernels  18.3 us (15%)
  local copies, waits for them, and re-layouts  4.44 us (4%)
  between operations  1.65 us (1%)
    ppermute x37, starting transfers between devices, permute(): return lax.ppermute(value, AXES, pairs)  43.2 us
    ppermute x37, waiting for transfers between devices, permute(): return lax.ppermute(value, AXES, pairs)  32.2 us
    all_to_all x1, blocking collectives, total_gram(): return lax.all_to_all(tiles, ('z', 'x', 'y'), 0, 0, tiled=True)  19.1 us
    pallas_call x4, Pallas kernels, product_call(): pl.pallas_call(kernel, out_shape=outs, in_specs=[SMEM, SMEM] + [VMEM] * l...  9.63 us
    unnamed x11, local copies, waits for them, and re-layouts  4.42 us
  transfers between devices with their start and end apart: 37, of which 20 were waited for; matrix products, arithmetic and copies ran while one was open for 1% of the time, Pallas kernels for 9%

profile of v6, /device:TPU:0, one launch (start us, length us, event | category | flops | bytes accessed | tf_op | source)
XLA Modules:
  0.0 119.4 jit_solution(18222211006615562063)
XLA Ops:
  0.6 1.7 %collective-permute-start.3 = (bf16[32,1024]{1,0:T(8,128)(2,1)}, bf16[32,1024]{1,0:T(8,128)(2,1)S(1)}, u32[]{:S(2)}, u32[]{:S(2)}) collective-permute-start(bf16[32,1024]{1,0:T(8,128)(2,1)} %bitcast.5), channel_id=1, source_target_pairs={{0,2},{1,7},{2,0},{3,5},{4,6},{5,3},{6,4},{7,1},{8,10},{9,15},{10,... | collective-permute-start | bytes 196616 | tf_op jit(solution)/shard_map/ppermute | solution.py:24
  2.4 4.0 %collective-permute-start.2 = (bf16[32,1024]{1,0:T(8,128)(2,1)}, bf16[32,1024]{1,0:T(8,128)(2,1)S(1)}, u32[]{:S(2)}, u32[]{:S(2)}) collective-permute-start(bf16[32,1024]{1,0:T(8,128)(2,1)} %bitcast.6), channel_id=1, source_target_pairs={{0,96},{1,25},{2,98},{3,27},{4,100},{5,29},{6,102},{7,31},{8,104},... | collective-permute-start | bytes 196616 | tf_op jit(solution)/shard_map/ppermute | solution.py:24
  6.4 1.3 %collective-permute-start = (bf16[32,1024]{1,0:T(8,128)(2,1)}, bf16[32,1024]{1,0:T(8,128)(2,1)S(1)}, u32[]{:S(2)}, u32[]{:S(2)}) collective-permute-start(bf16[32,1024]{1,0:T(8,128)(2,1)} %bitcast.8), channel_id=1, source_target_pairs={{0,32},{1,9},{2,34},{3,11},{4,36},{5,13},{6,38},{7,15},{8,40},{9,1... | collective-permute-start | bytes 196616 | tf_op jit(solution)/shard_map/ppermute | solution.py:24
  7.7 1.0 collective-permute-done.2.refs_3_
  8.6 3.9 %collective-permute-done.1.refs_2_ = bf16[32,1024]{1,0:T(8,128)(2,1)S(1)} collective-permute-done((bf16[32,1024]{1,0:T(8,128)(2,1)}, bf16[32,1024]{1,0:T(8,128)(2,1)S(1)}, u32[]{:S(2)}, u32[]{:S(2)}) %collective-permute-start.1) | collective-permute-done | bytes 65568 | tf_op jit(solution)/shard_map/ppermute | solution.py:24
  12.8 0.8 copy-done.1
  13.7 2.3 %collective-permute-start.4 = (bf16[2,32,1024]{2,1,0:T(8,128)(2,1)S(1)}, bf16[2,32,1024]{2,1,0:T(8,128)(2,1)S(1)}, u32[]{:S(2)}, u32[]{:S(2)}) collective-permute-start(bf16[2,32,1024]{2,1,0:T(8,128)(2,1)S(1)} %get-tuple-element.44), channel_id=1, source_target_pairs={{0,6},{1,3},{2,4},{3,1},{4,2},{5,7},{6,0},{7,5},{8,14},{9,11},{10,... | collective-permute-start | bytes 393224 | tf_op jit(solution)/shard_map/ppermute | solution.py:24
  15.9 2.8 %collective-permute-start.11 = (bf16[66,16,128]{2,1,0:T(8,128)(2,1)S(1)}, bf16[66,16,128]{2,1,0:T(8,128)(2,1)S(1)}, u32[]{:S(2)}, u32[]{:S(2)}) collective-permute-start(bf16[66,16,128]{2,1,0:T(8,128)(2,1)S(1)} %get-tuple-element.50.g0), channel_id=1, source_target_pairs={{0,24},{1,97},{2,26},{3,99},{4,28},{5,101},{6,30},{7,103},{8,0},{9... | collective-permute-start | bytes 811016 | tf_op jit(solution)/shard_map/ppermute | solution.py:24
  18.7 0.8 collective-permute-start.10
  19.5 0.9 collective-permute-start.9
  21.2 0.8 copy.9.pairs
  21.9 2.8 %copy-done = bf16[3,1024,1024]{2,1,0:T(8,128)(2,1)S(1)} copy-done((bf16[3,1024,1024]{2,1,0:T(8,128)(2,1)S(1)}, bf16[3,1024,1024]{2,1,0:T(8,128)(2,1)}, u32[]{:S(2)}) %copy-start) | copy-done | bytes 6291480
  24.7 1.8 %turn.1.turned = bf16[3,1024,1024]{2,1,0:T(8,128)(2,1)S(1)} custom-call(bf16[3,1024,1024]{2,1,0:T(8,128)(2,1)S(1)} %copy-done), custom_call_target="tpu_custom_call" | custom-call | bytes 6000000 | tf_op jit(solution)/shard_map/turn/pallas_call | solution.py:559
  26.6 2.5 %mirror.2 = (f32[4,32,1024]{2,1,0:T(8,128)S(1)}, f32[50,16,128]{2,1,0:T(8,128)S(1)}, f32[50,16,128]{2,1,0:T(8,128)S(1)}, f32[50,16,128]{2,1,0:T(8,128)S(1)}) custom-call(s32[1,3,2]{2,1,0:T(4,128)S(1)} %copy.9.pairs, s32[1]{0:T(128)S(6)} %copy.12.live, bf16[3,1024,1024]{2,1,0:T(8,128)(2,1)S(1)} %copy-done, ...), custom_call_target="tpu_custom_call" | custom-call | tf_op jit(solution)/shard_map/mirror/pallas_call | solution.py:228
  29.6 2.5 %direct.2 = (f32[4,32,1024]{2,1,0:T(8,128)S(1)}, f32[4,32,1152]{2,1,0:T(8,128)S(1)}) custom-call(s32[1,3,2]{2,1,0:T(4,128)S(1)} %copy.9.pairs, s32[1]{0:T(128)S(6)} %copy.12.live, bf16[3,1024,1024]{2,1,0:T(8,128)(2,1)S(1)} %turn.1.turned, bf16[66,16,128]{2,1,0:T(8,128)(2,1)S(1)} %get-tuple-element.50.g0, bf16[66,16,128]{2,1,0:T(8,128)(2,1)S(1)} %collective-permute-done.9.g1, ...), custom_call_target="tpu_custom_call" | custom-call | tf_op jit(solution)/shard_map/direct/pallas_call | solution.py:228
  32.3 1.2 collective-permute-start.8
  33.5 2.8 %collective-permute-start.7 = (f16[50,16,128]{2,1,0:T(8,128)(2,1)S(1)}, f16[50,16,128]{2,1,0:T(8,128)(2,1)S(1)}, u32[]{:S(2)}, u32[]{:S(2)}) collective-permute-start(f16[50,16,128]{2,1,0:T(8,128)(2,1)S(1)} %convert_element_type.56), channel_id=1, source_target_pairs={{0,16},{1,65},{2,18},{3,67},{4,20},{5,69},{6,22},{7,71},{8,24},{9,... | collective-permute-start | bytes 614408 | tf_op jit(solution)/shard_map/ppermute | solution.py:24
  36.8 2.2 %collective-permute-start.13 = (f16[2,32,1152]{2,1,0:T(8,128)(2,1)S(1)}, f16[2,32,1152]{2,1,0:T(8,128)(2,1)S(1)}, u32[]{:S(2)}, u32[]{:S(2)}) collective-permute-start(f16[2,32,1152]{2,1,0:T(8,128)(2,1)S(1)} %convert_element_type.62), channel_id=1, source_target_pairs={{0,6},{1,3},{2,4},{3,1},{4,2},{5,7},{6,0},{7,5},{8,14},{9,11},{10,... | collective-permute-start | bytes 442376 | tf_op jit(solution)/shard_map/ppermute | solution.py:24
  39.0 1.8 %collective-permute-done.7 = f16[50,16,128]{2,1,0:T(8,128)(2,1)S(1)} collective-permute-done((f16[50,16,128]{2,1,0:T(8,128)(2,1)S(1)}, f16[50,16,128]{2,1,0:T(8,128)(2,1)S(1)}, u32[]{:S(2)}, u32[]{:S(2)}) %collective-permute-start.7) | collective-permute-done | bytes 204832 | tf_op jit(solution)/shard_map/ppermute | solution.py:24
  40.8 2.6 %collective-permute-done.6 = f16[50,16,128]{2,1,0:T(8,128)(2,1)S(1)} collective-permute-done((f16[50,16,128]{2,1,0:T(8,128)(2,1)S(1)}, f16[50,16,128]{2,1,0:T(8,128)(2,1)S(1)}, u32[]{:S(2)}, u32[]{:S(2)}) %collective-permute-start.6) | collective-permute-done | bytes 204832 | tf_op jit(solution)/shard_map/ppermute | solution.py:24
  43.4 1.0 add_outer.2
  44.5 2.0 %collective-permute-start.15 = (f16[32,1152]{1,0:T(8,128)(2,1)S(1)}, f16[32,1152]{1,0:T(8,128)(2,1)S(1)}, u32[]{:S(2)}, u32[]{:S(2)}) collective-permute-start(f16[32,1152]{1,0:T(8,128)(2,1)S(1)} %convert_element_type.66), channel_id=1, source_target_pairs={{0,64},{1,17},{2,66},{3,19},{4,68},{5,21},{6,70},{7,23},{8,72},{9,... | collective-permute-start | bytes 221192 | tf_op jit(solution)/shard_map/ppermute | solution.py:24
  46.5 1.3 %collective-permute-start.14 = (f16[32,1152]{1,0:T(8,128)(2,1)S(1)}, f16[32,1152]{1,0:T(8,128)(2,1)S(1)}, u32[]{:S(2)}, u32[]{:S(2)}) collective-permute-start(f16[32,1152]{1,0:T(8,128)(2,1)S(1)} %convert_element_type.64), channel_id=1, source_target_pairs={{0,32},{1,9},{2,34},{3,11},{4,36},{5,13},{6,38},{7,15},{8,40},{9,1... | collective-permute-start | bytes 221192 | tf_op jit(solution)/shard_map/ppermute | solution.py:24
  48.9 1.6 %collective-permute-done.15 = f16[32,1152]{1,0:T(8,128)(2,1)S(1)} collective-permute-done((f16[32,1152]{1,0:T(8,128)(2,1)S(1)}, f16[32,1152]{1,0:T(8,128)(2,1)S(1)}, u32[]{:S(2)}, u32[]{:S(2)}) %collective-permute-start.15) | collective-permute-done | bytes 73760 | tf_op jit(solution)/shard_map/ppermute | solution.py:24
  50.5 1.6 %collective-permute-done.14 = f16[32,1152]{1,0:T(8,128)(2,1)S(1)} collective-permute-done((f16[32,1152]{1,0:T(8,128)(2,1)S(1)}, f16[32,1152]{1,0:T(8,128)(2,1)S(1)}, u32[]{:S(2)}, u32[]{:S(2)}) %collective-permute-start.14) | collective-permute-done | bytes 73760 | tf_op jit(solution)/shard_map/ppermute | solution.py:24
  52.8 1.9 %collective-permute-start.20 = (bf16[32,1152]{1,0:T(8,128)(2,1)S(1)}, bf16[32,1152]{1,0:T(8,128)(2,1)S(1)}, u32[]{:S(2)}, u32[]{:S(2)}) collective-permute-start(bf16[32,1152]{1,0:T(8,128)(2,1)S(1)} %get-tuple-element.60.refs_0_), channel_id=1, source_target_pairs={{0,96},{1,25},{2,98},{3,27},{4,100},{5,29},{6,102},{7,31},{8,104},... | collective-permute-start | bytes 221192 | tf_op jit(solution)/shard_map/ppermute | solution.py:24
  54.8 1.0 collective-permute-start.19
  55.8 1.3 %collective-permute-start.18 = (bf16[32,1152]{1,0:T(8,128)(2,1)S(1)}, bf16[32,1152]{1,0:T(8,128)(2,1)S(1)}, u32[]{:S(2)}, u32[]{:S(2)}) collective-permute-start(bf16[32,1152]{1,0:T(8,128)(2,1)S(1)} %get-tuple-element.60.refs_0_), channel_id=1, source_target_pairs={{0,32},{1,9},{2,34},{3,11},{4,36},{5,13},{6,38},{7,15},{8,40},{9,1... | collective-permute-start | bytes 221192 | tf_op jit(solution)/shard_map/ppermute | solution.py:24
  57.8 3.7 %collective-permute-done.21.refs_5_ = bf16[32,1024]{1,0:T(8,128)(2,1)S(1)} collective-permute-done((bf16[32,1024]{1,0:T(8,128)(2,1)S(1)}, bf16[32,1024]{1,0:T(8,128)(2,1)S(1)}, u32[]{:S(2)}, u32[]{:S(2)}) %collective-permute-start.21) | collective-permute-done | bytes 65568 | tf_op jit(solution)/shard_map/ppermute | solution.py:24
  61.6 2.1 %collective-permute-start.25 = (bf16[2,32,1024]{2,1,0:T(8,128)(2,1)S(1)}, bf16[2,32,1024]{2,1,0:T(8,128)(2,1)S(1)}, u32[]{:S(2)}, u32[]{:S(2)}) collective-permute-start(bf16[2,32,1024]{2,1,0:T(8,128)(2,1)S(1)} %get-tuple-element.63), channel_id=1, source_target_pairs={{0,6},{1,3},{2,4},{3,1},{4,2},{5,7},{6,0},{7,5},{8,14},{9,11},{10,... | collective-permute-start | bytes 393224 | tf_op jit(solution)/shard_map/ppermute | solution.py:24
  63.8 2.0 %collective-permute-start.23 = (bf16[66,16,128]{2,1,0:T(8,128)(2,1)S(1)}, bf16[66,16,128]{2,1,0:T(8,128)(2,1)S(1)}, u32[]{:S(2)}, u32[]{:S(2)}) collective-permute-start(bf16[66,16,128]{2,1,0:T(8,128)(2,1)S(1)} %get-tuple-element.62.g0), channel_id=1, source_target_pairs={{0,16},{1,65},{2,18},{3,67},{4,20},{5,69},{6,22},{7,71},{8,24},{9,... | collective-permute-start | bytes 811016 | tf_op jit(solution)/shard_map/ppermute | solution.py:24
  65.8 0.8 collective-permute-start.22
  66.7 1.2 collective-permute-done.25
  68.0 1.5 %collective-permute-done.26.h1 = bf16[4,32,1024]{2,1,0:T(8,128)(2,1)S(1)} collective-permute-done((bf16[4,32,1024]{2,1,0:T(8,128)(2,1)S(1)}, bf16[4,32,1024]{2,1,0:T(8,128)(2,1)S(1)}, u32[]{:S(2)}, u32[]{:S(2)}) %collective-permute-start.26) | collective-permute-done | bytes 262176 | tf_op jit(solution)/shard_map/ppermute | solution.py:24
  69.5 2.3 %mirror.3 = (f32[4,32,1024]{2,1,0:T(8,128)S(1)}, bf16[50,16,128]{2,1,0:T(8,128)(2,1)S(1)}, bf16[50,16,128]{2,1,0:T(8,128)(2,1)S(1)}, bf16[50,16,128]{2,1,0:T(8,128)(2,1)S(1)}) custom-call(s32[1,3,2]{2,1,0:T(4,128)S(1)} %copy.9.pairs, s32[1]{0:T(128)S(6)} %copy.12.live, bf16[3,1024,1024]{2,1,0:T(8,128)(2,1)S(1)} %bitcast.4, ...), custom_call_target="tpu_custom_call" | custom-call | tf_op jit(solution)/shard_map/mirror/pallas_call | solution.py:228
  71.9 2.8 %collective-permute-done.22.g1 = bf16[66,16,128]{2,1,0:T(8,128)(2,1)S(1)} collective-permute-done((bf16[66,16,128]{2,1,0:T(8,128)(2,1)S(1)}, bf16[66,16,128]{2,1,0:T(8,128)(2,1)S(1)}, u32[]{:S(2)}, u32[]{:S(2)}) %collective-permute-start.22) | collective-permute-done | bytes 270368 | tf_op jit(solution)/shard_map/ppermute | solution.py:24
  74.7 2.3 %direct.3 = (f32[4,32,1024]{2,1,0:T(8,128)S(1)}, bf16[4,32,1152]{2,1,0:T(8,128)(2,1)S(1)}, f32[8,128]{1,0:T(8,128)S(1)}) custom-call(s32[1,3,2]{2,1,0:T(4,128)S(1)} %copy.9.pairs, s32[1]{0:T(128)S(6)} %copy.12.live, bf16[3,1024,1024]{2,1,0:T(8,128)(2,1)S(1)} %turn.1.turned, bf16[66,16,128]{2,1,0:T(8,128)(2,1)S(1)} %get-tuple-element.62.g0, ...), custom_call_target="tpu_custom_call" | custom-call | tf_op jit(solution)/shard_map/direct/pallas_call | solution.py:228
  77.7 1.0 collective-permute-start.31
  78.7 2.5 %collective-permute-start.32 = (bf16[50,16,128]{2,1,0:T(8,128)(2,1)S(1)}, bf16[50,16,128]{2,1,0:T(8,128)(2,1)S(1)}, u32[]{:S(2)}, u32[]{:S(2)}) collective-permute-start(bf16[50,16,128]{2,1,0:T(8,128)(2,1)S(1)} %get-tuple-element.76), channel_id=1, source_target_pairs={{0,24},{1,97},{2,26},{3,99},{4,28},{5,101},{6,30},{7,103},{8,0},{9... | collective-permute-start | bytes 614408 | tf_op jit(solution)/shard_map/ppermute | solution.py:24
  81.3 1.1 collective-permute-start.28
  82.4 5.4 %collective-permute-done.28.received = bf16[2,32,1152]{2,1,0:T(8,128)(2,1)S(1)} collective-permute-done((bf16[2,32,1152]{2,1,0:T(8,128)(2,1)S(1)}, bf16[2,32,1152]{2,1,0:T(8,128)(2,1)S(1)}, u32[]{:S(2)}, u32[]{:S(2)}) %collective-permute-start.28) | collective-permute-done | bytes 147488 | tf_op jit(solution)/shard_map/ppermute | solution.py:24
  88.6 3.6 %collective-permute-start.34 = (bf16[32,1024]{1,0:T(8,128)(2,1)S(1)}, bf16[32,1024]{1,0:T(8,128)(2,1)S(1)}, u32[]{:S(2)}, u32[]{:S(2)}) collective-permute-start(bf16[32,1024]{1,0:T(8,128)(2,1)S(1)} %get-tuple-element.80), channel_id=1, source_target_pairs={{0,64},{1,17},{2,66},{3,19},{4,68},{5,21},{6,70},{7,23},{8,72},{9,... | collective-permute-start | bytes 196616 | tf_op jit(solution)/shard_map/ppermute | solution.py:24
  92.4 1.0 invert_first.1.refs_6_.inverse
  94.0 1.2 %collective-permute-done.34.refs_3_ = bf16[32,1024]{1,0:T(8,128)(2,1)S(1)} collective-permute-done((bf16[32,1024]{1,0:T(8,128)(2,1)S(1)}, bf16[32,1024]{1,0:T(8,128)(2,1)S(1)}, u32[]{:S(2)}, u32[]{:S(2)}) %collective-permute-start.34) | collective-permute-done | bytes 65568 | tf_op jit(solution)/shard_map/ppermute | solution.py:24
  95.2 1.3 %collective-permute-done.35.refs_4_ = bf16[32,1024]{1,0:T(8,128)(2,1)S(1)} collective-permute-done((bf16[32,1024]{1,0:T(8,128)(2,1)S(1)}, bf16[32,1024]{1,0:T(8,128)(2,1)S(1)}, u32[]{:S(2)}, u32[]{:S(2)}) %collective-permute-start.35) | collective-permute-done | bytes 65568 | tf_op jit(solution)/shard_map/ppermute | solution.py:24
  97.1 0.9 apply_first.1
  98.3 19.1 %all_to_all.5.gram = f32[64,8,128]{2,1,0:T(8,128)S(1)} all-to-all(f32[64,8,128]{2,1,0:T(8,128)S(1)} %total_gram.1), channel_id=1, replica_groups=mesh['z'=4,'x'=4,'y'=4,'core'=2] {'z','x','y'}, dimensions={0} | all-to-all | bytes 524288 | tf_op jit(solution)/shard_map/all_to_all | solution.py:430
  117.4 2.0 %factor_second.1 = f32[32,1024]{1,0:T(8,128)} custom-call(f32[64,8,128]{2,1,0:T(8,128)S(1)} %all_to_all.5.gram, f32[32,1024]{1,0:T(8,128)S(1)} %get-tuple-element.85.panel), custom_call_target="tpu_custom_call" | custom-call | tf_op jit(solution)/shard_map/factor_second/pallas_call | solution.py:519
  (78 shorter events, 7.9 us)
Async XLA Ops:
  0.6 7.0 %collective-permute-start.3 = (bf16[32,1024]{1,0:T(8,128)(2,1)}, bf16[32,1024]{1,0:T(8,128)(2,1)S(1)}, u32[]{:S(2)}, u32[]{:S(2)}) collective-permute-start(bf16[32,1024]{1,0:T(8,128)(2,1)} %bitcast.5), channel_id=1, source_target_pairs={{0,2},{1,7},{2,0},{3,5},{4,6},{5,3},{6,4},{7,1},{8,10},{9,15},{10,... | collective-permute-start | bytes 196616 | tf_op jit(solution)/shard_map/ppermute | solution.py:24
  2.4 6.3 %collective-permute-start.2 = (bf16[32,1024]{1,0:T(8,128)(2,1)}, bf16[32,1024]{1,0:T(8,128)(2,1)S(1)}, u32[]{:S(2)}, u32[]{:S(2)}) collective-permute-start(bf16[32,1024]{1,0:T(8,128)(2,1)} %bitcast.6), channel_id=1, source_target_pairs={{0,96},{1,25},{2,98},{3,27},{4,100},{5,29},{6,102},{7,31},{8,104},... | collective-permute-start | bytes 196616 | tf_op jit(solution)/shard_map/ppermute | solution.py:24
  6.4 6.1 %collective-permute-start.1 = (bf16[32,1024]{1,0:T(8,128)(2,1)}, bf16[32,1024]{1,0:T(8,128)(2,1)S(1)}, u32[]{:S(2)}, u32[]{:S(2)}) collective-permute-start(bf16[32,1024]{1,0:T(8,128)(2,1)} %bitcast.7), channel_id=1, source_target_pairs={{0,64},{1,17},{2,66},{3,19},{4,68},{5,21},{6,70},{7,23},{8,72},{9,... | collective-permute-start | bytes 196616 | tf_op jit(solution)/shard_map/ppermute | solution.py:24
  6.4 6.4 %collective-permute-start = (bf16[32,1024]{1,0:T(8,128)(2,1)}, bf16[32,1024]{1,0:T(8,128)(2,1)S(1)}, u32[]{:S(2)}, u32[]{:S(2)}) collective-permute-start(bf16[32,1024]{1,0:T(8,128)(2,1)} %bitcast.8), channel_id=1, source_target_pairs={{0,32},{1,9},{2,34},{3,11},{4,36},{5,13},{6,38},{7,15},{8,40},{9,1... | collective-permute-start | bytes 196616 | tf_op jit(solution)/shard_map/ppermute | solution.py:24
  12.8 0.8 copy-start.1
  13.7 6.7 %collective-permute-start.4 = (bf16[2,32,1024]{2,1,0:T(8,128)(2,1)S(1)}, bf16[2,32,1024]{2,1,0:T(8,128)(2,1)S(1)}, u32[]{:S(2)}, u32[]{:S(2)}) collective-permute-start(bf16[2,32,1024]{2,1,0:T(8,128)(2,1)S(1)} %get-tuple-element.44), channel_id=1, source_target_pairs={{0,6},{1,3},{2,4},{3,1},{4,2},{5,7},{6,0},{7,5},{8,14},{9,11},{10,... | collective-permute-start | bytes 393224 | tf_op jit(solution)/shard_map/ppermute | solution.py:24
  15.9 13.2 %collective-permute-start.11 = (bf16[66,16,128]{2,1,0:T(8,128)(2,1)S(1)}, bf16[66,16,128]{2,1,0:T(8,128)(2,1)S(1)}, u32[]{:S(2)}, u32[]{:S(2)}) collective-permute-start(bf16[66,16,128]{2,1,0:T(8,128)(2,1)S(1)} %get-tuple-element.50.g0), channel_id=1, source_target_pairs={{0,24},{1,97},{2,26},{3,99},{4,28},{5,101},{6,30},{7,103},{8,0},{9... | collective-permute-start | bytes 811016 | tf_op jit(solution)/shard_map/ppermute | solution.py:24
  18.7 10.4 %collective-permute-start.10 = (bf16[66,16,128]{2,1,0:T(8,128)(2,1)S(1)}, bf16[66,16,128]{2,1,0:T(8,128)(2,1)S(1)}, u32[]{:S(2)}, u32[]{:S(2)}) collective-permute-start(bf16[66,16,128]{2,1,0:T(8,128)(2,1)S(1)} %get-tuple-element.50.g0), channel_id=1, source_target_pairs={{0,16},{1,65},{2,18},{3,67},{4,20},{5,69},{6,22},{7,71},{8,24},{9,... | collective-permute-start | bytes 811016 | tf_op jit(solution)/shard_map/ppermute | solution.py:24
  19.5 10.1 %collective-permute-start.9 = (bf16[66,16,128]{2,1,0:T(8,128)(2,1)S(1)}, bf16[66,16,128]{2,1,0:T(8,128)(2,1)S(1)}, u32[]{:S(2)}, u32[]{:S(2)}) collective-permute-start(bf16[66,16,128]{2,1,0:T(8,128)(2,1)S(1)} %get-tuple-element.50.g0), channel_id=1, source_target_pairs={{0,8},{1,33},{2,10},{3,35},{4,12},{5,37},{6,14},{7,39},{8,16},{9,4... | collective-permute-start | bytes 811016 | tf_op jit(solution)/shard_map/ppermute | solution.py:24
  20.4 6.1 %collective-permute-start.5 = (bf16[4,32,1024]{2,1,0:T(8,128)(2,1)S(1)}, bf16[4,32,1024]{2,1,0:T(8,128)(2,1)S(1)}, u32[]{:S(2)}, u32[]{:S(2)}) collective-permute-start(bf16[4,32,1024]{2,1,0:T(8,128)(2,1)S(1)} %constant_dynamic-update-slice_fusion.h0), channel_id=1, source_target_pairs={{0,1},{1,0},{2,3},{3,2},{4,5},{5,4},{6,7},{7,6},{8,9},{9,8},{10,11... | collective-permute-start | bytes 786440 | tf_op jit(solution)/shard_map/ppermute | solution.py:24
  21.9 2.8 %copy-start = (bf16[3,1024,1024]{2,1,0:T(8,128)(2,1)S(1)}, bf16[3,1024,1024]{2,1,0:T(8,128)(2,1)}, u32[]{:S(2)}) copy-start(bf16[3,1024,1024]{2,1,0:T(8,128)(2,1)} %blocks.3) | copy-start | bytes 18874372
  29.6 39.9 %slice-start = ((s8[6291456]{0:T(1024)(128)(4,1)}), s8[2097152]{0:T(1024)(128)(4,1)S(1)}, s32[]{:S(2)}) async-start(s8[6291456]{0:T(1024)(128)(4,1)} %bitcast.3), calls=%async_computation.1 | async-start | bytes 4194304
  32.1 4.4 %collective-permute-start.12 = (f16[4,32,1152]{2,1,0:T(8,128)(2,1)S(1)}, f16[4,32,1152]{2,1,0:T(8,128)(2,1)S(1)}, u32[]{:S(2)}, u32[]{:S(2)}) collective-permute-start(f16[4,32,1152]{2,1,0:T(8,128)(2,1)S(1)} %convert_element_type.60), channel_id=1, source_target_pairs={{0,1},{1,0},{2,3},{3,2},{4,5},{5,4},{6,7},{7,6},{8,9},{9,8},{10,11... | collective-permute-start | bytes 884744 | tf_op jit(solution)/shard_map/ppermute | solution.py:24
  32.3 6.6 %collective-permute-start.8 = (f16[50,16,128]{2,1,0:T(8,128)(2,1)S(1)}, f16[50,16,128]{2,1,0:T(8,128)(2,1)S(1)}, u32[]{:S(2)}, u32[]{:S(2)}) collective-permute-start(f16[50,16,128]{2,1,0:T(8,128)(2,1)S(1)} %convert_element_type.58), channel_id=1, source_target_pairs={{0,24},{1,97},{2,26},{3,99},{4,28},{5,101},{6,30},{7,103},{8,0},{9... | collective-permute-start | bytes 614408 | tf_op jit(solution)/shard_map/ppermute | solution.py:24
  33.5 7.3 %collective-permute-start.7 = (f16[50,16,128]{2,1,0:T(8,128)(2,1)S(1)}, f16[50,16,128]{2,1,0:T(8,128)(2,1)S(1)}, u32[]{:S(2)}, u32[]{:S(2)}) collective-permute-start(f16[50,16,128]{2,1,0:T(8,128)(2,1)S(1)} %convert_element_type.56), channel_id=1, source_target_pairs={{0,16},{1,65},{2,18},{3,67},{4,20},{5,69},{6,22},{7,71},{8,24},{9,... | collective-permute-start | bytes 614408 | tf_op jit(solution)/shard_map/ppermute | solution.py:24
  36.3 33.2 %slice-start.1 = ((s8[6291456]{0:T(1024)(128)(4,1)}), s8[4194304]{0:T(1024)(128)(4,1)S(1)}, s32[]{:S(2)}) async-start(s8[6291456]{0:T(1024)(128)(4,1)} %bitcast.3), calls=%async_computation.2 | async-start | bytes 8388608
  36.3 7.0 %collective-permute-start.6 = (f16[50,16,128]{2,1,0:T(8,128)(2,1)S(1)}, f16[50,16,128]{2,1,0:T(8,128)(2,1)S(1)}, u32[]{:S(2)}, u32[]{:S(2)}) collective-permute-start(f16[50,16,128]{2,1,0:T(8,128)(2,1)S(1)} %convert_element_type.54), channel_id=1, source_target_pairs={{0,8},{1,33},{2,10},{3,35},{4,12},{5,37},{6,14},{7,39},{8,16},{9,4... | collective-permute-start | bytes 614408 | tf_op jit(solution)/shard_map/ppermute | solution.py:24
  36.8 11.1 %collective-permute-start.13 = (f16[2,32,1152]{2,1,0:T(8,128)(2,1)S(1)}, f16[2,32,1152]{2,1,0:T(8,128)(2,1)S(1)}, u32[]{:S(2)}, u32[]{:S(2)}) collective-permute-start(f16[2,32,1152]{2,1,0:T(8,128)(2,1)S(1)} %convert_element_type.62), channel_id=1, source_target_pairs={{0,6},{1,3},{2,4},{3,1},{4,2},{5,7},{6,0},{7,5},{8,14},{9,11},{10,... | collective-permute-start | bytes 442376 | tf_op jit(solution)/shard_map/ppermute | solution.py:24
  44.4 4.4 %collective-permute-start.16 = (f16[32,1152]{1,0:T(8,128)(2,1)S(1)}, f16[32,1152]{1,0:T(8,128)(2,1)S(1)}, u32[]{:S(2)}, u32[]{:S(2)}) collective-permute-start(f16[32,1152]{1,0:T(8,128)(2,1)S(1)} %convert_element_type.68), channel_id=1, source_target_pairs={{0,96},{1,25},{2,98},{3,27},{4,100},{5,29},{6,102},{7,31},{8,104},... | collective-permute-start | bytes 221192 | tf_op jit(solution)/shard_map/ppermute | solution.py:24
  44.5 5.9 %collective-permute-start.15 = (f16[32,1152]{1,0:T(8,128)(2,1)S(1)}, f16[32,1152]{1,0:T(8,128)(2,1)S(1)}, u32[]{:S(2)}, u32[]{:S(2)}) collective-permute-start(f16[32,1152]{1,0:T(8,128)(2,1)S(1)} %convert_element_type.66), channel_id=1, source_target_pairs={{0,64},{1,17},{2,66},{3,19},{4,68},{5,21},{6,70},{7,23},{8,72},{9,... | collective-permute-start | bytes 221192 | tf_op jit(solution)/shard_map/ppermute | solution.py:24
  46.5 5.6 %collective-permute-start.14 = (f16[32,1152]{1,0:T(8,128)(2,1)S(1)}, f16[32,1152]{1,0:T(8,128)(2,1)S(1)}, u32[]{:S(2)}, u32[]{:S(2)}) collective-permute-start(f16[32,1152]{1,0:T(8,128)(2,1)S(1)} %convert_element_type.64), channel_id=1, source_target_pairs={{0,32},{1,9},{2,34},{3,11},{4,36},{5,13},{6,38},{7,15},{8,40},{9,1... | collective-permute-start | bytes 221192 | tf_op jit(solution)/shard_map/ppermute | solution.py:24
  48.1 4.4 %collective-permute-start.17 = (f16[1,32,1152]{2,1,0:T(8,128)(2,1)S(1)}, f16[1,32,1152]{2,1,0:T(8,128)(2,1)S(1)}, u32[]{:S(2)}, u32[]{:S(2)}) collective-permute-start(f16[1,32,1152]{2,1,0:T(8,128)(2,1)S(1)} %convert_element_type.70), channel_id=1, source_target_pairs={{0,2},{1,7},{2,0},{3,5},{4,6},{5,3},{6,4},{7,1},{8,10},{9,15},{10,... | collective-permute-start | bytes 221192 | tf_op jit(solution)/shard_map/ppermute | solution.py:24
  52.8 8.7 %collective-permute-start.20 = (bf16[32,1152]{1,0:T(8,128)(2,1)S(1)}, bf16[32,1152]{1,0:T(8,128)(2,1)S(1)}, u32[]{:S(2)}, u32[]{:S(2)}) collective-permute-start(bf16[32,1152]{1,0:T(8,128)(2,1)S(1)} %get-tuple-element.60.refs_0_), channel_id=1, source_target_pairs={{0,96},{1,25},{2,98},{3,27},{4,100},{5,29},{6,102},{7,31},{8,104},... | collective-permute-start | bytes 221192 | tf_op jit(solution)/shard_map/ppermute | solution.py:24
  54.8 6.8 %collective-permute-start.19 = (bf16[32,1152]{1,0:T(8,128)(2,1)S(1)}, bf16[32,1152]{1,0:T(8,128)(2,1)S(1)}, u32[]{:S(2)}, u32[]{:S(2)}) collective-permute-start(bf16[32,1152]{1,0:T(8,128)(2,1)S(1)} %get-tuple-element.60.refs_0_), channel_id=1, source_target_pairs={{0,64},{1,17},{2,66},{3,19},{4,68},{5,21},{6,70},{7,23},{8,72},{9,... | collective-permute-start | bytes 221192 | tf_op jit(solution)/shard_map/ppermute | solution.py:24
  55.8 5.8 %collective-permute-start.18 = (bf16[32,1152]{1,0:T(8,128)(2,1)S(1)}, bf16[32,1152]{1,0:T(8,128)(2,1)S(1)}, u32[]{:S(2)}, u32[]{:S(2)}) collective-permute-start(bf16[32,1152]{1,0:T(8,128)(2,1)S(1)} %get-tuple-element.60.refs_0_), channel_id=1, source_target_pairs={{0,32},{1,9},{2,34},{3,11},{4,36},{5,13},{6,38},{7,15},{8,40},{9,1... | collective-permute-start | bytes 221192 | tf_op jit(solution)/shard_map/ppermute | solution.py:24
  57.1 4.4 %collective-permute-start.21 = (bf16[32,1024]{1,0:T(8,128)(2,1)S(1)}, bf16[32,1024]{1,0:T(8,128)(2,1)S(1)}, u32[]{:S(2)}, u32[]{:S(2)}) collective-permute-start(bf16[32,1024]{1,0:T(8,128)(2,1)S(1)} %get-tuple-element.61.refs_4_), channel_id=1, source_target_pairs={{0,2},{1,7},{2,0},{3,5},{4,6},{5,3},{6,4},{7,1},{8,10},{9,15},{10,... | collective-permute-start | bytes 196616 | tf_op jit(solution)/shard_map/ppermute | solution.py:24
  61.6 6.3 %collective-permute-start.25 = (bf16[2,32,1024]{2,1,0:T(8,128)(2,1)S(1)}, bf16[2,32,1024]{2,1,0:T(8,128)(2,1)S(1)}, u32[]{:S(2)}, u32[]{:S(2)}) collective-permute-start(bf16[2,32,1024]{2,1,0:T(8,128)(2,1)S(1)} %get-tuple-element.63), channel_id=1, source_target_pairs={{0,6},{1,3},{2,4},{3,1},{4,2},{5,7},{6,0},{7,5},{8,14},{9,11},{10,... | collective-permute-start | bytes 393224 | tf_op jit(solution)/shard_map/ppermute | solution.py:24
  63.7 8.1 %collective-permute-start.24 = (bf16[66,16,128]{2,1,0:T(8,128)(2,1)S(1)}, bf16[66,16,128]{2,1,0:T(8,128)(2,1)S(1)}, u32[]{:S(2)}, u32[]{:S(2)}) collective-permute-start(bf16[66,16,128]{2,1,0:T(8,128)(2,1)S(1)} %get-tuple-element.62.g0), channel_id=1, source_target_pairs={{0,24},{1,97},{2,26},{3,99},{4,28},{5,101},{6,30},{7,103},{8,0},{9... | collective-permute-start | bytes 811016 | tf_op jit(solution)/shard_map/ppermute | solution.py:24
  63.8 8.1 %collective-permute-start.23 = (bf16[66,16,128]{2,1,0:T(8,128)(2,1)S(1)}, bf16[66,16,128]{2,1,0:T(8,128)(2,1)S(1)}, u32[]{:S(2)}, u32[]{:S(2)}) collective-permute-start(bf16[66,16,128]{2,1,0:T(8,128)(2,1)S(1)} %get-tuple-element.62.g0), channel_id=1, source_target_pairs={{0,16},{1,65},{2,18},{3,67},{4,20},{5,69},{6,22},{7,71},{8,24},{9,... | collective-permute-start | bytes 811016 | tf_op jit(solution)/shard_map/ppermute | solution.py:24
  65.8 8.8 %collective-permute-start.22 = (bf16[66,16,128]{2,1,0:T(8,128)(2,1)S(1)}, bf16[66,16,128]{2,1,0:T(8,128)(2,1)S(1)}, u32[]{:S(2)}, u32[]{:S(2)}) collective-permute-start(bf16[66,16,128]{2,1,0:T(8,128)(2,1)S(1)} %get-tuple-element.62.g0), channel_id=1, source_target_pairs={{0,8},{1,33},{2,10},{3,35},{4,12},{5,37},{6,14},{7,39},{8,16},{9,4... | collective-permute-start | bytes 811016 | tf_op jit(solution)/shard_map/ppermute | solution.py:24
  67.9 1.6 %collective-permute-start.26 = (bf16[4,32,1024]{2,1,0:T(8,128)(2,1)S(1)}, bf16[4,32,1024]{2,1,0:T(8,128)(2,1)S(1)}, u32[]{:S(2)}, u32[]{:S(2)}) collective-permute-start(bf16[4,32,1024]{2,1,0:T(8,128)(2,1)S(1)} %constant_dynamic-update-slice_fusion.2.h0), channel_id=1, source_target_pairs={{0,1},{1,0},{2,3},{3,2},{4,5},{5,4},{6,7},{7,6},{8,9},{9,8},{10,11... | collective-permute-start | bytes 786440 | tf_op jit(solution)/shard_map/ppermute | solution.py:24
  77.0 4.2 %collective-permute-start.27 = (bf16[4,32,1152]{2,1,0:T(8,128)(2,1)S(1)}, bf16[4,32,1152]{2,1,0:T(8,128)(2,1)S(1)}, u32[]{:S(2)}, u32[]{:S(2)}) collective-permute-start(bf16[4,32,1152]{2,1,0:T(8,128)(2,1)S(1)} %get-tuple-element.66), channel_id=1, source_target_pairs={{0,1},{1,0},{2,3},{3,2},{4,5},{5,4},{6,7},{7,6},{8,9},{9,8},{10,11... | collective-permute-start | bytes 884744 | tf_op jit(solution)/shard_map/ppermute | solution.py:24
  77.1 10.8 %collective-permute-start.30 = (bf16[50,16,128]{2,1,0:T(8,128)(2,1)S(1)}, bf16[50,16,128]{2,1,0:T(8,128)(2,1)S(1)}, u32[]{:S(2)}, u32[]{:S(2)}) collective-permute-start(bf16[50,16,128]{2,1,0:T(8,128)(2,1)S(1)} %get-tuple-element.74), channel_id=1, source_target_pairs={{0,8},{1,33},{2,10},{3,35},{4,12},{5,37},{6,14},{7,39},{8,16},{9,4... | collective-permute-start | bytes 614408 | tf_op jit(solution)/shard_map/ppermute | solution.py:24
  77.7 10.1 %collective-permute-start.31 = (bf16[50,16,128]{2,1,0:T(8,128)(2,1)S(1)}, bf16[50,16,128]{2,1,0:T(8,128)(2,1)S(1)}, u32[]{:S(2)}, u32[]{:S(2)}) collective-permute-start(bf16[50,16,128]{2,1,0:T(8,128)(2,1)S(1)} %get-tuple-element.75), channel_id=1, source_target_pairs={{0,16},{1,65},{2,18},{3,67},{4,20},{5,69},{6,22},{7,71},{8,24},{9,... | collective-permute-start | bytes 614408 | tf_op jit(solution)/shard_map/ppermute | solution.py:24
  78.7 9.2 %collective-permute-start.32 = (bf16[50,16,128]{2,1,0:T(8,128)(2,1)S(1)}, bf16[50,16,128]{2,1,0:T(8,128)(2,1)S(1)}, u32[]{:S(2)}, u32[]{:S(2)}) collective-permute-start(bf16[50,16,128]{2,1,0:T(8,128)(2,1)S(1)} %get-tuple-element.76), channel_id=1, source_target_pairs={{0,24},{1,97},{2,26},{3,99},{4,28},{5,101},{6,30},{7,103},{8,0},{9... | collective-permute-start | bytes 614408 | tf_op jit(solution)/shard_map/ppermute | solution.py:24
  81.3 6.4 %collective-permute-start.28 = (bf16[2,32,1152]{2,1,0:T(8,128)(2,1)S(1)}, bf16[2,32,1152]{2,1,0:T(8,128)(2,1)S(1)}, u32[]{:S(2)}, u32[]{:S(2)}) collective-permute-start(bf16[2,32,1152]{2,1,0:T(8,128)(2,1)S(1)} %get-tuple-element.69), channel_id=1, source_target_pairs={{0,6},{1,3},{2,4},{3,1},{4,2},{5,7},{6,0},{7,5},{8,14},{9,11},{10,... | collective-permute-start | bytes 442376 | tf_op jit(solution)/shard_map/ppermute | solution.py:24
  87.8 4.6 %collective-permute-start.29 = (bf16[1,32,1152]{2,1,0:T(8,128)(2,1)S(1)}, bf16[1,32,1152]{2,1,0:T(8,128)(2,1)S(1)}, u32[]{:S(2)}, u32[]{:S(2)}) collective-permute-start(bf16[1,32,1152]{2,1,0:T(8,128)(2,1)S(1)} %get-tuple-element.72), channel_id=1, source_target_pairs={{0,2},{1,7},{2,0},{3,5},{4,6},{5,3},{6,4},{7,1},{8,10},{9,15},{10,... | collective-permute-start | bytes 221192 | tf_op jit(solution)/shard_map/ppermute | solution.py:24
  88.4 5.5 %collective-permute-start.33 = (bf16[32,1024]{1,0:T(8,128)(2,1)S(1)}, bf16[32,1024]{1,0:T(8,128)(2,1)S(1)}, u32[]{:S(2)}, u32[]{:S(2)}) collective-permute-start(bf16[32,1024]{1,0:T(8,128)(2,1)S(1)} %get-tuple-element.79), channel_id=1, source_target_pairs={{0,32},{1,9},{2,34},{3,11},{4,36},{5,13},{6,38},{7,15},{8,40},{9,1... | collective-permute-start | bytes 196616 | tf_op jit(solution)/shard_map/ppermute | solution.py:24
  88.6 6.6 %collective-permute-start.34 = (bf16[32,1024]{1,0:T(8,128)(2,1)S(1)}, bf16[32,1024]{1,0:T(8,128)(2,1)S(1)}, u32[]{:S(2)}, u32[]{:S(2)}) collective-permute-start(bf16[32,1024]{1,0:T(8,128)(2,1)S(1)} %get-tuple-element.80), channel_id=1, source_target_pairs={{0,64},{1,17},{2,66},{3,19},{4,68},{5,21},{6,70},{7,23},{8,72},{9,... | collective-permute-start | bytes 196616 | tf_op jit(solution)/shard_map/ppermute | solution.py:24
  92.2 4.3 %collective-permute-start.35 = (bf16[32,1024]{1,0:T(8,128)(2,1)S(1)}, bf16[32,1024]{1,0:T(8,128)(2,1)S(1)}, u32[]{:S(2)}, u32[]{:S(2)}) collective-permute-start(bf16[32,1024]{1,0:T(8,128)(2,1)S(1)} %get-tuple-element.81), channel_id=1, source_target_pairs={{0,96},{1,25},{2,98},{3,27},{4,100},{5,29},{6,102},{7,31},{8,104},... | collective-permute-start | bytes 196616 | tf_op jit(solution)/shard_map/ppermute | solution.py:24
  97.1 1.2 collective-permute-start.36

commit v7 on v5

--- a/solution.py
+++ b/solution.py
@@ -314,9 +314,10 @@
     received, outs, (weights, total) = refs[:3], refs[3:7], refs[7:]
     entries = [(array, k) for array in received for k in range(3)]
     extras = [take_extra(array, 3).astype(jnp.float32) for array in received]
+    powers = [jnp.exp2(extra) for extra in extras]
     for e, (array, k) in enumerate(entries):
         extra = extras[e // 3]
-        scale = jnp.exp2(extra[:, 8 * k + 4 : 8 * k + 5]) if half else 1.0
+        scale = powers[e // 3][:, 8 * k + 4 : 8 * k + 5] if half else 1.0
         for s in range(4):
             weights[4 * e + s] = jnp.broadcast_to(extra[:, 8 * k + s : 8 * k + s + 1] * scale, (32, 128))
     for i in range(2):

time: 119 us -> 120 us (level)
  waiting for transfers between devices: 32.6 us -> 34.4 us
  starting transfers between devices: 42.7 us -> 41.1 us
  blocking collectives: 18.5 us -> 19.9 us
    ppermute x37, waiting for transfers between devices: 32.6 us -> 34.4 us  [permute(): return lax.ppermute(value, AXES, pairs)]
    ppermute x37, starting transfers between devices: 42.7 us -> 41.1 us  [permute(): return lax.ppermute(value, AXES, pairs)]
    all_to_all x1, blocking collectives: 18.5 us -> 19.9 us  [total_gram(): return lax.all_to_all(tiles, ('z', 'x', 'y'), 0, 0, tiled=True)]
where the time goes in v7:
time: 120 us
  starting transfers between devices  41.1 us (34%)
  waiting for transfers between devices  34.4 us (29%)
  blocking collectives  19.9 us (17%)
  Pallas kernels  18 us (15%)
  local copies, waits for them, and re-layouts  4.44 us (4%)
  between operations  1.64 us (1%)
    ppermute x37, starting transfers between devices, permute(): return lax.ppermute(value, AXES, pairs)  41.1 us
    ppermute x37, waiting for transfers between devices, permute(): return lax.ppermute(value, AXES, pairs)  34.4 us
    all_to_all x1, blocking collectives, total_gram(): return lax.all_to_all(tiles, ('z', 'x', 'y'), 0, 0, tiled=True)  19.9 us
    pallas_call x4, Pallas kernels, product_call(): pl.pallas_call(kernel, out_shape=outs, in_specs=[SMEM, SMEM] + [VMEM] * l...  9.34 us
    unnamed x11, local copies, waits for them, and re-layouts  4.42 us
  transfers between devices with their start and end apart: 37, of which 21 were waited for; matrix products, arithmetic and copies ran while one was open for 1% of the time, Pallas kernels for 9%

profile of v7, /device:TPU:0, one launch (start us, length us, event | category | flops | bytes accessed | tf_op | source)
XLA Modules:
  0.0 119.9 jit_solution(2511993287227104086)
XLA Ops:
  0.6 1.7 %collective-permute-start.3 = (bf16[32,1024]{1,0:T(8,128)(2,1)}, bf16[32,1024]{1,0:T(8,128)(2,1)S(1)}, u32[]{:S(2)}, u32[]{:S(2)}) collective-permute-start(bf16[32,1024]{1,0:T(8,128)(2,1)} %bitcast.5), channel_id=1, source_target_pairs={{0,2},{1,7},{2,0},{3,5},{4,6},{5,3},{6,4},{7,1},{8,10},{9,15},{10,... | collective-permute-start | bytes 196616 | tf_op jit(solution)/shard_map/ppermute | solution.py:24
  2.4 4.0 %collective-permute-start.2 = (bf16[32,1024]{1,0:T(8,128)(2,1)}, bf16[32,1024]{1,0:T(8,128)(2,1)S(1)}, u32[]{:S(2)}, u32[]{:S(2)}) collective-permute-start(bf16[32,1024]{1,0:T(8,128)(2,1)} %bitcast.6), channel_id=1, source_target_pairs={{0,96},{1,25},{2,98},{3,27},{4,100},{5,29},{6,102},{7,31},{8,104},... | collective-permute-start | bytes 196616 | tf_op jit(solution)/shard_map/ppermute | solution.py:24
  6.4 1.3 %collective-permute-start = (bf16[32,1024]{1,0:T(8,128)(2,1)}, bf16[32,1024]{1,0:T(8,128)(2,1)S(1)}, u32[]{:S(2)}, u32[]{:S(2)}) collective-permute-start(bf16[32,1024]{1,0:T(8,128)(2,1)} %bitcast.8), channel_id=1, source_target_pairs={{0,32},{1,9},{2,34},{3,11},{4,36},{5,13},{6,38},{7,15},{8,40},{9,1... | collective-permute-start | bytes 196616 | tf_op jit(solution)/shard_map/ppermute | solution.py:24
  7.7 1.0 collective-permute-done.2.refs_3_
  8.6 3.9 %collective-permute-done.1.refs_2_ = bf16[32,1024]{1,0:T(8,128)(2,1)S(1)} collective-permute-done((bf16[32,1024]{1,0:T(8,128)(2,1)}, bf16[32,1024]{1,0:T(8,128)(2,1)S(1)}, u32[]{:S(2)}, u32[]{:S(2)}) %collective-permute-start.1) | collective-permute-done | bytes 65568 | tf_op jit(solution)/shard_map/ppermute | solution.py:24
  12.8 0.8 copy-done.1
  13.7 2.3 %collective-permute-start.4 = (bf16[2,32,1024]{2,1,0:T(8,128)(2,1)S(1)}, bf16[2,32,1024]{2,1,0:T(8,128)(2,1)S(1)}, u32[]{:S(2)}, u32[]{:S(2)}) collective-permute-start(bf16[2,32,1024]{2,1,0:T(8,128)(2,1)S(1)} %get-tuple-element.44), channel_id=1, source_target_pairs={{0,6},{1,3},{2,4},{3,1},{4,2},{5,7},{6,0},{7,5},{8,14},{9,11},{10,... | collective-permute-start | bytes 393224 | tf_op jit(solution)/shard_map/ppermute | solution.py:24
  15.9 2.8 %collective-permute-start.11 = (bf16[66,16,128]{2,1,0:T(8,128)(2,1)S(1)}, bf16[66,16,128]{2,1,0:T(8,128)(2,1)S(1)}, u32[]{:S(2)}, u32[]{:S(2)}) collective-permute-start(bf16[66,16,128]{2,1,0:T(8,128)(2,1)S(1)} %get-tuple-element.50.g0), channel_id=1, source_target_pairs={{0,24},{1,97},{2,26},{3,99},{4,28},{5,101},{6,30},{7,103},{8,0},{9... | collective-permute-start | bytes 811016 | tf_op jit(solution)/shard_map/ppermute | solution.py:24
  18.7 0.8 collective-permute-start.10
  19.5 0.9 collective-permute-start.9
  21.9 2.8 %copy-done = bf16[3,1024,1024]{2,1,0:T(8,128)(2,1)S(1)} copy-done((bf16[3,1024,1024]{2,1,0:T(8,128)(2,1)S(1)}, bf16[3,1024,1024]{2,1,0:T(8,128)(2,1)}, u32[]{:S(2)}) %copy-start) | copy-done | bytes 6291480
  24.7 1.8 %turn.1.turned = bf16[3,1024,1024]{2,1,0:T(8,128)(2,1)S(1)} custom-call(bf16[3,1024,1024]{2,1,0:T(8,128)(2,1)S(1)} %copy-done), custom_call_target="tpu_custom_call" | custom-call | bytes 6000000 | tf_op jit(solution)/shard_map/turn/pallas_call | solution.py:545
  26.6 2.3 %mirror.2 = (f32[4,32,1024]{2,1,0:T(8,128)S(1)}, f32[50,16,128]{2,1,0:T(8,128)S(1)}, f32[50,16,128]{2,1,0:T(8,128)S(1)}, f32[50,16,128]{2,1,0:T(8,128)S(1)}) custom-call(s32[1,3,2]{2,1,0:T(4,128)S(1)} %copy.9.pairs, s32[1]{0:T(128)S(6)} %copy.12.live, bf16[3,1024,1024]{2,1,0:T(8,128)(2,1)S(1)} %copy-done, ...), custom_call_target="tpu_custom_call" | custom-call | tf_op jit(solution)/shard_map/mirror/pallas_call | solution.py:228
  29.6 2.5 %direct.2 = (f32[4,32,1024]{2,1,0:T(8,128)S(1)}, f32[4,32,1152]{2,1,0:T(8,128)S(1)}) custom-call(s32[1,3,2]{2,1,0:T(4,128)S(1)} %copy.9.pairs, s32[1]{0:T(128)S(6)} %copy.12.live, bf16[3,1024,1024]{2,1,0:T(8,128)(2,1)S(1)} %turn.1.turned, bf16[66,16,128]{2,1,0:T(8,128)(2,1)S(1)} %get-tuple-element.50.g0, bf16[66,16,128]{2,1,0:T(8,128)(2,1)S(1)} %collective-permute-done.9.g1, ...), custom_call_target="tpu_custom_call" | custom-call | tf_op jit(solution)/shard_map/direct/pallas_call | solution.py:228
  32.3 1.9 %collective-permute-start.8 = (f16[50,16,128]{2,1,0:T(8,128)(2,1)S(1)}, f16[50,16,128]{2,1,0:T(8,128)(2,1)S(1)}, u32[]{:S(2)}, u32[]{:S(2)}) collective-permute-start(f16[50,16,128]{2,1,0:T(8,128)(2,1)S(1)} %convert_element_type.58), channel_id=1, source_target_pairs={{0,24},{1,97},{2,26},{3,99},{4,28},{5,101},{6,30},{7,103},{8,0},{9... | collective-permute-start | bytes 614408 | tf_op jit(solution)/shard_map/ppermute | solution.py:24
  34.2 1.4 %collective-permute-start.7 = (f16[50,16,128]{2,1,0:T(8,128)(2,1)S(1)}, f16[50,16,128]{2,1,0:T(8,128)(2,1)S(1)}, u32[]{:S(2)}, u32[]{:S(2)}) collective-permute-start(f16[50,16,128]{2,1,0:T(8,128)(2,1)S(1)} %convert_element_type.56), channel_id=1, source_target_pairs={{0,16},{1,65},{2,18},{3,67},{4,20},{5,69},{6,22},{7,71},{8,24},{9,... | collective-permute-start | bytes 614408 | tf_op jit(solution)/shard_map/ppermute | solution.py:24
  35.7 0.8 collective-permute-start.6
  36.8 1.4 %collective-permute-start.13 = (f16[2,32,1152]{2,1,0:T(8,128)(2,1)S(1)}, f16[2,32,1152]{2,1,0:T(8,128)(2,1)S(1)}, u32[]{:S(2)}, u32[]{:S(2)}) collective-permute-start(f16[2,32,1152]{2,1,0:T(8,128)(2,1)S(1)} %convert_element_type.62), channel_id=1, source_target_pairs={{0,6},{1,3},{2,4},{3,1},{4,2},{5,7},{6,0},{7,5},{8,14},{9,11},{10,... | collective-permute-start | bytes 442376 | tf_op jit(solution)/shard_map/ppermute | solution.py:24
  38.2 1.5 %collective-permute-done.8 = f16[50,16,128]{2,1,0:T(8,128)(2,1)S(1)} collective-permute-done((f16[50,16,128]{2,1,0:T(8,128)(2,1)S(1)}, f16[50,16,128]{2,1,0:T(8,128)(2,1)S(1)}, u32[]{:S(2)}, u32[]{:S(2)}) %collective-permute-start.8) | collective-permute-done | bytes 204832 | tf_op jit(solution)/shard_map/ppermute | solution.py:24
  39.7 1.8 %collective-permute-done.7 = f16[50,16,128]{2,1,0:T(8,128)(2,1)S(1)} collective-permute-done((f16[50,16,128]{2,1,0:T(8,128)(2,1)S(1)}, f16[50,16,128]{2,1,0:T(8,128)(2,1)S(1)}, u32[]{:S(2)}, u32[]{:S(2)}) %collective-permute-start.7) | collective-permute-done | bytes 204832 | tf_op jit(solution)/shard_map/ppermute | solution.py:24
  41.6 2.1 %collective-permute-done.6 = f16[50,16,128]{2,1,0:T(8,128)(2,1)S(1)} collective-permute-done((f16[50,16,128]{2,1,0:T(8,128)(2,1)S(1)}, f16[50,16,128]{2,1,0:T(8,128)(2,1)S(1)}, u32[]{:S(2)}, u32[]{:S(2)}) %collective-permute-start.6) | collective-permute-done | bytes 204832 | tf_op jit(solution)/shard_map/ppermute | solution.py:24
  43.7 1.0 add_outer.2
  44.9 2.2 %collective-permute-start.15 = (f16[32,1152]{1,0:T(8,128)(2,1)S(1)}, f16[32,1152]{1,0:T(8,128)(2,1)S(1)}, u32[]{:S(2)}, u32[]{:S(2)}) collective-permute-start(f16[32,1152]{1,0:T(8,128)(2,1)S(1)} %convert_element_type.66), channel_id=1, source_target_pairs={{0,64},{1,17},{2,66},{3,19},{4,68},{5,21},{6,70},{7,23},{8,72},{9,... | collective-permute-start | bytes 221192 | tf_op jit(solution)/shard_map/ppermute | solution.py:24
  47.1 1.3 %collective-permute-start.14 = (f16[32,1152]{1,0:T(8,128)(2,1)S(1)}, f16[32,1152]{1,0:T(8,128)(2,1)S(1)}, u32[]{:S(2)}, u32[]{:S(2)}) collective-permute-start(f16[32,1152]{1,0:T(8,128)(2,1)S(1)} %convert_element_type.64), channel_id=1, source_target_pairs={{0,32},{1,9},{2,34},{3,11},{4,36},{5,13},{6,38},{7,15},{8,40},{9,1... | collective-permute-start | bytes 221192 | tf_op jit(solution)/shard_map/ppermute | solution.py:24
  49.2 1.6 %collective-permute-done.15 = f16[32,1152]{1,0:T(8,128)(2,1)S(1)} collective-permute-done((f16[32,1152]{1,0:T(8,128)(2,1)S(1)}, f16[32,1152]{1,0:T(8,128)(2,1)S(1)}, u32[]{:S(2)}, u32[]{:S(2)}) %collective-permute-start.15) | collective-permute-done | bytes 73760 | tf_op jit(solution)/shard_map/ppermute | solution.py:24
  50.8 1.9 %collective-permute-done.14 = f16[32,1152]{1,0:T(8,128)(2,1)S(1)} collective-permute-done((f16[32,1152]{1,0:T(8,128)(2,1)S(1)}, f16[32,1152]{1,0:T(8,128)(2,1)S(1)}, u32[]{:S(2)}, u32[]{:S(2)}) %collective-permute-start.14) | collective-permute-done | bytes 73760 | tf_op jit(solution)/shard_map/ppermute | solution.py:24
  53.4 1.9 %collective-permute-start.20 = (bf16[32,1152]{1,0:T(8,128)(2,1)S(1)}, bf16[32,1152]{1,0:T(8,128)(2,1)S(1)}, u32[]{:S(2)}, u32[]{:S(2)}) collective-permute-start(bf16[32,1152]{1,0:T(8,128)(2,1)S(1)} %get-tuple-element.60.refs_0_), channel_id=1, source_target_pairs={{0,96},{1,25},{2,98},{3,27},{4,100},{5,29},{6,102},{7,31},{8,104},... | collective-permute-start | bytes 221192 | tf_op jit(solution)/shard_map/ppermute | solution.py:24
  56.1 1.3 %collective-permute-start.18 = (bf16[32,1152]{1,0:T(8,128)(2,1)S(1)}, bf16[32,1152]{1,0:T(8,128)(2,1)S(1)}, u32[]{:S(2)}, u32[]{:S(2)}) collective-permute-start(bf16[32,1152]{1,0:T(8,128)(2,1)S(1)} %get-tuple-element.60.refs_0_), channel_id=1, source_target_pairs={{0,32},{1,9},{2,34},{3,11},{4,36},{5,13},{6,38},{7,15},{8,40},{9,1... | collective-permute-start | bytes 221192 | tf_op jit(solution)/shard_map/ppermute | solution.py:24
  57.7 4.0 %collective-permute-done.21.refs_5_ = bf16[32,1024]{1,0:T(8,128)(2,1)S(1)} collective-permute-done((bf16[32,1024]{1,0:T(8,128)(2,1)S(1)}, bf16[32,1024]{1,0:T(8,128)(2,1)S(1)}, u32[]{:S(2)}, u32[]{:S(2)}) %collective-permute-start.21) | collective-permute-done | bytes 65568 | tf_op jit(solution)/shard_map/ppermute | solution.py:24
  62.1 2.4 %collective-permute-start.25 = (bf16[2,32,1024]{2,1,0:T(8,128)(2,1)S(1)}, bf16[2,32,1024]{2,1,0:T(8,128)(2,1)S(1)}, u32[]{:S(2)}, u32[]{:S(2)}) collective-permute-start(bf16[2,32,1024]{2,1,0:T(8,128)(2,1)S(1)} %get-tuple-element.63), channel_id=1, source_target_pairs={{0,6},{1,3},{2,4},{3,1},{4,2},{5,7},{6,0},{7,5},{8,14},{9,11},{10,... | collective-permute-start | bytes 393224 | tf_op jit(solution)/shard_map/ppermute | solution.py:24
  64.8 1.1 collective-permute-start.23
  65.9 0.9 collective-permute-start.22
  66.7 1.6 %collective-permute-done.25 = bf16[2,32,1024]{2,1,0:T(8,128)(2,1)S(1)} collective-permute-done((bf16[2,32,1024]{2,1,0:T(8,128)(2,1)S(1)}, bf16[2,32,1024]{2,1,0:T(8,128)(2,1)S(1)}, u32[]{:S(2)}, u32[]{:S(2)}) %collective-permute-start.25) | collective-permute-done | bytes 131104 | tf_op jit(solution)/shard_map/ppermute | solution.py:24
  68.4 1.5 %collective-permute-done.26.h1 = bf16[4,32,1024]{2,1,0:T(8,128)(2,1)S(1)} collective-permute-done((bf16[4,32,1024]{2,1,0:T(8,128)(2,1)S(1)}, bf16[4,32,1024]{2,1,0:T(8,128)(2,1)S(1)}, u32[]{:S(2)}, u32[]{:S(2)}) %collective-permute-start.26) | collective-permute-done | bytes 262176 | tf_op jit(solution)/shard_map/ppermute | solution.py:24
  70.0 2.3 %mirror.3 = (f32[4,32,1024]{2,1,0:T(8,128)S(1)}, bf16[50,16,128]{2,1,0:T(8,128)(2,1)S(1)}, bf16[50,16,128]{2,1,0:T(8,128)(2,1)S(1)}, bf16[50,16,128]{2,1,0:T(8,128)(2,1)S(1)}) custom-call(s32[1,3,2]{2,1,0:T(4,128)S(1)} %copy.9.pairs, s32[1]{0:T(128)S(6)} %copy.12.live, bf16[3,1024,1024]{2,1,0:T(8,128)(2,1)S(1)} %bitcast.4, ...), custom_call_target="tpu_custom_call" | custom-call | tf_op jit(solution)/shard_map/mirror/pallas_call | solution.py:228
  72.9 2.8 %collective-permute-done.22.g1 = bf16[66,16,128]{2,1,0:T(8,128)(2,1)S(1)} collective-permute-done((bf16[66,16,128]{2,1,0:T(8,128)(2,1)S(1)}, bf16[66,16,128]{2,1,0:T(8,128)(2,1)S(1)}, u32[]{:S(2)}, u32[]{:S(2)}) %collective-permute-start.22) | collective-permute-done | bytes 270368 | tf_op jit(solution)/shard_map/ppermute | solution.py:24
  75.7 2.3 %direct.3 = (f32[4,32,1024]{2,1,0:T(8,128)S(1)}, bf16[4,32,1152]{2,1,0:T(8,128)(2,1)S(1)}, f32[8,128]{1,0:T(8,128)S(1)}) custom-call(s32[1,3,2]{2,1,0:T(4,128)S(1)} %copy.9.pairs, s32[1]{0:T(128)S(6)} %copy.12.live, bf16[3,1024,1024]{2,1,0:T(8,128)(2,1)S(1)} %turn.1.turned, bf16[66,16,128]{2,1,0:T(8,128)(2,1)S(1)} %get-tuple-element.62.g0, ...), custom_call_target="tpu_custom_call" | custom-call | tf_op jit(solution)/shard_map/direct/pallas_call | solution.py:228
  78.2 2.3 %collective-permute-start.31 = (bf16[50,16,128]{2,1,0:T(8,128)(2,1)S(1)}, bf16[50,16,128]{2,1,0:T(8,128)(2,1)S(1)}, u32[]{:S(2)}, u32[]{:S(2)}) collective-permute-start(bf16[50,16,128]{2,1,0:T(8,128)(2,1)S(1)} %get-tuple-element.76), channel_id=1, source_target_pairs={{0,16},{1,65},{2,18},{3,67},{4,20},{5,69},{6,22},{7,71},{8,24},{9,... | collective-permute-start | bytes 614408 | tf_op jit(solution)/shard_map/ppermute | solution.py:24
  80.5 1.4 %collective-permute-start.32 = (bf16[50,16,128]{2,1,0:T(8,128)(2,1)S(1)}, bf16[50,16,128]{2,1,0:T(8,128)(2,1)S(1)}, u32[]{:S(2)}, u32[]{:S(2)}) collective-permute-start(bf16[50,16,128]{2,1,0:T(8,128)(2,1)S(1)} %get-tuple-element.77), channel_id=1, source_target_pairs={{0,24},{1,97},{2,26},{3,99},{4,28},{5,101},{6,30},{7,103},{8,0},{9... | collective-permute-start | bytes 614408 | tf_op jit(solution)/shard_map/ppermute | solution.py:24
  81.9 1.0 collective-permute-start.28
  82.9 5.4 %collective-permute-done.28.received = bf16[2,32,1152]{2,1,0:T(8,128)(2,1)S(1)} collective-permute-done((bf16[2,32,1152]{2,1,0:T(8,128)(2,1)S(1)}, bf16[2,32,1152]{2,1,0:T(8,128)(2,1)S(1)}, u32[]{:S(2)}, u32[]{:S(2)}) %collective-permute-start.28) | collective-permute-done | bytes 147488 | tf_op jit(solution)/shard_map/ppermute | solution.py:24
  89.4 2.6 %collective-permute-start.34 = (bf16[32,1024]{1,0:T(8,128)(2,1)S(1)}, bf16[32,1024]{1,0:T(8,128)(2,1)S(1)}, u32[]{:S(2)}, u32[]{:S(2)}) collective-permute-start(bf16[32,1024]{1,0:T(8,128)(2,1)S(1)} %get-tuple-element.81), channel_id=1, source_target_pairs={{0,64},{1,17},{2,66},{3,19},{4,68},{5,21},{6,70},{7,23},{8,72},{9,... | collective-permute-start | bytes 196616 | tf_op jit(solution)/shard_map/ppermute | solution.py:24
  92.0 0.9 collective-permute-start.35
  92.9 1.9 %factor_first.1 = (f32[32,1024]{1,0:T(8,128)}, f32[32,32]{1,0:T(8,128)S(1)}) custom-call(f32[8,128]{1,0:T(8,128)S(1)} %get-tuple-element.71.gram, bf16[1,32,1152]{2,1,0:T(8,128)(2,1)S(1)} %collective-permute-done.29.received.refs_5_, f32[32,1024]{1,0:T(8,128)S(1)} %get-tuple-element.73.panel), custom_call_target="tpu_custom_call" | custom-call | flops 1000000 | bytes 10000000 | tf_op jit(solution)/shard_map/factor_first/pallas_call | solution.py:493
  95.3 0.9 collective-permute-done.35.refs_4_
  96.9 1.2 collective-permute-done.36.other
  98.0 19.9 %all_to_all.5.gram = f32[64,8,128]{2,1,0:T(8,128)S(1)} all-to-all(f32[64,8,128]{2,1,0:T(8,128)S(1)} %total_gram.1), channel_id=1, replica_groups=mesh['z'=4,'x'=4,'y'=4,'core'=2] {'z','x','y'}, dimensions={0} | all-to-all | bytes 524288 | tf_op jit(solution)/shard_map/all_to_all | solution.py:430
  117.9 2.0 %factor_second.1 = f32[32,1024]{1,0:T(8,128)} custom-call(f32[64,8,128]{2,1,0:T(8,128)S(1)} %all_to_all.5.gram, f32[32,1024]{1,0:T(8,128)S(1)} %get-tuple-element.85.panel), custom_call_target="tpu_custom_call" | custom-call | tf_op jit(solution)/shard_map/factor_second/pallas_call | solution.py:505
  (77 shorter events, 9.0 us)
Async XLA Ops:
  0.6 7.0 %collective-permute-start.3 = (bf16[32,1024]{1,0:T(8,128)(2,1)}, bf16[32,1024]{1,0:T(8,128)(2,1)S(1)}, u32[]{:S(2)}, u32[]{:S(2)}) collective-permute-start(bf16[32,1024]{1,0:T(8,128)(2,1)} %bitcast.5), channel_id=1, source_target_pairs={{0,2},{1,7},{2,0},{3,5},{4,6},{5,3},{6,4},{7,1},{8,10},{9,15},{10,... | collective-permute-start | bytes 196616 | tf_op jit(solution)/shard_map/ppermute | solution.py:24
  2.4 6.3 %collective-permute-start.2 = (bf16[32,1024]{1,0:T(8,128)(2,1)}, bf16[32,1024]{1,0:T(8,128)(2,1)S(1)}, u32[]{:S(2)}, u32[]{:S(2)}) collective-permute-start(bf16[32,1024]{1,0:T(8,128)(2,1)} %bitcast.6), channel_id=1, source_target_pairs={{0,96},{1,25},{2,98},{3,27},{4,100},{5,29},{6,102},{7,31},{8,104},... | collective-permute-start | bytes 196616 | tf_op jit(solution)/shard_map/ppermute | solution.py:24
  6.4 6.1 %collective-permute-start.1 = (bf16[32,1024]{1,0:T(8,128)(2,1)}, bf16[32,1024]{1,0:T(8,128)(2,1)S(1)}, u32[]{:S(2)}, u32[]{:S(2)}) collective-permute-start(bf16[32,1024]{1,0:T(8,128)(2,1)} %bitcast.7), channel_id=1, source_target_pairs={{0,64},{1,17},{2,66},{3,19},{4,68},{5,21},{6,70},{7,23},{8,72},{9,... | collective-permute-start | bytes 196616 | tf_op jit(solution)/shard_map/ppermute | solution.py:24
  6.4 6.4 %collective-permute-start = (bf16[32,1024]{1,0:T(8,128)(2,1)}, bf16[32,1024]{1,0:T(8,128)(2,1)S(1)}, u32[]{:S(2)}, u32[]{:S(2)}) collective-permute-start(bf16[32,1024]{1,0:T(8,128)(2,1)} %bitcast.8), channel_id=1, source_target_pairs={{0,32},{1,9},{2,34},{3,11},{4,36},{5,13},{6,38},{7,15},{8,40},{9,1... | collective-permute-start | bytes 196616 | tf_op jit(solution)/shard_map/ppermute | solution.py:24
  12.8 0.8 copy-start.1
  13.7 6.7 %collective-permute-start.4 = (bf16[2,32,1024]{2,1,0:T(8,128)(2,1)S(1)}, bf16[2,32,1024]{2,1,0:T(8,128)(2,1)S(1)}, u32[]{:S(2)}, u32[]{:S(2)}) collective-permute-start(bf16[2,32,1024]{2,1,0:T(8,128)(2,1)S(1)} %get-tuple-element.44), channel_id=1, source_target_pairs={{0,6},{1,3},{2,4},{3,1},{4,2},{5,7},{6,0},{7,5},{8,14},{9,11},{10,... | collective-permute-start | bytes 393224 | tf_op jit(solution)/shard_map/ppermute | solution.py:24
  15.9 12.9 %collective-permute-start.11 = (bf16[66,16,128]{2,1,0:T(8,128)(2,1)S(1)}, bf16[66,16,128]{2,1,0:T(8,128)(2,1)S(1)}, u32[]{:S(2)}, u32[]{:S(2)}) collective-permute-start(bf16[66,16,128]{2,1,0:T(8,128)(2,1)S(1)} %get-tuple-element.50.g0), channel_id=1, source_target_pairs={{0,24},{1,97},{2,26},{3,99},{4,28},{5,101},{6,30},{7,103},{8,0},{9... | collective-permute-start | bytes 811016 | tf_op jit(solution)/shard_map/ppermute | solution.py:24
  18.7 10.1 %collective-permute-start.10 = (bf16[66,16,128]{2,1,0:T(8,128)(2,1)S(1)}, bf16[66,16,128]{2,1,0:T(8,128)(2,1)S(1)}, u32[]{:S(2)}, u32[]{:S(2)}) collective-permute-start(bf16[66,16,128]{2,1,0:T(8,128)(2,1)S(1)} %get-tuple-element.50.g0), channel_id=1, source_target_pairs={{0,16},{1,65},{2,18},{3,67},{4,20},{5,69},{6,22},{7,71},{8,24},{9,... | collective-permute-start | bytes 811016 | tf_op jit(solution)/shard_map/ppermute | solution.py:24
  19.5 10.1 %collective-permute-start.9 = (bf16[66,16,128]{2,1,0:T(8,128)(2,1)S(1)}, bf16[66,16,128]{2,1,0:T(8,128)(2,1)S(1)}, u32[]{:S(2)}, u32[]{:S(2)}) collective-permute-start(bf16[66,16,128]{2,1,0:T(8,128)(2,1)S(1)} %get-tuple-element.50.g0), channel_id=1, source_target_pairs={{0,8},{1,33},{2,10},{3,35},{4,12},{5,37},{6,14},{7,39},{8,16},{9,4... | collective-permute-start | bytes 811016 | tf_op jit(solution)/shard_map/ppermute | solution.py:24
  20.4 6.1 %collective-permute-start.5 = (bf16[4,32,1024]{2,1,0:T(8,128)(2,1)S(1)}, bf16[4,32,1024]{2,1,0:T(8,128)(2,1)S(1)}, u32[]{:S(2)}, u32[]{:S(2)}) collective-permute-start(bf16[4,32,1024]{2,1,0:T(8,128)(2,1)S(1)} %constant_dynamic-update-slice_fusion.h0), channel_id=1, source_target_pairs={{0,1},{1,0},{2,3},{3,2},{4,5},{5,4},{6,7},{7,6},{8,9},{9,8},{10,11... | collective-permute-start | bytes 786440 | tf_op jit(solution)/shard_map/ppermute | solution.py:24
  21.9 2.8 %copy-start = (bf16[3,1024,1024]{2,1,0:T(8,128)(2,1)S(1)}, bf16[3,1024,1024]{2,1,0:T(8,128)(2,1)}, u32[]{:S(2)}) copy-start(bf16[3,1024,1024]{2,1,0:T(8,128)(2,1)} %blocks.3) | copy-start | bytes 18874372
  29.6 40.4 %slice-start = ((s8[6291456]{0:T(1024)(128)(4,1)}), s8[2097152]{0:T(1024)(128)(4,1)S(1)}, s32[]{:S(2)}) async-start(s8[6291456]{0:T(1024)(128)(4,1)} %bitcast.3), calls=%async_computation.1 | async-start | bytes 4194304
  32.1 4.4 %collective-permute-start.12 = (f16[4,32,1152]{2,1,0:T(8,128)(2,1)S(1)}, f16[4,32,1152]{2,1,0:T(8,128)(2,1)S(1)}, u32[]{:S(2)}, u32[]{:S(2)}) collective-permute-start(f16[4,32,1152]{2,1,0:T(8,128)(2,1)S(1)} %convert_element_type.60), channel_id=1, source_target_pairs={{0,1},{1,0},{2,3},{3,2},{4,5},{5,4},{6,7},{7,6},{8,9},{9,8},{10,11... | collective-permute-start | bytes 884744 | tf_op jit(solution)/shard_map/ppermute | solution.py:24
  32.3 7.4 %collective-permute-start.8 = (f16[50,16,128]{2,1,0:T(8,128)(2,1)S(1)}, f16[50,16,128]{2,1,0:T(8,128)(2,1)S(1)}, u32[]{:S(2)}, u32[]{:S(2)}) collective-permute-start(f16[50,16,128]{2,1,0:T(8,128)(2,1)S(1)} %convert_element_type.58), channel_id=1, source_target_pairs={{0,24},{1,97},{2,26},{3,99},{4,28},{5,101},{6,30},{7,103},{8,0},{9... | collective-permute-start | bytes 614408 | tf_op jit(solution)/shard_map/ppermute | solution.py:24
  34.2 7.4 %collective-permute-start.7 = (f16[50,16,128]{2,1,0:T(8,128)(2,1)S(1)}, f16[50,16,128]{2,1,0:T(8,128)(2,1)S(1)}, u32[]{:S(2)}, u32[]{:S(2)}) collective-permute-start(f16[50,16,128]{2,1,0:T(8,128)(2,1)S(1)} %convert_element_type.56), channel_id=1, source_target_pairs={{0,16},{1,65},{2,18},{3,67},{4,20},{5,69},{6,22},{7,71},{8,24},{9,... | collective-permute-start | bytes 614408 | tf_op jit(solution)/shard_map/ppermute | solution.py:24
  35.6 34.3 %slice-start.1 = ((s8[6291456]{0:T(1024)(128)(4,1)}), s8[4194304]{0:T(1024)(128)(4,1)S(1)}, s32[]{:S(2)}) async-start(s8[6291456]{0:T(1024)(128)(4,1)} %bitcast.3), calls=%async_computation.2 | async-start | bytes 8388608
  35.7 8.0 %collective-permute-start.6 = (f16[50,16,128]{2,1,0:T(8,128)(2,1)S(1)}, f16[50,16,128]{2,1,0:T(8,128)(2,1)S(1)}, u32[]{:S(2)}, u32[]{:S(2)}) collective-permute-start(f16[50,16,128]{2,1,0:T(8,128)(2,1)S(1)} %convert_element_type.54), channel_id=1, source_target_pairs={{0,8},{1,33},{2,10},{3,35},{4,12},{5,37},{6,14},{7,39},{8,16},{9,4... | collective-permute-start | bytes 614408 | tf_op jit(solution)/shard_map/ppermute | solution.py:24
  36.8 11.7 %collective-permute-start.13 = (f16[2,32,1152]{2,1,0:T(8,128)(2,1)S(1)}, f16[2,32,1152]{2,1,0:T(8,128)(2,1)S(1)}, u32[]{:S(2)}, u32[]{:S(2)}) collective-permute-start(f16[2,32,1152]{2,1,0:T(8,128)(2,1)S(1)} %convert_element_type.62), channel_id=1, source_target_pairs={{0,6},{1,3},{2,4},{3,1},{4,2},{5,7},{6,0},{7,5},{8,14},{9,11},{10,... | collective-permute-start | bytes 442376 | tf_op jit(solution)/shard_map/ppermute | solution.py:24
  44.7 4.4 %collective-permute-start.16 = (f16[32,1152]{1,0:T(8,128)(2,1)S(1)}, f16[32,1152]{1,0:T(8,128)(2,1)S(1)}, u32[]{:S(2)}, u32[]{:S(2)}) collective-permute-start(f16[32,1152]{1,0:T(8,128)(2,1)S(1)} %convert_element_type.68), channel_id=1, source_target_pairs={{0,96},{1,25},{2,98},{3,27},{4,100},{5,29},{6,102},{7,31},{8,104},... | collective-permute-start | bytes 221192 | tf_op jit(solution)/shard_map/ppermute | solution.py:24
  44.9 5.9 %collective-permute-start.15 = (f16[32,1152]{1,0:T(8,128)(2,1)S(1)}, f16[32,1152]{1,0:T(8,128)(2,1)S(1)}, u32[]{:S(2)}, u32[]{:S(2)}) collective-permute-start(f16[32,1152]{1,0:T(8,128)(2,1)S(1)} %convert_element_type.66), channel_id=1, source_target_pairs={{0,64},{1,17},{2,66},{3,19},{4,68},{5,21},{6,70},{7,23},{8,72},{9,... | collective-permute-start | bytes 221192 | tf_op jit(solution)/shard_map/ppermute | solution.py:24
  47.1 5.6 %collective-permute-start.14 = (f16[32,1152]{1,0:T(8,128)(2,1)S(1)}, f16[32,1152]{1,0:T(8,128)(2,1)S(1)}, u32[]{:S(2)}, u32[]{:S(2)}) collective-permute-start(f16[32,1152]{1,0:T(8,128)(2,1)S(1)} %convert_element_type.64), channel_id=1, source_target_pairs={{0,32},{1,9},{2,34},{3,11},{4,36},{5,13},{6,38},{7,15},{8,40},{9,1... | collective-permute-start | bytes 221192 | tf_op jit(solution)/shard_map/ppermute | solution.py:24
  48.7 4.4 %collective-permute-start.17 = (f16[1,32,1152]{2,1,0:T(8,128)(2,1)S(1)}, f16[1,32,1152]{2,1,0:T(8,128)(2,1)S(1)}, u32[]{:S(2)}, u32[]{:S(2)}) collective-permute-start(f16[1,32,1152]{2,1,0:T(8,128)(2,1)S(1)} %convert_element_type.70), channel_id=1, source_target_pairs={{0,2},{1,7},{2,0},{3,5},{4,6},{5,3},{6,4},{7,1},{8,10},{9,15},{10,... | collective-permute-start | bytes 221192 | tf_op jit(solution)/shard_map/ppermute | solution.py:24
  53.4 8.2 %collective-permute-start.20 = (bf16[32,1152]{1,0:T(8,128)(2,1)S(1)}, bf16[32,1152]{1,0:T(8,128)(2,1)S(1)}, u32[]{:S(2)}, u32[]{:S(2)}) collective-permute-start(bf16[32,1152]{1,0:T(8,128)(2,1)S(1)} %get-tuple-element.60.refs_0_), channel_id=1, source_target_pairs={{0,96},{1,25},{2,98},{3,27},{4,100},{5,29},{6,102},{7,31},{8,104},... | collective-permute-start | bytes 221192 | tf_op jit(solution)/shard_map/ppermute | solution.py:24
  55.4 6.3 %collective-permute-start.19 = (bf16[32,1152]{1,0:T(8,128)(2,1)S(1)}, bf16[32,1152]{1,0:T(8,128)(2,1)S(1)}, u32[]{:S(2)}, u32[]{:S(2)}) collective-permute-start(bf16[32,1152]{1,0:T(8,128)(2,1)S(1)} %get-tuple-element.60.refs_0_), channel_id=1, source_target_pairs={{0,64},{1,17},{2,66},{3,19},{4,68},{5,21},{6,70},{7,23},{8,72},{9,... | collective-permute-start | bytes 221192 | tf_op jit(solution)/shard_map/ppermute | solution.py:24
  56.1 5.9 %collective-permute-start.18 = (bf16[32,1152]{1,0:T(8,128)(2,1)S(1)}, bf16[32,1152]{1,0:T(8,128)(2,1)S(1)}, u32[]{:S(2)}, u32[]{:S(2)}) collective-permute-start(bf16[32,1152]{1,0:T(8,128)(2,1)S(1)} %get-tuple-element.60.refs_0_), channel_id=1, source_target_pairs={{0,32},{1,9},{2,34},{3,11},{4,36},{5,13},{6,38},{7,15},{8,40},{9,1... | collective-permute-start | bytes 221192 | tf_op jit(solution)/shard_map/ppermute | solution.py:24
  57.4 4.3 %collective-permute-start.21 = (bf16[32,1024]{1,0:T(8,128)(2,1)S(1)}, bf16[32,1024]{1,0:T(8,128)(2,1)S(1)}, u32[]{:S(2)}, u32[]{:S(2)}) collective-permute-start(bf16[32,1024]{1,0:T(8,128)(2,1)S(1)} %get-tuple-element.61.refs_4_), channel_id=1, source_target_pairs={{0,2},{1,7},{2,0},{3,5},{4,6},{5,3},{6,4},{7,1},{8,10},{9,15},{10,... | collective-permute-start | bytes 196616 | tf_op jit(solution)/shard_map/ppermute | solution.py:24
  62.1 6.3 %collective-permute-start.25 = (bf16[2,32,1024]{2,1,0:T(8,128)(2,1)S(1)}, bf16[2,32,1024]{2,1,0:T(8,128)(2,1)S(1)}, u32[]{:S(2)}, u32[]{:S(2)}) collective-permute-start(bf16[2,32,1024]{2,1,0:T(8,128)(2,1)S(1)} %get-tuple-element.63), channel_id=1, source_target_pairs={{0,6},{1,3},{2,4},{3,1},{4,2},{5,7},{6,0},{7,5},{8,14},{9,11},{10,... | collective-permute-start | bytes 393224 | tf_op jit(solution)/shard_map/ppermute | solution.py:24
  64.5 7.7 %collective-permute-start.24 = (bf16[66,16,128]{2,1,0:T(8,128)(2,1)S(1)}, bf16[66,16,128]{2,1,0:T(8,128)(2,1)S(1)}, u32[]{:S(2)}, u32[]{:S(2)}) collective-permute-start(bf16[66,16,128]{2,1,0:T(8,128)(2,1)S(1)} %get-tuple-element.62.g0), channel_id=1, source_target_pairs={{0,24},{1,97},{2,26},{3,99},{4,28},{5,101},{6,30},{7,103},{8,0},{9... | collective-permute-start | bytes 811016 | tf_op jit(solution)/shard_map/ppermute | solution.py:24
  64.8 8.1 %collective-permute-start.23 = (bf16[66,16,128]{2,1,0:T(8,128)(2,1)S(1)}, bf16[66,16,128]{2,1,0:T(8,128)(2,1)S(1)}, u32[]{:S(2)}, u32[]{:S(2)}) collective-permute-start(bf16[66,16,128]{2,1,0:T(8,128)(2,1)S(1)} %get-tuple-element.62.g0), channel_id=1, source_target_pairs={{0,16},{1,65},{2,18},{3,67},{4,20},{5,69},{6,22},{7,71},{8,24},{9,... | collective-permute-start | bytes 811016 | tf_op jit(solution)/shard_map/ppermute | solution.py:24
  65.9 9.8 %collective-permute-start.22 = (bf16[66,16,128]{2,1,0:T(8,128)(2,1)S(1)}, bf16[66,16,128]{2,1,0:T(8,128)(2,1)S(1)}, u32[]{:S(2)}, u32[]{:S(2)}) collective-permute-start(bf16[66,16,128]{2,1,0:T(8,128)(2,1)S(1)} %get-tuple-element.62.g0), channel_id=1, source_target_pairs={{0,8},{1,33},{2,10},{3,35},{4,12},{5,37},{6,14},{7,39},{8,16},{9,4... | collective-permute-start | bytes 811016 | tf_op jit(solution)/shard_map/ppermute | solution.py:24
  68.3 1.6 %collective-permute-start.26 = (bf16[4,32,1024]{2,1,0:T(8,128)(2,1)S(1)}, bf16[4,32,1024]{2,1,0:T(8,128)(2,1)S(1)}, u32[]{:S(2)}, u32[]{:S(2)}) collective-permute-start(bf16[4,32,1024]{2,1,0:T(8,128)(2,1)S(1)} %constant_dynamic-update-slice_fusion.2.h0), channel_id=1, source_target_pairs={{0,1},{1,0},{2,3},{3,2},{4,5},{5,4},{6,7},{7,6},{8,9},{9,8},{10,11... | collective-permute-start | bytes 786440 | tf_op jit(solution)/shard_map/ppermute | solution.py:24
  78.0 3.9 %collective-permute-start.27 = (bf16[4,32,1152]{2,1,0:T(8,128)(2,1)S(1)}, bf16[4,32,1152]{2,1,0:T(8,128)(2,1)S(1)}, u32[]{:S(2)}, u32[]{:S(2)}) collective-permute-start(bf16[4,32,1152]{2,1,0:T(8,128)(2,1)S(1)} %get-tuple-element.66), channel_id=1, source_target_pairs={{0,1},{1,0},{2,3},{3,2},{4,5},{5,4},{6,7},{7,6},{8,9},{9,8},{10,11... | collective-permute-start | bytes 884744 | tf_op jit(solution)/shard_map/ppermute | solution.py:24
  78.1 10.4 %collective-permute-start.30 = (bf16[50,16,128]{2,1,0:T(8,128)(2,1)S(1)}, bf16[50,16,128]{2,1,0:T(8,128)(2,1)S(1)}, u32[]{:S(2)}, u32[]{:S(2)}) collective-permute-start(bf16[50,16,128]{2,1,0:T(8,128)(2,1)S(1)} %get-tuple-element.75), channel_id=1, source_target_pairs={{0,8},{1,33},{2,10},{3,35},{4,12},{5,37},{6,14},{7,39},{8,16},{9,4... | collective-permute-start | bytes 614408 | tf_op jit(solution)/shard_map/ppermute | solution.py:24
  78.2 10.3 %collective-permute-start.31 = (bf16[50,16,128]{2,1,0:T(8,128)(2,1)S(1)}, bf16[50,16,128]{2,1,0:T(8,128)(2,1)S(1)}, u32[]{:S(2)}, u32[]{:S(2)}) collective-permute-start(bf16[50,16,128]{2,1,0:T(8,128)(2,1)S(1)} %get-tuple-element.76), channel_id=1, source_target_pairs={{0,16},{1,65},{2,18},{3,67},{4,20},{5,69},{6,22},{7,71},{8,24},{9,... | collective-permute-start | bytes 614408 | tf_op jit(solution)/shard_map/ppermute | solution.py:24
  80.5 8.0 %collective-permute-start.32 = (bf16[50,16,128]{2,1,0:T(8,128)(2,1)S(1)}, bf16[50,16,128]{2,1,0:T(8,128)(2,1)S(1)}, u32[]{:S(2)}, u32[]{:S(2)}) collective-permute-start(bf16[50,16,128]{2,1,0:T(8,128)(2,1)S(1)} %get-tuple-element.77), channel_id=1, source_target_pairs={{0,24},{1,97},{2,26},{3,99},{4,28},{5,101},{6,30},{7,103},{8,0},{9... | collective-permute-start | bytes 614408 | tf_op jit(solution)/shard_map/ppermute | solution.py:24
  81.9 6.4 %collective-permute-start.28 = (bf16[2,32,1152]{2,1,0:T(8,128)(2,1)S(1)}, bf16[2,32,1152]{2,1,0:T(8,128)(2,1)S(1)}, u32[]{:S(2)}, u32[]{:S(2)}) collective-permute-start(bf16[2,32,1152]{2,1,0:T(8,128)(2,1)S(1)} %get-tuple-element.69), channel_id=1, source_target_pairs={{0,6},{1,3},{2,4},{3,1},{4,2},{5,7},{6,0},{7,5},{8,14},{9,11},{10,... | collective-permute-start | bytes 442376 | tf_op jit(solution)/shard_map/ppermute | solution.py:24
  88.4 4.5 %collective-permute-start.29 = (bf16[1,32,1152]{2,1,0:T(8,128)(2,1)S(1)}, bf16[1,32,1152]{2,1,0:T(8,128)(2,1)S(1)}, u32[]{:S(2)}, u32[]{:S(2)}) collective-permute-start(bf16[1,32,1152]{2,1,0:T(8,128)(2,1)S(1)} %get-tuple-element.72), channel_id=1, source_target_pairs={{0,2},{1,7},{2,0},{3,5},{4,6},{5,3},{6,4},{7,1},{8,10},{9,15},{10,... | collective-permute-start | bytes 221192 | tf_op jit(solution)/shard_map/ppermute | solution.py:24
  89.1 6.2 %collective-permute-start.33 = (bf16[32,1024]{1,0:T(8,128)(2,1)S(1)}, bf16[32,1024]{1,0:T(8,128)(2,1)S(1)}, u32[]{:S(2)}, u32[]{:S(2)}) collective-permute-start(bf16[32,1024]{1,0:T(8,128)(2,1)S(1)} %get-tuple-element.80), channel_id=1, source_target_pairs={{0,32},{1,9},{2,34},{3,11},{4,36},{5,13},{6,38},{7,15},{8,40},{9,1... | collective-permute-start | bytes 196616 | tf_op jit(solution)/shard_map/ppermute | solution.py:24
  89.4 5.9 %collective-permute-start.34 = (bf16[32,1024]{1,0:T(8,128)(2,1)S(1)}, bf16[32,1024]{1,0:T(8,128)(2,1)S(1)}, u32[]{:S(2)}, u32[]{:S(2)}) collective-permute-start(bf16[32,1024]{1,0:T(8,128)(2,1)S(1)} %get-tuple-element.81), channel_id=1, source_target_pairs={{0,64},{1,17},{2,66},{3,19},{4,68},{5,21},{6,70},{7,23},{8,72},{9,... | collective-permute-start | bytes 196616 | tf_op jit(solution)/shard_map/ppermute | solution.py:24
  92.0 4.3 %collective-permute-start.35 = (bf16[32,1024]{1,0:T(8,128)(2,1)S(1)}, bf16[32,1024]{1,0:T(8,128)(2,1)S(1)}, u32[]{:S(2)}, u32[]{:S(2)}) collective-permute-start(bf16[32,1024]{1,0:T(8,128)(2,1)S(1)} %get-tuple-element.82), channel_id=1, source_target_pairs={{0,96},{1,25},{2,98},{3,27},{4,100},{5,29},{6,102},{7,31},{8,104},... | collective-permute-start | bytes 196616 | tf_op jit(solution)/shard_map/ppermute | solution.py:24
  96.8 1.2 collective-permute-start.36
